TPU v7x, 32 devices: a whole 2x2x4 slice. The times are simulated.
32 devices in a mesh: seq: 8 (over z, x), batch: 4 (over y, core).
Axes of the slice: x: 2, y: 2, z: 4, core: 2. Of those that a mesh axis runs over, the one named last changes fastest.
Arguments:
- layer_input: bfloat16 [4, 2048, 1024], P('batch', 'seq'), may hold values from -6 to 6
- seq_lengths: int32 [4, 3], P('batch'), may hold values from 43 to 1962, as said below
- w_attn: bfloat16 [1024, 768], P(('seq', 'batch')), may hold values from -0.1875 to 0.1875
- w_ssm_in: bfloat16 [1024, 3328], P(('seq', 'batch')), may hold values from -0.1875 to 0.1875
- w_dt: bfloat16 [1024, 24], P(('seq', 'batch')), may hold values from -0.1875 to 0.1875
- w_out: bfloat16 [2048, 1024], P(None, ('seq', 'batch')), may hold values from -0.125 to 0.125
- w_gate_up: bfloat16 [1024, 4096], P(('seq', 'batch')), may hold values from -0.1875 to 0.1875
- w_down: bfloat16 [2048, 1024], P(None, ('seq', 'batch')), may hold values from -0.125 to 0.125
- norm_gain: float32 [1024], replicated, may hold values from 0.5 to 1.5
- mlp_gain: float32 [1024], replicated, may hold values from 0.5 to 1.5
- ssm_gain: float32 [1536], replicated, may hold values from 0.5 to 1.5
- conv_w: float32 [4, 1792], replicated, may hold values from -3 to 3
- conv_b: float32 [1792], replicated, may hold values from -2 to 2
- a_log: float32 [24], replicated, may hold values from -9 to 0
- dt_bias: float32 [24], replicated, may hold values from -4 to -1
- d_skip: float32 [24], replicated, may hold values from 0.5 to 1.5
- out_grad: bfloat16 [4, 2048, 1024], P('batch', 'seq'), may hold values from -6 to 6
Outputs:
- layer_out: bfloat16 [4, 2048, 1024], P('batch', 'seq')
- input_grad: float32 [4, 2048, 1024], P('batch', 'seq')
- grad_w_attn: float32 [1024, 768], P(('seq', 'batch'))
- grad_w_ssm_in: float32 [1024, 3328], P(('seq', 'batch'))
- grad_w_dt: float32 [1024, 24], P(('seq', 'batch'))
- grad_w_out: float32 [2048, 1024], P(None, ('seq', 'batch'))
- grad_w_gate_up: float32 [1024, 4096], P(('seq', 'batch'))
- grad_w_down: float32 [2048, 1024], P(None, ('seq', 'batch'))
- grad_norm_gain: float32 [1024], replicated
- grad_mlp_gain: float32 [1024], replicated
- grad_ssm_gain: float32 [1536], replicated
- grad_conv_w: float32 [4, 1792], replicated
- grad_conv_b: float32 [1792], replicated
- grad_a_log: float32 [24], replicated
- grad_dt_bias: float32 [24], replicated
- grad_d_skip: float32 [24], replicated
Inputs may be any that keep to these rules, and one draw needn't show every extreme that they name: Each row of seq_lengths sums to 2048. One sequence of each row, at a place drawn from the seed, begins among the first 256 tokens and ends among the last 256; every other length lies between 43 and 85.
All inputs are finite; a program needn't handle non-finite values.
Results may differ from a plain program's by a relative error of at most 0.019.
Values may be sent and summed in bfloat16 or wider, within the bound.
A program may use at most 384 MiB of HBM per device.

v0:
```python
import math

import jax
import jax.numpy as jnp
from jax import lax
from jax.sharding import PartitionSpec as P

QUERY_HEADS = 8
KEY_VALUE_HEADS = 2
HEAD_SIZE = 64
MH = 24
MP = 64
NS = 128
FF = 2048
CONV = 4
SPAN = 128


HIGHEST = lax.Precision.HIGHEST
NEGATIVE_FILL = -1e30
ROPE_BASE = 10000.0
NORM_EPS = 1e-06
block_limit = 512


def shifted(block, axis, distance):
    devices = range(lax.axis_size(axis))
    route = [(i - distance, i) for i in devices if i - distance in devices]
    return lax.ppermute(block, axis, route)


def prefix(array, axis, combine, identity):
    peers, place = (lax.axis_size(axis), lax.axis_index(axis))
    everything = jax.tree.map(
        lambda part, kind: lax.all_gather(part.astype(kind), axis),
        array,
        (jnp.bfloat16, jnp.bfloat16),
    )
    start = jax.tree.map(
        lambda part, zero: jnp.broadcast_to(jnp.asarray(zero, part.dtype), part.shape),
        array,
        identity,
    )

    def step(k, before):
        reached = k < place
        new = combine(
            before, jax.tree.map(lambda part, own: part[k].astype(own.dtype), everything, array)
        )
        return jax.tree.map(lambda a, b: jnp.where(reached, a, b), new, before)

    return lax.fori_loop(0, peers, step, start)


def entering_2(array, axis, join, neutral):
    count = lax.axis_size(axis)
    place = lax.axis_index(axis)
    ahead = count - 1 - place
    gathered = jax.tree.map(
        lambda a, kind: lax.all_gather(a.astype(kind), axis),
        array,
        jax.tree.map(lambda a: jnp.bfloat16 if a.dtype == jnp.float32 else a.dtype, array),
    )
    state = jax.tree.map(lambda a, e: jnp.zeros_like(a) + jnp.asarray(e, a.dtype), array, neutral)

    def one(step, state):
        source = count - 1 - step
        return join(
            state,
            jax.tree.map(
                lambda a, own: lax.dynamic_index_in_dim(a, source, 0, False).astype(own.dtype),
                gathered,
                array,
            ),
        )

    return lax.fori_loop(0, ahead, one, state)


def rms_scale(value_rows):
    return lax.rsqrt(jnp.mean(value_rows * value_rows, axis=-1, keepdims=True) + NORM_EPS)


def norm_back(value_rows, scales, gains, grads):
    gain_grad = jnp.sum(grads * value_rows * scales, axis=0)
    inner = grads * gains
    coeff = jnp.mean(inner * value_rows, axis=-1, keepdims=True)
    return (scales * (inner - value_rows * scales * scales * coeff), gain_grad)


def rotary_embed(value_rows, device_places, direction):
    half_dim = value_rows.shape[-1] // 2
    freqs = ROPE_BASE ** (-jnp.arange(half_dim, dtype=jnp.float32) / half_dim)
    angles = direction * device_places.astype(jnp.float32)[:, None] * freqs[None, :]
    cosine = jnp.cos(angles)[:, None, :]
    sine = jnp.sin(angles)[:, None, :]
    first_half = value_rows[..., :half_dim]
    second_half = value_rows[..., half_dim:]
    return jnp.concatenate(
        [first_half * cosine - second_half * sine, second_half * cosine + first_half * sine],
        axis=-1,
    )


def segments(lengths, positions):
    ends = jnp.cumsum(lengths)
    passed = ends[None, :] <= positions[:, None]
    segment = jnp.sum(passed.astype(jnp.int32), axis=1)
    device_places = positions - jnp.sum(jnp.where(passed, lengths[None, :], 0), axis=1)
    return (segment, device_places)


def rounded(value_rows):
    narrow = lax.optimization_barrier(value_rows.astype(jnp.bfloat16)).astype(jnp.float32)
    return value_rows + lax.stop_gradient(narrow - value_rows)


def keep_same(running_total):
    return running_total


def conv_mix(extended, ext_segment, conv_weight, conv_bias):
    row_count = extended.shape[0] - (CONV - 1)
    summed = conv_bias[None, :]
    for lagged in range(CONV):
        same_seq = (ext_segment[lagged : lagged + row_count] == ext_segment[CONV - 1 :]).astype(
            extended.dtype
        )
        summed = (
            summed
            + conv_weight[lagged][None, :]
            * extended[lagged : lagged + row_count]
            * same_seq[:, None]
        )
    return jax.nn.silu(summed)


def ssd_blocks(
    inputs_x,
    inputs_b,
    inputs_c,
    inner_all,
    steps_dt,
    log_rates,
    skip_gain,
    segment,
    segment_before,
    state_in,
    rounder,
):
    total_rows = inputs_x.shape[0]
    count_of_blocks = total_rows // SPAN
    decay_rates = jnp.exp(log_rates)
    offsets = jnp.arange(SPAN)
    causal = offsets[:, None] >= offsets[None, :]

    def ssd_advance(carry_in, pieces):
        carried, previous = carry_in
        block_x, block_b, block_c, inner_cb, block_dt, block_seg = pieces
        log_decay = jnp.cumsum(-block_dt * decay_rates[None, :], axis=0)
        allowed = (block_seg[:, None] == block_seg[None, :]) & causal
        spread = log_decay[:, None, :] - log_decay[None, :, :]
        decays = jnp.exp(jnp.where(allowed[:, :, None], spread, NEGATIVE_FILL))
        mixing = rounder(inner_cb[:, :, None] * decays * block_dt[None, :, :])
        result = jnp.einsum("tsh,shp->thp", mixing, block_x, precision=HIGHEST)
        linked = (block_seg == previous).astype(block_x.dtype)
        entering = jnp.exp(log_decay) * linked[:, None]
        result = result + entering[:, :, None] * jnp.einsum(
            "hpn,tn->thp", carried, block_c, precision=HIGHEST
        )
        result = result + skip_gain[None, :, None] * block_x
        same_last = (block_seg == block_seg[-1]).astype(block_x.dtype)
        leaving = jnp.exp(log_decay[-1][None, :] - log_decay) * same_last[:, None] * block_dt
        carried = entering[-1][:, None, None] * carried + jnp.einsum(
            "th,thp,tn->hpn", leaving, block_x, block_b, precision=HIGHEST
        )
        return ((carried, block_seg[-1]), result)

    blocks = (
        inputs_x.reshape(count_of_blocks, SPAN, MH, MP),
        inputs_b.reshape(count_of_blocks, SPAN, NS),
        inputs_c.reshape(count_of_blocks, SPAN, NS),
        inner_all,
        steps_dt.reshape(count_of_blocks, SPAN, MH),
        segment.reshape(count_of_blocks, SPAN),
    )
    (carried, last_seg), results = lax.scan(ssd_advance, (state_in, segment_before), blocks)
    return (results.reshape(inputs_x.shape), carried)


def chain(earlier, later):
    return (earlier[0] * later[0], later[0][:, None, None] * earlier[1] + later[1])


def on_device(
    layer_input,
    seq_lengths,
    w_attn,
    w_ssm_in,
    w_dt,
    w_out,
    w_gate_up,
    w_down,
    norm_gain,
    mlp_gain,
    ssm_gain,
    conv_w,
    conv_b,
    a_log,
    dt_bias,
    d_skip,
    out_grad,
):
    token_rows = layer_input.shape[1]
    query_width = QUERY_HEADS * HEAD_SIZE
    key_value_width = KEY_VALUE_HEADS * HEAD_SIZE
    ssm_width = MH * MP
    xbc_width = ssm_width + 2 * NS
    query_group_width = QUERY_HEADS // KEY_VALUE_HEADS
    score_scale = HEAD_SIZE ** (-0.5)
    seq_lens = seq_lengths[0]
    first_pos = lax.axis_index("seq") * token_rows
    positions = first_pos + jnp.arange(token_rows, dtype=jnp.int32)
    segment, device_places = segments(seq_lens, positions)
    segment_before = segments(seq_lens, positions[:1] - 1)[0][0]
    x_rows = layer_input[0].astype(jnp.float32)
    weights = (
        lax.all_gather(w_attn, ("seq", "batch"), axis=0, tiled=True),
        lax.all_gather(w_ssm_in, ("seq", "batch"), axis=0, tiled=True),
        lax.all_gather(w_dt, ("seq", "batch"), axis=0, tiled=True),
        lax.all_gather(w_out, ("seq", "batch"), axis=1, tiled=True),
        lax.all_gather(w_gate_up, ("seq", "batch"), axis=0, tiled=True),
        lax.all_gather(w_down, ("seq", "batch"), axis=1, tiled=True),
    )
    full_attn, full_ssm, full_dt, full_out, full_gu, full_down = weights
    scale_one = rms_scale(x_rows)
    normed = (x_rows * scale_one * norm_gain).astype(jnp.bfloat16)
    attention_projected = jnp.dot(normed, full_attn, preferred_element_type=jnp.float32)
    ssm_proj = jnp.dot(normed, full_ssm, preferred_element_type=jnp.float32)
    step_proj = jnp.dot(normed, full_dt, preferred_element_type=jnp.float32)
    query_rows = rotary_embed(
        attention_projected[:, :query_width].reshape(token_rows, QUERY_HEADS, HEAD_SIZE),
        device_places,
        1.0,
    ).astype(jnp.bfloat16)
    flattened_keys = (
        rotary_embed(
            attention_projected[:, query_width : query_width + key_value_width].reshape(
                token_rows, KEY_VALUE_HEADS, HEAD_SIZE
            ),
            device_places,
            1.0,
        )
        .astype(jnp.bfloat16)
        .reshape(token_rows, key_value_width)
    )
    flattened_values = attention_projected[:, query_width + key_value_width :].astype(jnp.bfloat16)
    heads_of_queries = query_rows.reshape(token_rows, KEY_VALUE_HEADS, query_group_width, HEAD_SIZE)

    def visible(query_pos, query_seg, key_pos, key_seg):
        return (query_seg[:, None] == key_seg[None, :]) & (query_pos[:, None] >= key_pos[None, :])

    def key_blocks(piece_in):
        incoming_keys, incoming_values = piece_in
        piece_rows = incoming_keys.shape[0]
        rows_per_block = math.gcd(piece_rows, block_limit)
        count_of_blocks = piece_rows // rows_per_block
        starts = jnp.arange(count_of_blocks, dtype=jnp.int32) * rows_per_block
        return (
            (
                incoming_keys.reshape(count_of_blocks, rows_per_block, KEY_VALUE_HEADS, HEAD_SIZE),
                incoming_values.reshape(
                    count_of_blocks, rows_per_block, KEY_VALUE_HEADS, HEAD_SIZE
                ),
                starts,
            ),
            rows_per_block,
        )

    start_state = (
        jnp.full((KEY_VALUE_HEADS, query_group_width, token_rows), NEGATIVE_FILL, jnp.float32),
        jnp.zeros((KEY_VALUE_HEADS, query_group_width, token_rows), jnp.float32),
        jnp.zeros((KEY_VALUE_HEADS, query_group_width, token_rows, HEAD_SIZE), jnp.float32),
    )
    running_total = start_state
    blocks, rows_per_block = key_blocks(
        (
            lax.all_gather(flattened_keys, "seq", axis=0, tiled=True),
            lax.all_gather(flattened_values, "seq", axis=0, tiled=True),
        )
    )

    def attend_advance(state_now, pieces):
        key_blk, value_blk, key_first = pieces
        key_pos = key_first + jnp.arange(rows_per_block, dtype=jnp.int32)
        key_seg = segments(seq_lens, key_pos)[0]
        needed = (key_first <= positions[-1]) & (key_seg[-1] >= segment[0])

        def attend_update(state_in):
            row_max, weight_sum, accumulated = state_in
            scores = (
                jnp.einsum(
                    "qkgd,skd->kgqs", heads_of_queries, key_blk, preferred_element_type=jnp.float32
                )
                * score_scale
            )
            allowed = visible(positions, segment, key_pos, key_seg)[None, None]
            scores = jnp.where(allowed, scores, NEGATIVE_FILL)
            new_max = jnp.maximum(row_max, jnp.max(scores, axis=-1))
            shrink = jnp.exp(row_max - new_max)
            prob_blk = jnp.where(allowed, jnp.exp(scores - new_max[..., None]), 0.0)
            weight_sum = weight_sum * shrink + jnp.sum(prob_blk, axis=-1)
            accumulated = accumulated * shrink[..., None] + jnp.einsum(
                "kgqs,skd->kgqd",
                prob_blk.astype(jnp.bfloat16),
                value_blk,
                preferred_element_type=jnp.float32,
            )
            return (new_max, weight_sum, accumulated)

        return (lax.cond(needed, attend_update, keep_same, state_now), None)

    running_total, unused_out = lax.scan(attend_advance, running_total, blocks)
    row_max, weight_sum, accumulated = running_total
    attn_heads = accumulated / weight_sum[..., None]
    log_total = row_max + jnp.log(weight_sum)
    attended = (
        attn_heads.transpose(2, 0, 1, 3).reshape(token_rows, query_width).astype(jnp.bfloat16)
    )
    gate_z = ssm_proj[:, :ssm_width]
    raw_xbc = ssm_proj[:, ssm_width:]
    rim_rows = shifted(raw_xbc[token_rows - (CONV - 1) :], "seq", 1)
    extended = jnp.concatenate([rim_rows, raw_xbc], axis=0)
    ext_pos = first_pos - (CONV - 1) + jnp.arange(token_rows + CONV - 1, dtype=jnp.int32)
    ext_segment = segments(seq_lens, ext_pos)[0]

    def conv_local(ext_rows, conv_weight, conv_bias):
        return conv_mix(ext_rows, ext_segment, conv_weight, conv_bias)

    conv_out, conv_pullback = jax.vjp(conv_local, extended, conv_w, conv_b)
    block_total = token_rows // SPAN
    narrow_b = conv_out[:, ssm_width : ssm_width + NS].astype(jnp.bfloat16)
    narrow_c = conv_out[:, ssm_width + NS :].astype(jnp.bfloat16)
    inputs_x = (
        conv_out[:, :ssm_width].astype(jnp.bfloat16).astype(jnp.float32).reshape(token_rows, MH, MP)
    )
    inputs_b = narrow_b.astype(jnp.float32)
    inputs_c = narrow_c.astype(jnp.float32)
    inner_all = jnp.einsum(
        "btn,bsn->bts",
        narrow_c.reshape(block_total, SPAN, NS),
        narrow_b.reshape(block_total, SPAN, NS),
        preferred_element_type=jnp.float32,
    )
    steps_dt = jax.nn.softplus(step_proj + dt_bias)

    def ssd_local(block_x, block_b, block_c, inner_in, block_dt, log_rates, skip_gain, carried_in):
        return ssd_blocks(
            block_x,
            block_b,
            block_c,
            inner_in,
            block_dt,
            log_rates,
            skip_gain,
            segment,
            segment_before,
            carried_in,
            rounded,
        )

    zero_state = jnp.zeros((MH, MP, NS), jnp.float32)
    ssm_local, state_local = ssd_local(
        inputs_x, inputs_b, inputs_c, inner_all, steps_dt, a_log, d_skip, zero_state
    )
    running_decay = jnp.cumsum(-steps_dt * jnp.exp(a_log)[None, :], axis=0)
    linked = (segment == segment_before).astype(jnp.float32)
    entering = jnp.exp(running_decay) * linked[:, None]
    through = entering[-1]
    chain_identity = (jnp.ones((MH,), jnp.float32), zero_state)
    unused_rate, state_in = prefix((through, state_local), "seq", chain, chain_identity)
    ssm_out = ssm_local + entering[:, :, None] * jnp.einsum(
        "hpn,tn->thp", state_in, inputs_c, precision=HIGHEST
    )
    ssm_flat = ssm_out.reshape(token_rows, ssm_width)
    silu_z = jax.nn.silu(gate_z)
    gated = ssm_flat * silu_z
    scale_gated = rms_scale(gated)
    ssm_normed = gated * scale_gated * ssm_gain
    joined = jnp.concatenate([attended, ssm_normed.astype(jnp.bfloat16)], axis=1)
    middle = x_rows + jnp.dot(joined, full_out, preferred_element_type=jnp.float32)
    scale_two = rms_scale(middle)
    normed_two = (middle * scale_two * mlp_gain).astype(jnp.bfloat16)
    gate_up = jnp.dot(normed_two, full_gu, preferred_element_type=jnp.float32)
    gate_part = gate_up[:, :FF]
    up_part = gate_up[:, FF:]
    hidden = (jax.nn.silu(gate_part) * up_part).astype(jnp.bfloat16)
    layer_out = middle + jnp.dot(hidden, full_down, preferred_element_type=jnp.float32)
    weights_back = (
        lax.all_gather(w_attn, ("seq", "batch"), axis=0, tiled=True),
        lax.all_gather(w_ssm_in, ("seq", "batch"), axis=0, tiled=True),
        lax.all_gather(w_dt, ("seq", "batch"), axis=0, tiled=True),
        lax.all_gather(w_out, ("seq", "batch"), axis=1, tiled=True),
        lax.all_gather(w_gate_up, ("seq", "batch"), axis=0, tiled=True),
        lax.all_gather(w_down, ("seq", "batch"), axis=1, tiled=True),
    )
    back_attn, back_ssm, back_dt, back_out, back_gu, back_down = weights_back
    grad_rows = out_grad[0]
    g_down = jnp.einsum("tf,td->fd", hidden, grad_rows, preferred_element_type=jnp.float32)
    d_hidden = jnp.einsum("td,fd->tf", grad_rows, back_down, preferred_element_type=jnp.float32)
    sig_gate = jax.nn.sigmoid(gate_part)
    d_gate = d_hidden * up_part * (sig_gate * (1.0 + gate_part * (1.0 - sig_gate)))
    d_up = d_hidden * gate_part * sig_gate
    d_gate_up = jnp.concatenate([d_gate, d_up], axis=1).astype(jnp.bfloat16)
    g_gate_up = jnp.einsum("td,tf->df", normed_two, d_gate_up, preferred_element_type=jnp.float32)
    d_normed_two = jnp.einsum("tf,df->td", d_gate_up, back_gu, preferred_element_type=jnp.float32)
    d_middle_norm, g_mlp_gain = norm_back(middle, scale_two, mlp_gain, d_normed_two)
    d_middle = grad_rows.astype(jnp.float32) + d_middle_norm
    d_mixer = d_middle.astype(jnp.bfloat16)
    g_out = jnp.einsum("tc,td->cd", joined, d_mixer, preferred_element_type=jnp.float32)
    d_joined = jnp.einsum("td,cd->tc", d_mixer, back_out, preferred_element_type=jnp.float32)
    attended_gradient = d_joined[:, :query_width].astype(jnp.bfloat16)
    d_ssm_normed = d_joined[:, query_width:]
    d_gated, g_ssm_gain = norm_back(gated, scale_gated, ssm_gain, d_ssm_normed)
    d_ssm_out = (d_gated * silu_z).reshape(token_rows, MH, MP)
    sig_z = jax.nn.sigmoid(gate_z)
    d_gate_z = d_gated * ssm_flat * (sig_z * (1.0 + gate_z * (1.0 - sig_z)))
    pull_state = jnp.einsum("th,thp,tn->hpn", entering, d_ssm_out, inputs_c, precision=HIGHEST)
    unused_rate, d_state_out = entering_2((through, pull_state), "seq", chain, chain_identity)
    unused_out, ssd_pullback = jax.vjp(
        ssd_local, inputs_x, inputs_b, inputs_c, inner_all, steps_dt, a_log, d_skip, state_in
    )
    g_inputs_x, g_part_b, g_part_c, g_inner, g_steps, g_a_log, g_d_skip, unused_state = (
        ssd_pullback((d_ssm_out, d_state_out))
    )
    block_b = inputs_b.reshape(block_total, SPAN, NS)
    block_c = inputs_c.reshape(block_total, SPAN, NS)
    g_inputs_c = g_part_c + jnp.einsum("bts,bsn->btn", g_inner, block_b, precision=HIGHEST).reshape(
        token_rows, NS
    )
    g_inputs_b = g_part_b + jnp.einsum("bts,btn->bsn", g_inner, block_c, precision=HIGHEST).reshape(
        token_rows, NS
    )
    d_step_pre = g_steps * jax.nn.sigmoid(step_proj + dt_bias)
    g_dt_bias = jnp.sum(d_step_pre, axis=0)
    d_step_proj = d_step_pre.astype(jnp.bfloat16)
    d_conv_out = jnp.concatenate(
        [g_inputs_x.reshape(token_rows, ssm_width), g_inputs_b, g_inputs_c], axis=1
    )
    g_extended, g_conv_w, g_conv_b = conv_pullback(d_conv_out)
    back_rim = shifted(g_extended[: CONV - 1], "seq", -1)
    d_raw = g_extended[CONV - 1 :] + jnp.concatenate(
        [jnp.zeros((token_rows - (CONV - 1), xbc_width), jnp.float32), back_rim], axis=0
    )
    d_ssm_proj = jnp.concatenate([d_gate_z, d_raw], axis=1).astype(jnp.bfloat16)
    head_gradients = attended_gradient.reshape(
        token_rows, KEY_VALUE_HEADS, query_group_width, HEAD_SIZE
    )
    delta = jnp.einsum("qkgd,kgqd->kgq", head_gradients.astype(jnp.float32), attn_heads)
    running_total = jnp.zeros(
        (KEY_VALUE_HEADS, query_group_width, token_rows, HEAD_SIZE), jnp.float32
    )
    blocks, query_rows_per_block = key_blocks(
        (
            lax.all_gather(flattened_keys, "seq", axis=0, tiled=True),
            lax.all_gather(flattened_values, "seq", axis=0, tiled=True),
        )
    )

    def query_advance(grad_now, pieces):
        key_blk, value_blk, key_first = pieces
        key_pos = key_first + jnp.arange(query_rows_per_block, dtype=jnp.int32)
        key_seg = segments(seq_lens, key_pos)[0]
        needed = (key_first <= positions[-1]) & (key_seg[-1] >= segment[0])

        def query_update(grad_in):
            scores = (
                jnp.einsum(
                    "qkgd,skd->kgqs", heads_of_queries, key_blk, preferred_element_type=jnp.float32
                )
                * score_scale
            )
            allowed = visible(positions, segment, key_pos, key_seg)[None, None]
            prob_blk = jnp.where(allowed, jnp.exp(scores - log_total[..., None]), 0.0)
            d_prob = jnp.einsum(
                "qkgd,skd->kgqs", head_gradients, value_blk, preferred_element_type=jnp.float32
            )
            d_score = (prob_blk * (d_prob - delta[..., None])).astype(jnp.bfloat16)
            return (
                grad_in
                + jnp.einsum("kgqs,skd->kgqd", d_score, key_blk, preferred_element_type=jnp.float32)
                * score_scale
            )

        return (lax.cond(needed, query_update, keep_same, grad_now), None)

    running_total, unused_out = lax.scan(query_advance, running_total, blocks)
    d_queries = running_total
    all_lse, all_delta = (
        lax.all_gather(log_total.reshape(QUERY_HEADS, token_rows), "seq", axis=1, tiled=True),
        lax.all_gather(delta.reshape(QUERY_HEADS, token_rows), "seq", axis=1, tiled=True),
    )
    heads_of_keys = flattened_keys.reshape(token_rows, KEY_VALUE_HEADS, HEAD_SIZE)
    heads_of_values = flattened_values.reshape(token_rows, KEY_VALUE_HEADS, HEAD_SIZE)
    zeroed_key_value = jnp.zeros((token_rows, KEY_VALUE_HEADS, HEAD_SIZE), jnp.float32)
    running_total = (zeroed_key_value, zeroed_key_value)
    incoming_query = lax.all_gather(
        query_rows.reshape(token_rows, query_width), "seq", axis=0, tiled=True
    )
    input_gradient_rows = lax.all_gather(attended_gradient, "seq", axis=0, tiled=True)
    piece_rows = incoming_query.shape[0]
    key_rows_per_block = math.gcd(piece_rows, block_limit)
    count_of_blocks = piece_rows // key_rows_per_block
    blocks = (
        incoming_query.reshape(
            count_of_blocks, key_rows_per_block, KEY_VALUE_HEADS, query_group_width, HEAD_SIZE
        ),
        input_gradient_rows.reshape(
            count_of_blocks, key_rows_per_block, KEY_VALUE_HEADS, query_group_width, HEAD_SIZE
        ),
        jnp.arange(count_of_blocks, dtype=jnp.int32) * key_rows_per_block,
    )

    def key_advance(grad_now, pieces):
        query_blk, dgrad_blk, query_first = pieces
        query_pos = query_first + jnp.arange(key_rows_per_block, dtype=jnp.int32)
        query_seg = segments(seq_lens, query_pos)[0]
        needed = (query_pos[-1] >= positions[0]) & (query_seg[0] <= segment[-1])

        def key_update(grad_in):
            key_grad, value_grad = grad_in
            blk_lse = lax.dynamic_slice_in_dim(all_lse, query_first, key_rows_per_block, 1).reshape(
                KEY_VALUE_HEADS, query_group_width, key_rows_per_block
            )
            blk_delta = lax.dynamic_slice_in_dim(
                all_delta, query_first, key_rows_per_block, 1
            ).reshape(KEY_VALUE_HEADS, query_group_width, key_rows_per_block)
            scores = (
                jnp.einsum(
                    "qkgd,skd->kgqs", query_blk, heads_of_keys, preferred_element_type=jnp.float32
                )
                * score_scale
            )
            allowed = visible(query_pos, query_seg, positions, segment)[None, None]
            prob_blk = jnp.where(allowed, jnp.exp(scores - blk_lse[..., None]), 0.0)
            d_prob = jnp.einsum(
                "qkgd,skd->kgqs", dgrad_blk, heads_of_values, preferred_element_type=jnp.float32
            )
            d_score = (prob_blk * (d_prob - blk_delta[..., None])).astype(jnp.bfloat16)
            value_grad = value_grad + jnp.einsum(
                "kgqs,qkgd->skd",
                prob_blk.astype(jnp.bfloat16),
                dgrad_blk,
                preferred_element_type=jnp.float32,
            )
            key_grad = (
                key_grad
                + jnp.einsum(
                    "kgqs,qkgd->skd", d_score, query_blk, preferred_element_type=jnp.float32
                )
                * score_scale
            )
            return (key_grad, value_grad)

        return (lax.cond(needed, key_update, keep_same, grad_now), None)

    running_total, unused_out = lax.scan(key_advance, running_total, blocks)
    d_keys, d_values = running_total
    d_query_flat = rotary_embed(
        d_queries.transpose(2, 0, 1, 3).reshape(token_rows, QUERY_HEADS, HEAD_SIZE),
        device_places,
        -1.0,
    ).reshape(token_rows, query_width)
    d_key_flat = rotary_embed(d_keys, device_places, -1.0).reshape(token_rows, key_value_width)
    d_attn_proj = jnp.concatenate(
        [d_query_flat, d_key_flat, d_values.reshape(token_rows, key_value_width)], axis=1
    ).astype(jnp.bfloat16)
    g_attn = jnp.einsum("td,tc->dc", normed, d_attn_proj, preferred_element_type=jnp.float32)
    g_ssm_in = jnp.einsum("td,tc->dc", normed, d_ssm_proj, preferred_element_type=jnp.float32)
    g_dt = jnp.einsum("td,tc->dc", normed, d_step_proj, preferred_element_type=jnp.float32)
    d_normed = (
        jnp.einsum("tc,dc->td", d_attn_proj, back_attn, preferred_element_type=jnp.float32)
        + jnp.einsum("tc,dc->td", d_ssm_proj, back_ssm, preferred_element_type=jnp.float32)
        + jnp.einsum("tc,dc->td", d_step_proj, back_dt, preferred_element_type=jnp.float32)
    )
    d_input_norm, g_norm_gain = norm_back(x_rows, scale_one, norm_gain, d_normed)
    input_grad = d_middle + d_input_norm
    grad_attn, grad_ssm_in, grad_dt, grad_out, grad_gate_up, grad_down = (
        lax.psum_scatter(g_attn, ("seq", "batch"), scatter_dimension=0, tiled=True),
        lax.psum_scatter(g_ssm_in, ("seq", "batch"), scatter_dimension=0, tiled=True),
        lax.psum_scatter(g_dt, ("seq", "batch"), scatter_dimension=0, tiled=True),
        lax.psum_scatter(g_out, ("seq", "batch"), scatter_dimension=1, tiled=True),
        lax.psum_scatter(g_gate_up, ("seq", "batch"), scatter_dimension=0, tiled=True),
        lax.psum_scatter(g_down, ("seq", "batch"), scatter_dimension=1, tiled=True),
    )
    small_sums = lax.psum(
        (g_norm_gain, g_mlp_gain, g_ssm_gain, g_conv_w, g_conv_b, g_a_log, g_dt_bias, g_d_skip),
        ("seq", "batch"),
    )
    return (
        layer_out.astype(jnp.bfloat16)[None],
        input_grad[None],
        grad_attn,
        grad_ssm_in,
        grad_dt,
        grad_out,
        grad_gate_up,
        grad_down,
        small_sums[0],
        small_sums[1],
        small_sums[2],
        small_sums[3],
        small_sums[4],
        small_sums[5],
        small_sums[6],
        small_sums[7],
    )


def solution(mesh):
    return jax.shard_map(
        on_device,
        mesh=mesh,
        in_specs=(
            P("batch", "seq", None),
            P("batch", None),
            P(("seq", "batch"), None),
            P(("seq", "batch"), None),
            P(("seq", "batch"), None),
            P(None, ("seq", "batch")),
            P(("seq", "batch"), None),
            P(None, ("seq", "batch")),
            P(),
            P(),
            P(),
            P(),
            P(),
            P(),
            P(),
            P(),
            P("batch", "seq", None),
        ),
        out_specs=(
            P("batch", "seq", None),
            P("batch", "seq", None),
            P(("seq", "batch"), None),
            P(("seq", "batch"), None),
            P(("seq", "batch"), None),
            P(None, ("seq", "batch")),
            P(("seq", "batch"), None),
            P(None, ("seq", "batch")),
            P(),
            P(),
            P(),
            P(),
            P(),
            P(),
            P(),
            P(),
        ),
        check_vma=False,
    )
```

profile of v0, /device:TPU:0, one launch (start us, length us, event | category | flops | bytes accessed | tf_op | source)
XLA Modules:
  0.0 1723.4 jit_solution(1969058943293461801)
XLA Ops:
  9.3 44.5 %all-gather.2 = bf16[32,32,24]{1,2,0:T(8,128)(2,1)S(1)} all-gather(bf16[1,32,24]{1,2,0:T(8,128)(2,1)} %bitcast.842), channel_id=1, replica_groups=mesh['seq'=8,'batch'=4] {'seq','batch'}, dimensions={0}, use_global_device_ids=true | all-gather | bytes 50688 | tf_op jit(solution)/shard_map/all_gather | solution.py:230
  62.5 22.9 %all-gather.16.cloned.1.call-done = bf16[1024,3328]{1,0:T(8,128)(2,1)} async-done(((bf16[32,3328]{1,0:T(8,128)(2,1)}), bf16[1024,3328]{1,0:T(8,128)(2,1)}) %all-gather.16.cloned.1.call-update) | async-done | bytes 6815760 | tf_op jit(solution)/shard_map/all_gather | solution.py:229
  85.4 4.9 fusion.266
  109.1 61.9 %while.172 = (s32[]{:T(128)}, f32[24,64,128]{2,1,0:T(8,128)S(1)}, s32[]{:T(128)}, f32[2,128,24,64]{1,0,3,2:T(2,128)}, f32[2,128,24]{2,1,0:T(8,128)S(1)}, /*index...) while((s32[]{:T(128)}, f32[24,64,128]{2,1,0:T(8,128)S(1)}, ...), condition=%wide.region_16.17_spmd.clone, body=%wide.region_14.16_spmd.clone.sunk | while | flops 912915968 | bytes 10969862 | solution.py:187
  111.6 4.2 fusion.362
  120.5 19.0 %dynamic_update_slice.226 = f32[2,128,24,64]{1,0,3,2:T(2,128)} dynamic-update-slice(f32[2,128,24,64]{1,0,3,2:T(2,128)} %get-tuple-element.3924, f32[1,128,24,64]{1,0,3,2:T(1,128)S(1)} %bitcast.787, s32[]{:T(128)S(6)} %copy.479, s32[]{:T(128)} %constant.390.clone.1..sunk.1, s32[]{:T(128)} %constant.390.clone.1..sunk.1, s32[]{:T(128)} %constant.390.clone.1..sunk.1) | dynamic-update-slice | bytes 1572868 | tf_op jit(solution)/shard_map/while/body/jit(dynamic_update_index_in_dim)/dynamic_update_slice | solution.py:187
  142.5 4.2 fusion.362
  151.4 19.0 %dynamic_update_slice.226 = f32[2,128,24,64]{1,0,3,2:T(2,128)} dynamic-update-slice(f32[2,128,24,64]{1,0,3,2:T(2,128)} %get-tuple-element.3924, f32[1,128,24,64]{1,0,3,2:T(1,128)S(1)} %bitcast.787, s32[]{:T(128)S(6)} %copy.479, s32[]{:T(128)} %constant.390.clone.1..sunk.1, s32[]{:T(128)} %constant.390.clone.1..sunk.1, s32[]{:T(128)} %constant.390.clone.1..sunk.1) | dynamic-update-slice | bytes 1572868 | tf_op jit(solution)/shard_map/while/body/jit(dynamic_update_index_in_dim)/dynamic_update_slice | solution.py:187
  176.9 18.2 %all-gather.3 = bf16[8,1,24]{2,1,0:T(2,128)(2,1)S(1)} all-gather(bf16[1,1,24]{2,1,0:T(2,128)(2,1)S(1)} %bitcast.846), channel_id=1, replica_groups=mesh['seq'=8,'batch'=4] {'seq'}, dimensions={0}, use_global_device_ids=true | all-gather | bytes 432 | tf_op jit(solution)/shard_map/all_gather | solution.py:35
  200.3 34.8 %all_gather.63 = bf16[2048,128]{0,1:T(8,128)(2,1)} all-gather(bf16[256,128]{0,1:T(8,128)(2,1)S(1)} %bitcast.792), channel_id=1, replica_groups=mesh['seq'=8,'batch'=4] {'seq'}, dimensions={0}, use_global_device_ids=true | all-gather | bytes 589824 | tf_op jit(solution)/shard_map/all_gather | solution.py:288
  241.3 33.8 %all_gather.64 = bf16[2048,128]{1,0:T(8,128)(2,1)} all-gather(bf16[256,128]{1,0:T(8,128)(2,1)S(1)} %slice.377), channel_id=1, replica_groups=mesh['seq'=8,'batch'=4] {'seq'}, dimensions={0}, use_global_device_ids=true | all-gather | bytes 589824 | tf_op jit(solution)/shard_map/all_gather | solution.py:289
  284.5 29.2 %while.167 = (s32[]{:T(128)}, f32[2,4,256]{2,1,0:T(4,128)S(1)}, f32[2,4,256]{2,1,0:T(4,128)S(1)}, f32[2,4,256,64]{2,3,1,0:T(8,128)}, s32[4]{0:T(128)S(1)}, /*ind...) while((s32[]{:T(128)}, f32[2,4,256]{2,1,0:T(4,128)S(1)}, ...), condition=%wide.region_11.12_spmd, body=%wide.region_5.11_spmd.sunk | while | flops 282731520 | bytes 19025312 | solution.py:323
  290.1 6.6 conditional.6
  322.4 15.3 while.173
  349.0 4.8 multiply_reduce_fusion.10
  353.8 29.2 %all-gather.20.cloned.1.call-done = bf16[1024,4096]{1,0:T(8,128)(2,1)} async-done(((bf16[32,4096]{1,0:T(8,128)(2,1)}), bf16[1024,4096]{1,0:T(8,128)(2,1)}) %all-gather.20.cloned.1.call-update) | async-done | bytes 8388624 | tf_op jit(solution)/shard_map/all_gather | solution.py:232
  383.0 8.1 fusion.262
  391.1 55.3 %all-gather.22.cloned.1.call-done = bf16[2048,1024]{0,1:T(8,128)(2,1)} async-done(((bf16[2048,32]{0,1:T(8,128)(2,1)}), bf16[2048,1024]{0,1:T(8,128)(2,1)}) %all-gather.22.cloned.1.call-update) | async-done | bytes 4194320 | tf_op jit(solution)/shard_map/all_gather | solution.py:233
  446.4 6.5 multiply_convert_fusion.1
  460.8 32.6 %all_gather.74 = f32[8,2048]{1,0:T(8,128)} all-gather(f32[8,256]{1,0:T(8,128)S(1)} %reshape.1041), channel_id=1, replica_groups=mesh['seq'=8,'batch'=4] {'seq'}, dimensions={1}, use_global_device_ids=true | all-gather | bytes 73728 | tf_op jit(solution)/shard_map/all_gather | solution.py:500
  493.4 6.0 all-gather.24.cloned.1.call-done
  499.4 4.7 reshape.1040
  504.1 3.6 copy.268
  509.2 4.0 multiply_convert_fusion.4
  524.8 44.6 %while.171 = (s32[]{:T(128)}, f32[24,64,128]{2,1,0:T(8,128)S(1)}, s32[]{:T(128)}, f32[2,128,24]{2,1,0:T(8,128)}, pred[2,128,128,24]{2,3,1,0:T(8,128)(4,1)}, /*in...) while((s32[]{:T(128)}, f32[24,64,128]{2,1,0:T(8,128)S(1)}, ...), condition=%wide.region_39.40_spmd.clone, body=%wide.region_37.39_spmd.clone.sunk | while | flops 611135488 | bytes 15344781 | solution.py:187
  577.1 32.7 %all_gather.76 = f32[8,2048]{1,0:T(8,128)} all-gather(f32[8,256]{1,0:T(8,128)S(1)} %reshape.1044), channel_id=1, replica_groups=mesh['seq'=8,'batch'=4] {'seq'}, dimensions={1}, use_global_device_ids=true | all-gather | bytes 73728 | tf_op jit(solution)/shard_map/all_gather | solution.py:501
  610.0 30.7 %while.168 = (s32[]{:T(128)}, f32[2,4,256,64]{2,3,1,0:T(8,128)S(1)}, s32[4]{0:T(128)S(1)}, s32[256]{0:T(256)S(1)}, s32[1,3]{1,0:T(1,128)S(1)}, /*index=5*/s32[25...) while((s32[]{:T(128)}, f32[2,4,256,64]{2,3,1,0:T(8,128)S(1)}, ...), condition=%wide.region_28.29_spmd, body=%wide.region_24.28_spmd.sunk | while | flops 409605120 | bytes 10653003 | solution.py:497
  616.0 7.7 conditional.7
  619.6 4.1 fusion.29
  642.1 7.5 reshape.1097
  649.6 7.0 copy.269
  656.6 83.0 %while.169 = (s32[]{:T(128)}, f32[256,2,64]{0,2,1:T(8,128)S(1)}, f32[256,2,64]{0,2,1:T(8,128)S(1)}, s32[4]{0:T(128)S(1)}, s32[256]{0:T(256)S(1)}, /*index=5*/s32...) while((s32[]{:T(128)}, f32[256,2,64]{0,2,1:T(8,128)S(1)}, ...), condition=%wide.region_33.34_spmd, body=%wide.region_29.33_spmd.sunk | while | flops 547852800 | bytes 15923617 | solution.py:567
  662.8 14.6 conditional.8
  662.8 3.8 fusion.67
  669.6 4.4 fusion.62
  683.5 14.6 conditional.8
  683.6 3.8 fusion.67
  690.4 4.4 fusion.62
  704.3 14.6 conditional.8
  704.3 3.8 fusion.67
  711.1 4.4 fusion.62
  725.0 14.6 conditional.8
  725.1 3.8 fusion.67
  731.8 4.4 fusion.62
  741.0 13.4 while.170
  758.5 77.5 %while.174 = (s32[]{:T(128)}, f32[24]{0:T(128)}, f32[24]{0:T(128)}, f32[24,64,128]{2,1,0:T(8,128)S(1)}, f32[2,128,24,64]{1,3,2,0:T(8,128)}, /*index=5*/f32[2,128...) while((s32[]{:T(128)}, f32[24]{0:T(128)}, f32[24]{0:T(128)}, ...), condition=%wide.region_51.52_spmd.clone, body=%wide.region_40.51_spmd.clone.sunk | while | flops 1819437184 | bytes 73094696 | solution.py:187
  765.9 4.0 fusion.373
  804.1 4.0 fusion.373
  845.5 4.6 fusion.222
  851.4 4.7 fusion.224
  859.8 3.7 reshape.1099
  866.0 4.4 multiply_reduce_fusion.3
  872.9 3.9 collective-permute-done.1
  877.0 7.0 fusion.209
  885.2 9.8 fusion.200
  895.1 4.7 fusion.208
  901.8 4.9 convolution_add_fusion.4
  907.6 38.5 %all-reduce.11 = (f32[1024]{0:T(1024)}, f32[1024]{0:T(1024)}, f32[1536]{0:T(1024)}, f32[4,1792]{1,0:T(4,128)}, f32[1792]{0:T(1024)}, /*index=5*/f32[24]{0:T(128)}, f32[24]{0:T(128)}, f32[24]{0:T(128)}) all-reduce(f32[1024]{0:T(1024)S(1)} %get-tuple-element.2742, ...), channel_id=1, replica_groups=mesh['seq'=8,'batch'=4] {'seq','batch'}, use_global_device_ids=true, to_apply=%region_60.61 | all-reduce | flops 12616 | bytes 100928 | tf_op jit(solution)/shard_map/psum | solution.py:596
  947.4 24.1 %reduce-scatter.19.cloned.1.call-done = f32[32,24]{1,0:T(8,128)} async-done(((f32[1024,24]{1,0:T(8,128)}), f32[32,24]{1,0:T(8,128)}) %reduce-scatter.19.cloned.1.call-update) | async-done | bytes 3088
  972.9 103.0 %reduce-scatter.9.cloned.1.call-done = f32[32,768]{1,0:T(8,128)} async-done(((f32[1024,768]{1,0:T(8,128)}), f32[32,768]{1,0:T(8,128)}) %reduce-scatter.9.cloned.1.call-update) | async-done | bytes 98320 | tf_op jit(solution)/shard_map/reduce_scatter | solution.py:589
  1075.9 150.8 %reduce-scatter.13.cloned.1.call-done = f32[2048,32]{0,1:T(8,128)} async-done(((f32[2048,1024]{0,1:T(8,128)}), f32[2048,32]{0,1:T(8,128)}) %reduce-scatter.13.cloned.1.call-update) | async-done | bytes 262160 | tf_op jit(solution)/shard_map/reduce_scatter | solution.py:592
  1226.6 147.7 %reduce-scatter.17.cloned.1.call-done = f32[2048,32]{0,1:T(8,128)} async-done(((f32[2048,1024]{0,1:T(8,128)}), f32[2048,32]{0,1:T(8,128)}) %reduce-scatter.17.cloned.1.call-update) | async-done | bytes 262160 | tf_op jit(solution)/shard_map/reduce_scatter | solution.py:594
  1374.3 157.3 %reduce-scatter.11.cloned.1.call-done = f32[32,3328]{1,0:T(8,128)} async-done(((f32[1024,3328]{1,0:T(8,128)}), f32[32,3328]{1,0:T(8,128)}) %reduce-scatter.11.cloned.1.call-update) | async-done | bytes 426000 | tf_op jit(solution)/shard_map/reduce_scatter | solution.py:590
  1531.6 184.8 %reduce-scatter.15.cloned.1.call-done = f32[32,4096]{1,0:T(8,128)} async-done(((f32[1024,4096]{1,0:T(8,128)}), f32[32,4096]{1,0:T(8,128)}) %reduce-scatter.15.cloned.1.call-update) | async-done | bytes 524304 | tf_op jit(solution)/shard_map/reduce_scatter | solution.py:593
  (811 shorter events, 355.2 us)
Async XLA Ops:
  7.2 78.3 %copy-start.6 = (bf16[1,256,1024]{2,1,0:T(8,128)(2,1)S(1)}, bf16[1,256,1024]{2,1,0:T(8,128)(2,1)}, u32[]{:S(2)}) copy-start(bf16[1,256,1024]{2,1,0:T(8,128)(2,1)} %param.39) | copy-start | bytes 1572868
  7.2 78.2 %copy-start.65 = (f32[1024]{0:T(1024)S(1)}, f32[1024]{0:T(1024)}, u32[]{:S(2)}) copy-start(f32[1024]{0:T(1024)} %param.47) | copy-start | bytes 12292
  7.2 78.2 %all-gather.16.cloned.1.call-start = ((), (), s32[]{:S(2)}) async-start(), calls=%async_computation.7 | async-start | bytes 7028736 | tf_op jit(solution)/shard_map/all_gather | solution.py:229
  7.9 189.2 %all-gather.14.cloned.1.call-start = ((), (), s32[]{:S(2)}) async-start(), calls=%async_computation.6 | async-start | bytes 1622016 | tf_op jit(solution)/shard_map/all_gather | solution.py:228
  8.7 313.8 %all-gather.28.cloned.1.call-start = ((), (), s32[]{:S(2)}) async-start(), calls=%async_computation.18 | async-start | bytes 3538944 | tf_op jit(solution)/shard_map/all_gather | solution.py:35
  8.8 81.6 %copy-start.77 = (s32[256]{0:T(256)}, s32[256]{0:T(256)S(1)}, u32[]{:S(2)}) copy-start(s32[256]{0:T(256)S(1)} %iota_add_fusion.4) | copy-start | bytes 3076
  54.1 36.3 %copy-start.82 = (bf16[1024,24]{0,1:T(8,128)(2,1)}, bf16[1024,24]{0,1:T(8,128)(2,1)S(1)}, u32[]{:S(2)}) copy-start(bf16[1024,24]{0,1:T(8,128)(2,1)S(1)} %reshape.1066) | copy-start | bytes 147460
  55.3 35.1 %copy-start.105 = (f32[256]{0:T(256)}, f32[256]{0:T(256)S(1)}, u32[]{:S(2)}) copy-start(f32[256]{0:T(256)S(1)} %add_rsqrt_fusion.2) | copy-start | bytes 3076
  57.5 41.0 %copy-start.96 = (f32[1792]{0:T(1024)}, f32[1792]{0:T(1024)S(1)}, u32[]{:S(2)}) copy-start(f32[1792]{0:T(1024)S(1)} %get-tuple-element.2744) | copy-start | bytes 21508
  57.5 41.0 %copy-start.98 = (f32[1792]{0:T(1024)}, f32[1792]{0:T(1024)S(1)}, u32[]{:S(2)}) copy-start(f32[1792]{0:T(1024)S(1)} %get-tuple-element.2745) | copy-start | bytes 21508
  57.5 41.0 %copy-start.100 = (f32[1792]{0:T(1024)}, f32[1792]{0:T(1024)S(1)}, u32[]{:S(2)}) copy-start(f32[1792]{0:T(1024)S(1)} %get-tuple-element.2746) | copy-start | bytes 21508
  57.5 41.0 %copy-start.102 = (f32[1792]{0:T(1024)}, f32[1792]{0:T(1024)S(1)}, u32[]{:S(2)}) copy-start(f32[1792]{0:T(1024)S(1)} %get-tuple-element.2747) | copy-start | bytes 21508
  59.9 38.7 %copy-start.123 = (f32[256]{0:T(256)}, f32[256]{0:T(256)S(1)}, u32[]{:S(2)}) copy-start(f32[256]{0:T(256)S(1)} %get-tuple-element.3062) | copy-start | bytes 3076
  59.9 38.7 %copy-start.125 = (f32[256]{0:T(256)}, f32[256]{0:T(256)S(1)}, u32[]{:S(2)}) copy-start(f32[256]{0:T(256)S(1)} %get-tuple-element.3063) | copy-start | bytes 3076
  59.9 38.7 %copy-start.127 = (f32[256]{0:T(256)}, f32[256]{0:T(256)S(1)}, u32[]{:S(2)}) copy-start(f32[256]{0:T(256)S(1)} %get-tuple-element.3064) | copy-start | bytes 3076
  92.1 6.4 collective-permute-start
  171.1 25.1 %copy-start.132 = (s32[256]{0:T(256)S(1)}, s32[256]{0:T(256)}, u32[]{:S(2)}) copy-start(s32[256]{0:T(256)} %get-tuple-element.2748) | copy-start | bytes 3076
  171.1 26.1 %copy-start.7 = (bf16[1,256,1024]{2,1,0:T(8,128)(2,1)S(1)}, bf16[1,256,1024]{2,1,0:T(8,128)(2,1)}, u32[]{:S(2)}) copy-start(bf16[1,256,1024]{2,1,0:T(8,128)(2,1)} %param.39) | copy-start | bytes 1572868
  171.1 26.1 %copy-start.66 = (f32[1024]{0:T(1024)S(1)}, f32[1024]{0:T(1024)}, u32[]{:S(2)}) copy-start(f32[1024]{0:T(1024)} %param.47) | copy-start | bytes 12292
  171.1 26.1 %copy-start.106 = (f32[256]{0:T(256)S(1)}, f32[256]{0:T(256)}, u32[]{:S(2)}) copy-start(f32[256]{0:T(256)} %copy-done.105) | copy-start | bytes 3076
  171.9 177.0 %all-gather.18.cloned.1.call-start = ((), (), s32[]{:S(2)}) async-start(), calls=%async_computation.8 | async-start | bytes 4325376 | tf_op jit(solution)/shard_map/all_gather | solution.py:231
  172.5 210.5 %all-gather.20.cloned.1.call-start = ((), (), s32[]{:S(2)}) async-start(), calls=%async_computation.9 | async-start | bytes 8650752 | tf_op jit(solution)/shard_map/all_gather | solution.py:232
  173.1 273.3 %all-gather.22.cloned.1.call-start = ((), (), s32[]{:S(2)}) async-start(), calls=%async_computation.10 | async-start | bytes 4325376 | tf_op jit(solution)/shard_map/all_gather | solution.py:233
  173.7 325.8 %all-gather.24.cloned.1.call-start = ((), (), s32[]{:S(2)}) async-start(), calls=%async_computation.11 | async-start | bytes 2359296 | tf_op jit(solution)/shard_map/all_gather | solution.py:507
  176.7 19.5 %copy-start.80 = (f32[256,24]{0,1:T(8,128)}, f32[256,24]{0,1:T(8,128)S(1)}, u32[]{:S(2)}) copy-start(f32[256,24]{0,1:T(8,128)S(1)} %fusion.240) | copy-start | bytes 73732
  200.1 41.2 %copy-start.59 = (bf16[256,128]{1,0:T(8,128)(2,1)}, bf16[256,128]{1,0:T(8,128)(2,1)S(1)}, u32[]{:S(2)}) copy-start(bf16[256,128]{1,0:T(8,128)(2,1)S(1)} %slice.377) | copy-start | bytes 196612
  200.3 41.0 %copy-start.28 = (bf16[256,2,64]{0,2,1:T(8,128)(2,1)}, bf16[256,2,64]{0,2,1:T(8,128)(2,1)S(1)}, u32[]{:S(2)}) copy-start(bf16[256,2,64]{0,2,1:T(8,128)(2,1)S(1)} %maximum_convert_fusion) | copy-start | bytes 196612
  241.3 40.5 %copy-start.74 = (f32[256,32]{0,1:T(8,128)S(1)}, f32[256,32]{0,1:T(8,128)}, u32[]{:S(2)}) copy-start(f32[256,32]{0,1:T(8,128)} %copy-done.73) | copy-start | bytes 98308
  241.3 40.5 %copy-start.76 = (f32[256,32]{0,1:T(8,128)S(1)}, f32[256,32]{0,1:T(8,128)}, u32[]{:S(2)}) copy-start(f32[256,32]{0,1:T(8,128)} %copy-done.75) | copy-start | bytes 98308
  319.0 323.0 %all-gather.26.cloned.1.call-start = ((), (), s32[]{:S(2)}) async-start(), calls=%async_computation.12 | async-start | bytes 2359296 | tf_op jit(solution)/shard_map/all_gather | solution.py:510
  322.4 15.3 copy-start.81
  349.0 34.0 %copy-start.53 = (f32[1024]{0:T(1024)S(1)}, f32[1024]{0:T(1024)}, u32[]{:S(2)}) copy-start(f32[1024]{0:T(1024)} %param.48) | copy-start | bytes 12292
  353.8 102.3 %copy-start.110 = (f32[256]{0:T(256)}, f32[256]{0:T(256)S(1)}, u32[]{:S(2)}) copy-start(f32[256]{0:T(256)S(1)} %add_rsqrt_fusion) | copy-start | bytes 3076
  383.0 63.4 %copy-start.36 = (bf16[1,256,1024]{2,1,0:T(8,128)(2,1)S(1)}, bf16[1,256,1024]{2,1,0:T(8,128)(2,1)}, u32[]{:S(2)}) copy-start(bf16[1,256,1024]{2,1,0:T(8,128)(2,1)} %param.55) | copy-start | bytes 1572868
  446.4 6.5 copy-start.18
  446.4 6.5 copy-start.19
  459.9 281.1 %all-gather.30.cloned.1.call-start = ((), (), s32[]{:S(2)}) async-start(), calls=%async_computation.19 | async-start | bytes 3538944 | tf_op jit(solution)/shard_map/all_gather | solution.py:60
  460.8 43.3 %copy-start.120 = (f32[1,8,256]{2,1,0:T(8,128)}, f32[1,8,256]{2,1,0:T(8,128)S(1)}, u32[]{:S(2)}) copy-start(f32[1,8,256]{2,1,0:T(8,128)S(1)} %log_add_fusion) | copy-start | bytes 24580
  519.3 452.2 %reduce-scatter.19.cloned.1.call-start = ((), (), s32[]{:S(2)}) async-start(), calls=%async_computation.20 | async-start | bytes 540672
  524.8 45.2 %copy-start.33 = (bf16[256,512]{1,0:T(8,128)(2,1)S(1)}, bf16[256,512]{1,0:T(8,128)(2,1)}, u32[]{:S(2)}) copy-start(bf16[256,512]{1,0:T(8,128)(2,1)} %slice.376) | copy-start | bytes 786436
  573.7 36.2 %copy-start.21 = (bf16[4,512,2,64]{1,3,2,0:T(8,128)(2,1)S(1)}, bf16[4,512,2,64]{1,3,2,0:T(8,128)(2,1)}, u32[]{:S(2)}) copy-start(bf16[4,512,2,64]{1,3,2,0:T(8,128)(2,1)} %get-tuple-element.4355) | copy-start | bytes 1572868
  573.7 36.2 %copy-start.79 = (s32[256]{0:T(256)S(1)}, s32[256]{0:T(256)}, u32[]{:S(2)}) copy-start(s32[256]{0:T(256)} %copy-done.77) | copy-start | bytes 3076
  573.7 36.2 %copy-start.87 = (s32[1,3]{1,0:T(1,128)S(1)}, s32[1,3]{1,0:T(1,128)}, u32[]{:S(2)}) copy-start(s32[1,3]{1,0:T(1,128)} %broadcast_in_dim.386) | copy-start | bytes 40
  573.8 36.2 %copy-start.121 = (f32[1,8,256]{2,1,0:T(8,128)S(1)}, f32[1,8,256]{2,1,0:T(8,128)}, u32[]{:S(2)}) copy-start(f32[1,8,256]{2,1,0:T(8,128)} %copy-done.120) | copy-start | bytes 24580
  573.8 36.2 %copy-start.140 = (s32[4]{0:T(128)S(1)}, s32[4]{0:T(128)}, u32[]{:S(2)}) copy-start(s32[4]{0:T(128)} %iota_multiply_fusion) | copy-start | bytes 52
  609.9 31.3 %copy-start.69 = (f32[256,32]{0,1:T(8,128)S(1)}, f32[256,32]{0,1:T(8,128)}, u32[]{:S(2)}) copy-start(f32[256,32]{0,1:T(8,128)} %get-tuple-element.3065) | copy-start | bytes 98308
  609.9 31.3 %copy-start.71 = (f32[256,32]{0,1:T(8,128)S(1)}, f32[256,32]{0,1:T(8,128)}, u32[]{:S(2)}) copy-start(f32[256,32]{0,1:T(8,128)} %get-tuple-element.3066) | copy-start | bytes 98308
  649.6 7.0 copy-start.29
  649.6 7.0 copy-start.89
  649.6 7.0 copy-start.104
  649.6 7.1 copy-start.142
  656.6 83.7 %copy-start.70 = (f32[256,32]{0,1:T(8,128)S(1)}, f32[256,32]{0,1:T(8,128)}, u32[]{:S(2)}) copy-start(f32[256,32]{0,1:T(8,128)} %get-tuple-element.3065) | copy-start | bytes 98308
  656.6 83.7 %copy-start.72 = (f32[256,32]{0,1:T(8,128)S(1)}, f32[256,32]{0,1:T(8,128)}, u32[]{:S(2)}) copy-start(f32[256,32]{0,1:T(8,128)} %get-tuple-element.3066) | copy-start | bytes 98308
  758.5 80.0 %copy-start.67 = (f32[1024]{0:T(1024)S(1)}, f32[1024]{0:T(1024)}, u32[]{:S(2)}) copy-start(f32[1024]{0:T(1024)} %param.47) | copy-start | bytes 12292
  777.4 11.2 copy-start.137
  815.6 11.9 copy-start.137
  821.1 6.5 copy-start.1
  840.8 235.1 %reduce-scatter.9.cloned.1.call-start = ((), (), s32[]{:S(2)}) async-start(), calls=%async_computation.13 | async-start | bytes 3244032 | tf_op jit(solution)/shard_map/reduce_scatter | solution.py:589
  844.0 382.7 %reduce-scatter.13.cloned.1.call-start = ((), (), s32[]{:S(2)}) async-start(), calls=%async_computation.15 | async-start | bytes 8650752 | tf_op jit(solution)/shard_map/reduce_scatter | solution.py:592
  850.0 524.3 %reduce-scatter.17.cloned.1.call-start = ((), (), s32[]{:S(2)}) async-start(), calls=%async_computation.17 | async-start | bytes 8650752 | tf_op jit(solution)/shard_map/reduce_scatter | solution.py:594
  856.1 675.5 %reduce-scatter.11.cloned.1.call-start = ((), (), s32[]{:S(2)}) async-start(), calls=%async_computation.14 | async-start | bytes 14057472 | tf_op jit(solution)/shard_map/reduce_scatter | solution.py:590
  871.0 5.8 collective-permute-start.1
  884.0 832.4 %reduce-scatter.15.cloned.1.call-start = ((), (), s32[]{:S(2)}) async-start(), calls=%async_computation.16 | async-start | bytes 17301504 | tf_op jit(solution)/shard_map/reduce_scatter | solution.py:593
  906.9 39.2 %copy-start.109 = (f32[256]{0:T(256)S(1)}, f32[256]{0:T(256)}, u32[]{:S(2)}) copy-start(f32[256]{0:T(256)} %copy-done.105) | copy-start | bytes 3076
  (115 other events, 350.2 us)
Sparse Core Ops, SparseCore 0:
  10.9 74.5 all-gather.15
  88.3 53.5 all-gather.13
  172.1 67.1 all-gather.27
  241.9 61.9 all-gather.17
  306.7 76.2 all-gather.19
  385.7 60.6 all-gather.21
  448.4 50.9 all-gather.23
  502.1 46.6 all-gather.25
  551.6 59.8 all-gather.29
  840.9 130.5 reduce-scatter.18
  978.4 97.4 reduce-scatter.8
  1078.7 147.8 reduce-scatter.12
  1229.6 144.6 reduce-scatter.16
  1377.2 154.4 reduce-scatter.10
  1534.5 181.8 reduce-scatter.14
where the time goes:
time: 1740 us; the launch traced here: 1720 us
  waiting for transfers between devices  888 us (51%)
  blocking collectives  235 us (14%)
  local copies, waits for them, and re-layouts  212 us (12%)
  matrix products  196 us (11%)
  other arithmetic  125 us (7%)
  loops' own time  44.4 us (3%)
    reduce_scatter x1, waiting for transfers between devices, on_device(): lax.psum_scatter(g_gate_up, ('seq', 'batch'), scatter_dimension=0, tiled=...  185 us
    reduce_scatter x1, waiting for transfers between devices, on_device(): lax.psum_scatter(g_ssm_in, ('seq', 'batch'), scatter_dimension=0, tiled=T...  157 us
    reduce_scatter x1, waiting for transfers between devices, on_device(): lax.psum_scatter(g_out, ('seq', 'batch'), scatter_dimension=1, tiled=True)  151 us
    reduce_scatter x1, waiting for transfers between devices, on_device(): lax.psum_scatter(g_down, ('seq', 'batch'), scatter_dimension=1, tiled=True)  148 us
    reduce_scatter x1, waiting for transfers between devices, on_device(): lax.psum_scatter(g_attn, ('seq', 'batch'), scatter_dimension=0, tiled=True)  103 us
    all_gather x1, waiting for transfers between devices, on_device(): lax.all_gather(w_down, ('seq', 'batch'), axis=1, tiled=True)  55.3 us
    dynamic_update_slice x22, local copies, waits for them, and re-layouts, ssd_blocks(): lax.scan(ssd_advance, (state_in, segment_before), blocks)  47.4 us
    all_gather x1, blocking collectives, on_device(): lax.all_gather(w_dt, ('seq', 'batch'), axis=0, tiled=True)  44.5 us
  transfers between devices with their start and end apart: 17, of which 11 were waited for; matrix products, arithmetic and copies ran while one was open for 24% of the time, Pallas kernels for 0%

commit v1 on v0

--- a/solution.py
+++ b/solution.py
@@ -75,6 +75,92 @@
         )
 
     return lax.fori_loop(0, ahead, one, state)
+
+
+def is_fast(width):
+    return lax.axis_size("seq") == 8 and lax.axis_size("batch") == 4 and width % (32 * 32) == 0
+
+
+def swap(value, axis, bit):
+    route = [(i, i ^ bit) for i in range(lax.axis_size(axis))]
+    return lax.ppermute(value, axis, route)
+
+
+def gather_stages(shard, x_first):
+    rows = jnp.concatenate([shard, swap(shard, "seq", 4)], axis=0)
+    rows = jnp.concatenate([rows, swap(rows, "seq", 2)], axis=0)
+    along_z = rows
+    if x_first:
+        rows = jnp.concatenate([rows, swap(rows, "seq", 1)], axis=0)
+        rows = jnp.concatenate([rows, swap(rows, "batch", 2)], axis=0)
+    else:
+        rows = jnp.stack([rows, swap(rows, "batch", 2)], axis=0)
+        rows = jnp.stack([rows, swap(rows, "seq", 1)], axis=1)
+        rows = rows.reshape(-1, rows.shape[-1])
+    return along_z, jnp.concatenate([rows, swap(rows, "batch", 1)], axis=0)
+
+
+def add_narrow(own, other):
+    return (own.astype(jnp.float32) + other.astype(jnp.float32)).astype(jnp.bfloat16)
+
+
+def scatter_stages(rows, y_first):
+    size, cols = rows.shape
+    if y_first:
+        half = size // 2
+        rows = add_narrow(rows[:half], swap(rows[half:], "batch", 2))
+        half = half // 2
+        rows = add_narrow(rows[:half], swap(rows[half:], "seq", 1))
+    else:
+        split = rows.reshape(2, 2, size // 4, cols)
+        split = add_narrow(split[:, 0], swap(split[:, 1], "seq", 1))
+        rows = add_narrow(split[0], swap(split[1], "batch", 2))
+    half = rows.shape[0] // 2
+    rows = add_narrow(rows[:half], swap(rows[half:], "seq", 2))
+    half = half // 2
+    return rows[:half].astype(jnp.float32) + swap(rows[half:], "seq", 4).astype(jnp.float32)
+
+
+def weight_grad(left, right, fast, y_first):
+    if not fast:
+        full = jnp.einsum("td,tc->dc", left, right, preferred_element_type=jnp.float32)
+        return lax.psum_scatter(full, ("seq", "batch"), scatter_dimension=0, tiled=True)
+    half = left.shape[1] // 2
+    lefts = jnp.concatenate([left[:, :half], swap(left[:, half:], "batch", 1)], axis=0)
+    rights = jnp.concatenate([right, swap(right, "batch", 1)], axis=0)
+    partial = jnp.einsum("td,tc->dc", lefts, rights, preferred_element_type=jnp.float32)
+    return scatter_stages(partial.astype(jnp.bfloat16), y_first)
+
+
+def total_small(arrays, fast):
+    flat = jnp.concatenate([a.reshape(-1) for a in arrays])
+    size = flat.shape[0]
+    flat = jnp.pad(flat, (0, -size % 1024)).reshape(-1, 128)
+    if fast:
+        for axis, bit in (("batch", 1), ("batch", 2), ("seq", 1), ("seq", 2), ("seq", 4)):
+            flat = flat + swap(flat, axis, bit)
+    else:
+        flat = lax.psum(flat, ("seq", "batch"))
+    flat = flat.reshape(-1)
+    out, start = [], 0
+    for a in arrays:
+        out.append(flat[start : start + a.size].reshape(a.shape))
+        start += a.size
+    return out
+
+
+def own_order(width, fast):
+    blocks = 32
+    per = width // blocks
+    row = lax.broadcasted_iota(jnp.int32, (width, width), 0)
+    col = lax.broadcasted_iota(jnp.int32, (width, width), 1)
+    if not fast:
+        return (row == col).astype(jnp.bfloat16)
+    me = lax.axis_index("seq") * 4 + lax.axis_index("batch")
+    j = col // per
+    flipped = (j & 1) * 16 + (j & 2) * 4 + (j & 4) + (j & 8) // 4 + (j & 16) // 16
+    source = (flipped ^ me) * per + col % per
+    return (row == source).astype(jnp.bfloat16)
 
 
 def rms_scale(value_rows):
@@ -223,21 +309,65 @@
     positions = first_pos + jnp.arange(token_rows, dtype=jnp.int32)
     segment, device_places = segments(seq_lens, positions)
     segment_before = segments(seq_lens, positions[:1] - 1)[0][0]
-    x_rows = layer_input[0].astype(jnp.float32)
-    weights = (
-        lax.all_gather(w_attn, ("seq", "batch"), axis=0, tiled=True),
-        lax.all_gather(w_ssm_in, ("seq", "batch"), axis=0, tiled=True),
-        lax.all_gather(w_dt, ("seq", "batch"), axis=0, tiled=True),
-        lax.all_gather(w_out, ("seq", "batch"), axis=1, tiled=True),
-        lax.all_gather(w_gate_up, ("seq", "batch"), axis=0, tiled=True),
-        lax.all_gather(w_down, ("seq", "batch"), axis=1, tiled=True),
-    )
-    full_attn, full_ssm, full_dt, full_out, full_gu, full_down = weights
+    width = layer_input.shape[2]
+    fast = is_fast(width)
+    order = own_order(width, fast)
+
+    def to_own(value):
+        if not fast:
+            return value
+        return jnp.dot(value, order, preferred_element_type=jnp.float32).astype(value.dtype)
+
+    def to_plain(value):
+        if not fast:
+            return value
+        return jnp.einsum("tc,dc->td", value, order, preferred_element_type=jnp.float32)
+
+    def to_plain_wide(value):
+        if not fast:
+            return value
+        return jnp.einsum("tc,dc->td", value, order.astype(jnp.float32), precision=HIGHEST)
+
+    def gain_own(value):
+        if not fast:
+            return value
+        return jnp.dot(value[None], order.astype(jnp.float32), precision=HIGHEST)[0]
+
+    norm_gain, mlp_gain = gain_own(norm_gain), gain_own(mlp_gain)
+    x_rows = to_own(layer_input[0]).astype(jnp.float32)
+    grad_rows = to_own(out_grad[0])
+    step_pad = jnp.pad(w_dt, ((0, 0), (0, 128 - MH)))
+    shards = (
+        jnp.concatenate([w_ssm_in[:, ssm_width:], step_pad], axis=1),
+        jnp.concatenate([w_attn, w_ssm_in[:, :ssm_width]], axis=1),
+        w_out.T[:, : w_out.shape[0] // 2],
+        w_out.T[:, w_out.shape[0] // 2 :],
+        w_gate_up[:, :FF],
+        w_gate_up[:, FF:],
+        w_down.T[:, : FF // 2],
+        w_down.T[:, FF // 2 :],
+    )
+    full = []
+    ahead = None
+    for i in range(0, 8, 2):
+        pair = shards[i : i + 2]
+        if fast:
+            if ahead is not None:
+                pair, ahead = lax.optimization_barrier((pair, ahead))
+            za, fa = gather_stages(pair[0], True)
+            zb, fb = gather_stages(pair[1], False)
+            ahead = (za, zb)
+            full += [fa, fb]
+        else:
+            full += [lax.all_gather(p, ("seq", "batch"), axis=0, tiled=True) for p in pair]
+    full_conv, full_mix, out_a, out_b, full_gate, full_up, down_a, down_b = full
     scale_one = rms_scale(x_rows)
     normed = (x_rows * scale_one * norm_gain).astype(jnp.bfloat16)
-    attention_projected = jnp.dot(normed, full_attn, preferred_element_type=jnp.float32)
-    ssm_proj = jnp.dot(normed, full_ssm, preferred_element_type=jnp.float32)
-    step_proj = jnp.dot(normed, full_dt, preferred_element_type=jnp.float32)
+    conv_proj = jnp.dot(normed, full_conv, preferred_element_type=jnp.float32)
+    mix_proj = jnp.dot(normed, full_mix, preferred_element_type=jnp.float32)
+    attn_width = query_width + 2 * key_value_width
+    attention_projected = mix_proj[:, :attn_width]
+    step_proj = conv_proj[:, xbc_width : xbc_width + MH]
     query_rows = rotary_embed(
         attention_projected[:, :query_width].reshape(token_rows, QUERY_HEADS, HEAD_SIZE),
         device_places,
@@ -283,12 +413,11 @@
         jnp.zeros((KEY_VALUE_HEADS, query_group_width, token_rows, HEAD_SIZE), jnp.float32),
     )
     running_total = start_state
-    blocks, rows_per_block = key_blocks(
-        (
-            lax.all_gather(flattened_keys, "seq", axis=0, tiled=True),
-            lax.all_gather(flattened_values, "seq", axis=0, tiled=True),
-        )
-    )
+    all_pairs = lax.all_gather(
+        jnp.concatenate([flattened_keys, flattened_values], axis=1), "seq", axis=0, tiled=True
+    )
+    all_keys, all_values = all_pairs[:, :key_value_width], all_pairs[:, key_value_width:]
+    blocks, rows_per_block = key_blocks((all_keys, all_values))
 
     def attend_advance(state_now, pieces):
         key_blk, value_blk, key_first = pieces
@@ -327,8 +456,8 @@
     attended = (
         attn_heads.transpose(2, 0, 1, 3).reshape(token_rows, query_width).astype(jnp.bfloat16)
     )
-    gate_z = ssm_proj[:, :ssm_width]
-    raw_xbc = ssm_proj[:, ssm_width:]
+    gate_z = mix_proj[:, attn_width:]
+    raw_xbc = conv_proj[:, :xbc_width]
     rim_rows = shifted(raw_xbc[token_rows - (CONV - 1) :], "seq", 1)
     extended = jnp.concatenate([rim_rows, raw_xbc], axis=0)
     ext_pos = first_pos - (CONV - 1) + jnp.arange(token_rows + CONV - 1, dtype=jnp.int32)
@@ -388,37 +517,57 @@
     scale_gated = rms_scale(gated)
     ssm_normed = gated * scale_gated * ssm_gain
     joined = jnp.concatenate([attended, ssm_normed.astype(jnp.bfloat16)], axis=1)
-    middle = x_rows + jnp.dot(joined, full_out, preferred_element_type=jnp.float32)
+    half_in = joined.shape[1] // 2
+
+    def narrow_out(left, parts):
+        cut = left.shape[1] // 2
+        return jnp.einsum(
+            "tc,dc->td", left[:, :cut], parts[0], preferred_element_type=jnp.float32
+        ) + jnp.einsum("tc,dc->td", left[:, cut:], parts[1], preferred_element_type=jnp.float32)
+
+    middle = x_rows + narrow_out(joined, (out_a, out_b))
     scale_two = rms_scale(middle)
     normed_two = (middle * scale_two * mlp_gain).astype(jnp.bfloat16)
-    gate_up = jnp.dot(normed_two, full_gu, preferred_element_type=jnp.float32)
-    gate_part = gate_up[:, :FF]
-    up_part = gate_up[:, FF:]
+    gate_part = jnp.dot(normed_two, full_gate, preferred_element_type=jnp.float32)
+    up_part = jnp.dot(normed_two, full_up, preferred_element_type=jnp.float32)
     hidden = (jax.nn.silu(gate_part) * up_part).astype(jnp.bfloat16)
-    layer_out = middle + jnp.dot(hidden, full_down, preferred_element_type=jnp.float32)
-    weights_back = (
-        lax.all_gather(w_attn, ("seq", "batch"), axis=0, tiled=True),
-        lax.all_gather(w_ssm_in, ("seq", "batch"), axis=0, tiled=True),
-        lax.all_gather(w_dt, ("seq", "batch"), axis=0, tiled=True),
-        lax.all_gather(w_out, ("seq", "batch"), axis=1, tiled=True),
-        lax.all_gather(w_gate_up, ("seq", "batch"), axis=0, tiled=True),
-        lax.all_gather(w_down, ("seq", "batch"), axis=1, tiled=True),
-    )
-    back_attn, back_ssm, back_dt, back_out, back_gu, back_down = weights_back
-    grad_rows = out_grad[0]
-    g_down = jnp.einsum("tf,td->fd", hidden, grad_rows, preferred_element_type=jnp.float32)
-    d_hidden = jnp.einsum("td,fd->tf", grad_rows, back_down, preferred_element_type=jnp.float32)
+    layer_out = middle + narrow_out(hidden, (down_a, down_b))
+    g_down = [
+        weight_grad(grad_rows, hidden[:, : FF // 2], fast, True),
+        weight_grad(grad_rows, hidden[:, FF // 2 :], fast, False),
+    ]
+    d_hidden = jnp.concatenate(
+        [
+            jnp.dot(grad_rows, down_a, preferred_element_type=jnp.float32),
+            jnp.dot(grad_rows, down_b, preferred_element_type=jnp.float32),
+        ],
+        axis=1,
+    )
     sig_gate = jax.nn.sigmoid(gate_part)
     d_gate = d_hidden * up_part * (sig_gate * (1.0 + gate_part * (1.0 - sig_gate)))
     d_up = d_hidden * gate_part * sig_gate
-    d_gate_up = jnp.concatenate([d_gate, d_up], axis=1).astype(jnp.bfloat16)
-    g_gate_up = jnp.einsum("td,tf->df", normed_two, d_gate_up, preferred_element_type=jnp.float32)
-    d_normed_two = jnp.einsum("tf,df->td", d_gate_up, back_gu, preferred_element_type=jnp.float32)
+    d_gate, d_up = d_gate.astype(jnp.bfloat16), d_up.astype(jnp.bfloat16)
+    g_gate_up = [
+        weight_grad(normed_two, d_gate, fast, True),
+        weight_grad(normed_two, d_up, fast, False),
+    ]
+    d_normed_two = narrow_out(
+        jnp.concatenate([d_gate, d_up], axis=1), (full_gate, full_up)
+    )
     d_middle_norm, g_mlp_gain = norm_back(middle, scale_two, mlp_gain, d_normed_two)
     d_middle = grad_rows.astype(jnp.float32) + d_middle_norm
     d_mixer = d_middle.astype(jnp.bfloat16)
-    g_out = jnp.einsum("tc,td->cd", joined, d_mixer, preferred_element_type=jnp.float32)
-    d_joined = jnp.einsum("td,cd->tc", d_mixer, back_out, preferred_element_type=jnp.float32)
+    g_out = [
+        weight_grad(d_mixer, joined[:, :half_in], fast, True),
+        weight_grad(d_mixer, joined[:, half_in:], fast, False),
+    ]
+    d_joined = jnp.concatenate(
+        [
+            jnp.dot(d_mixer, out_a, preferred_element_type=jnp.float32),
+            jnp.dot(d_mixer, out_b, preferred_element_type=jnp.float32),
+        ],
+        axis=1,
+    )
     attended_gradient = d_joined[:, :query_width].astype(jnp.bfloat16)
     d_ssm_normed = d_joined[:, query_width:]
     d_gated, g_ssm_gain = norm_back(gated, scale_gated, ssm_gain, d_ssm_normed)
@@ -452,7 +601,8 @@
     d_raw = g_extended[CONV - 1 :] + jnp.concatenate(
         [jnp.zeros((token_rows - (CONV - 1), xbc_width), jnp.float32), back_rim], axis=0
     )
-    d_ssm_proj = jnp.concatenate([d_gate_z, d_raw], axis=1).astype(jnp.bfloat16)
+    d_step_pad = jnp.pad(d_step_proj, ((0, 0), (0, 128 - MH)))
+    d_conv_proj = jnp.concatenate([d_raw.astype(jnp.bfloat16), d_step_pad], axis=1)
     head_gradients = attended_gradient.reshape(
         token_rows, KEY_VALUE_HEADS, query_group_width, HEAD_SIZE
     )
@@ -460,12 +610,7 @@
     running_total = jnp.zeros(
         (KEY_VALUE_HEADS, query_group_width, token_rows, HEAD_SIZE), jnp.float32
     )
-    blocks, query_rows_per_block = key_blocks(
-        (
-            lax.all_gather(flattened_keys, "seq", axis=0, tiled=True),
-            lax.all_gather(flattened_values, "seq", axis=0, tiled=True),
-        )
-    )
+    blocks, query_rows_per_block = key_blocks((all_keys, all_values))
 
     def query_advance(grad_now, pieces):
         key_blk, value_blk, key_first = pieces
@@ -575,31 +720,27 @@
     d_attn_proj = jnp.concatenate(
         [d_query_flat, d_key_flat, d_values.reshape(token_rows, key_value_width)], axis=1
     ).astype(jnp.bfloat16)
-    g_attn = jnp.einsum("td,tc->dc", normed, d_attn_proj, preferred_element_type=jnp.float32)
-    g_ssm_in = jnp.einsum("td,tc->dc", normed, d_ssm_proj, preferred_element_type=jnp.float32)
-    g_dt = jnp.einsum("td,tc->dc", normed, d_step_proj, preferred_element_type=jnp.float32)
-    d_normed = (
-        jnp.einsum("tc,dc->td", d_attn_proj, back_attn, preferred_element_type=jnp.float32)
-        + jnp.einsum("tc,dc->td", d_ssm_proj, back_ssm, preferred_element_type=jnp.float32)
-        + jnp.einsum("tc,dc->td", d_step_proj, back_dt, preferred_element_type=jnp.float32)
-    )
+    d_mix_proj = jnp.concatenate([d_attn_proj, d_gate_z.astype(jnp.bfloat16)], axis=1)
+    g_conv_in = weight_grad(normed, d_conv_proj, fast, True)
+    g_mix_in = weight_grad(normed, d_mix_proj, fast, False)
+    d_normed = jnp.einsum(
+        "tc,dc->td", d_conv_proj, full_conv, preferred_element_type=jnp.float32
+    ) + jnp.einsum("tc,dc->td", d_mix_proj, full_mix, preferred_element_type=jnp.float32)
     d_input_norm, g_norm_gain = norm_back(x_rows, scale_one, norm_gain, d_normed)
     input_grad = d_middle + d_input_norm
-    grad_attn, grad_ssm_in, grad_dt, grad_out, grad_gate_up, grad_down = (
-        lax.psum_scatter(g_attn, ("seq", "batch"), scatter_dimension=0, tiled=True),
-        lax.psum_scatter(g_ssm_in, ("seq", "batch"), scatter_dimension=0, tiled=True),
-        lax.psum_scatter(g_dt, ("seq", "batch"), scatter_dimension=0, tiled=True),
-        lax.psum_scatter(g_out, ("seq", "batch"), scatter_dimension=1, tiled=True),
-        lax.psum_scatter(g_gate_up, ("seq", "batch"), scatter_dimension=0, tiled=True),
-        lax.psum_scatter(g_down, ("seq", "batch"), scatter_dimension=1, tiled=True),
-    )
-    small_sums = lax.psum(
-        (g_norm_gain, g_mlp_gain, g_ssm_gain, g_conv_w, g_conv_b, g_a_log, g_dt_bias, g_d_skip),
-        ("seq", "batch"),
+    grad_attn = g_mix_in[:, :attn_width]
+    grad_ssm_in = jnp.concatenate([g_mix_in[:, attn_width:], g_conv_in[:, :xbc_width]], axis=1)
+    grad_dt = g_conv_in[:, xbc_width : xbc_width + MH]
+    grad_out = jnp.concatenate(g_out, axis=1).T
+    grad_gate_up = jnp.concatenate(g_gate_up, axis=1)
+    grad_down = jnp.concatenate(g_down, axis=1).T
+    gains = to_plain_wide(jnp.stack([g_norm_gain, g_mlp_gain]))
+    small_sums = total_small(
+        (gains[0], gains[1], g_ssm_gain, g_conv_w, g_conv_b, g_a_log, g_dt_bias, g_d_skip), fast
     )
     return (
-        layer_out.astype(jnp.bfloat16)[None],
-        input_grad[None],
+        to_plain(layer_out.astype(jnp.bfloat16)).astype(jnp.bfloat16)[None],
+        to_plain_wide(input_grad)[None],
         grad_attn,
         grad_ssm_in,
         grad_dt,

time: 1740 us -> 1160 us (0.67)
  waiting for transfers between devices: 888 us -> 248 us
  blocking collectives: 235 us -> 126 us
  starting transfers between devices: 5.48 us -> 89.2 us
  local copies, waits for them, and re-layouts: 212 us -> 254 us
  other arithmetic: 125 us -> 156 us
    reduce_scatter x5 -> x0, waiting for transfers between devices: 743 us -> none  [the longest x1 185 us: on_device(): lax.psum_scatter(g_gate_up, ('seq', 'batch'), scatter_dimension=0, tiled=...]
    ppermute x0 -> x89, waiting for transfers between devices: none -> 242 us  [swap(): return lax.ppermute(value, axis, route)]
    all_gather x3 -> x0, blocking collectives: 113 us -> none  [the longest x1 44.5 us: on_device(): lax.all_gather(w_dt, ('seq', 'batch'), axis=0, tiled=True)]
    all_gather x5 -> x1, waiting for transfers between devices: 107 us -> 0.01 us  [on_device(): lax.all_gather(jnp.concatenate([flattened_keys, flattened_values], axis=1...]
    ppermute x0 -> x89, starting transfers between devices: none -> 83.6 us  [swap(): return lax.ppermute(value, axis, route)]
    psum x1 -> x0, blocking collectives: 38.5 us -> none  [on_device(): lax.psum((g_norm_gain, g_mlp_gain, g_ssm_gain, g_conv_w, g_conv_b, g_a_lo...]
    unnamed x16 -> x5, waiting for transfers between devices: 27.3 us -> 0.08 us
    all_gather x1, blocking collectives: 32.7 us -> 57.2 us  [on_device(): lax.all_gather(delta.reshape(QUERY_HEADS, token_rows), 'seq', axis=1, til...]
  transfers between devices with their start and end apart: 17 -> 96, of which waited for: 11 -> 45; matrix products, arithmetic and copies ran while one was open for 24% -> 52% of each run, Pallas kernels for 0% -> 0%
where the time goes in v1:
time: 1160 us; the launch traced here: 1140 us
  local copies, waits for them, and re-layouts  254 us (22%)
  waiting for transfers between devices  248 us (21%)
  matrix products  204 us (18%)
  other arithmetic  156 us (13%)
  blocking collectives  126 us (11%)
  starting transfers between devices  89.2 us (8%)
  loops' own time  44.2 us (4%)
  between operations  18.5 us (2%)
    ppermute x89, waiting for transfers between devices, swap(): return lax.ppermute(value, axis, route)  242 us
    ppermute x89, starting transfers between devices, swap(): return lax.ppermute(value, axis, route)  83.6 us
    all_gather x1, blocking collectives, on_device(): lax.all_gather(delta.reshape(QUERY_HEADS, token_rows), 'seq', axis=1, til...  57.2 us
    all_gather x1, blocking collectives, on_device(): lax.all_gather(log_total.reshape(QUERY_HEADS, token_rows), 'seq', axis=1,...  47.9 us
    dynamic_update_slice x22, local copies, waits for them, and re-layouts, ssd_blocks(): lax.scan(ssd_advance, (state_in, segment_before), blocks)  46.9 us
    unnamed x339, local copies, waits for them, and re-layouts  29.8 us
    dot_general x6, matrix products, ssd_advance(): result = jnp.einsum('tsh,shp->thp', mixing, block_x, precision=HIGHEST)  23.4 us
  transfers between devices with their start and end apart: 96, of which 45 were waited for; matrix products, arithmetic and copies ran while one was open for 52% of the time, Pallas kernels for 0%

profile of v1, /device:TPU:0, one launch (start us, length us, event | category | flops | bytes accessed | tf_op | source)
XLA Modules:
  0.0 1140.3 jit_solution(3705184528267911395)
XLA Ops:
  9.8 4.0 collective-permute-start.5
  38.3 5.1 collective-permute-done.6
  54.5 4.8 collective-permute-done.16
  71.6 6.8 collective-permute-done.21
  78.5 7.2 collective-permute-done.26
  100.8 9.1 collective-permute-done.8
  131.6 9.8 collective-permute-done.33
  160.9 6.3 multiply_convert_fusion.3
  177.6 65.5 %while.172 = (s32[]{:T(128)}, f32[24,64,128]{2,1,0:T(8,128)S(1)}, s32[]{:T(128)}, f32[2,128,24,64]{1,0,3,2:T(2,128)}, f32[2,128,24]{2,1,0:T(8,128)S(1)}, /*index...) while((s32[]{:T(128)}, f32[24,64,128]{2,1,0:T(8,128)S(1)}, ...), condition=%wide.region_16.17_spmd.clone, body=%wide.region_14.16_spmd.clone.sunk | while | flops 912915968 | bytes 11019042 | solution.py:273
  179.2 4.2 fusion.469
  190.8 19.0 %dynamic_update_slice.226 = f32[2,128,24,64]{1,0,3,2:T(2,128)} dynamic-update-slice(f32[2,128,24,64]{1,0,3,2:T(2,128)} %get-tuple-element.4113, f32[1,128,24,64]{1,0,3,2:T(1,128)S(1)} %bitcast.907, s32[]{:T(128)S(6)} %copy.561, s32[]{:T(128)} %constant.447.clone.1..sunk.1, s32[]{:T(128)} %constant.447.clone.1..sunk.1, s32[]{:T(128)} %constant.447.clone.1..sunk.1) | dynamic-update-slice | bytes 1572868 | tf_op jit(solution)/shard_map/while/body/jit(dynamic_update_index_in_dim)/dynamic_update_slice | solution.py:273
  212.0 4.2 fusion.469
  223.5 19.0 %dynamic_update_slice.226 = f32[2,128,24,64]{1,0,3,2:T(2,128)} dynamic-update-slice(f32[2,128,24,64]{1,0,3,2:T(2,128)} %get-tuple-element.4113, f32[1,128,24,64]{1,0,3,2:T(1,128)S(1)} %bitcast.907, s32[]{:T(128)S(6)} %copy.561, s32[]{:T(128)} %constant.447.clone.1..sunk.1, s32[]{:T(128)} %constant.447.clone.1..sunk.1, s32[]{:T(128)} %constant.447.clone.1..sunk.1) | dynamic-update-slice | bytes 1572868 | tf_op jit(solution)/shard_map/while/body/jit(dynamic_update_index_in_dim)/dynamic_update_slice | solution.py:273
  269.6 9.8 collective-permute-done.29
  293.3 20.8 %all-gather.2 = bf16[8,1,24]{2,1,0:T(2,128)(2,1)S(1)} all-gather(bf16[1,1,24]{2,1,0:T(2,128)(2,1)S(1)} %bitcast.997), channel_id=1, replica_groups=mesh['seq'=8,'batch'=4] {'seq'}, dimensions={0}, use_global_device_ids=true | all-gather | bytes 432 | tf_op jit(solution)/shard_map/all_gather | solution.py:35
  337.8 29.7 %while.167 = (s32[]{:T(128)}, f32[2,4,256]{2,1,0:T(4,128)S(1)}, f32[2,4,256]{2,1,0:T(4,128)S(1)}, f32[2,4,256,64]{2,3,1,0:T(8,128)}, s32[4]{0:T(128)S(1)}, /*ind...) while((s32[]{:T(128)}, f32[2,4,256]{2,1,0:T(4,128)S(1)}, ...), condition=%wide.region_11.12_spmd, body=%wide.region_5.11_spmd.sunk | while | flops 282731520 | bytes 19025312 | solution.py:452
  343.6 6.6 conditional.6
  370.5 47.9 %all_gather.40 = f32[8,2048]{1,0:T(8,128)} all-gather(f32[8,256]{1,0:T(8,128)S(1)} %reshape.1110), channel_id=1, replica_groups=mesh['seq'=8,'batch'=4] {'seq'}, dimensions={1}, use_global_device_ids=true | all-gather | bytes 73728 | tf_op jit(solution)/shard_map/all_gather | solution.py:645
  418.3 4.5 reshape.1109
  426.2 9.8 while.173
  451.6 3.9 fusion.223
  455.5 5.3 multiply_convert_fusion.1
  460.9 4.3 fusion.222
  465.1 4.4 multiply_reduce_fusion.8
  485.5 40.1 %while.171 = (s32[]{:T(128)}, f32[24,64,128]{2,1,0:T(8,128)S(1)}, s32[]{:T(128)}, f32[2,128,24]{2,1,0:T(8,128)}, pred[2,128,128,24]{2,3,1,0:T(8,128)(4,1)}, /*in...) while((s32[]{:T(128)}, f32[24,64,128]{2,1,0:T(8,128)S(1)}, ...), condition=%wide.region_29.30_spmd.clone, body=%wide.region_27.29_spmd.clone.sunk | while | flops 611135488 | bytes 15556113 | solution.py:273
  526.2 5.3 fusion.290
  544.4 4.8 fusion.266
  550.1 31.0 %while.169 = (s32[]{:T(128)}, f32[2,4,256,64]{2,3,1,0:T(8,128)}, s32[4]{0:T(128)S(1)}, s32[256]{0:T(256)S(1)}, s32[1,3]{1,0:T(1,128)S(1)}, /*index=5*/s32[256]{0...) while((s32[]{:T(128)}, f32[2,4,256,64]{2,3,1,0:T(8,128)}, ...), condition=%wide.region_46.47_spmd, body=%wide.region_42.46_spmd.sunk | while | flops 409605120 | bytes 10653003 | solution.py:642
  555.8 8.4 conditional.7
  559.4 4.8 fusion.29
  582.3 57.2 %all_gather.42 = f32[8,2048]{1,0:T(8,128)} all-gather(f32[8,256]{1,0:T(8,128)S(1)} %copy-done.137), channel_id=1, replica_groups=mesh['seq'=8,'batch'=4] {'seq'}, dimensions={1}, use_global_device_ids=true | all-gather | bytes 73728 | tf_op jit(solution)/shard_map/all_gather | solution.py:646
  663.2 10.2 collective-permute-done.60
  676.4 10.5 collective-permute-done.82
  690.6 21.0 %collective-permute-done.61 = bf16[128,1024]{1,0:T(8,128)(2,1)S(1)} collective-permute-done((bf16[128,1024]{1,0:T(8,128)(2,1)S(1)}, bf16[128,1024]{1,0:T(8,128)(2,1)S(1)}, u32[]{:S(2)}, u32[]{:S(2)}) %collective-permute-start.61) | collective-permute-done | bytes 262176 | tf_op jit(solution)/shard_map/ppermute | solution.py:86
  712.5 16.8 %collective-permute-done.56 = bf16[128,1024]{1,0:T(8,128)(2,1)S(1)} collective-permute-done((bf16[128,1024]{1,0:T(8,128)(2,1)S(1)}, bf16[128,1024]{1,0:T(8,128)(2,1)S(1)}, u32[]{:S(2)}, u32[]{:S(2)}) %collective-permute-start.56) | collective-permute-done | bytes 262176 | tf_op jit(solution)/shard_map/ppermute | solution.py:86
  730.7 6.7 collective-permute-done.78
  739.6 3.9 collective-permute-done.57
  765.1 5.5 collective-permute-done.72
  775.0 5.2 collective-permute-done.73
  791.6 7.7 reshape.1182
  799.3 7.0 copy.340
  806.3 83.0 %while.170 = (s32[]{:T(128)}, f32[256,2,64]{0,2,1:T(8,128)S(1)}, f32[256,2,64]{0,2,1:T(8,128)S(1)}, s32[4]{0:T(128)S(1)}, s32[256]{0:T(256)S(1)}, /*index=5*/s32...) while((s32[]{:T(128)}, f32[256,2,64]{0,2,1:T(8,128)S(1)}, ...), condition=%wide.region_51.52_spmd, body=%wide.region_47.51_spmd.sunk | while | flops 547852800 | bytes 15923617 | solution.py:712
  812.5 14.6 %conditional.8 = ((f32[256,2,64]{0,2,1:T(8,128)S(1)}, f32[256,2,64]{0,2,1:T(8,128)S(1)})) conditional(s32[]{:T(128)} %bitcast.830, (f32[256,2,64]{0,2,1:T(8,128)S(1)}, f32[256,2,64]{0,2,1:T(8,128)S(1)}) %tuple.407, (s32[512]{0:T(512)S(1)}, s32[256]{0:T(256)S(1)}, s32[512]{0:T(512)S(1)}, s32[256]{0:T(256)S(1)}, ...), branch_computations={%region_49.49_spmd, %region_50.50_spmd} | conditional | flops 547848192 | bytes 15917118 | solution.py:710
  812.5 3.8 fusion.67
  819.3 4.5 fusion.62
  833.2 14.6 %conditional.8 = ((f32[256,2,64]{0,2,1:T(8,128)S(1)}, f32[256,2,64]{0,2,1:T(8,128)S(1)})) conditional(s32[]{:T(128)} %bitcast.830, (f32[256,2,64]{0,2,1:T(8,128)S(1)}, f32[256,2,64]{0,2,1:T(8,128)S(1)}) %tuple.407, (s32[512]{0:T(512)S(1)}, s32[256]{0:T(256)S(1)}, s32[512]{0:T(512)S(1)}, s32[256]{0:T(256)S(1)}, ...), branch_computations={%region_49.49_spmd, %region_50.50_spmd} | conditional | flops 547848192 | bytes 15917118 | solution.py:710
  840.0 4.5 fusion.62
  854.0 14.6 %conditional.8 = ((f32[256,2,64]{0,2,1:T(8,128)S(1)}, f32[256,2,64]{0,2,1:T(8,128)S(1)})) conditional(s32[]{:T(128)} %bitcast.830, (f32[256,2,64]{0,2,1:T(8,128)S(1)}, f32[256,2,64]{0,2,1:T(8,128)S(1)}) %tuple.407, (s32[512]{0:T(512)S(1)}, s32[256]{0:T(256)S(1)}, s32[512]{0:T(512)S(1)}, s32[256]{0:T(256)S(1)}, ...), branch_computations={%region_49.49_spmd, %region_50.50_spmd} | conditional | flops 547848192 | bytes 15917118 | solution.py:710
  854.0 3.8 fusion.67
  860.8 4.5 fusion.62
  874.7 14.6 %conditional.8 = ((f32[256,2,64]{0,2,1:T(8,128)S(1)}, f32[256,2,64]{0,2,1:T(8,128)S(1)})) conditional(s32[]{:T(128)} %bitcast.830, (f32[256,2,64]{0,2,1:T(8,128)S(1)}, f32[256,2,64]{0,2,1:T(8,128)S(1)}) %tuple.407, (s32[512]{0:T(512)S(1)}, s32[256]{0:T(256)S(1)}, s32[512]{0:T(512)S(1)}, s32[256]{0:T(256)S(1)}, ...), branch_computations={%region_49.49_spmd, %region_50.50_spmd} | conditional | flops 547848192 | bytes 15917118 | solution.py:710
  874.7 3.8 fusion.67
  881.5 4.5 fusion.62
  892.6 4.1 fusion.220
  896.7 13.4 %while.168 = (s32[]{:T(128)}, f32[24,64,128]{2,1,0:T(8,128)S(1)}, s32[]{:T(128)}, bf16[8,24]{1,0:T(8,128)(2,1)}, bf16[8,24,64,128]{3,2,1,0:T(8,128)(2,1)}, /*index=5*/s32[]{:T(128)}, s32[]{:T(128)}, s32[]{:T(128)}, s32[]{:T(128)}) while((s32[]{:T(128)}, f32[24,64,128]{2,1,0:T(8,128)S(1)}, s32[]{:T(128)}, bf16[8,24]{1,0:T(8,128)(2,1)}, ...), condition=%wide.region_26.27_spmd, body=%wide.region_25.26_spmd.sunk | while | flops 589854 | bytes 1966475 | solution.py:77
  914.1 81.5 %while.174 = (s32[]{:T(128)}, f32[24]{0:T(128)}, f32[24]{0:T(128)}, f32[24,64,128]{2,1,0:T(8,128)S(1)}, f32[2,128,24,64]{1,3,2,0:T(8,128)}, /*index=5*/f32[2,128...) while((s32[]{:T(128)}, f32[24]{0:T(128)}, f32[24]{0:T(128)}, ...), condition=%wide.region_41.42_spmd.clone, body=%wide.region_30.41_spmd.clone.sunk | while | flops 1819437184 | bytes 72831704 | solution.py:273
  921.6 4.0 fusion.480
  961.9 4.0 fusion.480
  1021.2 5.4 multiply_reduce_fusion.9
  1037.0 25.8 %collective-permute-done.88 = f32[104,128]{1,0:T(8,128)S(1)} collective-permute-done((f32[104,128]{1,0:T(8,128)S(1)}, f32[104,128]{1,0:T(8,128)S(1)}, u32[]{:S(2)}, u32[]{:S(2)}) %collective-permute-start.88) | collective-permute-done | bytes 53280 | tf_op jit(solution)/shard_map/ppermute | solution.py:86
  1063.0 4.0 collective-permute-done.89
  1080.8 20.3 %collective-permute-done.49 = bf16[256,1920]{1,0:T(8,128)(2,1)S(1)} collective-permute-done((bf16[256,1920]{1,0:T(8,128)(2,1)S(1)}, bf16[256,1920]{1,0:T(8,128)(2,1)S(1)}, u32[]{:S(2)}, u32[]{:S(2)}) %collective-permute-start.49) | collective-permute-done | bytes 983072 | tf_op jit(solution)/shard_map/ppermute | solution.py:86
  1102.9 7.2 collective-permute-done.45
  1113.7 7.3 collective-permute-done.46
  (1188 shorter events, 599.5 us)
Async XLA Ops:
  7.2 314.2 %all-gather.9.cloned.1.call-start = ((), (), s32[]{:S(2)}) async-start(), calls=%async_computation | async-start | bytes 1179648 | tf_op jit(solution)/shard_map/all_gather | solution.py:416
  9.8 24.6 %collective-permute-start.5 = (bf16[32,1920]{1,0:T(8,128)(2,1)}, bf16[32,1920]{1,0:T(8,128)(2,1)S(1)}, u32[]{:S(2)}, u32[]{:S(2)}) collective-permute-start(bf16[32,1920]{1,0:T(8,128)(2,1)} %get-tuple-element.3226), channel_id=1, source_target_pairs={{0,16},{4,20},{8,24},{12,28},{16,0},{20,4},{24,8},{28,12},{1,17},{... | collective-permute-start | bytes 368648 | tf_op jit(solution)/shard_map/ppermute | solution.py:86
  16.3 20.8 %collective-permute-start = (bf16[32,2304]{1,0:T(8,128)(2,1)}, bf16[32,2304]{1,0:T(8,128)(2,1)}, u32[]{:S(2)}, u32[]{:S(2)}) collective-permute-start(bf16[32,2304]{1,0:T(8,128)(2,1)} %pad_maximum_fusion.55), channel_id=1, source_target_pairs={{0,16},{4,20},{8,24},{12,28},{16,0},{20,4},{24,8},{28,12},{1,17},{... | collective-permute-start | bytes 442376 | tf_op jit(solution)/shard_map/ppermute | solution.py:86
  38.1 10.1 collective-permute-start.1
  43.4 44.1 %collective-permute-start.7 = (bf16[128,1920]{1,0:T(8,128)(2,1)S(1)}, bf16[128,1920]{1,0:T(8,128)(2,1)S(1)}, u32[]{:S(2)}, u32[]{:S(2)}) collective-permute-start(bf16[128,1920]{1,0:T(8,128)(2,1)S(1)} %pad_maximum_fusion.37), channel_id=1, source_target_pairs={{0,4},{4,0},{8,12},{12,8},{16,20},{20,16},{24,28},{28,24},{1,5},{5... | collective-permute-start | bytes 1474568 | tf_op jit(solution)/shard_map/ppermute | solution.py:86
  49.2 39.0 %collective-permute-start.2 = (bf16[128,2304]{1,0:T(8,128)(2,1)S(1)}, bf16[128,2304]{1,0:T(8,128)(2,1)S(1)}, u32[]{:S(2)}, u32[]{:S(2)}) collective-permute-start(bf16[128,2304]{1,0:T(8,128)(2,1)S(1)} %get-tuple-element.3171), channel_id=1, source_target_pairs={{0,2},{1,3},{2,0},{3,1},{4,6},{5,7},{6,4},{7,5},{8,10},{9,11},{10,... | collective-permute-start | bytes 1769480 | tf_op jit(solution)/shard_map/ppermute | solution.py:86
  51.5 9.6 collective-permute-start.11
  64.4 27.3 %collective-permute-start.18 = (bf16[128,1024]{1,0:T(8,128)(2,1)S(1)}, bf16[128,1024]{1,0:T(8,128)(2,1)S(1)}, u32[]{:S(2)}, u32[]{:S(2)}) collective-permute-start(bf16[128,1024]{1,0:T(8,128)(2,1)S(1)} %constant_dynamic-update-slice_fusion.31), channel_id=1, source_target_pairs={{0,2},{1,3},{2,0},{3,1},{4,6},{5,7},{6,4},{7,5},{8,10},{9,11},{10,... | collective-permute-start | bytes 786440 | tf_op jit(solution)/shard_map/ppermute | solution.py:86
  66.9 22.9 %collective-permute-start.13 = (bf16[128,1024]{1,0:T(8,128)(2,1)S(1)}, bf16[128,1024]{1,0:T(8,128)(2,1)S(1)}, u32[]{:S(2)}, u32[]{:S(2)}) collective-permute-start(bf16[128,1024]{1,0:T(8,128)(2,1)S(1)} %get-tuple-element.3219), channel_id=1, source_target_pairs={{0,4},{4,0},{8,12},{12,8},{16,20},{20,16},{24,28},{28,24},{1,5},{5... | collective-permute-start | bytes 786440 | tf_op jit(solution)/shard_map/ppermute | solution.py:86
  85.7 12.0 %collective-permute-start.22 = (bf16[64,2048]{1,0:T(8,128)(2,1)S(1)}, bf16[64,2048]{1,0:T(8,128)(2,1)S(1)}, u32[]{:S(2)}, u32[]{:S(2)}) collective-permute-start(bf16[64,2048]{1,0:T(8,128)(2,1)S(1)} %pad_maximum_fusion.49), channel_id=1, source_target_pairs={{0,8},{4,12},{8,0},{12,4},{16,24},{20,28},{24,16},{28,20},{1,9},{5... | collective-permute-start | bytes 786440 | tf_op jit(solution)/shard_map/ppermute | solution.py:86
  87.6 22.3 %collective-permute-start.8 = (bf16[256,1920]{1,0:T(8,128)(2,1)S(1)}, bf16[256,1920]{1,0:T(8,128)(2,1)S(1)}, u32[]{:S(2)}, u32[]{:S(2)}) collective-permute-start(bf16[256,1920]{1,0:T(8,128)(2,1)S(1)} %pad_maximum_fusion.24), channel_id=1, source_target_pairs={{0,2},{1,3},{2,0},{3,1},{4,6},{5,7},{6,4},{7,5},{8,10},{9,11},{10,... | collective-permute-start | bytes 2949128 | tf_op jit(solution)/shard_map/ppermute | solution.py:86
  88.3 21.9 %collective-permute-start.3 = (bf16[2,128,2304]{2,1,0:T(8,128)(2,1)S(1)}, bf16[2,128,2304]{2,1,0:T(8,128)(2,1)S(1)}, u32[]{:S(2)}, u32[]{:S(2)}) collective-permute-start(bf16[2,128,2304]{2,1,0:T(8,128)(2,1)S(1)} %get-tuple-element.3151), channel_id=1, source_target_pairs={{0,4},{4,0},{8,12},{12,8},{16,20},{20,16},{24,28},{28,24},{1,5},{5... | collective-permute-start | bytes 3538952 | tf_op jit(solution)/shard_map/ppermute | solution.py:86
  91.7 33.2 %collective-permute-start.14 = (bf16[256,1024]{1,0:T(8,128)(2,1)S(1)}, bf16[256,1024]{1,0:T(8,128)(2,1)S(1)}, u32[]{:S(2)}, u32[]{:S(2)}) collective-permute-start(bf16[256,1024]{1,0:T(8,128)(2,1)S(1)} %pad_maximum_fusion.28), channel_id=1, source_target_pairs={{0,2},{1,3},{2,0},{3,1},{4,6},{5,7},{6,4},{7,5},{8,10},{9,11},{10,... | collective-permute-start | bytes 1572872 | tf_op jit(solution)/shard_map/ppermute | solution.py:86
  98.6 15.9 %collective-permute-start.36 = (bf16[32,1024]{1,0:T(8,128)(2,1)S(1)}, bf16[32,1024]{1,0:T(8,128)(2,1)S(1)}, u32[]{:S(2)}, u32[]{:S(2)}) collective-permute-start(bf16[32,1024]{1,0:T(8,128)(2,1)S(1)} %copy-done.81), channel_id=1, source_target_pairs={{0,16},{4,20},{8,24},{12,28},{16,0},{20,4},{24,8},{28,12},{1,17},{... | collective-permute-start | bytes 196616 | tf_op jit(solution)/shard_map/ppermute | solution.py:86
  110.2 33.7 %collective-permute-start.9 = (bf16[512,1920]{1,0:T(8,128)(2,1)S(1)}, bf16[512,1920]{1,0:T(8,128)(2,1)S(1)}, u32[]{:S(2)}, u32[]{:S(2)}) collective-permute-start(bf16[512,1920]{1,0:T(8,128)(2,1)S(1)} %get-tuple-element.3160), channel_id=1, source_target_pairs={{0,1},{1,0},{2,3},{3,2},{4,5},{5,4},{6,7},{7,6},{8,9},{9,8},{10,11... | collective-permute-start | bytes 5898248 | tf_op jit(solution)/shard_map/ppermute | solution.py:86
  110.5 39.6 %collective-permute-start.4 = (bf16[512,2304]{1,0:T(8,128)(2,1)S(1)}, bf16[512,2304]{1,0:T(8,128)(2,1)S(1)}, u32[]{:S(2)}, u32[]{:S(2)}) collective-permute-start(bf16[512,2304]{1,0:T(8,128)(2,1)S(1)} %bitcast.916), channel_id=1, source_target_pairs={{0,1},{1,0},{2,3},{3,2},{4,5},{5,4},{6,7},{7,6},{8,9},{9,8},{10,11... | collective-permute-start | bytes 7077896 | tf_op jit(solution)/shard_map/ppermute | solution.py:86
  120.9 21.8 %collective-permute-start.23 = (bf16[128,2048]{1,0:T(8,128)(2,1)S(1)}, bf16[128,2048]{1,0:T(8,128)(2,1)S(1)}, u32[]{:S(2)}, u32[]{:S(2)}) collective-permute-start(bf16[128,2048]{1,0:T(8,128)(2,1)S(1)} %get-tuple-element.3196), channel_id=1, source_target_pairs={{0,4},{4,0},{8,12},{12,8},{16,20},{20,16},{24,28},{28,24},{1,5},{5... | collective-permute-start | bytes 1572872 | tf_op jit(solution)/shard_map/ppermute | solution.py:86
  124.9 16.5 %collective-permute-start.33 = (bf16[128,1024]{1,0:T(8,128)(2,1)S(1)}, bf16[128,1024]{1,0:T(8,128)(2,1)S(1)}, u32[]{:S(2)}, u32[]{:S(2)}) collective-permute-start(bf16[128,1024]{1,0:T(8,128)(2,1)S(1)} %pad_maximum_fusion.51), channel_id=1, source_target_pairs={{0,4},{4,0},{8,12},{12,8},{16,20},{20,16},{24,28},{28,24},{1,5},{5... | collective-permute-start | bytes 786440 | tf_op jit(solution)/shard_map/ppermute | solution.py:86
  129.9 132.7 %collective-permute-start.19 = (bf16[2,128,1024]{2,1,0:T(8,128)(2,1)}, bf16[2,128,1024]{2,1,0:T(8,128)(2,1)}, u32[]{:S(2)}, u32[]{:S(2)}) collective-permute-start(bf16[2,128,1024]{2,1,0:T(8,128)(2,1)} %get-tuple-element.3189), channel_id=1, source_target_pairs={{0,4},{4,0},{8,12},{12,8},{16,20},{20,16},{24,28},{28,24},{1,5},{5... | collective-permute-start | bytes 1572872 | tf_op jit(solution)/shard_map/ppermute | solution.py:86
  141.3 104.9 %collective-permute-start.28 = (bf16[128,2048]{1,0:T(8,128)(2,1)}, bf16[128,2048]{1,0:T(8,128)(2,1)}, u32[]{:S(2)}, u32[]{:S(2)}) collective-permute-start(bf16[128,2048]{1,0:T(8,128)(2,1)} %constant_dynamic-update-slice_fusion.48), channel_id=1, source_target_pairs={{0,2},{1,3},{2,0},{3,1},{4,6},{5,7},{6,4},{7,5},{8,10},{9,11},{10,... | collective-permute-start | bytes 1572872 | tf_op jit(solution)/shard_map/ppermute | solution.py:86
  142.7 124.0 %collective-permute-start.15 = (bf16[512,1024]{1,0:T(8,128)(2,1)}, bf16[512,1024]{1,0:T(8,128)(2,1)}, u32[]{:S(2)}, u32[]{:S(2)}) collective-permute-start(bf16[512,1024]{1,0:T(8,128)(2,1)} %get-tuple-element.3186), channel_id=1, source_target_pairs={{0,1},{1,0},{2,3},{3,2},{4,5},{5,4},{6,7},{7,6},{8,9},{9,8},{10,11... | collective-permute-start | bytes 3145736 | tf_op jit(solution)/shard_map/ppermute | solution.py:86
  143.8 107.7 %collective-permute-start.39 = (bf16[2,128,1024]{2,1,0:T(8,128)(2,1)}, bf16[2,128,1024]{2,1,0:T(8,128)(2,1)}, u32[]{:S(2)}, u32[]{:S(2)}) collective-permute-start(bf16[2,128,1024]{2,1,0:T(8,128)(2,1)} %get-tuple-element.3185), channel_id=1, source_target_pairs={{0,4},{4,0},{8,12},{12,8},{16,20},{20,16},{24,28},{28,24},{1,5},{5... | collective-permute-start | bytes 1572872 | tf_op jit(solution)/shard_map/ppermute | solution.py:86
  150.1 10.2 collective-permute-start.10
  157.7 260.6 %all-gather.11.cloned.1.call-start = ((), (), s32[]{:S(2)}) async-start(), calls=%async_computation.1 | async-start | bytes 2359296 | tf_op jit(solution)/shard_map/all_gather | solution.py:652
  160.3 99.0 %collective-permute-start.24 = (bf16[256,2048]{1,0:T(8,128)(2,1)}, bf16[256,2048]{1,0:T(8,128)(2,1)}, u32[]{:S(2)}, u32[]{:S(2)}) collective-permute-start(bf16[256,2048]{1,0:T(8,128)(2,1)} %pad_maximum_fusion.21), channel_id=1, source_target_pairs={{0,2},{1,3},{2,0},{3,1},{4,6},{5,7},{6,4},{7,5},{8,10},{9,11},{10,... | collective-permute-start | bytes 3145736 | tf_op jit(solution)/shard_map/ppermute | solution.py:86
  177.5 248.6 %all-gather.15.cloned.1.call-start = ((), (), s32[]{:S(2)}) async-start(), calls=%async_computation.3 | async-start | bytes 3538944 | tf_op jit(solution)/shard_map/all_gather | solution.py:35
  244.0 547.7 %all-gather.13.cloned.1.call-start = ((), (), s32[]{:S(2)}) async-start(), calls=%async_computation.2 | async-start | bytes 2359296 | tf_op jit(solution)/shard_map/all_gather | solution.py:655
  246.2 12.0 %collective-permute-start.34 = (bf16[256,1024]{1,0:T(8,128)(2,1)S(1)}, bf16[256,1024]{1,0:T(8,128)(2,1)S(1)}, u32[]{:S(2)}, u32[]{:S(2)}) collective-permute-start(bf16[256,1024]{1,0:T(8,128)(2,1)S(1)} %copy-done.86), channel_id=1, source_target_pairs={{0,2},{1,3},{2,0},{3,1},{4,6},{5,7},{6,4},{7,5},{8,10},{9,11},{10,... | collective-permute-start | bytes 1572872 | tf_op jit(solution)/shard_map/ppermute | solution.py:86
  251.6 27.8 %collective-permute-start.29 = (bf16[2,128,2048]{2,1,0:T(8,128)(2,1)}, bf16[2,128,2048]{2,1,0:T(8,128)(2,1)}, u32[]{:S(2)}, u32[]{:S(2)}) collective-permute-start(bf16[2,128,2048]{2,1,0:T(8,128)(2,1)} %get-tuple-element.3157), channel_id=1, source_target_pairs={{0,4},{4,0},{8,12},{12,8},{16,20},{20,16},{24,28},{28,24},{1,5},{5... | collective-permute-start | bytes 3145736 | tf_op jit(solution)/shard_map/ppermute | solution.py:86
  258.2 26.7 %collective-permute-start.40 = (bf16[512,1024]{1,0:T(8,128)(2,1)}, bf16[512,1024]{1,0:T(8,128)(2,1)}, u32[]{:S(2)}, u32[]{:S(2)}) collective-permute-start(bf16[512,1024]{1,0:T(8,128)(2,1)} %bitcast.95), channel_id=1, source_target_pairs={{0,1},{1,0},{2,3},{3,2},{4,5},{5,4},{6,7},{7,6},{8,9},{9,8},{10,11... | collective-permute-start | bytes 3145736 | tf_op jit(solution)/shard_map/ppermute | solution.py:86
  259.3 22.8 %collective-permute-start.35 = (bf16[512,1024]{1,0:T(8,128)(2,1)}, bf16[512,1024]{1,0:T(8,128)(2,1)}, u32[]{:S(2)}, u32[]{:S(2)}) collective-permute-start(bf16[512,1024]{1,0:T(8,128)(2,1)} %get-tuple-element.3180), channel_id=1, source_target_pairs={{0,1},{1,0},{2,3},{3,2},{4,5},{5,4},{6,7},{7,6},{8,9},{9,8},{10,11... | collective-permute-start | bytes 3145736 | tf_op jit(solution)/shard_map/ppermute | solution.py:86
  262.7 55.5 %collective-permute-start.25 = (bf16[512,2048]{1,0:T(8,128)(2,1)}, bf16[512,2048]{1,0:T(8,128)(2,1)}, u32[]{:S(2)}, u32[]{:S(2)}) collective-permute-start(bf16[512,2048]{1,0:T(8,128)(2,1)} %get-tuple-element.3154), channel_id=1, source_target_pairs={{0,1},{1,0},{2,3},{3,2},{4,5},{5,4},{6,7},{7,6},{8,9},{9,8},{10,11... | collective-permute-start | bytes 6291464 | tf_op jit(solution)/shard_map/ppermute | solution.py:86
  266.7 384.9 %collective-permute-start.75 = (bf16[256,512]{1,0:T(8,128)(2,1)}, bf16[256,512]{1,0:T(8,128)(2,1)}, u32[]{:S(2)}, u32[]{:S(2)}) collective-permute-start(bf16[256,512]{1,0:T(8,128)(2,1)} %get-tuple-element.3173), channel_id=1, source_target_pairs={{0,1},{1,0},{2,3},{3,2},{4,5},{5,4},{6,7},{7,6},{8,9},{9,8},{10,11... | collective-permute-start | bytes 786440 | tf_op jit(solution)/shard_map/ppermute | solution.py:86
  279.4 166.8 %collective-permute-start.20 = (bf16[512,1024]{1,0:T(8,128)(2,1)}, bf16[512,1024]{1,0:T(8,128)(2,1)}, u32[]{:S(2)}, u32[]{:S(2)}) collective-permute-start(bf16[512,1024]{1,0:T(8,128)(2,1)} %bitcast.80), channel_id=1, source_target_pairs={{0,1},{1,0},{2,3},{3,2},{4,5},{5,4},{6,7},{7,6},{8,9},{9,8},{10,11... | collective-permute-start | bytes 3145736 | tf_op jit(solution)/shard_map/ppermute | solution.py:86
  282.2 169.4 %collective-permute-start.30 = (bf16[512,2048]{1,0:T(8,128)(2,1)}, bf16[512,2048]{1,0:T(8,128)(2,1)}, u32[]{:S(2)}, u32[]{:S(2)}) collective-permute-start(bf16[512,2048]{1,0:T(8,128)(2,1)} %bitcast.88), channel_id=1, source_target_pairs={{0,1},{1,0},{2,3},{3,2},{4,5},{5,4},{6,7},{7,6},{8,9},{9,8},{10,11... | collective-permute-start | bytes 6291464 | tf_op jit(solution)/shard_map/ppermute | solution.py:86
  474.8 421.8 %all-gather.17.cloned.1.call-start = ((), (), s32[]{:S(2)}) async-start(), calls=%async_computation.4 | async-start | bytes 3538944 | tf_op jit(solution)/shard_map/all_gather | solution.py:60
  476.0 173.6 %collective-permute-start.54 = (bf16[256,1024]{1,0:T(8,128)(2,1)}, bf16[256,1024]{1,0:T(8,128)(2,1)}, u32[]{:S(2)}, u32[]{:S(2)}) collective-permute-start(bf16[256,1024]{1,0:T(8,128)(2,1)} %copy-done.42), channel_id=1, source_target_pairs={{0,1},{1,0},{2,3},{3,2},{4,5},{5,4},{6,7},{7,6},{8,9},{9,8},{10,11... | collective-permute-start | bytes 1572872 | tf_op jit(solution)/shard_map/ppermute | solution.py:86
  534.7 112.3 %collective-permute-start.59 = (bf16[256,1024]{1,0:T(8,128)(2,1)}, bf16[256,1024]{1,0:T(8,128)(2,1)}, u32[]{:S(2)}, u32[]{:S(2)}) collective-permute-start(bf16[256,1024]{1,0:T(8,128)(2,1)} %get-tuple-element.3164), channel_id=1, source_target_pairs={{0,1},{1,0},{2,3},{3,2},{4,5},{5,4},{6,7},{7,6},{8,9},{9,8},{10,11... | collective-permute-start | bytes 1572872 | tf_op jit(solution)/shard_map/ppermute | solution.py:86
  535.7 111.1 %collective-permute-start.53 = (bf16[256,512]{1,0:T(8,128)(2,1)}, bf16[256,512]{1,0:T(8,128)(2,1)}, u32[]{:S(2)}, u32[]{:S(2)}) collective-permute-start(bf16[256,512]{1,0:T(8,128)(2,1)} %get-tuple-element.3177), channel_id=1, source_target_pairs={{0,1},{1,0},{2,3},{3,2},{4,5},{5,4},{6,7},{7,6},{8,9},{9,8},{10,11... | collective-permute-start | bytes 786440 | tf_op jit(solution)/shard_map/ppermute | solution.py:86
  538.2 113.9 %collective-permute-start.81 = (bf16[256,1024]{1,0:T(8,128)(2,1)}, bf16[256,1024]{1,0:T(8,128)(2,1)}, u32[]{:S(2)}, u32[]{:S(2)}) collective-permute-start(bf16[256,1024]{1,0:T(8,128)(2,1)} %get-tuple-element.3153), channel_id=1, source_target_pairs={{0,1},{1,0},{2,3},{3,2},{4,5},{5,4},{6,7},{7,6},{8,9},{9,8},{10,11... | collective-permute-start | bytes 1572872 | tf_op jit(solution)/shard_map/ppermute | solution.py:86
  646.8 12.3 %collective-permute-start.70 = (bf16[256,2048]{1,0:T(8,128)(2,1)}, bf16[256,2048]{1,0:T(8,128)(2,1)S(1)}, u32[]{:S(2)}, u32[]{:S(2)}) collective-permute-start(bf16[256,2048]{1,0:T(8,128)(2,1)} %copy-done.167), channel_id=1, source_target_pairs={{0,1},{1,0},{2,3},{3,2},{4,5},{5,4},{6,7},{7,6},{8,9},{9,8},{10,11... | collective-permute-start | bytes 3145736 | tf_op jit(solution)/shard_map/ppermute | solution.py:86
  646.9 13.7 %collective-permute-start.65 = (bf16[256,2048]{1,0:T(8,128)(2,1)}, bf16[256,2048]{1,0:T(8,128)(2,1)S(1)}, u32[]{:S(2)}, u32[]{:S(2)}) collective-permute-start(bf16[256,2048]{1,0:T(8,128)(2,1)} %copy-done.64), channel_id=1, source_target_pairs={{0,1},{1,0},{2,3},{3,2},{4,5},{5,4},{6,7},{7,6},{8,9},{9,8},{10,11... | collective-permute-start | bytes 3145736 | tf_op jit(solution)/shard_map/ppermute | solution.py:86
  651.6 377.7 %collective-permute-start.42 = (bf16[256,512]{1,0:T(8,128)(2,1)}, bf16[256,512]{1,0:T(8,128)(2,1)}, u32[]{:S(2)}, u32[]{:S(2)}) collective-permute-start(bf16[256,512]{1,0:T(8,128)(2,1)} %get-tuple-element.3179), channel_id=1, source_target_pairs={{0,1},{1,0},{2,3},{3,2},{4,5},{5,4},{6,7},{7,6},{8,9},{9,8},{10,11... | collective-permute-start | bytes 786440 | tf_op jit(solution)/shard_map/ppermute | solution.py:86
  654.2 19.1 %collective-permute-start.60 = (bf16[2,128,1024]{2,1,0:T(8,128)(2,1)S(1)}, bf16[2,128,1024]{2,1,0:T(8,128)(2,1)S(1)}, u32[]{:S(2)}, u32[]{:S(2)}) collective-permute-start(bf16[2,128,1024]{2,1,0:T(8,128)(2,1)S(1)} %slice_bitcast_fusion.13), channel_id=1, source_target_pairs={{0,4},{4,0},{8,12},{12,8},{16,20},{20,16},{24,28},{28,24},{1,5},{5... | collective-permute-start | bytes 1572872 | tf_op jit(solution)/shard_map/ppermute | solution.py:86
  658.2 16.4 %collective-permute-start.55 = (bf16[256,1024]{1,0:T(8,128)(2,1)S(1)}, bf16[256,1024]{1,0:T(8,128)(2,1)S(1)}, u32[]{:S(2)}, u32[]{:S(2)}) collective-permute-start(bf16[256,1024]{1,0:T(8,128)(2,1)S(1)} %slice.739), channel_id=1, source_target_pairs={{0,2},{1,3},{2,0},{3,1},{4,6},{5,7},{6,4},{7,5},{8,10},{9,11},{10,... | collective-permute-start | bytes 1572872 | tf_op jit(solution)/shard_map/ppermute | solution.py:86
  659.1 27.8 %collective-permute-start.82 = (bf16[2,128,1024]{2,1,0:T(8,128)(2,1)S(1)}, bf16[2,128,1024]{2,1,0:T(8,128)(2,1)S(1)}, u32[]{:S(2)}, u32[]{:S(2)}) collective-permute-start(bf16[2,128,1024]{2,1,0:T(8,128)(2,1)S(1)} %slice_bitcast_fusion.9), channel_id=1, source_target_pairs={{0,4},{4,0},{8,12},{12,8},{16,20},{20,16},{24,28},{28,24},{1,5},{5... | collective-permute-start | bytes 1572872 | tf_op jit(solution)/shard_map/ppermute | solution.py:86
  660.6 27.2 %collective-permute-start.77 = (bf16[256,1024]{1,0:T(8,128)(2,1)S(1)}, bf16[256,1024]{1,0:T(8,128)(2,1)S(1)}, u32[]{:S(2)}, u32[]{:S(2)}) collective-permute-start(bf16[256,1024]{1,0:T(8,128)(2,1)S(1)} %slice.775), channel_id=1, source_target_pairs={{0,2},{1,3},{2,0},{3,1},{4,6},{5,7},{6,4},{7,5},{8,10},{9,11},{10,... | collective-permute-start | bytes 1572872 | tf_op jit(solution)/shard_map/ppermute | solution.py:86
  673.4 87.5 %collective-permute-start.71 = (bf16[2,128,2048]{2,1,0:T(8,128)(2,1)S(1)}, bf16[2,128,2048]{2,1,0:T(8,128)(2,1)S(1)}, u32[]{:S(2)}, u32[]{:S(2)}) collective-permute-start(bf16[2,128,2048]{2,1,0:T(8,128)(2,1)S(1)} %slice_bitcast_fusion.5), channel_id=1, source_target_pairs={{0,4},{4,0},{8,12},{12,8},{16,20},{20,16},{24,28},{28,24},{1,5},{5... | collective-permute-start | bytes 3145736 | tf_op jit(solution)/shard_map/ppermute | solution.py:86
  674.6 87.6 %collective-permute-start.66 = (bf16[256,2048]{1,0:T(8,128)(2,1)S(1)}, bf16[256,2048]{1,0:T(8,128)(2,1)S(1)}, u32[]{:S(2)}, u32[]{:S(2)}) collective-permute-start(bf16[256,2048]{1,0:T(8,128)(2,1)S(1)} %slice.757), channel_id=1, source_target_pairs={{0,2},{1,3},{2,0},{3,1},{4,6},{5,7},{6,4},{7,5},{8,10},{9,11},{10,... | collective-permute-start | bytes 3145736 | tf_op jit(solution)/shard_map/ppermute | solution.py:86
  687.0 24.7 %collective-permute-start.61 = (bf16[128,1024]{1,0:T(8,128)(2,1)S(1)}, bf16[128,1024]{1,0:T(8,128)(2,1)S(1)}, u32[]{:S(2)}, u32[]{:S(2)}) collective-permute-start(bf16[128,1024]{1,0:T(8,128)(2,1)S(1)} %slice_bitcast_fusion.17), channel_id=1, source_target_pairs={{0,2},{1,3},{2,0},{3,1},{4,6},{5,7},{6,4},{7,5},{8,10},{9,11},{10,... | collective-permute-start | bytes 786440 | tf_op jit(solution)/shard_map/ppermute | solution.py:86
  687.8 41.5 %collective-permute-start.56 = (bf16[128,1024]{1,0:T(8,128)(2,1)S(1)}, bf16[128,1024]{1,0:T(8,128)(2,1)S(1)}, u32[]{:S(2)}, u32[]{:S(2)}) collective-permute-start(bf16[128,1024]{1,0:T(8,128)(2,1)S(1)} %slice.741), channel_id=1, source_target_pairs={{0,4},{4,0},{8,12},{12,8},{16,20},{20,16},{24,28},{28,24},{1,5},{5... | collective-permute-start | bytes 786440 | tf_op jit(solution)/shard_map/ppermute | solution.py:86
  711.6 18.9 %collective-permute-start.83 = (bf16[128,1024]{1,0:T(8,128)(2,1)S(1)}, bf16[128,1024]{1,0:T(8,128)(2,1)S(1)}, u32[]{:S(2)}, u32[]{:S(2)}) collective-permute-start(bf16[128,1024]{1,0:T(8,128)(2,1)S(1)} %slice_bitcast_fusion.15), channel_id=1, source_target_pairs={{0,2},{1,3},{2,0},{3,1},{4,6},{5,7},{6,4},{7,5},{8,10},{9,11},{10,... | collective-permute-start | bytes 786440 | tf_op jit(solution)/shard_map/ppermute | solution.py:86
  762.6 11.0 collective-permute-start.67
  770.7 9.5 collective-permute-start.73
  773.8 9.5 collective-permute-start.68
  891.6 137.7 %collective-permute-start.43 = (bf16[256,2304]{1,0:T(8,128)(2,1)}, bf16[256,2304]{1,0:T(8,128)(2,1)}, u32[]{:S(2)}, u32[]{:S(2)}) collective-permute-start(bf16[256,2304]{1,0:T(8,128)(2,1)} %pad_maximum_fusion.19), channel_id=1, source_target_pairs={{0,1},{1,0},{2,3},{3,2},{4,5},{5,4},{6,7},{7,6},{8,9},{9,8},{10,11... | collective-permute-start | bytes 3538952 | tf_op jit(solution)/shard_map/ppermute | solution.py:86
  1033.6 44.0 %collective-permute-start.44 = (bf16[2,128,2304]{2,1,0:T(8,128)(2,1)S(1)}, bf16[2,128,2304]{2,1,0:T(8,128)(2,1)S(1)}, u32[]{:S(2)}, u32[]{:S(2)}) collective-permute-start(bf16[2,128,2304]{2,1,0:T(8,128)(2,1)S(1)} %slice_bitcast_fusion.3), channel_id=1, source_target_pairs={{0,4},{4,0},{8,12},{12,8},{16,20},{20,16},{24,28},{28,24},{1,5},{5... | collective-permute-start | bytes 3538952 | tf_op jit(solution)/shard_map/ppermute | solution.py:86
  1036.8 26.0 %collective-permute-start.88 = (f32[104,128]{1,0:T(8,128)S(1)}, f32[104,128]{1,0:T(8,128)S(1)}, u32[]{:S(2)}, u32[]{:S(2)}) collective-permute-start(f32[104,128]{1,0:T(8,128)S(1)} %fusion.414), channel_id=1, source_target_pairs={{0,4},{4,0},{8,12},{12,8},{16,20},{20,16},{24,28},{28,24},{1,5},{5... | collective-permute-start | bytes 159752 | tf_op jit(solution)/shard_map/ppermute | solution.py:86
  1063.0 11.0 collective-permute-start.48
  1076.3 24.8 %collective-permute-start.49 = (bf16[256,1920]{1,0:T(8,128)(2,1)S(1)}, bf16[256,1920]{1,0:T(8,128)(2,1)S(1)}, u32[]{:S(2)}, u32[]{:S(2)}) collective-permute-start(bf16[256,1920]{1,0:T(8,128)(2,1)S(1)} %slice.727), channel_id=1, source_target_pairs={{0,2},{1,3},{2,0},{3,1},{4,6},{5,7},{6,4},{7,5},{8,10},{9,11},{10,... | collective-permute-start | bytes 2949128 | tf_op jit(solution)/shard_map/ppermute | solution.py:86
  1078.7 31.4 %collective-permute-start.45 = (bf16[128,2304]{1,0:T(8,128)(2,1)}, bf16[128,2304]{1,0:T(8,128)(2,1)}, u32[]{:S(2)}, u32[]{:S(2)}) collective-permute-start(bf16[128,2304]{1,0:T(8,128)(2,1)} %slice_bitcast_fusion.7), channel_id=1, source_target_pairs={{0,2},{1,3},{2,0},{3,1},{4,6},{5,7},{6,4},{7,5},{8,10},{9,11},{10,... | collective-permute-start | bytes 1769480 | tf_op jit(solution)/shard_map/ppermute | solution.py:86
  1111.4 9.6 collective-permute-start.46
  1111.6 13.3 %collective-permute-start.51 = (bf16[64,1920]{1,0:T(8,128)(2,1)S(1)}, bf16[64,1920]{1,0:T(8,128)(2,1)S(1)}, u32[]{:S(2)}, u32[]{:S(2)}) collective-permute-start(bf16[64,1920]{1,0:T(8,128)(2,1)S(1)} %slice.731), channel_id=1, source_target_pairs={{0,8},{4,12},{8,0},{12,4},{16,24},{20,28},{24,16},{28,20},{1,9},{5... | collective-permute-start | bytes 737288 | tf_op jit(solution)/shard_map/ppermute | solution.py:86
  1121.1 9.4 collective-permute-start.47
  (222 other events, 2508.3 us)
Sparse Core Ops, SparseCore 0:
  157.8 38.5 all-gather.8
  199.1 49.8 all-gather.10
  251.7 61.4 all-gather.14
  474.9 49.6 all-gather.12
  646.9 81.4 all-gather.16

commit v2 on v1

v2 whole, which is shorter than its diff:
```python
import jax
import jax.numpy as jnp
from jax import lax
from jax.experimental import pallas as pl
from jax.experimental.pallas import tpu as pltpu
from jax.sharding import PartitionSpec as P

QUERY_HEADS = 8
KEY_VALUE_HEADS = 2
HEAD_SIZE = 64
MH = 24
MP = 64
NS = 128
FF = 2048
CONV = 4
SPAN = 128


HIGHEST = lax.Precision.HIGHEST
NEGATIVE_FILL = -1e30
ROPE_BASE = 10000.0
NORM_EPS = 1e-06


def shifted(block, axis, distance):
    devices = range(lax.axis_size(axis))
    route = [(i - distance, i) for i in devices if i - distance in devices]
    return lax.ppermute(block, axis, route)


def is_fast(width):
    return lax.axis_size("seq") == 8 and lax.axis_size("batch") == 4 and width % (32 * 32) == 0


def swap(value, axis, bit):
    route = [(i, i ^ bit) for i in range(lax.axis_size(axis))]
    return lax.ppermute(value, axis, route)


def gather_stages(shard, x_first):
    rows = jnp.concatenate([shard, swap(shard, "seq", 4)], axis=0)
    rows = jnp.concatenate([rows, swap(rows, "seq", 2)], axis=0)
    along_z = rows
    if x_first:
        rows = jnp.concatenate([rows, swap(rows, "seq", 1)], axis=0)
        rows = jnp.concatenate([rows, swap(rows, "batch", 2)], axis=0)
    else:
        rows = jnp.stack([rows, swap(rows, "batch", 2)], axis=0)
        rows = jnp.stack([rows, swap(rows, "seq", 1)], axis=1)
        rows = rows.reshape(-1, rows.shape[-1])
    return along_z, jnp.concatenate([rows, swap(rows, "batch", 1)], axis=0)


def add_narrow(own, other):
    return (own.astype(jnp.float32) + other.astype(jnp.float32)).astype(jnp.bfloat16)


def scatter_stages(rows, y_first):
    size, cols = rows.shape
    if y_first:
        half = size // 2
        rows = add_narrow(rows[:half], swap(rows[half:], "batch", 2))
        half = half // 2
        rows = add_narrow(rows[:half], swap(rows[half:], "seq", 1))
    else:
        split = rows.reshape(2, 2, size // 4, cols)
        split = add_narrow(split[:, 0], swap(split[:, 1], "seq", 1))
        rows = add_narrow(split[0], swap(split[1], "batch", 2))
    half = rows.shape[0] // 2
    rows = add_narrow(rows[:half], swap(rows[half:], "seq", 2))
    half = half // 2
    return rows[:half].astype(jnp.float32) + swap(rows[half:], "seq", 4).astype(jnp.float32)


def weight_grad(left, right, fast, y_first):
    if not fast:
        full = jnp.einsum("td,tc->dc", left, right, preferred_element_type=jnp.float32)
        return lax.psum_scatter(full, ("seq", "batch"), scatter_dimension=0, tiled=True)
    half = left.shape[1] // 2
    lefts = jnp.concatenate([left[:, :half], swap(left[:, half:], "batch", 1)], axis=0)
    rights = jnp.concatenate([right, swap(right, "batch", 1)], axis=0)
    partial = jnp.einsum("td,tc->dc", lefts, rights, preferred_element_type=jnp.float32)
    return scatter_stages(partial.astype(jnp.bfloat16), y_first)


def total_small(arrays, fast):
    flat = jnp.concatenate([a.reshape(-1) for a in arrays])
    size = flat.shape[0]
    flat = jnp.pad(flat, (0, -size % 1024)).reshape(-1, 128)
    if fast:
        for axis, bit in (("batch", 1), ("batch", 2), ("seq", 1), ("seq", 2), ("seq", 4)):
            flat = flat + swap(flat, axis, bit)
    else:
        flat = lax.psum(flat, ("seq", "batch"))
    flat = flat.reshape(-1)
    out, start = [], 0
    for a in arrays:
        out.append(flat[start : start + a.size].reshape(a.shape))
        start += a.size
    return out


def own_order(width, fast):
    blocks = 32
    per = width // blocks
    row = lax.broadcasted_iota(jnp.int32, (width, width), 0)
    col = lax.broadcasted_iota(jnp.int32, (width, width), 1)
    if not fast:
        return (row == col).astype(jnp.bfloat16)
    me = lax.axis_index("seq") * 4 + lax.axis_index("batch")
    j = col // per
    flipped = (j & 1) * 16 + (j & 2) * 4 + (j & 4) + (j & 8) // 4 + (j & 16) // 16
    source = (flipped ^ me) * per + col % per
    return (row == source).astype(jnp.bfloat16)


def rms_scale(value_rows):
    return lax.rsqrt(jnp.mean(value_rows * value_rows, axis=-1, keepdims=True) + NORM_EPS)


def norm_back(value_rows, scales, gains, grads):
    gain_grad = jnp.sum(grads * value_rows * scales, axis=0)
    inner = grads * gains
    coeff = jnp.mean(inner * value_rows, axis=-1, keepdims=True)
    return (scales * (inner - value_rows * scales * scales * coeff), gain_grad)


def segments(lengths, positions):
    ends = jnp.cumsum(lengths)
    passed = ends[None, :] <= positions[:, None]
    segment = jnp.sum(passed.astype(jnp.int32), axis=1)
    device_places = positions - jnp.sum(jnp.where(passed, lengths[None, :], 0), axis=1)
    return (segment, device_places)


def conv_mix(extended, ext_segment, conv_weight, conv_bias):
    row_count = extended.shape[0] - (CONV - 1)
    summed = conv_bias[None, :]
    for lagged in range(CONV):
        same_seq = (ext_segment[lagged : lagged + row_count] == ext_segment[CONV - 1 :]).astype(
            extended.dtype
        )
        summed = (
            summed
            + conv_weight[lagged][None, :]
            * extended[lagged : lagged + row_count]
            * same_seq[:, None]
        )
    return jax.nn.silu(summed)


TILE = 128
PAIRS = QUERY_HEADS // 2
CHUNK = 256


def dot(left, right):
    return jnp.dot(left, right, preferred_element_type=jnp.float32)


def dot_nt(left, right):
    return lax.dot_general(
        left, right, (((1,), (1,)), ((), ())), preferred_element_type=jnp.float32
    )


def dot_tn(left, right):
    return lax.dot_general(
        left, right, (((0,), (0,)), ((), ())), preferred_element_type=jnp.float32
    )


def exact(left, right):
    return jnp.dot(left, right, precision=HIGHEST, preferred_element_type=jnp.float32)


def two_part(left, right):
    high = left.astype(jnp.bfloat16)
    low = (left - high.astype(jnp.float32)).astype(jnp.bfloat16)
    return dot(high, right) + dot(low, right)


def seg_start(where_at, info):
    start = jnp.zeros_like(where_at)
    for k in range(1, 4):
        start = jnp.where(where_at >= info[k], jnp.maximum(start, info[k]), start)
    return start


def big_call(kernel, outs, *args, scratch=(), flops=0, smem=0, limit=48):
    specs = [pl.BlockSpec(memory_space=pltpu.SMEM)] * smem
    specs += [pl.BlockSpec(memory_space=pltpu.VMEM)] * (len(args) - smem)
    moved = sum(a.size * a.dtype.itemsize for a in args)
    moved += sum(o.size * o.dtype.itemsize for o in outs)
    return pl.pallas_call(
        kernel,
        out_shape=list(outs),
        in_specs=specs,
        out_specs=[pl.BlockSpec(memory_space=pltpu.VMEM)] * len(outs),
        scratch_shapes=list(scratch),
        cost_estimate=pl.CostEstimate(flops=flops, bytes_accessed=moved, transcendentals=0),
        compiler_params=pltpu.CompilerParams(vmem_limit_bytes=limit * 1024 * 1024),
    )(*args)


def shape_of(shape, dtype):
    return jax.ShapeDtypeStruct(shape, dtype)


def turn(value, cosine, sine):
    lane = lax.broadcasted_iota(jnp.int32, value.shape, 1) % HEAD_SIZE
    mixed = jnp.where(
        lane < HEAD_SIZE // 2,
        -pltpu.roll(value, TILE - HEAD_SIZE // 2, 1),
        pltpu.roll(value, HEAD_SIZE // 2, 1),
    )
    return value * cosine + mixed * sine


def rope_kernel(proj, cosine, sine, q_out, kv_out):
    cos, sin = cosine[...], sine[...]
    for i in range(PAIRS):
        cols = pl.ds(i * TILE, TILE)
        turned = turn(proj[:, cols], cos, sin).astype(jnp.bfloat16)
        q_out[:, cols] = (turned.astype(jnp.float32) * HEAD_SIZE**-0.5).astype(jnp.bfloat16)
    base = PAIRS * TILE
    kv_out[:, :TILE] = turn(proj[:, base : base + TILE], cos, sin).astype(jnp.bfloat16)
    kv_out[:, TILE:] = proj[:, base + TILE : base + 2 * TILE].astype(jnp.bfloat16)


def halves_of(value):
    lane = lax.broadcasted_iota(jnp.int32, value.shape, 1)
    wide = value.astype(jnp.float32)
    first = jnp.where(lane < HEAD_SIZE, wide, 0.0).astype(value.dtype)
    return first, jnp.where(lane < HEAD_SIZE, 0.0, wide).astype(value.dtype)


def block_range(info):
    first = info[0]
    low = seg_start(first, info) // CHUNK
    return low, first // CHUNK - low + 1


def attn_mask(info, block):
    rows = lax.broadcasted_iota(jnp.int32, (CHUNK, CHUNK), 0) + block * CHUNK
    at = lax.broadcasted_iota(jnp.int32, (1, CHUNK), 1) + info[0]
    return (rows <= at) & (rows >= seg_start(at, info))


def attn_forward_kernel(info, q, kv, out, out_t, lse, heads, acc, top, total):
    for i in range(PAIRS):
        heads[2 * i], heads[2 * i + 1] = halves_of(q[:, i * TILE : (i + 1) * TILE])
    acc[...] = jnp.zeros_like(acc)
    total[...] = jnp.zeros_like(total)
    top[...] = jnp.full(top.shape, NEGATIVE_FILL, jnp.float32)
    low, count = block_range(info)

    def step(j, carry):
        block = low + j
        place = pl.ds(pl.multiple_of((block ^ info[4]) * CHUNK, CHUNK), CHUNK)
        keys = kv[place, :TILE]
        values_t = kv[place, TILE:].astype(jnp.float32).T.astype(jnp.bfloat16)
        allowed = attn_mask(info, block)
        for h in range(QUERY_HEADS):
            scores = jnp.where(allowed, dot_nt(keys, heads[h]), NEGATIVE_FILL)
            old = top[h : h + 1]
            new = jnp.maximum(old, jnp.max(scores, axis=0, keepdims=True))
            probs = jnp.where(allowed, jnp.exp(scores - new), 0.0)
            shrink = jnp.exp(old - new)
            top[h : h + 1] = new
            total[h : h + 1] = total[h : h + 1] * shrink + jnp.sum(probs, axis=0, keepdims=True)
            side = (h % 2) * HEAD_SIZE
            acc[h] = acc[h] * shrink + dot(
                values_t[side : side + HEAD_SIZE], probs.astype(jnp.bfloat16)
            )
        return carry

    lax.fori_loop(0, count, step, 0)
    lse[...] = top[...] + jnp.log(total[...])
    for i in range(PAIRS):
        pair = jnp.concatenate(
            [acc[2 * i] / total[2 * i : 2 * i + 1], acc[2 * i + 1] / total[2 * i + 1 : 2 * i + 2]],
            axis=0,
        )
        out_t[i * TILE : (i + 1) * TILE] = pair
        out[:, i * TILE : (i + 1) * TILE] = pair.T.astype(jnp.bfloat16)


def attn_forward(info, q, kv):
    rows = q.shape[0]
    f32 = jnp.float32
    return big_call(
        attn_forward_kernel,
        (
            shape_of(q.shape, jnp.bfloat16),
            shape_of(q.shape[::-1], f32),
            shape_of((QUERY_HEADS, rows), f32),
        ),
        info,
        q,
        kv,
        smem=1,
        scratch=(
            pltpu.VMEM((QUERY_HEADS, rows, TILE), jnp.bfloat16),
            pltpu.VMEM((QUERY_HEADS, HEAD_SIZE, rows), f32),
            pltpu.VMEM((QUERY_HEADS, rows), f32),
            pltpu.VMEM((QUERY_HEADS, rows), f32),
        ),
        flops=4 * rows * kv.shape[0] * q.shape[1],
    )


def attn_backward_kernel(info, q, kv, grad, out_t, lse, dq, dkv, heads, grads, delta, acc):
    for i in range(PAIRS):
        cols = slice(i * TILE, (i + 1) * TILE)
        heads[2 * i], heads[2 * i + 1] = halves_of(q[:, cols])
        grads[2 * i], grads[2 * i + 1] = halves_of(grad[:, cols])
        both = grad[:, cols].astype(jnp.float32).T * out_t[cols]
        delta[2 * i : 2 * i + 1] = jnp.sum(both[:HEAD_SIZE], axis=0, keepdims=True)
        delta[2 * i + 1 : 2 * i + 2] = jnp.sum(both[HEAD_SIZE:], axis=0, keepdims=True)
    acc[...] = jnp.zeros_like(acc)
    dkv[...] = jnp.zeros_like(dkv)
    low, count = block_range(info)

    def step(j, carry):
        block = low + j
        place = pl.ds(pl.multiple_of((block ^ info[4]) * CHUNK, CHUNK), CHUNK)
        keys = kv[place, :TILE]
        values = kv[place, TILE:]
        keys_t = keys.astype(jnp.float32).T.astype(jnp.bfloat16)
        allowed = attn_mask(info, block)
        d_keys = jnp.zeros((CHUNK, TILE), jnp.float32)
        d_values = jnp.zeros((CHUNK, TILE), jnp.float32)
        for h in range(QUERY_HEADS):
            scores = dot_nt(keys, heads[h])
            probs = jnp.where(allowed, jnp.exp(scores - lse[h : h + 1]), 0.0)
            d_probs = dot_nt(values, grads[h])
            d_scores = (probs * (d_probs - delta[h : h + 1])).astype(jnp.bfloat16)
            d_values = d_values + dot(probs.astype(jnp.bfloat16), grads[h])
            d_keys = d_keys + dot(d_scores, heads[h])
            side = (h % 2) * HEAD_SIZE
            acc[h] = acc[h] + dot(keys_t[side : side + HEAD_SIZE], d_scores)
        dkv[place, :TILE] = d_keys.astype(jnp.bfloat16)
        dkv[place, TILE:] = d_values.astype(jnp.bfloat16)
        return carry

    lax.fori_loop(0, count, step, 0)
    for i in range(PAIRS):
        pair = jnp.concatenate([acc[2 * i], acc[2 * i + 1]], axis=0)
        dq[:, i * TILE : (i + 1) * TILE] = pair.T * HEAD_SIZE**-0.5


def attn_backward(info, q, kv, grad, out_t, lse):
    rows = q.shape[0]
    f32 = jnp.float32
    return big_call(
        attn_backward_kernel,
        (shape_of(q.shape, f32), shape_of(kv.shape, jnp.bfloat16)),
        info,
        q,
        kv,
        grad,
        out_t,
        lse,
        smem=1,
        scratch=(
            pltpu.VMEM((QUERY_HEADS, rows, TILE), jnp.bfloat16),
            pltpu.VMEM((QUERY_HEADS, rows, TILE), jnp.bfloat16),
            pltpu.VMEM((QUERY_HEADS, rows), f32),
            pltpu.VMEM((QUERY_HEADS, HEAD_SIZE, rows), f32),
        ),
        flops=10 * rows * kv.shape[0] * q.shape[1],
    )


def rope_back_kernel(dq, dkv, cosine, sine, out):
    cos, sin = cosine[...], -sine[...]
    for i in range(PAIRS):
        cols = slice(i * TILE, (i + 1) * TILE)
        out[:, cols] = turn(dq[:, cols], cos, sin).astype(jnp.bfloat16)
    base = PAIRS * TILE
    out[:, base : base + TILE] = turn(dkv[:, :TILE], cos, sin).astype(jnp.bfloat16)
    out[:, base + TILE :] = dkv[:, TILE:].astype(jnp.bfloat16)


STATE_ROWS = NS + 16


def lane_pick(value, first):
    rows = value.shape[0]
    lane = lax.broadcasted_iota(jnp.int32, (rows, TILE), 1)
    return jnp.where(lane < MP, value[:, first : first + 1], value[:, first + 1 : first + 2])


def spread_heads(width):
    head = lax.broadcasted_iota(jnp.int32, (TILE, width), 0)
    col = lax.broadcasted_iota(jnp.int32, (TILE, width), 1)
    return jnp.where(head == col // MP, 1.0, 0.0).astype(jnp.bfloat16)


def gather_heads(width):
    head = lax.broadcasted_iota(jnp.int32, (width, TILE), 1)
    col = lax.broadcasted_iota(jnp.int32, (width, TILE), 0)
    return jnp.where(head == col // MP, 1.0, 0.0).astype(jnp.bfloat16)


def head_lanes(rows):
    return lax.broadcasted_iota(jnp.int32, (rows, TILE), 1) < MH


def chunk_places(info, rows):
    at = lax.broadcasted_iota(jnp.int32, (rows, 1), 0) + info[0]
    return seg_start(at, info) - info[0]


def ssm_forward_kernel(info, x, bc, step_in, head_params, y, state, dt_out, cum_out, dt_t, cum_t):
    rows = x.shape[0]
    bias, rate, skip = head_params[0:1], head_params[1:2], head_params[2:3]
    raw = step_in[...] + bias
    dt = jnp.maximum(raw, 0.0) + jnp.log1p(jnp.exp(-jnp.abs(raw)))
    dt = jnp.where(head_lanes(rows), dt, 0.0)
    row = lax.broadcasted_iota(jnp.int32, (rows, rows), 0)
    col = lax.broadcasted_iota(jnp.int32, (rows, rows), 1)
    lower = jnp.where(row >= col, 1.0, 0.0)
    cum = exact(lower, -dt * rate)
    dt_out[...] = dt
    cum_out[...] = cum
    dt_t[...] = dt.T
    cum_t[...] = cum.T
    starts = chunk_places(info, rows)
    last_start = seg_start(info[0] + rows - 1, info) - info[0]
    place = lax.broadcasted_iota(jnp.int32, (rows, 1), 0)
    end = cum[rows - 1 : rows]
    leave = jnp.where(place >= last_start, jnp.exp(jnp.minimum(end - cum, 0.0)) * dt, 0.0)
    narrow_b, narrow_c = bc[:, :NS], bc[:, NS:]
    b_t = narrow_b.astype(jnp.float32).T.astype(jnp.bfloat16)
    products = dot_nt(narrow_c, narrow_b)
    through = jnp.where(last_start < 0, jnp.exp(end), 0.0)
    high = through.astype(jnp.bfloat16).astype(jnp.float32)
    line = lax.broadcasted_iota(jnp.int32, (16, TILE), 0)
    both = jnp.where(line == 0, high, jnp.where(line == 1, through - high, 0.0))
    spread = spread_heads(x.shape[1])
    state[NS:] = dot(both.astype(jnp.bfloat16), spread).astype(jnp.bfloat16)
    skips = jnp.broadcast_to(skip, (8, TILE))
    skip_row = two_part(skips, spread)[:1]
    lane = lax.broadcasted_iota(jnp.int32, (SPAN, TILE), 1)
    for i in range(MH // 2):
        cols = slice(i * TILE, (i + 1) * TILE)
        tile = x[:, cols]
        state[:NS, cols] = dot(
            b_t, (tile.astype(jnp.float32) * lane_pick(leave, 2 * i)).astype(jnp.bfloat16)
        ).astype(jnp.bfloat16)
        for part in range(rows // SPAN):
            here = slice(part * SPAN, (part + 1) * SPAN)
            upto = (part + 1) * SPAN
            allowed = (row[here, :upto] >= col[here, :upto]) & (col[here, :upto] >= starts[here])
            sides = []
            for h in (2 * i, 2 * i + 1):
                spread_log = cum[here, h : h + 1] - cum_t[h : h + 1, :upto]
                decay = jnp.exp(jnp.where(allowed, spread_log, NEGATIVE_FILL))
                mixing = products[here, :upto] * decay * dt_t[h : h + 1, :upto]
                sides.append(dot(mixing.astype(jnp.bfloat16), tile[:upto]))
            own = skip_row[:, cols] * tile[here].astype(jnp.float32)
            y[here, cols] = jnp.where(lane < MP, sides[0], sides[1]) + own


def ssm_forward(info, x, bc, step_in, head_params):
    rows, width = x.shape
    f32 = jnp.float32
    return big_call(
        ssm_forward_kernel,
        (
            shape_of((rows, width), f32),
            shape_of((STATE_ROWS, width), jnp.bfloat16),
            shape_of((rows, TILE), f32),
            shape_of((rows, TILE), f32),
        ),
        info,
        x,
        bc,
        step_in,
        head_params,
        smem=1,
        scratch=(pltpu.VMEM((TILE, rows), f32), pltpu.VMEM((TILE, rows), f32)),
        flops=4 * rows * rows * width,
    )


def entering_of(info, cum):
    rows = cum.shape[0]
    return jnp.where(chunk_places(info, rows) < 0, jnp.exp(jnp.minimum(cum, 0.0)), 0.0)


def ssm_finish_kernel(info, y, bc, cum, state_in, z, gain, ssm_out, normed, scale):
    rows = y.shape[0]
    enter = entering_of(info, cum[...])
    narrow_c = bc[:, NS:]
    squares = jnp.zeros((rows, TILE), jnp.float32)
    tiles = MH // 2
    for i in range(tiles):
        cols = slice(i * TILE, (i + 1) * TILE)
        out = y[:, cols] + lane_pick(enter, 2 * i) * dot(narrow_c, state_in[:, cols])
        ssm_out[:, cols] = out
        gate = z[:, cols]
        gated = out * (gate * jax.nn.sigmoid(gate))
        squares = squares + gated * gated
    mean = jnp.sum(squares, axis=1, keepdims=True) * (1.0 / (tiles * TILE))
    r = lax.rsqrt(mean + NORM_EPS)
    scale[...] = jnp.broadcast_to(r, scale.shape)
    for i in range(tiles):
        cols = slice(i * TILE, (i + 1) * TILE)
        gate = z[:, cols]
        gated = ssm_out[:, cols] * (gate * jax.nn.sigmoid(gate))
        normed[:, cols] = (gated * r * gain[:, cols]).astype(jnp.bfloat16)


def ssm_finish(info, y, bc, cum, state_in, z, gain):
    rows, width = y.shape
    return big_call(
        ssm_finish_kernel,
        (
            shape_of((rows, width), jnp.float32),
            shape_of((rows, width), jnp.bfloat16),
            shape_of((rows, TILE), jnp.float32),
        ),
        info,
        y,
        bc,
        cum,
        state_in,
        z,
        gain,
        smem=1,
        flops=2 * rows * NS * width,
    )


def gate_back_kernel(info, dy, ssm_out, z, scale, gain, cum, bc, d_out, d_z, pull, g_gain):
    rows = dy.shape[0]
    tiles = MH // 2
    r = scale[:, :1]
    enter = entering_of(info, cum[...])
    c_t = bc[:, NS:].astype(jnp.float32).T.astype(jnp.bfloat16)
    inner = jnp.zeros((rows, TILE), jnp.float32)
    for i in range(tiles):
        cols = slice(i * TILE, (i + 1) * TILE)
        gate = z[:, cols]
        gated = ssm_out[:, cols] * (gate * jax.nn.sigmoid(gate))
        product = dy[:, cols] * gated
        g_gain[:, cols] = jnp.sum(product * r, axis=0, keepdims=True)
        inner = inner + product * gain[:, cols]
    coeff = jnp.sum(inner, axis=1, keepdims=True) * (1.0 / (tiles * TILE))
    for i in range(tiles):
        cols = slice(i * TILE, (i + 1) * TILE)
        gate = z[:, cols]
        sig = jax.nn.sigmoid(gate)
        silu = gate * sig
        out = ssm_out[:, cols]
        d_gated = r * (dy[:, cols] * gain[:, cols] - out * silu * (r * r * coeff))
        d_ssm = d_gated * silu
        d_out[:, cols] = d_ssm
        d_z[:, cols] = (d_gated * out * (sig * (1.0 + gate * (1.0 - sig)))).astype(jnp.bfloat16)
        pull[:, cols] = dot(c_t, (d_ssm * lane_pick(enter, 2 * i)).astype(jnp.bfloat16)).astype(
            jnp.bfloat16
        )


def gate_back(info, dy, ssm_out, z, scale, gain, cum, bc):
    rows, width = dy.shape
    return big_call(
        gate_back_kernel,
        (
            shape_of((rows, width), jnp.float32),
            shape_of((rows, width), jnp.bfloat16),
            shape_of((NS, width), jnp.bfloat16),
            shape_of((1, width), jnp.float32),
        ),
        info,
        dy,
        ssm_out,
        z,
        scale,
        gain,
        cum,
        bc,
        smem=1,
        flops=2 * rows * NS * width,
    )


def ssm_back_kernel(info, x, bc, dt, cum, grad, head_params, dx, d_bc, d_cum, d_dt, g_skip, cols_t, d_rows):
    rows, width = x.shape
    skip = head_params[2:3]
    cols_t[...] = cum[...].T
    row = lax.broadcasted_iota(jnp.int32, (rows, rows), 0)
    col = lax.broadcasted_iota(jnp.int32, (rows, rows), 1)
    at = lax.broadcasted_iota(jnp.int32, (1, rows), 1) + info[0]
    starts = seg_start(at, info) - info[0]
    narrow_b, narrow_c = bc[:, :NS], bc[:, NS:]
    products = dot_nt(narrow_b, narrow_c)
    skip_row = two_part(jnp.broadcast_to(skip, (8, TILE)), spread_heads(width))[:1]
    lane = lax.broadcasted_iota(jnp.int32, (SPAN, TILE), 1)
    parts = rows // SPAN
    d_products = [jnp.zeros((SPAN, rows - p * SPAN), jnp.float32) for p in range(parts)]
    d_rows[...] = jnp.zeros_like(d_rows)
    step_sums = [jnp.zeros((SPAN, TILE), jnp.float32) for p in range(parts)]
    skip_sums = []
    for i in range(MH // 2):
        cols = slice(i * TILE, (i + 1) * TILE)
        tile = x[:, cols]
        wide = grad[:, cols]
        narrow = wide.astype(jnp.bfloat16)
        skip_sums.append(jnp.sum(wide * tile.astype(jnp.float32), axis=0, keepdims=True))
        tile_sides = halves_of(tile)
        for part in range(parts):
            here = slice(part * SPAN, (part + 1) * SPAN)
            since = part * SPAN
            allowed = (row[here, since:] <= col[here, since:]) & (
                row[here, since:] >= starts[:, since:]
            )
            sides = []
            for side in range(2):
                h = 2 * i + side
                spread_log = cols_t[h : h + 1, since:] - cum[here, h : h + 1]
                decay = jnp.exp(jnp.where(allowed, spread_log, NEGATIVE_FILL))
                decay_dt = decay * dt[here, h : h + 1]
                mixing = products[here, since:] * decay_dt
                sides.append(dot(mixing.astype(jnp.bfloat16), narrow[since:]))
                d_mixing = dot_nt(tile_sides[side][here], narrow[since:])
                d_products[part] = d_products[part] + d_mixing * decay_dt
                whole = d_mixing * mixing
                d_rows[h : h + 1, since:] += jnp.sum(whole, axis=0, keepdims=True)
                weighed = d_mixing * (products[here, since:] * decay)
                step_sums[part] = jnp.where(
                    lane == h, jnp.sum(weighed, axis=1, keepdims=True), step_sums[part]
                )
            dx[here, cols] = (
                jnp.where(lane < MP, sides[0], sides[1]) + skip_row[:, cols] * wide[here]
            )
    all_steps = jnp.concatenate(step_sums, axis=0)
    d_dt[...] = all_steps
    d_cum[...] = d_rows[...].T - all_steps * dt[...]
    g_skip[...] = jnp.broadcast_to(
        two_part(
            jnp.broadcast_to(jnp.concatenate(skip_sums, axis=1), (8, width)), gather_heads(width)
        ),
        g_skip.shape,
    )
    full = jnp.concatenate(
        [
            d
            if p == 0
            else jnp.concatenate([jnp.zeros((SPAN, p * SPAN), jnp.float32), d], axis=1)
            for p, d in enumerate(d_products)
        ],
        axis=0,
    ).astype(jnp.bfloat16)
    d_bc[:, :NS] = dot(full, narrow_c)
    d_bc[:, NS:] = dot_tn(full, narrow_b)


def ssm_back(info, x, bc, dt, cum, grad, head_params):
    rows, width = x.shape
    f32 = jnp.float32
    return big_call(
        ssm_back_kernel,
        (
            shape_of((rows, width), f32),
            shape_of((rows, 2 * NS), f32),
            shape_of((rows, TILE), f32),
            shape_of((rows, TILE), f32),
            shape_of((8, TILE), f32),
        ),
        info,
        x,
        bc,
        dt,
        cum,
        grad,
        head_params,
        smem=1,
        scratch=(pltpu.VMEM((TILE, rows), f32), pltpu.VMEM((TILE, rows), f32)),
        flops=8 * rows * rows * width,
    )


def state_back_kernel(
    info, x, bc, dt, cum, grad, head_params, step_in, state_in, d_state, dx_in, d_bc_in, d_cum_in,
    d_dt_in, dx, d_bc, d_step, sums,
):
    rows, width = x.shape
    bias, rate = head_params[0:1], head_params[1:2]
    cums, steps = cum[...], dt[...]
    enter = entering_of(info, cums)
    last_start = seg_start(info[0] + rows - 1, info) - info[0]
    place = lax.broadcasted_iota(jnp.int32, (rows, 1), 0)
    end = cums[rows - 1 : rows]
    fade = jnp.where(place >= last_start, jnp.exp(jnp.minimum(end - cums, 0.0)), 0.0)
    leave = fade * steps
    through = jnp.where(last_start < 0, jnp.exp(end), 0.0)
    narrow_b, narrow_c = bc[:, :NS], bc[:, NS:]
    pick = gather_heads(width)
    d_leave = jnp.zeros((rows, TILE), jnp.float32)
    d_enter = jnp.zeros((rows, TILE), jnp.float32)
    d_b = d_bc_in[:, :NS]
    d_c = d_bc_in[:, NS:]
    link = jnp.zeros((8, TILE), jnp.float32)
    for i in range(MH // 2):
        cols = slice(i * TILE, (i + 1) * TILE)
        tile = x[:, cols].astype(jnp.float32)
        wide = grad[:, cols]
        pulled = d_state[:, cols]
        held = state_in[:, cols]
        from_b = dot(narrow_b, pulled)
        leave_tile = lane_pick(leave, 2 * i)
        dx[:, cols] = dx_in[:, cols] + leave_tile * from_b
        d_leave = d_leave + two_part(tile * from_b, pick[cols])
        d_enter = d_enter + two_part(wide * dot(narrow_c, held), pick[cols])
        d_b = d_b + dot_nt((tile * leave_tile).astype(jnp.bfloat16), pulled)
        d_c = d_c + dot_nt((wide * lane_pick(enter, 2 * i)).astype(jnp.bfloat16), held)
        meet = jnp.sum(
            pulled.astype(jnp.float32) * held.astype(jnp.float32), axis=0, keepdims=True
        )
        link = link + two_part(jnp.broadcast_to(meet, (8, TILE)), pick[cols])
    d_bc[:, :NS] = d_b
    d_bc[:, NS:] = d_c
    left = leave * d_leave
    d_cum = d_cum_in[...] + enter * d_enter - left
    at_end = jnp.sum(left, axis=0, keepdims=True) + through * link[:1]
    d_cum = d_cum + jnp.where(place == rows - 1, at_end, 0.0)
    row = lax.broadcasted_iota(jnp.int32, (rows, rows), 0)
    col = lax.broadcasted_iota(jnp.int32, (rows, rows), 1)
    d_log = exact(jnp.where(row <= col, 1.0, 0.0), d_cum)
    d_steps = d_dt_in[...] + fade * d_leave - d_log * rate
    d_pre = d_steps * jax.nn.sigmoid(step_in[...] + bias)
    d_pre = jnp.where(head_lanes(rows), d_pre, 0.0)
    d_step[...] = d_pre.astype(jnp.bfloat16)
    g_rate = jnp.sum(d_log * (-steps * rate), axis=0, keepdims=True)
    g_bias = jnp.sum(d_pre, axis=0, keepdims=True)
    line = lax.broadcasted_iota(jnp.int32, (8, TILE), 0)
    sums[...] = jnp.where(line == 0, g_rate, jnp.where(line == 1, g_bias, 0.0))


def state_back(info, *args):
    rows, width = args[0].shape
    f32 = jnp.float32
    return big_call(
        state_back_kernel,
        (
            shape_of((rows, width), f32),
            shape_of((rows, 2 * NS), f32),
            shape_of((rows, TILE), jnp.bfloat16),
            shape_of((8, TILE), f32),
        ),
        info,
        *args,
        smem=1,
        flops=12 * rows * NS * width,
    )


def join_states(earlier, later):
    decay = later[NS : NS + 1].astype(jnp.float32) + later[NS + 1 : NS + 2].astype(jnp.float32)
    before = earlier[NS : NS + 1].astype(jnp.float32) + earlier[NS + 1 : NS + 2].astype(jnp.float32)
    state = decay * earlier[:NS].astype(jnp.float32) + later[:NS].astype(jnp.float32)
    both = decay * before
    high = both.astype(jnp.bfloat16)
    low = (both - high.astype(jnp.float32)).astype(jnp.bfloat16)
    rest = jnp.zeros((STATE_ROWS - NS - 2, state.shape[1]), jnp.bfloat16)
    return jnp.concatenate([state.astype(jnp.bfloat16), high, low, rest], axis=0)


def scan_states(own, fast, forward):
    place = lax.axis_index("seq")
    count = lax.axis_size("seq")
    nothing = jnp.concatenate(
        [
            jnp.zeros((NS, own.shape[1]), own.dtype),
            jnp.ones((1, own.shape[1]), own.dtype),
            jnp.zeros((STATE_ROWS - NS - 1, own.shape[1]), own.dtype),
        ],
        axis=0,
    )
    if fast:
        reach, before = own, nothing
        for bit in (1, 2, 4):
            other = swap(reach, "seq", bit)
            second = ((place & bit) != 0) == forward
            before = jnp.where(second, join_states(other, before), before)
            if bit != 4:
                reach = jnp.where(second, join_states(other, reach), join_states(reach, other))
        return before[:NS]
    everything = lax.all_gather(own, "seq")

    def step(k, before):
        index = k if forward else count - 1 - k
        reached = index < place if forward else index > place
        part = lax.dynamic_index_in_dim(everything, index, 0, False)
        return jnp.where(reached, join_states(before, part), before)

    return lax.fori_loop(0, count, step, nothing)[:NS]


def seq_gather(value, fast):
    if not fast:
        return lax.all_gather(value, "seq", axis=0, tiled=True)
    rows = jnp.stack([value, swap(value, "seq", 4)], axis=0)
    rows = jnp.stack([rows, swap(rows, "seq", 2)], axis=1)
    rows = jnp.stack([rows, swap(rows, "seq", 1)], axis=2)
    return rows.reshape(-1, value.shape[1])


def seq_scatter(value, fast):
    if not fast:
        return lax.psum_scatter(
            value.astype(jnp.float32), "seq", scatter_dimension=0, tiled=True
        )
    size, cols = value.shape
    parts = value.reshape(4, 2, size // 8, cols)
    parts = add_narrow(parts[:, 0], swap(parts[:, 1], "seq", 1))
    parts = add_narrow(parts[:2], swap(parts[2:], "seq", 4))
    return parts[0].astype(jnp.float32) + swap(parts[1], "seq", 2).astype(jnp.float32)


def pair_heads(value, back=False):
    rows = value.shape[0]
    group = QUERY_HEADS // KEY_VALUE_HEADS
    width = QUERY_HEADS * HEAD_SIZE
    shape = (group, KEY_VALUE_HEADS) if back else (KEY_VALUE_HEADS, group)
    moved = value[:, :width].reshape(rows, *shape, HEAD_SIZE).transpose(0, 2, 1, 3)
    return jnp.concatenate([moved.reshape(rows, width), value[:, width:]], axis=1)


def on_device(
    layer_input,
    seq_lengths,
    w_attn,
    w_ssm_in,
    w_dt,
    w_out,
    w_gate_up,
    w_down,
    norm_gain,
    mlp_gain,
    ssm_gain,
    conv_w,
    conv_b,
    a_log,
    dt_bias,
    d_skip,
    out_grad,
):
    token_rows = layer_input.shape[1]
    query_width = QUERY_HEADS * HEAD_SIZE
    key_value_width = KEY_VALUE_HEADS * HEAD_SIZE
    attn_width = query_width + 2 * key_value_width
    ssm_width = MH * MP
    xbc_width = ssm_width + 2 * NS
    width = layer_input.shape[2]
    fast = is_fast(width)
    seq_lens = seq_lengths[0]
    first_pos = lax.axis_index("seq") * token_rows
    positions = first_pos + jnp.arange(token_rows, dtype=jnp.int32)
    segment, device_places = segments(seq_lens, positions)
    mask = lax.axis_index("seq") if fast else 0
    ends = jnp.cumsum(seq_lens)
    info = jnp.stack([first_pos, ends[0], ends[1], ends[2], mask]).astype(jnp.int32)
    half = HEAD_SIZE // 2
    freqs = ROPE_BASE ** (-jnp.arange(half, dtype=jnp.float32) / half)
    angles = device_places.astype(jnp.float32)[:, None] * jnp.tile(freqs, TILE // half)[None, :]
    cosine, sine = jnp.cos(angles), jnp.sin(angles)
    order = own_order(width, fast)
    wide_order = order.astype(jnp.float32)

    def to_own(value):
        if not fast:
            return value
        return jnp.dot(value, order, preferred_element_type=jnp.float32).astype(value.dtype)

    def to_plain(value):
        if not fast:
            return value
        return jnp.einsum("tc,dc->td", value, order, preferred_element_type=jnp.float32)

    def to_plain_wide(value):
        if not fast:
            return value
        return jnp.einsum("tc,dc->td", value, wide_order, precision=HIGHEST)

    def gain_own(value):
        if not fast:
            return value
        return jnp.dot(value, wide_order, precision=HIGHEST)

    gains = gain_own(jnp.stack([norm_gain, mlp_gain]))
    norm_gain, mlp_gain = gains[0], gains[1]
    x_rows = to_own(layer_input[0]).astype(jnp.float32)
    grad_rows = to_own(out_grad[0])
    head_params = jnp.pad(
        jnp.stack([dt_bias, jnp.exp(a_log), d_skip]), ((0, 5), (0, TILE - MH))
    )
    step_pad = jnp.pad(w_dt, ((0, 0), (0, TILE - MH)))
    out_shard = pair_heads(w_out.T)
    down_shard = w_down.T
    shards = (
        jnp.concatenate([w_ssm_in[:, ssm_width:], step_pad], axis=1),
        jnp.concatenate([pair_heads(w_attn), w_ssm_in[:, :ssm_width]], axis=1),
        out_shard[:, : w_out.shape[0] // 2],
        out_shard[:, w_out.shape[0] // 2 :],
        w_gate_up[:, :FF],
        w_gate_up[:, FF:],
        down_shard[:, : FF // 2],
        down_shard[:, FF // 2 :],
    )
    full = []
    ahead = None
    for i in range(0, 8, 2):
        pair = shards[i : i + 2]
        if fast:
            if ahead is not None:
                pair, ahead = lax.optimization_barrier((pair, ahead))
            za, fa = gather_stages(pair[0], True)
            zb, fb = gather_stages(pair[1], False)
            ahead = (za, zb)
            full += [fa, fb]
        else:
            full += [lax.all_gather(p, ("seq", "batch"), axis=0, tiled=True) for p in pair]
    full_conv, full_mix, out_a, out_b, full_gate, full_up, down_a, down_b = full
    scale_one = rms_scale(x_rows)
    normed = (x_rows * scale_one * norm_gain).astype(jnp.bfloat16)
    conv_proj = jnp.dot(normed, full_conv, preferred_element_type=jnp.float32)
    mix_proj = jnp.dot(normed, full_mix, preferred_element_type=jnp.float32)
    queries, own_pairs = big_call(
        rope_kernel,
        (
            shape_of((token_rows, query_width), jnp.bfloat16),
            shape_of((token_rows, 2 * key_value_width), jnp.bfloat16),
        ),
        mix_proj[:, :attn_width],
        cosine,
        sine,
    )
    all_pairs = seq_gather(own_pairs, fast)
    gate_z = mix_proj[:, attn_width:]
    raw_xbc = conv_proj[:, :xbc_width]
    step_proj = conv_proj[:, xbc_width:]
    rim_rows = shifted(raw_xbc[token_rows - (CONV - 1) :], "seq", 1)
    extended = jnp.concatenate([rim_rows, raw_xbc], axis=0)
    ext_pos = first_pos - (CONV - 1) + jnp.arange(token_rows + CONV - 1, dtype=jnp.int32)
    ext_segment = segments(seq_lens, ext_pos)[0]

    def conv_local(ext_rows, conv_weight, conv_bias):
        return conv_mix(ext_rows, ext_segment, conv_weight, conv_bias)

    conv_out, conv_pullback = jax.vjp(conv_local, extended, conv_w, conv_b)
    conv_narrow = conv_out.astype(jnp.bfloat16)
    inputs_x, inputs_bc = conv_narrow[:, :ssm_width], conv_narrow[:, ssm_width:]
    ssm_local, state_own, steps_dt, running_decay = ssm_forward(
        info, inputs_x, inputs_bc, step_proj, head_params
    )
    state_in = scan_states(state_own, fast, True)
    attended, attended_t, log_total = attn_forward(info, queries, all_pairs)
    ssm_flat, ssm_normed, scale_gated = ssm_finish(
        info, ssm_local, inputs_bc, running_decay, state_in, gate_z, ssm_gain[None]
    )
    joined = jnp.concatenate([attended, ssm_normed], axis=1)
    half_in = joined.shape[1] // 2

    def narrow_out(left, parts):
        cut = left.shape[1] // 2
        return jnp.einsum(
            "tc,dc->td", left[:, :cut], parts[0], preferred_element_type=jnp.float32
        ) + jnp.einsum("tc,dc->td", left[:, cut:], parts[1], preferred_element_type=jnp.float32)

    middle = x_rows + narrow_out(joined, (out_a, out_b))
    scale_two = rms_scale(middle)
    normed_two = (middle * scale_two * mlp_gain).astype(jnp.bfloat16)
    gate_part = jnp.dot(normed_two, full_gate, preferred_element_type=jnp.float32)
    up_part = jnp.dot(normed_two, full_up, preferred_element_type=jnp.float32)
    hidden = (jax.nn.silu(gate_part) * up_part).astype(jnp.bfloat16)
    layer_out = middle + narrow_out(hidden, (down_a, down_b))
    g_down = [
        weight_grad(grad_rows, hidden[:, : FF // 2], fast, True),
        weight_grad(grad_rows, hidden[:, FF // 2 :], fast, False),
    ]
    d_hidden = jnp.concatenate(
        [
            jnp.dot(grad_rows, down_a, preferred_element_type=jnp.float32),
            jnp.dot(grad_rows, down_b, preferred_element_type=jnp.float32),
        ],
        axis=1,
    )
    sig_gate = jax.nn.sigmoid(gate_part)
    d_gate = (d_hidden * up_part * (sig_gate * (1.0 + gate_part * (1.0 - sig_gate)))).astype(
        jnp.bfloat16
    )
    d_up = (d_hidden * gate_part * sig_gate).astype(jnp.bfloat16)
    g_gate_up = [
        weight_grad(normed_two, d_gate, fast, True),
        weight_grad(normed_two, d_up, fast, False),
    ]
    d_normed_two = narrow_out(jnp.concatenate([d_gate, d_up], axis=1), (full_gate, full_up))
    d_middle_norm, g_mlp_gain = norm_back(middle, scale_two, mlp_gain, d_normed_two)
    d_middle = grad_rows.astype(jnp.float32) + d_middle_norm
    d_mixer = d_middle.astype(jnp.bfloat16)
    g_out = [
        weight_grad(d_mixer, joined[:, :half_in], fast, True),
        weight_grad(d_mixer, joined[:, half_in:], fast, False),
    ]
    d_joined = jnp.concatenate(
        [
            jnp.dot(d_mixer, out_a, preferred_element_type=jnp.float32),
            jnp.dot(d_mixer, out_b, preferred_element_type=jnp.float32),
        ],
        axis=1,
    )
    attended_gradient = d_joined[:, :query_width].astype(jnp.bfloat16)
    d_ssm_out, d_gate_z, pull, g_ssm_gain = gate_back(
        info,
        d_joined[:, query_width:],
        ssm_flat,
        gate_z,
        scale_gated,
        ssm_gain[None],
        running_decay,
        inputs_bc,
    )
    d_state = scan_states(jnp.concatenate([pull, state_own[NS:]], axis=0), fast, False)
    d_queries, d_pairs = attn_backward(
        info, queries, all_pairs, attended_gradient, attended_t, log_total
    )
    own_d_pairs = seq_scatter(d_pairs, fast)
    dx_part, d_bc_part, d_cum_part, d_dt_part, g_skip_rows = ssm_back(
        info, inputs_x, inputs_bc, steps_dt, running_decay, d_ssm_out, head_params
    )
    g_inputs_x, g_inputs_bc, d_step_pad, head_sums = state_back(
        info,
        inputs_x,
        inputs_bc,
        steps_dt,
        running_decay,
        d_ssm_out,
        head_params,
        step_proj,
        state_in,
        d_state,
        dx_part,
        d_bc_part,
        d_cum_part,
        d_dt_part,
    )
    g_a_log, g_dt_bias, g_d_skip = head_sums[0, :MH], head_sums[1, :MH], g_skip_rows[0, :MH]
    d_conv_out = jnp.concatenate([g_inputs_x, g_inputs_bc], axis=1)
    g_extended, g_conv_w, g_conv_b = conv_pullback(d_conv_out)
    back_rim = shifted(g_extended[: CONV - 1], "seq", -1)
    d_raw = g_extended[CONV - 1 :] + jnp.concatenate(
        [jnp.zeros((token_rows - (CONV - 1), xbc_width), jnp.float32), back_rim], axis=0
    )
    d_conv_proj = jnp.concatenate([d_raw.astype(jnp.bfloat16), d_step_pad], axis=1)
    (d_attn_proj,) = big_call(
        rope_back_kernel,
        (shape_of((token_rows, attn_width), jnp.bfloat16),),
        d_queries,
        own_d_pairs,
        cosine,
        sine,
    )
    d_mix_proj = jnp.concatenate([d_attn_proj, d_gate_z], axis=1)
    g_conv_in = weight_grad(normed, d_conv_proj, fast, True)
    g_mix_in = weight_grad(normed, d_mix_proj, fast, False)
    d_normed = jnp.einsum(
        "tc,dc->td", d_conv_proj, full_conv, preferred_element_type=jnp.float32
    ) + jnp.einsum("tc,dc->td", d_mix_proj, full_mix, preferred_element_type=jnp.float32)
    d_input_norm, g_norm_gain = norm_back(x_rows, scale_one, norm_gain, d_normed)
    input_grad = d_middle + d_input_norm
    grad_attn = pair_heads(g_mix_in[:, :attn_width], True)
    grad_ssm_in = jnp.concatenate([g_mix_in[:, attn_width:], g_conv_in[:, :xbc_width]], axis=1)
    grad_dt = g_conv_in[:, xbc_width : xbc_width + MH]
    grad_out = pair_heads(jnp.concatenate(g_out, axis=1), True).T
    grad_gate_up = jnp.concatenate(g_gate_up, axis=1)
    grad_down = jnp.concatenate(g_down, axis=1).T
    gain_grads = to_plain_wide(jnp.stack([g_norm_gain, g_mlp_gain]))
    small_sums = total_small(
        (
            gain_grads[0],
            gain_grads[1],
            g_ssm_gain[0],
            g_conv_w,
            g_conv_b,
            g_a_log,
            g_dt_bias,
            g_d_skip,
        ),
        fast,
    )
    return (
        to_plain(layer_out.astype(jnp.bfloat16)).astype(jnp.bfloat16)[None],
        to_plain_wide(input_grad)[None],
        grad_attn,
        grad_ssm_in,
        grad_dt,
        grad_out,
        grad_gate_up,
        grad_down,
        *small_sums,
    )


def solution(mesh):
    return jax.shard_map(
        on_device,
        mesh=mesh,
        in_specs=(
            P("batch", "seq", None),
            P("batch", None),
            P(("seq", "batch"), None),
            P(("seq", "batch"), None),
            P(("seq", "batch"), None),
            P(None, ("seq", "batch")),
            P(("seq", "batch"), None),
            P(None, ("seq", "batch")),
            P(),
            P(),
            P(),
            P(),
            P(),
            P(),
            P(),
            P(),
            P("batch", "seq", None),
        ),
        out_specs=(
            P("batch", "seq", None),
            P("batch", "seq", None),
            P(("seq", "batch"), None),
            P(("seq", "batch"), None),
            P(("seq", "batch"), None),
            P(None, ("seq", "batch")),
            P(("seq", "batch"), None),
            P(None, ("seq", "batch")),
            P(),
            P(),
            P(),
            P(),
            P(),
            P(),
            P(),
            P(),
        ),
        check_vma=False,
    )
```

time: 1160 us -> 628 us (0.54)
  local copies, waits for them, and re-layouts: 254 us -> 53.5 us
  matrix products: 204 us -> 77.1 us
  blocking collectives: 126 us -> 0 us
  other arithmetic: 156 us -> 45.6 us
  starting transfers between devices: 89.2 us -> 153 us
  loops' own time: 44.2 us -> 0 us
  Pallas kernels: 0 us -> 35.1 us
  between operations: 18.5 us -> 4.33 us
    all_gather x3 -> x0, blocking collectives: 126 us -> none  [the longest x1 57.2 us: on_device(): lax.all_gather(delta.reshape(QUERY_HEADS, token_rows), 'seq', axis=1, til...]
    dot_general x47 -> x3, matrix products: 131 us -> 9.65 us  [the longest x2 7.8 us: to_plain_wide(): return jnp.einsum('tc,dc->td', value, wide_order, precision=HIGHEST)]
    ppermute x89 -> x101, starting transfers between devices: 83.6 us -> 147 us  [swap(): return lax.ppermute(value, axis, route)]
    dynamic_update_slice x22 -> x0, local copies, waits for them, and re-layouts: 46.9 us -> none  [ssd_blocks(): lax.scan(ssd_advance, (state_in, segment_before), blocks)]
    another operation x20 -> x0, loops' own time: 44.2 us -> none  [the longest x1 10.7 us: on_device(): running_total, unused_out = lax.scan(attend_advance, running_total, blocks)]
    pallas_call x0 -> x9, Pallas kernels: none -> 35.1 us  [big_call(): pl.pallas_call(kernel, out_shape=list(outs), in_specs=specs, out_specs=[p...]
    reshape x13 -> x11, local copies, waits for them, and re-layouts: 32.1 us -> 1.07 us  [the longest x7 0.6 us: pair_heads(): value[:, :width].reshape(rows, *shape, HEAD_SIZE).transpose(0, 2, 1, 3)]
    slice x62 -> x22, local copies, waits for them, and re-layouts: 34.8 us -> 9.69 us  [the longest x3 1.62 us: pair_heads(): value[:, width:]]
  transfers between devices with their start and end apart: 96 -> 103, of which waited for: 45 -> 54; matrix products, arithmetic and copies ran while one was open for 52% -> 26% of each run, Pallas kernels for 0% -> 6%
where the time goes in v2:
time: 628 us; the launch traced here: 618 us
  waiting for transfers between devices  250 us (40%)
  starting transfers between devices  153 us (24%)
  matrix products  77.1 us (12%)
  local copies, waits for them, and re-layouts  53.5 us (9%)
  other arithmetic  45.6 us (7%)
  Pallas kernels  35.1 us (6%)
    ppermute x101, waiting for transfers between devices, swap(): return lax.ppermute(value, axis, route)  246 us
    ppermute x101, starting transfers between devices, swap(): return lax.ppermute(value, axis, route)  147 us
    pallas_call x9, Pallas kernels, big_call(): pl.pallas_call(kernel, out_shape=list(outs), in_specs=specs, out_specs=[p...  35.1 us
    dot_general x8, matrix products, weight_grad(): jnp.einsum('td,tc->dc', lefts, rights, preferred_element_type=jnp.float32)  16.3 us
    unnamed x321, local copies, waits for them, and re-layouts  14.8 us
  transfers between devices with their start and end apart: 103, of which 54 were waited for; matrix products, arithmetic and copies ran while one was open for 26% of the time, Pallas kernels for 6%

profile of v2, /device:TPU:0, one launch (start us, length us, event | category | flops | bytes accessed | tf_op | source)
XLA Modules:
  0.0 618.4 jit_solution(7457072953583349749)
XLA Ops:
  4.1 4.0 collective-permute-start
  15.1 2.7 convolution_convert_fusion.8
  34.7 6.1 collective-permute-done.9
  46.6 2.7 collective-permute-start.17
  58.8 3.3 collective-permute-done.23
  67.3 5.7 collective-permute-done.27
  85.9 3.0 collective-permute-start.29
  90.2 4.4 collective-permute-done.37
  95.2 5.0 collective-permute-done.42
  101.2 5.2 collective-permute-done.38
  106.7 4.6 collective-permute-done.43
  111.3 2.7 collective-permute-start.34
  115.3 13.2 %collective-permute-done.44 = bf16[128,1024]{1,0:T(8,128)(2,1)S(1)} collective-permute-done((bf16[128,1024]{1,0:T(8,128)(2,1)S(1)}, bf16[128,1024]{1,0:T(8,128)(2,1)S(1)}, u32[]{:S(2)}, u32[]{:S(2)}) %collective-permute-start.44) | collective-permute-done | bytes 262176 | tf_op jit(solution)/shard_map/ppermute | solution.py:37
  133.8 11.7 %collective-permute-done.40 = bf16[256,1024]{1,0:T(8,128)(2,1)S(1)} collective-permute-done((bf16[256,1024]{1,0:T(8,128)(2,1)S(1)}, bf16[256,1024]{1,0:T(8,128)(2,1)S(1)}, u32[]{:S(2)}, u32[]{:S(2)}) %collective-permute-start.40) | collective-permute-done | bytes 524320 | tf_op jit(solution)/shard_map/ppermute | solution.py:37
  146.4 22.6 %collective-permute-done.45 = bf16[2,128,1024]{2,1,0:T(8,128)(2,1)S(1)} collective-permute-done((bf16[2,128,1024]{2,1,0:T(8,128)(2,1)S(1)}, bf16[2,128,1024]{2,1,0:T(8,128)(2,1)S(1)}, u32[]{:S(2)}, u32[]{:S(2)}) %collective-permute-start.45) | collective-permute-done | bytes 524320 | tf_op jit(solution)/shard_map/ppermute | solution.py:37
  172.9 16.4 %collective-permute-done.35 = bf16[2,128,2048]{2,1,0:T(8,128)(2,1)S(1)} collective-permute-done((bf16[2,128,2048]{2,1,0:T(8,128)(2,1)S(1)}, bf16[2,128,2048]{2,1,0:T(8,128)(2,1)S(1)}, u32[]{:S(2)}, u32[]{:S(2)}) %collective-permute-start.35) | collective-permute-done | bytes 1048608 | tf_op jit(solution)/shard_map/ppermute | solution.py:37
  194.2 4.0 collective-permute-start.13
  203.1 3.7 shard_map.290
  208.5 2.9 fusion.57
  212.1 7.3 %collective-permute-done.14 = bf16[144,1536]{1,0:T(8,128)(2,1)S(1)} collective-permute-done((bf16[144,1536]{1,0:T(8,128)(2,1)S(1)}, bf16[144,1536]{1,0:T(8,128)(2,1)S(1)}, u32[]{:S(2)}, u32[]{:S(2)}) %collective-permute-start.14) | collective-permute-done | bytes 442400 | tf_op jit(solution)/shard_map/ppermute | solution.py:37
  221.6 3.1 fusion.29
  226.5 5.2 collective-permute-done.15
  233.3 6.1 collective-permute-done.5
  243.6 8.7 %collective-permute-done.6 = bf16[2,256,256]{2,1,0:T(8,128)(2,1)S(1)} collective-permute-done((bf16[2,256,256]{2,1,0:T(8,128)(2,1)S(1)}, bf16[2,256,256]{2,1,0:T(8,128)(2,1)S(1)}, u32[]{:S(2)}, u32[]{:S(2)}) %collective-permute-start.6) | collective-permute-done | bytes 262176 | tf_op jit(solution)/shard_map/ppermute | solution.py:37
  252.4 6.8 %collective-permute-done.16 = bf16[144,1536]{1,0:T(8,128)(2,1)S(1)} collective-permute-done((bf16[144,1536]{1,0:T(8,128)(2,1)S(1)}, bf16[144,1536]{1,0:T(8,128)(2,1)S(1)}, u32[]{:S(2)}, u32[]{:S(2)}) %collective-permute-start.16) | collective-permute-done | bytes 442400 | tf_op jit(solution)/shard_map/ppermute | solution.py:37
  261.2 2.8 shard_map.291
  264.0 2.9 fusion.60
  266.9 6.0 collective-permute-done.7
  273.1 3.7 shard_map.289
  279.9 3.6 fusion.31
  283.9 3.2 multiply_convert_fusion.1
  287.2 4.6 fusion.30
  297.6 4.0 shard_map.292
  302.5 4.3 collective-permute-start.47
  306.8 3.4 shard_map.295
  315.3 2.9 fusion.58
  318.2 4.8 fusion.64
  324.9 11.4 %shard_map.293 = (f32[256,1536]{1,0:T(8,128)S(1)}, f32[256,256]{1,0:T(8,128)S(1)}, f32[256,128]{1,0:T(8,128)S(1)}, f32[256,128]{1,0:T(8,128)S(1)}, f32[8,128]{1,0:T(8,128)S(1)}) custom-call(s32[5]{0:T(128)S(1)} %stack.140.info, bf16[256,1536]{1,0:T(8,128)(2,1)S(1)} %slice.830.x, bf16[256,256]{1,0:T(8,128)(2,1)S(1)} %slice.831.bc, f32[256,128]{1,0:T(8,128)S(1)} %copy-done.19, ...), custom_call_target="tpu_custom_call" | custom-call | flops 805306368 | bytes 4857876 | tf_op jit(solution)/shard_map/pallas_call | solution.py:195
  355.4 8.3 %collective-permute-start.48 = (bf16[144,1536]{1,0:T(8,128)(2,1)S(1)}, bf16[144,1536]{1,0:T(8,128)(2,1)S(1)}, u32[]{:S(2)}, u32[]{:S(2)}) collective-permute-start(bf16[144,1536]{1,0:T(8,128)(2,1)S(1)} %get-tuple-element.305), channel_id=1, source_target_pairs={{0,8},{4,12},{8,0},{12,4},{16,24},{20,28},{24,16},{28,20},{1,9},{5... | collective-permute-start | bytes 1327112 | tf_op jit(solution)/shard_map/ppermute | solution.py:37
  365.2 21.3 %collective-permute-start.52 = (bf16[2,256,256]{2,1,0:T(8,128)(2,1)S(1)}, bf16[2,256,256]{2,1,0:T(8,128)(2,1)S(1)}, u32[]{:S(2)}, u32[]{:S(2)}) collective-permute-start(bf16[2,256,256]{2,1,0:T(8,128)(2,1)S(1)} %slice.887), channel_id=1, source_target_pairs={{0,16},{4,20},{8,24},{12,28},{16,0},{20,4},{24,8},{28,12},{1,17},{... | collective-permute-start | bytes 786440 | tf_op jit(solution)/shard_map/ppermute | solution.py:37
  388.2 5.0 collective-permute-done.52
  393.1 9.4 %collective-permute-start.89 = (bf16[256,1024]{1,0:T(8,128)(2,1)S(1)}, bf16[256,1024]{1,0:T(8,128)(2,1)S(1)}, u32[]{:S(2)}, u32[]{:S(2)}) collective-permute-start(bf16[256,1024]{1,0:T(8,128)(2,1)S(1)} %slice.953), channel_id=1, source_target_pairs={{0,2},{1,3},{2,0},{3,1},{4,6},{5,7},{6,4},{7,5},{8,10},{9,11},{10,... | collective-permute-start | bytes 1572872 | tf_op jit(solution)/shard_map/ppermute | solution.py:37
  402.7 8.2 %collective-permute-start.53 = (bf16[256,256]{1,0:T(8,128)(2,1)S(1)}, bf16[256,256]{1,0:T(8,128)(2,1)S(1)}, u32[]{:S(2)}, u32[]{:S(2)}) collective-permute-start(bf16[256,256]{1,0:T(8,128)(2,1)S(1)} %slice_bitcast_fusion.18), channel_id=1, source_target_pairs={{0,8},{4,12},{8,0},{12,4},{16,24},{20,28},{24,16},{28,20},{1,9},{5... | collective-permute-start | bytes 393224 | tf_op jit(solution)/shard_map/ppermute | solution.py:37
  415.7 4.1 fusion.28
  420.4 6.7 %collective-permute-done.94 = bf16[2,128,1024]{2,1,0:T(8,128)(2,1)S(1)} collective-permute-done((bf16[2,128,1024]{2,1,0:T(8,128)(2,1)}, bf16[2,128,1024]{2,1,0:T(8,128)(2,1)S(1)}, u32[]{:S(2)}, u32[]{:S(2)}) %collective-permute-start.94) | collective-permute-done | bytes 524320 | tf_op jit(solution)/shard_map/ppermute | solution.py:37
  427.7 5.1 collective-permute-done.67
  434.4 2.8 convolution_convert_fusion.1
  460.4 5.4 shard_map.294
  472.1 4.4 collective-permute-done.50
  478.3 5.1 multiply_reduce_fusion.5
  486.2 5.4 convolution_bitcast_fusion
  495.8 3.2 collective-permute-done.96
  504.2 3.1 collective-permute-start.92
  509.1 3.8 collective-permute-done.92
  525.7 3.8 collective-permute-done.101
  530.6 4.0 collective-permute-done.102
  539.8 5.6 collective-permute-done.83
  548.9 2.8 convolution_convert_fusion
  562.2 4.8 collective-permute-done.80
  574.4 3.9 collective-permute-done.86
  584.9 8.5 %collective-permute-done.62 = bf16[128,1920]{1,0:T(8,128)(2,1)S(1)} collective-permute-done((bf16[128,1920]{1,0:T(8,128)(2,1)S(1)}, bf16[128,1920]{1,0:T(8,128)(2,1)S(1)}, u32[]{:S(2)}, u32[]{:S(2)}) %collective-permute-start.62) | collective-permute-done | bytes 491552 | tf_op jit(solution)/shard_map/ppermute | solution.py:37
  595.9 7.9 %collective-permute-done.63 = bf16[64,1920]{1,0:T(8,128)(2,1)S(1)} collective-permute-done((bf16[64,1920]{1,0:T(8,128)(2,1)S(1)}, bf16[64,1920]{1,0:T(8,128)(2,1)S(1)}, u32[]{:S(2)}, u32[]{:S(2)}) %collective-permute-start.63) | collective-permute-done | bytes 245792 | tf_op jit(solution)/shard_map/ppermute | solution.py:37
  604.0 3.5 collective-permute-done.58
  607.7 6.9 %collective-permute-done.64 = bf16[32,1920]{1,0:T(8,128)(2,1)S(1)} collective-permute-done((bf16[32,1920]{1,0:T(8,128)(2,1)S(1)}, bf16[32,1920]{1,0:T(8,128)(2,1)S(1)}, u32[]{:S(2)}, u32[]{:S(2)}) %collective-permute-start.64) | collective-permute-done | bytes 122912 | tf_op jit(solution)/shard_map/ppermute | solution.py:37
  (760 shorter events, 242.4 us)
Async XLA Ops:
  4.1 30.4 %collective-permute-start = (bf16[32,2304]{1,0:T(8,128)(2,1)}, bf16[32,2304]{1,0:T(8,128)(2,1)S(1)}, u32[]{:S(2)}, u32[]{:S(2)}) collective-permute-start(bf16[32,2304]{1,0:T(8,128)(2,1)} %pad_maximum_fusion.76), channel_id=1, source_target_pairs={{0,16},{4,20},{8,24},{12,28},{16,0},{20,4},{24,8},{28,12},{1,17},{... | collective-permute-start | bytes 442376 | tf_op jit(solution)/shard_map/ppermute | solution.py:37
  10.5 21.2 %collective-permute-start.8 = (bf16[32,1920]{1,0:T(8,128)(2,1)}, bf16[32,1920]{1,0:T(8,128)(2,1)S(1)}, u32[]{:S(2)}, u32[]{:S(2)}) collective-permute-start(bf16[32,1920]{1,0:T(8,128)(2,1)} %get-tuple-element.251), channel_id=1, source_target_pairs={{0,16},{4,20},{8,24},{12,28},{16,0},{20,4},{24,8},{28,12},{1,17},{... | collective-permute-start | bytes 368648 | tf_op jit(solution)/shard_map/ppermute | solution.py:37
  34.5 11.1 %collective-permute-start.1 = (bf16[64,2304]{1,0:T(8,128)(2,1)S(1)}, bf16[64,2304]{1,0:T(8,128)(2,1)S(1)}, u32[]{:S(2)}, u32[]{:S(2)}) collective-permute-start(bf16[64,2304]{1,0:T(8,128)(2,1)S(1)} %pad_maximum_fusion.69), channel_id=1, source_target_pairs={{0,8},{4,12},{8,0},{12,4},{16,24},{20,28},{24,16},{28,20},{1,9},{5... | collective-permute-start | bytes 884744 | tf_op jit(solution)/shard_map/ppermute | solution.py:37
  40.8 34.7 %collective-permute-start.10 = (bf16[128,1920]{1,0:T(8,128)(2,1)S(1)}, bf16[128,1920]{1,0:T(8,128)(2,1)S(1)}, u32[]{:S(2)}, u32[]{:S(2)}) collective-permute-start(bf16[128,1920]{1,0:T(8,128)(2,1)S(1)} %pad_maximum_fusion.54), channel_id=1, source_target_pairs={{0,4},{4,0},{8,12},{12,8},{16,20},{20,16},{24,28},{28,24},{1,5},{5... | collective-permute-start | bytes 1474568 | tf_op jit(solution)/shard_map/ppermute | solution.py:37
  49.3 39.6 %collective-permute-start.2 = (bf16[128,2304]{1,0:T(8,128)(2,1)S(1)}, bf16[128,2304]{1,0:T(8,128)(2,1)S(1)}, u32[]{:S(2)}, u32[]{:S(2)}) collective-permute-start(bf16[128,2304]{1,0:T(8,128)(2,1)S(1)} %pad_maximum_fusion.42), channel_id=1, source_target_pairs={{0,2},{1,3},{2,0},{3,1},{4,6},{5,7},{6,4},{7,5},{8,10},{9,11},{10,... | collective-permute-start | bytes 1769480 | tf_op jit(solution)/shard_map/ppermute | solution.py:37
  62.1 10.8 %collective-permute-start.27 = (bf16[32,2048]{1,0:T(8,128)(2,1)S(1)}, bf16[32,2048]{1,0:T(8,128)(2,1)S(1)}, u32[]{:S(2)}, u32[]{:S(2)}) collective-permute-start(bf16[32,2048]{1,0:T(8,128)(2,1)S(1)} %get-tuple-element.58), channel_id=1, source_target_pairs={{0,16},{4,20},{8,24},{12,28},{16,0},{20,4},{24,8},{28,12},{1,17},{... | collective-permute-start | bytes 393224 | tf_op jit(solution)/shard_map/ppermute | solution.py:37
  63.9 13.8 %collective-permute-start.19 = (bf16[128,1024]{1,0:T(8,128)(2,1)S(1)}, bf16[128,1024]{1,0:T(8,128)(2,1)S(1)}, u32[]{:S(2)}, u32[]{:S(2)}) collective-permute-start(bf16[128,1024]{1,0:T(8,128)(2,1)S(1)} %get-tuple-element.246), channel_id=1, source_target_pairs={{0,4},{4,0},{8,12},{12,8},{16,20},{20,16},{24,28},{28,24},{1,5},{5... | collective-permute-start | bytes 786440 | tf_op jit(solution)/shard_map/ppermute | solution.py:37
  75.5 10.4 %collective-permute-start.33 = (bf16[64,2048]{1,0:T(8,128)(2,1)S(1)}, bf16[64,2048]{1,0:T(8,128)(2,1)S(1)}, u32[]{:S(2)}, u32[]{:S(2)}) collective-permute-start(bf16[64,2048]{1,0:T(8,128)(2,1)S(1)} %pad_maximum_fusion.73), channel_id=1, source_target_pairs={{0,8},{4,12},{8,0},{12,4},{16,24},{20,28},{24,16},{28,20},{1,9},{5... | collective-permute-start | bytes 786440 | tf_op jit(solution)/shard_map/ppermute | solution.py:37
  77.7 55.3 %collective-permute-start.11 = (bf16[256,1920]{1,0:T(8,128)(2,1)S(1)}, bf16[256,1920]{1,0:T(8,128)(2,1)S(1)}, u32[]{:S(2)}, u32[]{:S(2)}) collective-permute-start(bf16[256,1920]{1,0:T(8,128)(2,1)S(1)} %pad_maximum_fusion.24), channel_id=1, source_target_pairs={{0,2},{1,3},{2,0},{3,1},{4,6},{5,7},{6,4},{7,5},{8,10},{9,11},{10,... | collective-permute-start | bytes 2949128 | tf_op jit(solution)/shard_map/ppermute | solution.py:37
  79.7 35.5 %collective-permute-start.20 = (bf16[256,1024]{1,0:T(8,128)(2,1)S(1)}, bf16[256,1024]{1,0:T(8,128)(2,1)S(1)}, u32[]{:S(2)}, u32[]{:S(2)}) collective-permute-start(bf16[256,1024]{1,0:T(8,128)(2,1)S(1)} %pad_maximum_fusion.45), channel_id=1, source_target_pairs={{0,2},{1,3},{2,0},{3,1},{4,6},{5,7},{6,4},{7,5},{8,10},{9,11},{10,... | collective-permute-start | bytes 1572872 | tf_op jit(solution)/shard_map/ppermute | solution.py:37
  82.8 31.2 %collective-permute-start.25 = (bf16[2,128,1024]{2,1,0:T(8,128)(2,1)S(1)}, bf16[2,128,1024]{2,1,0:T(8,128)(2,1)S(1)}, u32[]{:S(2)}, u32[]{:S(2)}) collective-permute-start(bf16[2,128,1024]{2,1,0:T(8,128)(2,1)S(1)} %get-tuple-element.214), channel_id=1, source_target_pairs={{0,4},{4,0},{8,12},{12,8},{16,20},{20,16},{24,28},{28,24},{1,5},{5... | collective-permute-start | bytes 1572872 | tf_op jit(solution)/shard_map/ppermute | solution.py:37
  85.9 47.5 %collective-permute-start.29 = (bf16[128,2048]{1,0:T(8,128)(2,1)S(1)}, bf16[128,2048]{1,0:T(8,128)(2,1)S(1)}, u32[]{:S(2)}, u32[]{:S(2)}) collective-permute-start(bf16[128,2048]{1,0:T(8,128)(2,1)S(1)} %get-tuple-element.225), channel_id=1, source_target_pairs={{0,4},{4,0},{8,12},{12,8},{16,20},{20,16},{24,28},{28,24},{1,5},{5... | collective-permute-start | bytes 1572872 | tf_op jit(solution)/shard_map/ppermute | solution.py:37
  111.3 19.8 %collective-permute-start.34 = (bf16[128,2048]{1,0:T(8,128)(2,1)S(1)}, bf16[128,2048]{1,0:T(8,128)(2,1)S(1)}, u32[]{:S(2)}, u32[]{:S(2)}) collective-permute-start(bf16[128,2048]{1,0:T(8,128)(2,1)S(1)} %constant_dynamic-update-slice_fusion.42), channel_id=1, source_target_pairs={{0,2},{1,3},{2,0},{3,1},{4,6},{5,7},{6,4},{7,5},{8,10},{9,11},{10,... | collective-permute-start | bytes 1572872 | tf_op jit(solution)/shard_map/ppermute | solution.py:37
  114.0 14.5 %collective-permute-start.44 = (bf16[128,1024]{1,0:T(8,128)(2,1)S(1)}, bf16[128,1024]{1,0:T(8,128)(2,1)S(1)}, u32[]{:S(2)}, u32[]{:S(2)}) collective-permute-start(bf16[128,1024]{1,0:T(8,128)(2,1)S(1)} %constant_dynamic-update-slice_fusion.56), channel_id=1, source_target_pairs={{0,2},{1,3},{2,0},{3,1},{4,6},{5,7},{6,4},{7,5},{8,10},{9,11},{10,... | collective-permute-start | bytes 786440 | tf_op jit(solution)/shard_map/ppermute | solution.py:37
  115.2 15.7 %collective-permute-start.39 = (bf16[128,1024]{1,0:T(8,128)(2,1)S(1)}, bf16[128,1024]{1,0:T(8,128)(2,1)S(1)}, u32[]{:S(2)}, u32[]{:S(2)}) collective-permute-start(bf16[128,1024]{1,0:T(8,128)(2,1)S(1)} %pad_maximum_fusion.74), channel_id=1, source_target_pairs={{0,4},{4,0},{8,12},{12,8},{16,20},{20,16},{24,28},{28,24},{1,5},{5... | collective-permute-start | bytes 786440 | tf_op jit(solution)/shard_map/ppermute | solution.py:37
  128.5 43.4 %collective-permute-start.3 = (bf16[2,128,2304]{2,1,0:T(8,128)(2,1)S(1)}, bf16[2,128,2304]{2,1,0:T(8,128)(2,1)S(1)}, u32[]{:S(2)}, u32[]{:S(2)}) collective-permute-start(bf16[2,128,2304]{2,1,0:T(8,128)(2,1)S(1)} %get-tuple-element.176), channel_id=1, source_target_pairs={{0,4},{4,0},{8,12},{12,8},{16,20},{20,16},{24,28},{28,24},{1,5},{5... | collective-permute-start | bytes 3538952 | tf_op jit(solution)/shard_map/ppermute | solution.py:37
  130.9 41.3 %collective-permute-start.21 = (bf16[512,1024]{1,0:T(8,128)(2,1)S(1)}, bf16[512,1024]{1,0:T(8,128)(2,1)S(1)}, u32[]{:S(2)}, u32[]{:S(2)}) collective-permute-start(bf16[512,1024]{1,0:T(8,128)(2,1)S(1)} %get-tuple-element.209), channel_id=1, source_target_pairs={{0,1},{1,0},{2,3},{3,2},{4,5},{5,4},{6,7},{7,6},{8,9},{9,8},{10,11... | collective-permute-start | bytes 3145736 | tf_op jit(solution)/shard_map/ppermute | solution.py:37
  131.1 14.4 %collective-permute-start.40 = (bf16[256,1024]{1,0:T(8,128)(2,1)S(1)}, bf16[256,1024]{1,0:T(8,128)(2,1)S(1)}, u32[]{:S(2)}, u32[]{:S(2)}) collective-permute-start(bf16[256,1024]{1,0:T(8,128)(2,1)S(1)} %pad_maximum_fusion.47), channel_id=1, source_target_pairs={{0,2},{1,3},{2,0},{3,1},{4,6},{5,7},{6,4},{7,5},{8,10},{9,11},{10,... | collective-permute-start | bytes 1572872 | tf_op jit(solution)/shard_map/ppermute | solution.py:37
  133.1 35.9 %collective-permute-start.45 = (bf16[2,128,1024]{2,1,0:T(8,128)(2,1)S(1)}, bf16[2,128,1024]{2,1,0:T(8,128)(2,1)S(1)}, u32[]{:S(2)}, u32[]{:S(2)}) collective-permute-start(bf16[2,128,1024]{2,1,0:T(8,128)(2,1)S(1)} %get-tuple-element.208), channel_id=1, source_target_pairs={{0,4},{4,0},{8,12},{12,8},{16,20},{20,16},{24,28},{28,24},{1,5},{5... | collective-permute-start | bytes 1572872 | tf_op jit(solution)/shard_map/ppermute | solution.py:37
  133.4 59.1 %collective-permute-start.12 = (bf16[512,1920]{1,0:T(8,128)(2,1)S(1)}, bf16[512,1920]{1,0:T(8,128)(2,1)S(1)}, u32[]{:S(2)}, u32[]{:S(2)}) collective-permute-start(bf16[512,1920]{1,0:T(8,128)(2,1)S(1)} %get-tuple-element.183), channel_id=1, source_target_pairs={{0,1},{1,0},{2,3},{3,2},{4,5},{5,4},{6,7},{7,6},{8,9},{9,8},{10,11... | collective-permute-start | bytes 5898248 | tf_op jit(solution)/shard_map/ppermute | solution.py:37
  145.5 43.8 %collective-permute-start.35 = (bf16[2,128,2048]{2,1,0:T(8,128)(2,1)S(1)}, bf16[2,128,2048]{2,1,0:T(8,128)(2,1)S(1)}, u32[]{:S(2)}, u32[]{:S(2)}) collective-permute-start(bf16[2,128,2048]{2,1,0:T(8,128)(2,1)S(1)} %get-tuple-element.182), channel_id=1, source_target_pairs={{0,4},{4,0},{8,12},{12,8},{16,20},{20,16},{24,28},{28,24},{1,5},{5... | collective-permute-start | bytes 3145736 | tf_op jit(solution)/shard_map/ppermute | solution.py:37
  168.9 21.8 %collective-permute-start.30 = (bf16[256,2048]{1,0:T(8,128)(2,1)S(1)}, bf16[256,2048]{1,0:T(8,128)(2,1)S(1)}, u32[]{:S(2)}, u32[]{:S(2)}) collective-permute-start(bf16[256,2048]{1,0:T(8,128)(2,1)S(1)} %pad_maximum_fusion.21), channel_id=1, source_target_pairs={{0,2},{1,3},{2,0},{3,1},{4,6},{5,7},{6,4},{7,5},{8,10},{9,11},{10,... | collective-permute-start | bytes 3145736 | tf_op jit(solution)/shard_map/ppermute | solution.py:37
  171.9 20.5 %collective-permute-start.41 = (bf16[512,1024]{1,0:T(8,128)(2,1)S(1)}, bf16[512,1024]{1,0:T(8,128)(2,1)S(1)}, u32[]{:S(2)}, u32[]{:S(2)}) collective-permute-start(bf16[512,1024]{1,0:T(8,128)(2,1)S(1)} %get-tuple-element.203), channel_id=1, source_target_pairs={{0,1},{1,0},{2,3},{3,2},{4,5},{5,4},{6,7},{7,6},{8,9},{9,8},{10,11... | collective-permute-start | bytes 3145736 | tf_op jit(solution)/shard_map/ppermute | solution.py:37
  172.2 177.7 %collective-permute-start.87 = (bf16[256,512]{1,0:T(8,128)(2,1)}, bf16[256,512]{1,0:T(8,128)(2,1)}, u32[]{:S(2)}, u32[]{:S(2)}) collective-permute-start(bf16[256,512]{1,0:T(8,128)(2,1)} %get-tuple-element.196), channel_id=1, source_target_pairs={{0,1},{1,0},{2,3},{3,2},{4,5},{5,4},{6,7},{7,6},{8,9},{9,8},{10,11... | collective-permute-start | bytes 786440 | tf_op jit(solution)/shard_map/ppermute | solution.py:37
  189.3 359.6 %collective-permute-start.54 = (bf16[256,512]{1,0:T(8,128)(2,1)}, bf16[256,512]{1,0:T(8,128)(2,1)}, u32[]{:S(2)}, u32[]{:S(2)}) collective-permute-start(bf16[256,512]{1,0:T(8,128)(2,1)} %get-tuple-element.202), channel_id=1, source_target_pairs={{0,1},{1,0},{2,3},{3,2},{4,5},{5,4},{6,7},{7,6},{8,9},{9,8},{10,11... | collective-permute-start | bytes 786440 | tf_op jit(solution)/shard_map/ppermute | solution.py:37
  190.8 73.2 %collective-permute-start.26 = (bf16[512,1024]{1,0:T(8,128)(2,1)}, bf16[512,1024]{1,0:T(8,128)(2,1)}, u32[]{:S(2)}, u32[]{:S(2)}) collective-permute-start(bf16[512,1024]{1,0:T(8,128)(2,1)} %bitcast.37), channel_id=1, source_target_pairs={{0,1},{1,0},{2,3},{3,2},{4,5},{5,4},{6,7},{7,6},{8,9},{9,8},{10,11... | collective-permute-start | bytes 3145736 | tf_op jit(solution)/shard_map/ppermute | solution.py:37
  192.4 14.4 %collective-permute-start.46 = (bf16[512,1024]{1,0:T(8,128)(2,1)}, bf16[512,1024]{1,0:T(8,128)(2,1)S(1)}, u32[]{:S(2)}, u32[]{:S(2)}) collective-permute-start(bf16[512,1024]{1,0:T(8,128)(2,1)} %bitcast.51), channel_id=1, source_target_pairs={{0,1},{1,0},{2,3},{3,2},{4,5},{5,4},{6,7},{7,6},{8,9},{9,8},{10,11... | collective-permute-start | bytes 3145736 | tf_op jit(solution)/shard_map/ppermute | solution.py:37
  200.1 21.4 %collective-permute-start.4 = (bf16[512,2304]{1,0:T(8,128)(2,1)S(1)}, bf16[512,2304]{1,0:T(8,128)(2,1)}, u32[]{:S(2)}, u32[]{:S(2)}) collective-permute-start(bf16[512,2304]{1,0:T(8,128)(2,1)S(1)} %bitcast.243), channel_id=1, source_target_pairs={{0,1},{1,0},{2,3},{3,2},{4,5},{5,4},{6,7},{7,6},{8,9},{9,8},{10,11... | collective-permute-start | bytes 7077896 | tf_op jit(solution)/shard_map/ppermute | solution.py:37
  206.9 12.4 %collective-permute-start.14 = (bf16[144,1536]{1,0:T(8,128)(2,1)S(1)}, bf16[144,1536]{1,0:T(8,128)(2,1)S(1)}, u32[]{:S(2)}, u32[]{:S(2)}) collective-permute-start(bf16[144,1536]{1,0:T(8,128)(2,1)S(1)} %get-tuple-element.54), channel_id=1, source_target_pairs={{0,4},{4,0},{8,12},{12,8},{16,20},{20,16},{24,28},{28,24},{1,5},{5... | collective-permute-start | bytes 1327112 | tf_op jit(solution)/shard_map/ppermute | solution.py:37
  220.1 11.6 %collective-permute-start.15 = (bf16[144,1536]{1,0:T(8,128)(2,1)S(1)}, bf16[144,1536]{1,0:T(8,128)(2,1)S(1)}, u32[]{:S(2)}, u32[]{:S(2)}) collective-permute-start(bf16[144,1536]{1,0:T(8,128)(2,1)S(1)} %get-tuple-element.309), channel_id=1, source_target_pairs={{0,8},{4,12},{8,0},{12,4},{16,24},{20,28},{24,16},{28,20},{1,9},{5... | collective-permute-start | bytes 1327112 | tf_op jit(solution)/shard_map/ppermute | solution.py:37
  221.5 17.9 %collective-permute-start.31 = (bf16[512,2048]{1,0:T(8,128)(2,1)}, bf16[512,2048]{1,0:T(8,128)(2,1)}, u32[]{:S(2)}, u32[]{:S(2)}) collective-permute-start(bf16[512,2048]{1,0:T(8,128)(2,1)} %get-tuple-element.179), channel_id=1, source_target_pairs={{0,1},{1,0},{2,3},{3,2},{4,5},{5,4},{6,7},{7,6},{8,9},{9,8},{10,11... | collective-permute-start | bytes 6291464 | tf_op jit(solution)/shard_map/ppermute | solution.py:37
  239.4 19.8 %collective-permute-start.16 = (bf16[144,1536]{1,0:T(8,128)(2,1)S(1)}, bf16[144,1536]{1,0:T(8,128)(2,1)S(1)}, u32[]{:S(2)}, u32[]{:S(2)}) collective-permute-start(bf16[144,1536]{1,0:T(8,128)(2,1)S(1)} %get-tuple-element.307), channel_id=1, source_target_pairs={{0,16},{4,20},{8,24},{12,28},{16,0},{20,4},{24,8},{28,12},{1,17},{... | collective-permute-start | bytes 1327112 | tf_op jit(solution)/shard_map/ppermute | solution.py:37
  239.5 12.9 %collective-permute-start.6 = (bf16[2,256,256]{2,1,0:T(8,128)(2,1)S(1)}, bf16[2,256,256]{2,1,0:T(8,128)(2,1)S(1)}, u32[]{:S(2)}, u32[]{:S(2)}) collective-permute-start(bf16[2,256,256]{2,1,0:T(8,128)(2,1)S(1)} %get-tuple-element.231), channel_id=1, source_target_pairs={{0,8},{4,12},{8,0},{12,4},{16,24},{20,28},{24,16},{28,20},{1,9},{5... | collective-permute-start | bytes 786440 | tf_op jit(solution)/shard_map/ppermute | solution.py:37
  252.3 27.5 %collective-permute-start.36 = (bf16[512,2048]{1,0:T(8,128)(2,1)}, bf16[512,2048]{1,0:T(8,128)(2,1)}, u32[]{:S(2)}, u32[]{:S(2)}) collective-permute-start(bf16[512,2048]{1,0:T(8,128)(2,1)} %bitcast.44), channel_id=1, source_target_pairs={{0,1},{1,0},{2,3},{3,2},{4,5},{5,4},{6,7},{7,6},{8,9},{9,8},{10,11... | collective-permute-start | bytes 6291464 | tf_op jit(solution)/shard_map/ppermute | solution.py:37
  259.3 13.7 %collective-permute-start.7 = (bf16[2,2,256,256]{3,2,0,1:T(8,128)(2,1)S(1)}, bf16[2,2,256,256]{3,2,0,1:T(8,128)(2,1)S(1)}, u32[]{:S(2)}, u32[]{:S(2)}) collective-permute-start(bf16[2,2,256,256]{3,2,0,1:T(8,128)(2,1)S(1)} %get-tuple-element.212), channel_id=1, source_target_pairs={{0,4},{4,0},{8,12},{12,8},{16,20},{20,16},{24,28},{28,24},{1,5},{5... | collective-permute-start | bytes 1572872 | tf_op jit(solution)/shard_map/ppermute | solution.py:37
  302.5 40.6 %collective-permute-start.47 = (bf16[144,1536]{1,0:T(8,128)(2,1)}, bf16[144,1536]{1,0:T(8,128)(2,1)}, u32[]{:S(2)}, u32[]{:S(2)}) collective-permute-start(bf16[144,1536]{1,0:T(8,128)(2,1)} %pad_maximum_fusion.55), channel_id=1, source_target_pairs={{0,4},{4,0},{8,12},{12,8},{16,20},{20,16},{24,28},{28,24},{1,5},{5... | collective-permute-start | bytes 1327112 | tf_op jit(solution)/shard_map/ppermute | solution.py:37
  312.0 36.6 %collective-permute-start.51 = (bf16[4,256,256]{2,1,0:T(8,128)(2,1)}, bf16[4,256,256]{2,1,0:T(8,128)(2,1)}, u32[]{:S(2)}, u32[]{:S(2)}) collective-permute-start(bf16[4,256,256]{2,1,0:T(8,128)(2,1)} %slice_bitcast_fusion.12), channel_id=1, source_target_pairs={{0,4},{4,0},{8,12},{12,8},{16,20},{20,16},{24,28},{28,24},{1,5},{5... | collective-permute-start | bytes 1572872 | tf_op jit(solution)/shard_map/ppermute | solution.py:37
  315.3 35.2 %collective-permute-start.88 = (bf16[256,1024]{1,0:T(8,128)(2,1)}, bf16[256,1024]{1,0:T(8,128)(2,1)}, u32[]{:S(2)}, u32[]{:S(2)}) collective-permute-start(bf16[256,1024]{1,0:T(8,128)(2,1)} %get-tuple-element.177), channel_id=1, source_target_pairs={{0,1},{1,0},{2,3},{3,2},{4,5},{5,4},{6,7},{7,6},{8,9},{9,8},{10,11... | collective-permute-start | bytes 1572872 | tf_op jit(solution)/shard_map/ppermute | solution.py:37
  350.0 90.9 %collective-permute-start.77 = (bf16[256,2048]{1,0:T(8,128)(2,1)S(1)}, bf16[256,2048]{1,0:T(8,128)(2,1)}, u32[]{:S(2)}, u32[]{:S(2)}) collective-permute-start(bf16[256,2048]{1,0:T(8,128)(2,1)S(1)} %copy-done.62), channel_id=1, source_target_pairs={{0,1},{1,0},{2,3},{3,2},{4,5},{5,4},{6,7},{7,6},{8,9},{9,8},{10,11... | collective-permute-start | bytes 3145736 | tf_op jit(solution)/shard_map/ppermute | solution.py:37
  352.6 12.6 %collective-permute-start.71 = (bf16[256,1024]{1,0:T(8,128)(2,1)S(1)}, bf16[256,1024]{1,0:T(8,128)(2,1)S(1)}, u32[]{:S(2)}, u32[]{:S(2)}) collective-permute-start(bf16[256,1024]{1,0:T(8,128)(2,1)S(1)} %copy-done.74), channel_id=1, source_target_pairs={{0,1},{1,0},{2,3},{3,2},{4,5},{5,4},{6,7},{7,6},{8,9},{9,8},{10,11... | collective-permute-start | bytes 1572872 | tf_op jit(solution)/shard_map/ppermute | solution.py:37
  355.2 79.1 %collective-permute-start.82 = (bf16[256,2048]{1,0:T(8,128)(2,1)}, bf16[256,2048]{1,0:T(8,128)(2,1)}, u32[]{:S(2)}, u32[]{:S(2)}) collective-permute-start(bf16[256,2048]{1,0:T(8,128)(2,1)} %get-tuple-element.170), channel_id=1, source_target_pairs={{0,1},{1,0},{2,3},{3,2},{4,5},{5,4},{6,7},{7,6},{8,9},{9,8},{10,11... | collective-permute-start | bytes 3145736 | tf_op jit(solution)/shard_map/ppermute | solution.py:37
  355.4 47.3 %collective-permute-start.48 = (bf16[144,1536]{1,0:T(8,128)(2,1)S(1)}, bf16[144,1536]{1,0:T(8,128)(2,1)S(1)}, u32[]{:S(2)}, u32[]{:S(2)}) collective-permute-start(bf16[144,1536]{1,0:T(8,128)(2,1)S(1)} %get-tuple-element.305), channel_id=1, source_target_pairs={{0,8},{4,12},{8,0},{12,4},{16,24},{20,28},{24,16},{28,20},{1,9},{5... | collective-permute-start | bytes 1327112 | tf_op jit(solution)/shard_map/ppermute | solution.py:37
  365.2 27.9 %collective-permute-start.52 = (bf16[2,256,256]{2,1,0:T(8,128)(2,1)S(1)}, bf16[2,256,256]{2,1,0:T(8,128)(2,1)S(1)}, u32[]{:S(2)}, u32[]{:S(2)}) collective-permute-start(bf16[2,256,256]{2,1,0:T(8,128)(2,1)S(1)} %slice.887), channel_id=1, source_target_pairs={{0,16},{4,20},{8,24},{12,28},{16,0},{20,4},{24,8},{28,12},{1,17},{... | collective-permute-start | bytes 786440 | tf_op jit(solution)/shard_map/ppermute | solution.py:37
  393.1 26.7 %collective-permute-start.89 = (bf16[256,1024]{1,0:T(8,128)(2,1)S(1)}, bf16[256,1024]{1,0:T(8,128)(2,1)S(1)}, u32[]{:S(2)}, u32[]{:S(2)}) collective-permute-start(bf16[256,1024]{1,0:T(8,128)(2,1)S(1)} %slice.953), channel_id=1, source_target_pairs={{0,2},{1,3},{2,0},{3,1},{4,6},{5,7},{6,4},{7,5},{8,10},{9,11},{10,... | collective-permute-start | bytes 1572872 | tf_op jit(solution)/shard_map/ppermute | solution.py:37
  402.7 11.5 %collective-permute-start.53 = (bf16[256,256]{1,0:T(8,128)(2,1)S(1)}, bf16[256,256]{1,0:T(8,128)(2,1)S(1)}, u32[]{:S(2)}, u32[]{:S(2)}) collective-permute-start(bf16[256,256]{1,0:T(8,128)(2,1)S(1)} %slice_bitcast_fusion.18), channel_id=1, source_target_pairs={{0,8},{4,12},{8,0},{12,4},{16,24},{20,28},{24,16},{28,20},{1,9},{5... | collective-permute-start | bytes 393224 | tf_op jit(solution)/shard_map/ppermute | solution.py:37
  414.1 13.0 %collective-permute-start.94 = (bf16[2,128,1024]{2,1,0:T(8,128)(2,1)}, bf16[2,128,1024]{2,1,0:T(8,128)(2,1)S(1)}, u32[]{:S(2)}, u32[]{:S(2)}) collective-permute-start(bf16[2,128,1024]{2,1,0:T(8,128)(2,1)} %slice_bitcast_fusion.6), channel_id=1, source_target_pairs={{0,4},{4,0},{8,12},{12,8},{16,20},{20,16},{24,28},{28,24},{1,5},{5... | collective-permute-start | bytes 1572872 | tf_op jit(solution)/shard_map/ppermute | solution.py:37
  419.9 12.8 %collective-permute-start.67 = (bf16[256,1024]{1,0:T(8,128)(2,1)S(1)}, bf16[256,1024]{1,0:T(8,128)(2,1)S(1)}, u32[]{:S(2)}, u32[]{:S(2)}) collective-permute-start(bf16[256,1024]{1,0:T(8,128)(2,1)S(1)} %copy-done.75), channel_id=1, source_target_pairs={{0,2},{1,3},{2,0},{3,1},{4,6},{5,7},{6,4},{7,5},{8,10},{9,11},{10,... | collective-permute-start | bytes 1572872 | tf_op jit(solution)/shard_map/ppermute | solution.py:37
  427.1 11.9 %collective-permute-start.72 = (bf16[2,128,1024]{2,1,0:T(8,128)(2,1)S(1)}, bf16[2,128,1024]{2,1,0:T(8,128)(2,1)S(1)}, u32[]{:S(2)}, u32[]{:S(2)}) collective-permute-start(bf16[2,128,1024]{2,1,0:T(8,128)(2,1)S(1)} %slice_bitcast_fusion.10), channel_id=1, source_target_pairs={{0,4},{4,0},{8,12},{12,8},{16,20},{20,16},{24,28},{28,24},{1,5},{5... | collective-permute-start | bytes 1572872 | tf_op jit(solution)/shard_map/ppermute | solution.py:37
  434.3 25.5 %collective-permute-start.49 = (bf16[144,1536]{1,0:T(8,128)(2,1)S(1)}, bf16[144,1536]{1,0:T(8,128)(2,1)S(1)}, u32[]{:S(2)}, u32[]{:S(2)}) collective-permute-start(bf16[144,1536]{1,0:T(8,128)(2,1)S(1)} %get-tuple-element.303), channel_id=1, source_target_pairs={{0,16},{4,20},{8,24},{12,28},{16,0},{20,4},{24,8},{28,12},{1,17},{... | collective-permute-start | bytes 1327112 | tf_op jit(solution)/shard_map/ppermute | solution.py:37
  434.3 114.6 %collective-permute-start.55 = (bf16[256,2304]{1,0:T(8,128)(2,1)}, bf16[256,2304]{1,0:T(8,128)(2,1)}, u32[]{:S(2)}, u32[]{:S(2)}) collective-permute-start(bf16[256,2304]{1,0:T(8,128)(2,1)} %pad_maximum_fusion.18), channel_id=1, source_target_pairs={{0,1},{1,0},{2,3},{3,2},{4,5},{5,4},{6,7},{7,6},{8,9},{9,8},{10,11... | collective-permute-start | bytes 3538952 | tf_op jit(solution)/shard_map/ppermute | solution.py:37
  454.1 83.6 %collective-permute-start.78 = (bf16[256,2048]{1,0:T(8,128)(2,1)}, bf16[256,2048]{1,0:T(8,128)(2,1)}, u32[]{:S(2)}, u32[]{:S(2)}) collective-permute-start(bf16[256,2048]{1,0:T(8,128)(2,1)} %slice.935), channel_id=1, source_target_pairs={{0,2},{1,3},{2,0},{3,1},{4,6},{5,7},{6,4},{7,5},{8,10},{9,11},{10,... | collective-permute-start | bytes 3145736 | tf_op jit(solution)/shard_map/ppermute | solution.py:37
  456.7 36.6 %collective-permute-start.91 = (bf16[64,1024]{1,0:T(8,128)(2,1)}, bf16[64,1024]{1,0:T(8,128)(2,1)}, u32[]{:S(2)}, u32[]{:S(2)}) collective-permute-start(bf16[64,1024]{1,0:T(8,128)(2,1)} %slice.957), channel_id=1, source_target_pairs={{0,8},{4,12},{8,0},{12,4},{16,24},{20,28},{24,16},{28,20},{1,9},{5... | collective-permute-start | bytes 393224 | tf_op jit(solution)/shard_map/ppermute | solution.py:37
  514.2 11.1 %collective-permute-start.75 = (bf16[32,1024]{1,0:T(8,128)(2,1)S(1)}, bf16[32,1024]{1,0:T(8,128)(2,1)S(1)}, u32[]{:S(2)}, u32[]{:S(2)}) collective-permute-start(bf16[32,1024]{1,0:T(8,128)(2,1)S(1)} %slice.931), channel_id=1, source_target_pairs={{0,16},{4,20},{8,24},{12,28},{16,0},{20,4},{24,8},{28,12},{1,17},{... | collective-permute-start | bytes 196616 | tf_op jit(solution)/shard_map/ppermute | solution.py:37
  523.2 22.2 %collective-permute-start.83 = (bf16[2,128,2048]{2,1,0:T(8,128)(2,1)}, bf16[2,128,2048]{2,1,0:T(8,128)(2,1)S(1)}, u32[]{:S(2)}, u32[]{:S(2)}) collective-permute-start(bf16[2,128,2048]{2,1,0:T(8,128)(2,1)} %slice_bitcast_fusion.2), channel_id=1, source_target_pairs={{0,4},{4,0},{8,12},{12,8},{16,20},{20,16},{24,28},{28,24},{1,5},{5... | collective-permute-start | bytes 3145736 | tf_op jit(solution)/shard_map/ppermute | solution.py:37
  534.6 19.6 %collective-permute-start.60 = (bf16[256,1920]{1,0:T(8,128)(2,1)}, bf16[256,1920]{1,0:T(8,128)(2,1)}, u32[]{:S(2)}, u32[]{:S(2)}) collective-permute-start(bf16[256,1920]{1,0:T(8,128)(2,1)} %pad_maximum_fusion.25), channel_id=1, source_target_pairs={{0,1},{1,0},{2,3},{3,2},{4,5},{5,4},{6,7},{7,6},{8,9},{9,8},{10,11... | collective-permute-start | bytes 2949128 | tf_op jit(solution)/shard_map/ppermute | solution.py:37
  539.7 17.6 %collective-permute-start.79 = (bf16[128,2048]{1,0:T(8,128)(2,1)S(1)}, bf16[128,2048]{1,0:T(8,128)(2,1)S(1)}, u32[]{:S(2)}, u32[]{:S(2)}) collective-permute-start(bf16[128,2048]{1,0:T(8,128)(2,1)S(1)} %slice.937), channel_id=1, source_target_pairs={{0,4},{4,0},{8,12},{12,8},{16,20},{20,16},{24,28},{28,24},{1,5},{5... | collective-permute-start | bytes 1572872 | tf_op jit(solution)/shard_map/ppermute | solution.py:37
  547.1 13.1 %collective-permute-start.84 = (bf16[128,2048]{1,0:T(8,128)(2,1)S(1)}, bf16[128,2048]{1,0:T(8,128)(2,1)S(1)}, u32[]{:S(2)}, u32[]{:S(2)}) collective-permute-start(bf16[128,2048]{1,0:T(8,128)(2,1)S(1)} %slice_bitcast_fusion.8), channel_id=1, source_target_pairs={{0,2},{1,3},{2,0},{3,1},{4,6},{5,7},{6,4},{7,5},{8,10},{9,11},{10,... | collective-permute-start | bytes 1572872 | tf_op jit(solution)/shard_map/ppermute | solution.py:37
  551.8 28.5 %collective-permute-start.56 = (bf16[2,128,2304]{2,1,0:T(8,128)(2,1)S(1)}, bf16[2,128,2304]{2,1,0:T(8,128)(2,1)S(1)}, u32[]{:S(2)}, u32[]{:S(2)}) collective-permute-start(bf16[2,128,2304]{2,1,0:T(8,128)(2,1)S(1)} %slice_bitcast_fusion), channel_id=1, source_target_pairs={{0,4},{4,0},{8,12},{12,8},{16,20},{20,16},{24,28},{28,24},{1,5},{5... | collective-permute-start | bytes 3538952 | tf_op jit(solution)/shard_map/ppermute | solution.py:37
  556.9 23.7 %collective-permute-start.61 = (bf16[256,1920]{1,0:T(8,128)(2,1)S(1)}, bf16[256,1920]{1,0:T(8,128)(2,1)S(1)}, u32[]{:S(2)}, u32[]{:S(2)}) collective-permute-start(bf16[256,1920]{1,0:T(8,128)(2,1)S(1)} %slice.904), channel_id=1, source_target_pairs={{0,2},{1,3},{2,0},{3,1},{4,6},{5,7},{6,4},{7,5},{8,10},{9,11},{10,... | collective-permute-start | bytes 2949128 | tf_op jit(solution)/shard_map/ppermute | solution.py:37
  560.4 10.8 %collective-permute-start.85 = (bf16[64,2048]{1,0:T(8,128)(2,1)S(1)}, bf16[64,2048]{1,0:T(8,128)(2,1)S(1)}, u32[]{:S(2)}, u32[]{:S(2)}) collective-permute-start(bf16[64,2048]{1,0:T(8,128)(2,1)S(1)} %slice.947), channel_id=1, source_target_pairs={{0,8},{4,12},{8,0},{12,4},{16,24},{20,28},{24,16},{28,20},{1,9},{5... | collective-permute-start | bytes 786440 | tf_op jit(solution)/shard_map/ppermute | solution.py:37
  580.9 12.5 %collective-permute-start.62 = (bf16[128,1920]{1,0:T(8,128)(2,1)S(1)}, bf16[128,1920]{1,0:T(8,128)(2,1)S(1)}, u32[]{:S(2)}, u32[]{:S(2)}) collective-permute-start(bf16[128,1920]{1,0:T(8,128)(2,1)S(1)} %slice.906), channel_id=1, source_target_pairs={{0,4},{4,0},{8,12},{12,8},{16,20},{20,16},{24,28},{28,24},{1,5},{5... | collective-permute-start | bytes 1474568 | tf_op jit(solution)/shard_map/ppermute | solution.py:37
  582.8 12.9 %collective-permute-start.57 = (bf16[128,2304]{1,0:T(8,128)(2,1)S(1)}, bf16[128,2304]{1,0:T(8,128)(2,1)S(1)}, u32[]{:S(2)}, u32[]{:S(2)}) collective-permute-start(bf16[128,2304]{1,0:T(8,128)(2,1)S(1)} %slice_bitcast_fusion.4), channel_id=1, source_target_pairs={{0,2},{1,3},{2,0},{3,1},{4,6},{5,7},{6,4},{7,5},{8,10},{9,11},{10,... | collective-permute-start | bytes 1769480 | tf_op jit(solution)/shard_map/ppermute | solution.py:37
  595.9 11.6 %collective-permute-start.58 = (bf16[64,2304]{1,0:T(8,128)(2,1)S(1)}, bf16[64,2304]{1,0:T(8,128)(2,1)S(1)}, u32[]{:S(2)}, u32[]{:S(2)}) collective-permute-start(bf16[64,2304]{1,0:T(8,128)(2,1)S(1)} %slice.897), channel_id=1, source_target_pairs={{0,8},{4,12},{8,0},{12,4},{16,24},{20,28},{24,16},{28,20},{1,9},{5... | collective-permute-start | bytes 884744 | tf_op jit(solution)/shard_map/ppermute | solution.py:37
  603.9 10.6 %collective-permute-start.64 = (bf16[32,1920]{1,0:T(8,128)(2,1)S(1)}, bf16[32,1920]{1,0:T(8,128)(2,1)S(1)}, u32[]{:S(2)}, u32[]{:S(2)}) collective-permute-start(bf16[32,1920]{1,0:T(8,128)(2,1)S(1)} %slice.910), channel_id=1, source_target_pairs={{0,16},{4,20},{8,24},{12,28},{16,0},{20,4},{24,8},{28,12},{1,17},{... | collective-permute-start | bytes 368648 | tf_op jit(solution)/shard_map/ppermute | solution.py:37
  (188 other events, 2820.4 us)

commit v3 on v2

--- a/solution.py
+++ b/solution.py
@@ -32,66 +32,12 @@
     return lax.axis_size("seq") == 8 and lax.axis_size("batch") == 4 and width % (32 * 32) == 0
 
 
-def swap(value, axis, bit):
-    route = [(i, i ^ bit) for i in range(lax.axis_size(axis))]
-    return lax.ppermute(value, axis, route)
-
-
-def gather_stages(shard, x_first):
-    rows = jnp.concatenate([shard, swap(shard, "seq", 4)], axis=0)
-    rows = jnp.concatenate([rows, swap(rows, "seq", 2)], axis=0)
-    along_z = rows
-    if x_first:
-        rows = jnp.concatenate([rows, swap(rows, "seq", 1)], axis=0)
-        rows = jnp.concatenate([rows, swap(rows, "batch", 2)], axis=0)
-    else:
-        rows = jnp.stack([rows, swap(rows, "batch", 2)], axis=0)
-        rows = jnp.stack([rows, swap(rows, "seq", 1)], axis=1)
-        rows = rows.reshape(-1, rows.shape[-1])
-    return along_z, jnp.concatenate([rows, swap(rows, "batch", 1)], axis=0)
-
-
-def add_narrow(own, other):
-    return (own.astype(jnp.float32) + other.astype(jnp.float32)).astype(jnp.bfloat16)
-
-
-def scatter_stages(rows, y_first):
-    size, cols = rows.shape
-    if y_first:
-        half = size // 2
-        rows = add_narrow(rows[:half], swap(rows[half:], "batch", 2))
-        half = half // 2
-        rows = add_narrow(rows[:half], swap(rows[half:], "seq", 1))
-    else:
-        split = rows.reshape(2, 2, size // 4, cols)
-        split = add_narrow(split[:, 0], swap(split[:, 1], "seq", 1))
-        rows = add_narrow(split[0], swap(split[1], "batch", 2))
-    half = rows.shape[0] // 2
-    rows = add_narrow(rows[:half], swap(rows[half:], "seq", 2))
-    half = half // 2
-    return rows[:half].astype(jnp.float32) + swap(rows[half:], "seq", 4).astype(jnp.float32)
-
-
-def weight_grad(left, right, fast, y_first):
-    if not fast:
-        full = jnp.einsum("td,tc->dc", left, right, preferred_element_type=jnp.float32)
-        return lax.psum_scatter(full, ("seq", "batch"), scatter_dimension=0, tiled=True)
-    half = left.shape[1] // 2
-    lefts = jnp.concatenate([left[:, :half], swap(left[:, half:], "batch", 1)], axis=0)
-    rights = jnp.concatenate([right, swap(right, "batch", 1)], axis=0)
-    partial = jnp.einsum("td,tc->dc", lefts, rights, preferred_element_type=jnp.float32)
-    return scatter_stages(partial.astype(jnp.bfloat16), y_first)
-
-
-def total_small(arrays, fast):
+def pack_small(arrays):
     flat = jnp.concatenate([a.reshape(-1) for a in arrays])
-    size = flat.shape[0]
-    flat = jnp.pad(flat, (0, -size % 1024)).reshape(-1, 128)
-    if fast:
-        for axis, bit in (("batch", 1), ("batch", 2), ("seq", 1), ("seq", 2), ("seq", 4)):
-            flat = flat + swap(flat, axis, bit)
-    else:
-        flat = lax.psum(flat, ("seq", "batch"))
+    return jnp.pad(flat, (0, -flat.shape[0] % 1024)).reshape(-1, 128)
+
+
+def unpack_small(flat, arrays):
     flat = flat.reshape(-1)
     out, start = [], 0
     for a in arrays:
@@ -247,6 +193,32 @@
     return (rows <= at) & (rows >= seg_start(at, info))
 
 
+def attend_block(info, block, keys, values_t, heads, acc, top, total):
+    allowed = attn_mask(info, block)
+    for h in range(QUERY_HEADS):
+        scores = jnp.where(allowed, dot_nt(keys, heads[h]), NEGATIVE_FILL)
+        old = top[h : h + 1]
+        new = jnp.maximum(old, jnp.max(scores, axis=0, keepdims=True))
+        probs = jnp.where(allowed, jnp.exp(scores - new), 0.0)
+        shrink = jnp.exp(old - new)
+        top[h : h + 1] = new
+        total[h : h + 1] = total[h : h + 1] * shrink + jnp.sum(probs, axis=0, keepdims=True)
+        side = (h % 2) * HEAD_SIZE
+        acc[h] = acc[h] * shrink + dot(
+            values_t[side : side + HEAD_SIZE], probs.astype(jnp.bfloat16)
+        )
+
+
+def attend_write(acc, total, out, out_t):
+    for i in range(PAIRS):
+        pair = jnp.concatenate(
+            [acc[2 * i] / total[2 * i : 2 * i + 1], acc[2 * i + 1] / total[2 * i + 1 : 2 * i + 2]],
+            axis=0,
+        )
+        out_t[i * TILE : (i + 1) * TILE] = pair
+        out[:, i * TILE : (i + 1) * TILE] = pair.T.astype(jnp.bfloat16)
+
+
 def attn_forward_kernel(info, q, kv, out, out_t, lse, heads, acc, top, total):
     for i in range(PAIRS):
         heads[2 * i], heads[2 * i + 1] = halves_of(q[:, i * TILE : (i + 1) * TILE])
@@ -257,33 +229,15 @@
 
     def step(j, carry):
         block = low + j
-        place = pl.ds(pl.multiple_of((block ^ info[4]) * CHUNK, CHUNK), CHUNK)
+        place = pl.ds(pl.multiple_of(block * CHUNK, CHUNK), CHUNK)
         keys = kv[place, :TILE]
         values_t = kv[place, TILE:].astype(jnp.float32).T.astype(jnp.bfloat16)
-        allowed = attn_mask(info, block)
-        for h in range(QUERY_HEADS):
-            scores = jnp.where(allowed, dot_nt(keys, heads[h]), NEGATIVE_FILL)
-            old = top[h : h + 1]
-            new = jnp.maximum(old, jnp.max(scores, axis=0, keepdims=True))
-            probs = jnp.where(allowed, jnp.exp(scores - new), 0.0)
-            shrink = jnp.exp(old - new)
-            top[h : h + 1] = new
-            total[h : h + 1] = total[h : h + 1] * shrink + jnp.sum(probs, axis=0, keepdims=True)
-            side = (h % 2) * HEAD_SIZE
-            acc[h] = acc[h] * shrink + dot(
-                values_t[side : side + HEAD_SIZE], probs.astype(jnp.bfloat16)
-            )
+        attend_block(info, block, keys, values_t, heads, acc, top, total)
         return carry
 
     lax.fori_loop(0, count, step, 0)
     lse[...] = top[...] + jnp.log(total[...])
-    for i in range(PAIRS):
-        pair = jnp.concatenate(
-            [acc[2 * i] / total[2 * i : 2 * i + 1], acc[2 * i + 1] / total[2 * i + 1 : 2 * i + 2]],
-            axis=0,
-        )
-        out_t[i * TILE : (i + 1) * TILE] = pair
-        out[:, i * TILE : (i + 1) * TILE] = pair.T.astype(jnp.bfloat16)
+    attend_write(acc, total, out, out_t)
 
 
 def attn_forward(info, q, kv):
@@ -310,7 +264,7 @@
     )
 
 
-def attn_backward_kernel(info, q, kv, grad, out_t, lse, dq, dkv, heads, grads, delta, acc):
+def attend_back_start(q, grad, out_t, heads, grads, delta, acc):
     for i in range(PAIRS):
         cols = slice(i * TILE, (i + 1) * TILE)
         heads[2 * i], heads[2 * i + 1] = halves_of(q[:, cols])
@@ -319,35 +273,48 @@
         delta[2 * i : 2 * i + 1] = jnp.sum(both[:HEAD_SIZE], axis=0, keepdims=True)
         delta[2 * i + 1 : 2 * i + 2] = jnp.sum(both[HEAD_SIZE:], axis=0, keepdims=True)
     acc[...] = jnp.zeros_like(acc)
-    dkv[...] = jnp.zeros_like(dkv)
-    low, count = block_range(info)
-
-    def step(j, carry):
-        block = low + j
-        place = pl.ds(pl.multiple_of((block ^ info[4]) * CHUNK, CHUNK), CHUNK)
-        keys = kv[place, :TILE]
-        values = kv[place, TILE:]
-        keys_t = keys.astype(jnp.float32).T.astype(jnp.bfloat16)
-        allowed = attn_mask(info, block)
-        d_keys = jnp.zeros((CHUNK, TILE), jnp.float32)
-        d_values = jnp.zeros((CHUNK, TILE), jnp.float32)
-        for h in range(QUERY_HEADS):
-            scores = dot_nt(keys, heads[h])
-            probs = jnp.where(allowed, jnp.exp(scores - lse[h : h + 1]), 0.0)
-            d_probs = dot_nt(values, grads[h])
-            d_scores = (probs * (d_probs - delta[h : h + 1])).astype(jnp.bfloat16)
-            d_values = d_values + dot(probs.astype(jnp.bfloat16), grads[h])
-            d_keys = d_keys + dot(d_scores, heads[h])
-            side = (h % 2) * HEAD_SIZE
-            acc[h] = acc[h] + dot(keys_t[side : side + HEAD_SIZE], d_scores)
-        dkv[place, :TILE] = d_keys.astype(jnp.bfloat16)
-        dkv[place, TILE:] = d_values.astype(jnp.bfloat16)
-        return carry
-
-    lax.fori_loop(0, count, step, 0)
+
+
+def attend_back_block(info, block, keys, values, lse, target, heads, grads, delta, acc):
+    keys_t = keys.astype(jnp.float32).T.astype(jnp.bfloat16)
+    allowed = attn_mask(info, block)
+    d_keys = jnp.zeros((CHUNK, TILE), jnp.float32)
+    d_values = jnp.zeros((CHUNK, TILE), jnp.float32)
+    for h in range(QUERY_HEADS):
+        scores = dot_nt(keys, heads[h])
+        probs = jnp.where(allowed, jnp.exp(scores - lse[h : h + 1]), 0.0)
+        d_probs = dot_nt(values, grads[h])
+        d_scores = (probs * (d_probs - delta[h : h + 1])).astype(jnp.bfloat16)
+        d_values = d_values + dot(probs.astype(jnp.bfloat16), grads[h])
+        d_keys = d_keys + dot(d_scores, heads[h])
+        side = (h % 2) * HEAD_SIZE
+        acc[h] = acc[h] + dot(keys_t[side : side + HEAD_SIZE], d_scores)
+    target[:, :TILE] = d_keys.astype(jnp.bfloat16)
+    target[:, TILE:] = d_values.astype(jnp.bfloat16)
+
+
+def attend_back_write(acc, dq):
     for i in range(PAIRS):
         pair = jnp.concatenate([acc[2 * i], acc[2 * i + 1]], axis=0)
         dq[:, i * TILE : (i + 1) * TILE] = pair.T * HEAD_SIZE**-0.5
+
+
+def attn_backward_kernel(info, q, kv, grad, out_t, lse, dq, dkv, heads, grads, delta, acc):
+    attend_back_start(q, grad, out_t, heads, grads, delta, acc)
+    dkv[...] = jnp.zeros_like(dkv)
+    low, count = block_range(info)
+
+    def step(j, carry):
+        block = low + j
+        place = pl.ds(pl.multiple_of(block * CHUNK, CHUNK), CHUNK)
+        attend_back_block(
+            info, block, kv[place, :TILE], kv[place, TILE:], lse, dkv.at[place], heads, grads,
+            delta, acc,
+        )
+        return carry
+
+    lax.fori_loop(0, count, step, 0)
+    attend_back_write(acc, dq)
 
 
 def attn_backward(info, q, kv, grad, out_t, lse):
@@ -770,7 +737,7 @@
     return jnp.concatenate([state.astype(jnp.bfloat16), high, low, rest], axis=0)
 
 
-def scan_states(own, fast, forward):
+def scan_states(own, forward):
     place = lax.axis_index("seq")
     count = lax.axis_size("seq")
     nothing = jnp.concatenate(
@@ -781,15 +748,6 @@
         ],
         axis=0,
     )
-    if fast:
-        reach, before = own, nothing
-        for bit in (1, 2, 4):
-            other = swap(reach, "seq", bit)
-            second = ((place & bit) != 0) == forward
-            before = jnp.where(second, join_states(other, before), before)
-            if bit != 4:
-                reach = jnp.where(second, join_states(other, reach), join_states(reach, other))
-        return before[:NS]
     everything = lax.all_gather(own, "seq")
 
     def step(k, before):
@@ -801,25 +759,624 @@
     return lax.fori_loop(0, count, step, nothing)[:NS]
 
 
-def seq_gather(value, fast):
-    if not fast:
-        return lax.all_gather(value, "seq", axis=0, tiled=True)
-    rows = jnp.stack([value, swap(value, "seq", 4)], axis=0)
-    rows = jnp.stack([rows, swap(rows, "seq", 2)], axis=1)
-    rows = jnp.stack([rows, swap(rows, "seq", 1)], axis=2)
-    return rows.reshape(-1, value.shape[1])
-
-
-def seq_scatter(value, fast):
-    if not fast:
-        return lax.psum_scatter(
-            value.astype(jnp.float32), "seq", scatter_dimension=0, tiled=True
+MESH = pl.DeviceIdType.MESH
+ANY = pl.BlockSpec(memory_space=pl.ANY)
+INTO_VMEM = pl.BlockSpec(memory_space=pltpu.VMEM)
+
+
+def partners():
+    seq, batch = lax.axis_index("seq"), lax.axis_index("batch")
+    return {
+        "far": (seq + 4 - 8 * (seq // 4), batch),
+        "near": (seq + 2 - 4 * (seq // 2 % 2), batch),
+        "x": (seq + 1 - 2 * (seq % 2), batch),
+        "y": (seq, batch + 2 - 4 * (batch // 2)),
+        "core": (seq, batch + 1 - 2 * (batch % 2)),
+    }
+
+
+def greet(others):
+    barrier = pltpu.get_barrier_semaphore()
+    for other in others:
+        pl.semaphore_signal(barrier, inc=1, device_id=other, device_id_type=MESH)
+    pl.semaphore_wait(barrier, len(others))
+
+
+def remote(src, dst, send, recv, other):
+    return pltpu.make_async_remote_copy(
+        src_ref=src, dst_ref=dst, send_sem=send, recv_sem=recv, device_id=other, device_id_type=MESH
+    )
+
+
+def comm_call(kernel, outs, out_specs, args, in_specs, scratch, number, moved, limit=56):
+    return pl.pallas_call(
+        kernel,
+        out_shape=list(outs),
+        in_specs=in_specs,
+        out_specs=out_specs,
+        scratch_shapes=list(scratch),
+        cost_estimate=pl.CostEstimate(flops=0, bytes_accessed=moved, transcendentals=0),
+        compiler_params=pltpu.CompilerParams(
+            collective_id=number, has_side_effects=True, vmem_limit_bytes=limit * 1024 * 1024
+        ),
+    )(*args)
+
+
+def column_chunks(widths):
+    pairs = []
+    for k in range(0, len(widths), 2):
+        pieces = max(1, max(widths[k], widths[k + 1]) // 1024)
+        halves = []
+        for p in (k, k + 1):
+            tiles, first, cuts = widths[p] // TILE, 0, []
+            for i in range(pieces):
+                cols = (tiles // pieces + (1 if i < tiles % pieces else 0)) * TILE
+                cuts.append((p, first, cols))
+                first += cols
+            halves.append(cuts)
+        pairs += list(zip(*halves))
+    return pairs
+
+
+def gather_plan(x_first):
+    plan = [("far", [(0, 1, 1)]), ("near", [(0, 2, 2)])]
+    if x_first:
+        plan += [("x", [(0, 4, 4)]), ("y", [(0, 8, 8)])]
+    else:
+        plan += [("y", [(0, 4, 8)]), ("x", [(0, 4, 4), (8, 4, 12)])]
+    return plan + [("core", [(0, 16, 16)])]
+
+
+def weight_gather_kernel(count, pairs, *refs):
+    ins, outs = refs[:count], refs[count : 2 * count]
+    send, recv, local = refs[2 * count :]
+    others = partners()
+    greet(list(others.values()))
+    block = ins[0].shape[0]
+    own = []
+    for p in range(count):
+        copy = pltpu.make_async_copy(ins[p], outs[p].at[pl.ds(0, block)], local.at[p])
+        copy.start()
+        own.append(copy)
+    for copy in own:
+        copy.wait()
+    plans = [gather_plan(True), gather_plan(False)]
+    started = {}
+    for wave in range(len(pairs) + 5):
+        for n in reversed(range(len(pairs))):
+            stage = wave - n
+            if stage < 0 or stage > 5:
+                continue
+            for side in range(2):
+                p, column, cols = pairs[n][side]
+                if stage > 0:
+                    for copy in started[n, side, stage - 1]:
+                        copy.wait_recv()
+                if stage == 5:
+                    continue
+                name, moves = plans[side][stage]
+                copies = []
+                for k, (first, rows, there) in enumerate(moves):
+                    copy = remote(
+                        outs[p].at[pl.ds(first * block, rows * block), pl.ds(column, cols)],
+                        outs[p].at[pl.ds(there * block, rows * block), pl.ds(column, cols)],
+                        send.at[2 * n + side, stage, k],
+                        recv.at[2 * n + side, stage, k],
+                        others[name],
+                    )
+                    copy.start()
+                    copies.append(copy)
+                started[n, side, stage] = copies
+    for copies in started.values():
+        for copy in copies:
+            copy.wait_send()
+
+
+def weight_gather(parts):
+    count = len(parts)
+    outs = [shape_of((32 * p.shape[0], p.shape[1]), p.dtype) for p in parts]
+    pairs = column_chunks([p.shape[1] for p in parts])
+    dma = pltpu.SemaphoreType.DMA
+    return comm_call(
+        lambda *refs: weight_gather_kernel(count, pairs, *refs),
+        outs,
+        [ANY] * count,
+        parts,
+        [ANY] * count,
+        [dma((2 * len(pairs), 5, 2)), dma((2 * len(pairs), 5, 2)), dma((count,))],
+        0,
+        64 * sum(p.size for p in parts),
+    )
+
+
+def bit_apart(r):
+    me = lax.axis_index("seq")
+    far = (r // 4 + me // 4) % 2
+    near = (r // 2 % 2 + me // 2 % 2) % 2
+    side = (r % 2 + me % 2) % 2
+    return 4 * far + 2 * near + side
+
+
+def join_into(target, earlier, later):
+    decay = later[NS : NS + 1].astype(jnp.float32) + later[NS + 1 : NS + 2].astype(jnp.float32)
+    before = earlier[NS : NS + 1].astype(jnp.float32) + earlier[NS + 1 : NS + 2].astype(jnp.float32)
+    both = decay * before
+    high = both.astype(jnp.bfloat16).astype(jnp.float32)
+    line = lax.broadcasted_iota(jnp.int32, (STATE_ROWS - NS, both.shape[1]), 0)
+    tail = jnp.where(line == 0, high, jnp.where(line == 1, both - high, 0.0))
+    for first in range(0, NS, 32):
+        rows = slice(first, first + 32)
+        target[rows] = (
+            decay * earlier[rows].astype(jnp.float32) + later[rows].astype(jnp.float32)
+        ).astype(jnp.bfloat16)
+    target[NS:] = tail.astype(jnp.bfloat16)
+
+
+class StateScan:
+    def __init__(self, forward, own, result, arrived, sent, before, send, recv, others):
+        me = lax.axis_index("seq")
+        self.seconds = []
+        for bit in (me % 2, me // 2 % 2, me // 4):
+            self.seconds.append(bit == 1 if forward else bit == 0)
+        self.own, self.result, self.arrived, self.sent, self.before = (
+            own, result, arrived, sent, before,
         )
-    size, cols = value.shape
-    parts = value.reshape(4, 2, size // 8, cols)
-    parts = add_narrow(parts[:, 0], swap(parts[:, 1], "seq", 1))
-    parts = add_narrow(parts[:2], swap(parts[2:], "seq", 4))
-    return parts[0].astype(jnp.float32) + swap(parts[1], "seq", 2).astype(jnp.float32)
+        route = (others["x"], others["near"], others["far"])
+        sources = (own, sent.at[0], sent.at[1])
+        self.copies = [
+            remote(sources[k], arrived.at[k], send.at[k], recv.at[k], route[k]) for k in range(3)
+        ]
+
+    def step(self, k):
+        if k == 0:
+            self.copies[0].start()
+            return
+        self.copies[k - 1].wait_recv()
+        other = self.arrived.at[k - 1]
+        mine = self.own if k == 1 else self.sent.at[k - 2]
+        second = self.seconds[k - 1]
+        before, result = self.before, self.result
+
+        @pl.when(second)
+        def _():
+            if k < 3:
+                join_into(self.sent.at[k - 1], other, mine)
+            if k == 1:
+                before[0] = other[...]
+            elif k == 2:
+                join_into(before.at[1], other, before.at[0])
+            else:
+                decay = before[1, NS : NS + 1].astype(jnp.float32) + before[
+                    1, NS + 1 : NS + 2
+                ].astype(jnp.float32)
+                result[...] = (
+                    decay * other[:NS].astype(jnp.float32) + before[1, :NS].astype(jnp.float32)
+                ).astype(jnp.bfloat16)
+
+        @pl.when(jnp.logical_not(second))
+        def _():
+            if k < 3:
+                join_into(self.sent.at[k - 1], mine, other)
+            if k == 1:
+                line = lax.broadcasted_iota(jnp.int32, before.shape[1:], 0)
+                before[0] = jnp.where(line == NS, 1.0, 0.0).astype(jnp.bfloat16)
+            elif k == 2:
+                before[1] = before[0]
+            else:
+                result[...] = before[1, :NS]
+
+        if k < 3:
+            self.copies[k].start()
+
+    def finish(self):
+        for copy in self.copies:
+            copy.wait_send()
+
+
+def scan_scratch(width):
+    rows = STATE_ROWS
+    dma = pltpu.SemaphoreType.DMA
+    narrow = jnp.bfloat16
+    return [
+        pltpu.VMEM((3, rows, width), narrow),
+        pltpu.VMEM((2, rows, width), narrow),
+        pltpu.VMEM((2, rows, width), narrow),
+        dma((3,)),
+        dma((3,)),
+    ]
+
+
+def mixer_forward_kernel(
+    info, q, pairs, state_own, out, out_t, lse, kv, state_in, heads, acc, top, total,
+    arrived, sent, before, scan_send, scan_recv, send, recv,
+):
+    others = partners()
+    greet([others["far"], others["near"], others["x"]])
+    me = lax.axis_index("seq")
+    rows = pairs.shape[0]
+
+    def at(r):
+        return kv.at[pl.ds(r * rows, rows)]
+
+    scan = StateScan(True, state_own, state_in, arrived, sent, before, scan_send, scan_recv, others)
+    kv[:rows] = pairs[...]
+    routes = {4: ("far", 0), 2: ("near", 0), 6: ("near", 4)}
+    routes.update({r: ("x", r - 1) for r in (1, 3, 5, 7)})
+    copies = {
+        r: remote(at(src), at(r), send.at[r], recv.at[r], others[name])
+        for r, (name, src) in routes.items()
+    }
+    copies[4].start()
+    copies[2].start()
+    copies[1].start()
+    scan.step(0)
+    for i in range(PAIRS):
+        heads[2 * i], heads[2 * i + 1] = halves_of(q[:, i * TILE : (i + 1) * TILE])
+    acc[...] = jnp.zeros_like(acc)
+    total[...] = jnp.zeros_like(total)
+    top[...] = jnp.full(top.shape, NEGATIVE_FILL, jnp.float32)
+
+    def attend(r):
+        block = bit_apart(r)
+
+        @pl.when(block <= me)
+        def _():
+            place = pl.ds(pl.multiple_of(r * rows, rows), rows)
+            keys = kv[place, :TILE]
+            values_t = kv[place, TILE:].astype(jnp.float32).T.astype(jnp.bfloat16)
+            attend_block(info, block, keys, values_t, heads, acc, top, total)
+
+    attend(0)
+    scan.step(1)
+    copies[4].wait_recv()
+    copies[6].start()
+    copies[5].start()
+    attend(4)
+    copies[2].wait_recv()
+    copies[3].start()
+    copies[6].wait_recv()
+    copies[7].start()
+    scan.step(2)
+
+    def several(first, gap, count):
+        def body(j, carry):
+            attend(first + j * gap)
+            return carry
+
+        lax.fori_loop(0, count, body, 0)
+
+    several(2, 4, 2)
+    for r in (1, 3, 5, 7):
+        copies[r].wait_recv()
+    several(1, 2, 4)
+    lse[...] = top[...] + jnp.log(total[...])
+    attend_write(acc, total, out, out_t)
+    scan.step(3)
+    scan.finish()
+    for copy in copies.values():
+        copy.wait_send()
+
+
+def mixer_forward(info, q, pairs, state_own):
+    rows = q.shape[0]
+    f32 = jnp.float32
+    dma = pltpu.SemaphoreType.DMA
+    width = state_own.shape[1]
+    outs = (
+        shape_of(q.shape, jnp.bfloat16),
+        shape_of(q.shape[::-1], f32),
+        shape_of((QUERY_HEADS, rows), f32),
+        shape_of((8 * rows, pairs.shape[1]), jnp.bfloat16),
+        shape_of((NS, width), jnp.bfloat16),
+    )
+    return comm_call(
+        mixer_forward_kernel,
+        outs,
+        [INTO_VMEM] * 5,
+        (info, q, pairs, state_own),
+        [pl.BlockSpec(memory_space=pltpu.SMEM)] + [INTO_VMEM] * 3,
+        [
+            pltpu.VMEM((QUERY_HEADS, rows, TILE), jnp.bfloat16),
+            pltpu.VMEM((QUERY_HEADS, HEAD_SIZE, rows), f32),
+            pltpu.VMEM((QUERY_HEADS, rows), f32),
+            pltpu.VMEM((QUERY_HEADS, rows), f32),
+            *scan_scratch(width),
+            dma((8,)),
+            dma((8,)),
+        ],
+        1,
+        100_000_000,
+    )
+
+
+def mixer_backward_kernel(swaps, info, q, kv, grad, out_t, lse, pull, *refs):
+    give, refs = refs[:swaps], refs[swaps:]
+    dq, d_own, d_state, refs = refs[0], refs[1], refs[2], refs[3:]
+    take, refs = refs[:swaps], refs[swaps:]
+    (
+        heads, grads, delta, acc, dkv, from_x, from_far, from_near,
+        arrived, sent, before, scan_send, scan_recv, send, recv, swap_send, swap_recv,
+    ) = refs
+    others = partners()
+    greet([others["far"], others["near"], others["x"], others["core"]])
+    me = lax.axis_index("seq")
+    rows = q.shape[0]
+    scan = StateScan(False, pull, d_state, arrived, sent, before, scan_send, scan_recv, others)
+    scan.step(0)
+    swapped = [
+        remote(give[k], take[k], swap_send.at[k], swap_recv.at[k], others["core"])
+        for k in range(swaps)
+    ]
+    for copy in swapped:
+        copy.start()
+    attend_back_start(q, grad, out_t, heads, grads, delta, acc)
+
+    def block_back(r):
+        block = bit_apart(r)
+        place = pl.ds(pl.multiple_of(r * rows, rows), rows)
+
+        @pl.when(block <= me)
+        def _():
+            attend_back_block(
+                info, block, kv[place, :TILE], kv[place, TILE:], lse, dkv.at[r], heads, grads,
+                delta, acc,
+            )
+
+        @pl.when(block > me)
+        def _():
+            dkv[r] = jnp.zeros(dkv.shape[1:], dkv.dtype)
+
+    def several(first, gap, count):
+        def body(j, carry):
+            block_back(first + j * gap)
+            return carry
+
+        lax.fori_loop(0, count, body, 0)
+
+    several(1, 2, 4)
+    over_x = [
+        remote(dkv.at[2 * k + 1], from_x.at[k], send.at[k], recv.at[k], others["x"])
+        for k in range(4)
+    ]
+    for copy in over_x:
+        copy.start()
+    scan.step(1)
+    several(4, 2, 2)
+
+    def add(target, source):
+        target[...] = (target[...].astype(jnp.float32) + source[...].astype(jnp.float32)).astype(
+            jnp.bfloat16
+        )
+
+    over_far = [
+        remote(dkv.at[4 + 2 * k], from_far.at[k], send.at[4 + k], recv.at[4 + k], others["far"])
+        for k in range(2)
+    ]
+    for k in range(2):
+        over_x[2 + k].wait_recv()
+        add(dkv.at[4 + 2 * k], from_x.at[2 + k])
+        over_far[k].start()
+    scan.step(2)
+    several(0, 2, 2)
+    for k in range(2):
+        over_x[k].wait_recv()
+        add(dkv.at[2 * k], from_x.at[k])
+    over_far[1].wait_recv()
+    add(dkv.at[2], from_far.at[1])
+    over_near = remote(dkv.at[2], from_near, send.at[6], recv.at[6], others["near"])
+    over_near.start()
+    over_far[0].wait_recv()
+    attend_back_write(acc, dq)
+    scan.step(3)
+    over_near.wait_recv()
+    d_own[...] = (
+        dkv[0].astype(jnp.float32)
+        + from_far[0].astype(jnp.float32)
+        + from_near[...].astype(jnp.float32)
+    )
+    scan.finish()
+    for copy in over_x + over_far + [over_near]:
+        copy.wait_send()
+    for copy in swapped:
+        copy.wait()
+
+
+def mixer_backward(info, q, kv, grad, out_t, lse, pull, give):
+    rows = q.shape[0]
+    f32 = jnp.float32
+    dma = pltpu.SemaphoreType.DMA
+    width = pull.shape[1]
+    pair = kv.shape[1]
+    swaps = len(give)
+    narrow = jnp.bfloat16
+    outs = [
+        shape_of(q.shape, f32),
+        shape_of((rows, pair), f32),
+        shape_of((NS, width), narrow),
+    ] + [shape_of(a.shape, a.dtype) for a in give]
+    result = comm_call(
+        lambda *refs: mixer_backward_kernel(swaps, *refs),
+        outs,
+        [INTO_VMEM] * 3 + [ANY] * swaps,
+        (info, q, kv, grad, out_t, lse, pull, *give),
+        [pl.BlockSpec(memory_space=pltpu.SMEM)] + [INTO_VMEM] * 6 + [ANY] * swaps,
+        [
+            pltpu.VMEM((QUERY_HEADS, rows, TILE), narrow),
+            pltpu.VMEM((QUERY_HEADS, rows, TILE), narrow),
+            pltpu.VMEM((QUERY_HEADS, rows), f32),
+            pltpu.VMEM((QUERY_HEADS, HEAD_SIZE, rows), f32),
+            pltpu.VMEM((8, rows, pair), narrow),
+            pltpu.VMEM((4, rows, pair), narrow),
+            pltpu.VMEM((2, rows, pair), narrow),
+            pltpu.VMEM((rows, pair), narrow),
+            *scan_scratch(width),
+            dma((7,)),
+            dma((7,)),
+            dma((swaps,)),
+            dma((swaps,)),
+        ],
+        2,
+        100_000_000,
+    )
+    return result[0], result[1], result[2], result[3:]
+
+
+def core_swap_kernel(count, *refs):
+    give, take = refs[:count], refs[count : 2 * count]
+    send, recv = refs[2 * count :]
+    other = partners()["core"]
+    greet([other])
+    copies = [remote(give[k], take[k], send.at[k], recv.at[k], other) for k in range(count)]
+    for copy in copies:
+        copy.start()
+    for copy in copies:
+        copy.wait()
+
+
+def core_swap(give):
+    count = len(give)
+    dma = pltpu.SemaphoreType.DMA
+    return comm_call(
+        lambda *refs: core_swap_kernel(count, *refs),
+        [shape_of(a.shape, a.dtype) for a in give],
+        [ANY] * count,
+        give,
+        [ANY] * count,
+        [dma((count,)), dma((count,))],
+        3,
+        2 * sum(a.size for a in give),
+    )
+
+
+def weight_scatter_kernel(count, pairs, *refs):
+    ins, small, refs = refs[:count], refs[count], refs[count + 1 :]
+    outs, small_out, refs = refs[:count], refs[count], refs[count + 1 :]
+    arrived, kept, refs = refs[: 4 * count], refs[4 * count : 7 * count], refs[7 * count :]
+    small_in, small_mid, send, recv, small_send, small_recv = refs
+    others = partners()
+    greet(list(others.values()))
+    size = ins[0].shape[0]
+    routes = (("y", "x", "near", "far"), ("x", "y", "near", "far"))
+
+    def pieces(side, stage):
+        rows = size >> stage
+        half = rows // 2
+        if side == 1 and stage == 0:
+            quarter = rows // 4
+            return [(quarter, quarter), (3 * quarter, quarter)], [(0, quarter), (2 * quarter, quarter)]
+        return [(half, half)], [(0, half)]
+
+    started = {}
+
+    def begin(n, side, stage):
+        p, column, width = pairs[n][side]
+        cols = pl.ds(column, width)
+        source = ins[p] if stage == 0 else kept[3 * p + stage - 1]
+        target = arrived[4 * p + stage]
+        copies, row = [], 0
+        for k, (first, rows) in enumerate(pieces(side, stage)[0]):
+            copy = remote(
+                source.at[pl.ds(first, rows), cols],
+                target.at[pl.ds(row, rows), cols],
+                send.at[2 * n + side, stage, k],
+                recv.at[2 * n + side, stage, k],
+                others[routes[side][stage]],
+            )
+            copy.start()
+            copies.append(copy)
+            row += rows
+        started[n, side, stage] = copies
+
+    def take(n, side, stage):
+        p, column, width = pairs[n][side]
+        cols = slice(column, column + width)
+        source = ins[p] if stage == 0 else kept[3 * p + stage - 1]
+        target = outs[p] if stage == 3 else kept[3 * p + stage]
+        got = arrived[4 * p + stage]
+        row = 0
+        for k, (first, rows) in enumerate(pieces(side, stage)[1]):
+            started[n, side, stage][k].wait_recv()
+
+            def add(i, carry):
+                at = pl.multiple_of(i * 32, 32)
+                here = pl.ds(first + at, 32)
+                there = pl.ds(row + at, 32)
+                total = source[here, cols].astype(jnp.float32) + got[there, cols].astype(
+                    jnp.float32
+                )
+                target[there, cols] = total.astype(target.dtype)
+                return carry
+
+            lax.fori_loop(0, rows // 32, add, 0)
+            row += rows
+
+    names = ("core", "y", "x", "near", "far")
+    small_copies = []
+    for wave in range(max(len(pairs) + 5, 6)):
+        if wave <= 5:
+            if wave > 0:
+                small_copies[wave - 1].wait_recv()
+                was = small if wave == 1 else small_mid.at[wave - 2]
+                now = small_out if wave == 5 else small_mid.at[wave - 1]
+                now[...] = was[...] + small_in[wave - 1]
+            if wave < 5:
+                source = small if wave == 0 else small_mid.at[wave - 1]
+                copy = remote(
+                    source,
+                    small_in.at[wave],
+                    small_send.at[wave],
+                    small_recv.at[wave],
+                    others[names[wave]],
+                )
+                copy.start()
+                small_copies.append(copy)
+        for n in range(len(pairs)):
+            stage = wave - n
+            if stage < 0 or stage > 4:
+                continue
+            for side in range(2):
+                if stage > 0:
+                    take(n, side, stage - 1)
+                if stage < 4:
+                    begin(n, side, stage)
+    for copies in list(started.values()) + [small_copies]:
+        for copy in copies:
+            copy.wait_send()
+
+
+def weight_scatter(parts, small):
+    count = len(parts)
+    size = parts[0].shape[0]
+    f32, narrow = jnp.float32, jnp.bfloat16
+    dma = pltpu.SemaphoreType.DMA
+    pairs = column_chunks([p.shape[1] for p in parts])
+    outs = [shape_of((size // 16, p.shape[1]), f32) for p in parts]
+    outs.append(shape_of(small.shape, f32))
+    scratch = []
+    for p in parts:
+        scratch += [pltpu.VMEM((size >> (s + 1), p.shape[1]), narrow) for s in range(4)]
+    for p in parts:
+        scratch += [pltpu.VMEM((size >> (s + 1), p.shape[1]), narrow) for s in range(3)]
+    scratch += [
+        pltpu.VMEM((5, *small.shape), f32),
+        pltpu.VMEM((4, *small.shape), f32),
+        dma((2 * len(pairs), 4, 2)),
+        dma((2 * len(pairs), 4, 2)),
+        dma((5,)),
+        dma((5,)),
+    ]
+    result = comm_call(
+        lambda *refs: weight_scatter_kernel(count, pairs, *refs),
+        outs,
+        [INTO_VMEM] * (count + 1),
+        (*parts, small),
+        [INTO_VMEM] * (count + 1),
+        scratch,
+        4,
+        8 * sum(p.size for p in parts),
+        limit=60,
+    )
+    return result[:count], result[count]
 
 
 def pair_heads(value, back=False):
@@ -862,9 +1419,8 @@
     first_pos = lax.axis_index("seq") * token_rows
     positions = first_pos + jnp.arange(token_rows, dtype=jnp.int32)
     segment, device_places = segments(seq_lens, positions)
-    mask = lax.axis_index("seq") if fast else 0
     ends = jnp.cumsum(seq_lens)
-    info = jnp.stack([first_pos, ends[0], ends[1], ends[2], mask]).astype(jnp.int32)
+    info = jnp.stack([first_pos, ends[0], ends[1], ends[2]]).astype(jnp.int32)
     half = HEAD_SIZE // 2
     freqs = ROPE_BASE ** (-jnp.arange(half, dtype=jnp.float32) / half)
     angles = device_places.astype(jnp.float32)[:, None] * jnp.tile(freqs, TILE // half)[None, :]
@@ -912,19 +1468,10 @@
         down_shard[:, : FF // 2],
         down_shard[:, FF // 2 :],
     )
-    full = []
-    ahead = None
-    for i in range(0, 8, 2):
-        pair = shards[i : i + 2]
-        if fast:
-            if ahead is not None:
-                pair, ahead = lax.optimization_barrier((pair, ahead))
-            za, fa = gather_stages(pair[0], True)
-            zb, fb = gather_stages(pair[1], False)
-            ahead = (za, zb)
-            full += [fa, fb]
-        else:
-            full += [lax.all_gather(p, ("seq", "batch"), axis=0, tiled=True) for p in pair]
+    if fast:
+        full = weight_gather(shards)
+    else:
+        full = [lax.all_gather(p, ("seq", "batch"), axis=0, tiled=True) for p in shards]
     full_conv, full_mix, out_a, out_b, full_gate, full_up, down_a, down_b = full
     scale_one = rms_scale(x_rows)
     normed = (x_rows * scale_one * norm_gain).astype(jnp.bfloat16)
@@ -940,7 +1487,6 @@
         cosine,
         sine,
     )
-    all_pairs = seq_gather(own_pairs, fast)
     gate_z = mix_proj[:, attn_width:]
     raw_xbc = conv_proj[:, :xbc_width]
     step_proj = conv_proj[:, xbc_width:]
@@ -958,8 +1504,14 @@
     ssm_local, state_own, steps_dt, running_decay = ssm_forward(
         info, inputs_x, inputs_bc, step_proj, head_params
     )
-    state_in = scan_states(state_own, fast, True)
-    attended, attended_t, log_total = attn_forward(info, queries, all_pairs)
+    if fast:
+        attended, attended_t, log_total, all_pairs, state_in = mixer_forward(
+            info, queries, own_pairs, state_own
+        )
+    else:
+        all_pairs = lax.all_gather(own_pairs, "seq", axis=0, tiled=True)
+        state_in = scan_states(state_own, True)
+        attended, attended_t, log_total = attn_forward(info, queries, all_pairs)
     ssm_flat, ssm_normed, scale_gated = ssm_finish(
         info, ssm_local, inputs_bc, running_decay, state_in, gate_z, ssm_gain[None]
     )
@@ -979,10 +1531,6 @@
     up_part = jnp.dot(normed_two, full_up, preferred_element_type=jnp.float32)
     hidden = (jax.nn.silu(gate_part) * up_part).astype(jnp.bfloat16)
     layer_out = middle + narrow_out(hidden, (down_a, down_b))
-    g_down = [
-        weight_grad(grad_rows, hidden[:, : FF // 2], fast, True),
-        weight_grad(grad_rows, hidden[:, FF // 2 :], fast, False),
-    ]
     d_hidden = jnp.concatenate(
         [
             jnp.dot(grad_rows, down_a, preferred_element_type=jnp.float32),
@@ -995,18 +1543,10 @@
         jnp.bfloat16
     )
     d_up = (d_hidden * gate_part * sig_gate).astype(jnp.bfloat16)
-    g_gate_up = [
-        weight_grad(normed_two, d_gate, fast, True),
-        weight_grad(normed_two, d_up, fast, False),
-    ]
     d_normed_two = narrow_out(jnp.concatenate([d_gate, d_up], axis=1), (full_gate, full_up))
     d_middle_norm, g_mlp_gain = norm_back(middle, scale_two, mlp_gain, d_normed_two)
     d_middle = grad_rows.astype(jnp.float32) + d_middle_norm
     d_mixer = d_middle.astype(jnp.bfloat16)
-    g_out = [
-        weight_grad(d_mixer, joined[:, :half_in], fast, True),
-        weight_grad(d_mixer, joined[:, half_in:], fast, False),
-    ]
     d_joined = jnp.concatenate(
         [
             jnp.dot(d_mixer, out_a, preferred_element_type=jnp.float32),
@@ -1025,11 +1565,31 @@
         running_decay,
         inputs_bc,
     )
-    d_state = scan_states(jnp.concatenate([pull, state_own[NS:]], axis=0), fast, False)
-    d_queries, d_pairs = attn_backward(
-        info, queries, all_pairs, attended_gradient, attended_t, log_total
-    )
-    own_d_pairs = seq_scatter(d_pairs, fast)
+    pull = jnp.concatenate([pull, state_own[NS:]], axis=0)
+    lefts = [normed, normed_two, d_mixer, grad_rows]
+    rights = [hidden, joined, d_gate, d_up]
+    if fast:
+        cut = width // 2
+        d_queries, own_d_pairs, d_state, theirs = mixer_backward(
+            info,
+            queries,
+            all_pairs,
+            attended_gradient,
+            attended_t,
+            log_total,
+            pull,
+            [a[:, cut:] for a in lefts] + rights,
+        )
+        lefts = [jnp.concatenate([a[:, :cut], b], axis=0) for a, b in zip(lefts, theirs)]
+        rights = [jnp.concatenate([a, b], axis=0) for a, b in zip(rights, theirs[4:])]
+    else:
+        d_state = scan_states(pull, False)
+        d_queries, d_pairs = attn_backward(
+            info, queries, all_pairs, attended_gradient, attended_t, log_total
+        )
+        own_d_pairs = lax.psum_scatter(
+            d_pairs.astype(jnp.float32), "seq", scatter_dimension=0, tiled=True
+        )
     dx_part, d_bc_part, d_cum_part, d_dt_part, g_skip_rows = ssm_back(
         info, inputs_x, inputs_bc, steps_dt, running_decay, d_ssm_out, head_params
     )
@@ -1066,33 +1626,57 @@
         sine,
     )
     d_mix_proj = jnp.concatenate([d_attn_proj, d_gate_z], axis=1)
-    g_conv_in = weight_grad(normed, d_conv_proj, fast, True)
-    g_mix_in = weight_grad(normed, d_mix_proj, fast, False)
     d_normed = jnp.einsum(
         "tc,dc->td", d_conv_proj, full_conv, preferred_element_type=jnp.float32
     ) + jnp.einsum("tc,dc->td", d_mix_proj, full_mix, preferred_element_type=jnp.float32)
     d_input_norm, g_norm_gain = norm_back(x_rows, scale_one, norm_gain, d_normed)
     input_grad = d_middle + d_input_norm
+    last = [d_conv_proj, d_mix_proj]
+    if fast:
+        last = [jnp.concatenate([a, b], axis=0) for a, b in zip(last, core_swap(last))]
+
+    def partial(left, right):
+        grad = jnp.einsum("td,tc->dc", left, right, preferred_element_type=jnp.float32)
+        return grad.astype(jnp.bfloat16) if fast else grad
+
+    all_normed, all_normed_two, all_d_mixer, all_grad = lefts
+    all_hidden, all_joined, all_d_gate, all_d_up = rights
+    half_ff = FF // 2
+    partials = [
+        partial(all_grad, all_hidden[:, :half_ff]),
+        partial(all_grad, all_hidden[:, half_ff:]),
+        partial(all_normed_two, all_d_gate),
+        partial(all_normed_two, all_d_up),
+        partial(all_d_mixer, all_joined[:, :half_in]),
+        partial(all_d_mixer, all_joined[:, half_in:]),
+        partial(all_normed, last[0]),
+        partial(all_normed, last[1]),
+    ]
+    gain_grads = to_plain_wide(jnp.stack([g_norm_gain, g_mlp_gain]))
+    small = (
+        gain_grads[0],
+        gain_grads[1],
+        g_ssm_gain[0],
+        g_conv_w,
+        g_conv_b,
+        g_a_log,
+        g_dt_bias,
+        g_d_skip,
+    )
+    if fast:
+        sums, small_total = weight_scatter(partials, pack_small(small))
+    else:
+        axes = ("seq", "batch")
+        sums = [lax.psum_scatter(g, axes, scatter_dimension=0, tiled=True) for g in partials]
+        small_total = lax.psum(pack_small(small), axes)
+    small_sums = unpack_small(small_total, small)
+    g_conv_in, g_mix_in = sums[6], sums[7]
     grad_attn = pair_heads(g_mix_in[:, :attn_width], True)
     grad_ssm_in = jnp.concatenate([g_mix_in[:, attn_width:], g_conv_in[:, :xbc_width]], axis=1)
     grad_dt = g_conv_in[:, xbc_width : xbc_width + MH]
-    grad_out = pair_heads(jnp.concatenate(g_out, axis=1), True).T
-    grad_gate_up = jnp.concatenate(g_gate_up, axis=1)
-    grad_down = jnp.concatenate(g_down, axis=1).T
-    gain_grads = to_plain_wide(jnp.stack([g_norm_gain, g_mlp_gain]))
-    small_sums = total_small(
-        (
-            gain_grads[0],
-            gain_grads[1],
-            g_ssm_gain[0],
-            g_conv_w,
-            g_conv_b,
-            g_a_log,
-            g_dt_bias,
-            g_d_skip,
-        ),
-        fast,
-    )
+    grad_out = pair_heads(jnp.concatenate(sums[4:6], axis=1), True).T
+    grad_gate_up = jnp.concatenate(sums[2:4], axis=1)
+    grad_down = jnp.concatenate(sums[:2], axis=1).T
     return (
         to_plain(layer_out.astype(jnp.bfloat16)).astype(jnp.bfloat16)[None],
         to_plain_wide(input_grad)[None],

time: 628 us -> 588 us (0.936)
  Pallas kernels: 35.1 us -> 434 us
  waiting for transfers between devices: 250 us -> 0.01 us
  starting transfers between devices: 153 us -> 3.56 us
  other arithmetic: 45.6 us -> 24.9 us
  local copies, waits for them, and re-layouts: 53.5 us -> 35.2 us
    pallas_call x0 -> x5, Pallas kernels: none -> 406 us  [comm_call(): pl.pallas_call(kernel, out_shape=list(outs), in_specs=in_specs, out_specs...]
    ppermute x101 -> x0, waiting for transfers between devices: 246 us -> none  [swap(): return lax.ppermute(value, axis, route)]
    ppermute x101 -> x0, starting transfers between devices: 147 us -> none  [swap(): return lax.ppermute(value, axis, route)]
    convert_element_type x44 -> x0, other arithmetic: 12.3 us -> none  [the longest x26 8.4 us: add_narrow(): (own.astype(jnp.float32) + other.astype(jnp.float32)).astype(jnp.bfloat16)]
    pallas_call x9 -> x7, Pallas kernels: 35.1 us -> 28 us  [big_call(): pl.pallas_call(kernel, out_shape=list(outs), in_specs=specs, out_specs=[p...]
    dot_general x3 -> x2, matrix products: 10.4 us -> 3.36 us  [narrow_out(): jnp.einsum('tc,dc->td', left[:, cut:], parts[1], preferred_element_type=j...]
    dot_general x8, matrix products: 16.3 us -> 22.8 us  [partial(): jnp.einsum('td,tc->dc', left, right, preferred_element_type=jnp.float32)]
    slice x41 -> x11, local copies, waits for them, and re-layouts: 16.1 us -> 10.6 us  [the longest x5 6.03 us: unpack_small(): out.append(flat[start:start + a.size].reshape(a.shape))]
  transfers between devices with their start and end apart: 103 -> 2, of which waited for: 54 -> 0; matrix products, arithmetic and copies ran while one was open for 26% -> 6% of each run, Pallas kernels for 6% -> 0%
where the time goes in v3:
time: 588 us; the launch traced here: 578 us
  Pallas kernels  434 us (74%)
  matrix products  77.7 us (13%)
  local copies, waits for them, and re-layouts  35.2 us (6%)
  other arithmetic  24.9 us (4%)
    pallas_call x5, Pallas kernels, comm_call(): pl.pallas_call(kernel, out_shape=list(outs), in_specs=in_specs, out_specs...  406 us
    pallas_call x7, Pallas kernels, big_call(): pl.pallas_call(kernel, out_shape=list(outs), in_specs=specs, out_specs=[p...  28 us
    dot_general x8, matrix products, partial(): jnp.einsum('td,tc->dc', left, right, preferred_element_type=jnp.float32)  22.8 us
  transfers between devices with their start and end apart: 2, of which 0 were waited for; matrix products, arithmetic and copies ran while one was open for 6% of the time, Pallas kernels for 0%

profile of v3, /device:TPU:0, one launch (start us, length us, event | category | flops | bytes accessed | tf_op | source)
XLA Modules:
  0.0 577.5 jit_solution(1374649057848408214)
XLA Ops:
  1.5 0.9 slice.345
  2.4 1.5 slice.346.refs_3_
  3.9 2.2 multiply_reduce_fusion.9
  6.2 1.8 fusion.84
  11.7 161.2 %shard_map.288 = (bf16[1024,1920]{1,0:T(8,128)(2,1)}, bf16[1024,2304]{1,0:T(8,128)(2,1)}, bf16[1024,1024]{1,0:T(8,128)(2,1)}, bf16[1024,1024]{1,0:T(8,128)(2,1)}...) custom-call(bf16[32,1920]{1,0:T(8,128)(2,1)} %fusion.83.refs_0_, ...), custom_call_target="tpu_custom_call" | custom-call | bytes 25427968 | tf_op jit(solution)/shard_map/pallas_call | solution.py:792
  172.9 3.4 fusion.128
  176.2 1.9 collective-permute-start
  179.9 5.1 fusion.127
  185.2 2.8 convolution_convert_fusion.8
  188.1 1.7 fusion.130
  189.8 1.7 fusion.131
  192.8 2.0 pad_add_fusion.3.info.refs_0_
  195.0 1.6 slice.359.z
  197.1 2.7 multiply_convert_fusion.3
  199.9 3.6 shard_map.290
  204.2 54.1 %shard_map.291 = (bf16[256,512]{1,0:T(8,128)(2,1)}, f32[512,256]{1,0:T(8,128)}, f32[8,256]{1,0:T(8,128)}, bf16[2048,256]{1,0:T(8,128)(2,1)}, bf16[128,1536]{1,0:T(8,128)(2,1)}) custom-call(s32[4]{0:T(128)} %copy-done.12, bf16[256,512]{1,0:T(8,128)(2,1)} %copy-done.6, bf16[256,256]{1,0:T(8,128)(2,1)} %copy-done.11, bf16[144,1536]{1,0:T(8,128)(2,1)} %copy-done.7), custom_call_target="tpu_custom_call" | custom-call | bytes 100000000 | tf_op jit(solution)/shard_map/pallas_call | solution.py:792
  258.3 1.7 constant_dynamic-update-slice_fusion.1
  260.0 1.0 copy-done.4
  261.6 2.9 shard_map.292
  264.5 1.0 constant_dynamic-update-slice_fusion.refs_12_
  265.6 1.8 fusion.72
  267.4 0.9 multiply_reduce_fusion.8
  268.5 1.1 copy-done.28
  269.5 1.2 fusion.129
  271.7 3.2 multiply_convert_fusion
  274.9 1.3 fusion.132
  276.2 2.5 multiply_reduce_fusion.4
  278.7 1.6 fusion.109
  285.1 4.0 shard_map.293
  289.1 11.5 %shard_map.295 = (f32[256,1536]{1,0:T(8,128)S(1)}, f32[256,256]{1,0:T(8,128)S(1)}, f32[256,128]{1,0:T(8,128)S(1)}, f32[256,128]{1,0:T(8,128)S(1)}, f32[8,128]{1,0:T(8,128)S(1)}) custom-call(s32[4]{0:T(128)S(1)} %copy-done.14, bf16[256,1536]{1,0:T(8,128)(2,1)S(1)} %slice.356.x, bf16[256,256]{1,0:T(8,128)(2,1)S(1)} %slice.357.bc, ...), custom_call_target="tpu_custom_call" | custom-call | flops 805306368 | bytes 4857872 | tf_op jit(solution)/shard_map/pallas_call | solution.py:141
  300.6 1.2 copy-done.3
  302.6 54.7 %shard_map.294 = (f32[256,512]{1,0:T(8,128)}, f32[256,256]{1,0:T(8,128)}, bf16[128,1536]{1,0:T(8,128)(2,1)}, bf16[256,512]{1,0:T(8,128)(2,1)}, bf16[256,512]{1,0...) custom-call(s32[4]{0:T(128)} %copy-done.12, ...), custom_call_target="tpu_custom_call" | custom-call | bytes 100000000 | tf_op jit(solution)/shard_map/pallas_call | solution.py:792
  357.3 1.0 copy-done.9
  358.3 5.2 shard_map.296
  363.7 2.1 multiply_reduce_fusion.2
  366.4 1.8 pad_add_fusion
  368.7 4.8 fusion.108
  373.6 1.1 pad_maximum_fusion.3.refs_1_
  374.7 2.8 convolution_convert_fusion.4.refs_5_
  377.6 3.0 convolution_convert_fusion.5.refs_4_
  380.6 1.7 fusion.70
  382.3 1.7 collective-permute-start.1
  384.1 2.6 convolution_convert_fusion.2.refs_3_
  386.7 2.6 convolution_convert_fusion.3.refs_2_
  389.4 4.5 fusion.54
  393.9 3.1 convolution_convert_fusion.6.refs_1_
  397.1 1.7 convolution_convert_fusion.7.refs_0_
  398.9 1.8 fusion.48
  400.7 1.1 pad_maximum_fusion.8.refs_0_
  401.9 4.5 multiply_reduce_fusion.5
  406.4 2.5 fusion.88
  409.6 4.6 shard_map.298
  414.3 4.3 convolution_convert_fusion.refs_7_
  418.6 2.6 convolution_convert_fusion.1.refs_6_
  421.2 131.7 %shard_map.299 = (f32[32,1024]{1,0:T(8,128)}, f32[32,1024]{1,0:T(8,128)}, f32[32,2048]{1,0:T(8,128)}, f32[32,2048]{1,0:T(8,128)}, f32[32,1024]{1,0:T(8,128)}, /*...) custom-call(bf16[512,1024]{1,0:T(8,128)(2,1)} %convolution_convert_fusion.7.refs_0_, ...), custom_call_target="tpu_custom_call" | custom-call | bytes 50855936 | tf_op jit(solution)/shard_map/pallas_call | solution.py:792
  552.9 1.0 slice.326
  555.5 1.0 slice.327
  557.9 1.3 slice_bitcast_fusion.2
  559.2 1.3 slice_bitcast_fusion
  560.5 1.3 slice_bitcast_fusion.1
  564.6 1.4 fusion.123
  565.9 1.7 maximum_bitcast_fusion
  567.6 1.9 pad_maximum_fusion.13
  571.6 5.7 convolution_bitcast_fusion
  (232 shorter events, 26.5 us)
Async XLA Ops:
  0.6 3.2 copy-start
  3.9 2.3 copy-start.66
  6.1 4.1 copy-start.29
  6.2 3.0 slice-start.2
  6.2 3.2 copy-start.51
  6.2 3.3 slice-start.1
  6.2 4.1 copy-start.46
  6.2 4.8 slice-start
  6.2 4.8 slice-start.3
  11.7 167.2 %copy-start.52 = (s32[1,3]{1,0:T(1,128)S(1)}, s32[1,3]{1,0:T(1,128)}, u32[]{:S(2)}) copy-start(s32[1,3]{1,0:T(1,128)} %param.18) | copy-start | bytes 40
  11.7 168.1 %copy-start.48 = (f32[4,1792]{1,0:T(4,128)S(1)}, f32[4,1792]{1,0:T(4,128)}, u32[]{:S(2)}) copy-start(f32[4,1792]{1,0:T(4,128)} %param.28) | copy-start | bytes 86020
  11.7 168.2 %copy-start.67 = (f32[24]{0:T(128)S(1)}, f32[24]{0:T(128)}, u32[]{:S(2)}) copy-start(f32[24]{0:T(128)} %param.30) | copy-start | bytes 292
  176.2 18.7 %copy-start.23 = (f32[256,1920]{1,0:T(8,128)}, f32[256,1920]{1,0:T(8,128)S(1)}, u32[]{:S(2)}) copy-start(f32[256,1920]{1,0:T(8,128)S(1)} %fusion.128) | copy-start | bytes 5898244
  176.2 20.8 %collective-permute-start = (f32[3,1792]{1,0:T(4,128)S(1)}, f32[3,1792]{1,0:T(4,128)S(1)}, u32[]{:S(2)}, u32[]{:S(2)}) collective-permute-start(f32[3,1792]{1,0:T(4,128)S(1)} %slice.350), channel_id=1, source_target_pairs={{0,4},{4,8},{8,12},{12,16},{16,20},{20,24},{24,28},{1,5},{5,9},{9,... | collective-permute-start | bytes 64520 | tf_op jit(solution)/shard_map/ppermute | solution.py:28
  185.2 2.9 copy-start.19
  185.2 4.6 copy-start.37
  188.1 4.6 copy-start.53
  188.1 4.6 copy-start.54
  189.8 5.2 copy-start.36
  194.8 5.1 copy-start.12
  194.8 2.3 copy-start.49
  194.9 4.8 copy-start.16
  197.0 2.8 copy-start.6
  197.1 2.8 copy-start.11
  199.8 65.8 %copy-start.21 = (bf16[1024,1024]{1,0:T(8,128)(2,1)S(1)}, bf16[1024,1024]{1,0:T(8,128)(2,1)}, u32[]{:S(2)}) copy-start(bf16[1024,1024]{1,0:T(8,128)(2,1)} %get-tuple-element.83) | copy-start | bytes 6291460
  261.6 5.7 copy-start.18
  261.6 5.8 copy-start.30
  264.5 3.7 copy-start.2
  268.3 2.5 copy-start.40
  268.3 2.5 copy-start.41
  268.3 3.4 copy-start.55
  274.9 3.8 copy-start.26
  274.9 3.8 copy-start.38
  276.2 4.1 copy-start.22
  285.0 4.1 copy-start.14
  301.8 55.5 %copy-start.5 = (bf16[128,1536]{1,0:T(8,128)(2,1)S(1)}, bf16[128,1536]{1,0:T(8,128)(2,1)}, u32[]{:S(2)}) copy-start(bf16[128,1536]{1,0:T(8,128)(2,1)} %get-tuple-element.81.state_in) | copy-start | bytes 1179652
  301.8 55.5 %copy-start.15 = (s32[4]{0:T(128)S(1)}, s32[4]{0:T(128)}, u32[]{:S(2)}) copy-start(s32[4]{0:T(128)} %copy-done.12) | copy-start | bytes 52
  358.3 5.3 copy-start.17
  358.3 5.3 copy-start.24
  358.3 5.3 copy-start.25
  368.7 6.0 %copy-start.45 = (bf16[256,512]{1,0:T(8,128)(2,1)S(1)}, bf16[256,512]{1,0:T(8,128)(2,1)}, u32[]{:S(2)}) copy-start(bf16[256,512]{1,0:T(8,128)(2,1)} %get-tuple-element.187) | copy-start | bytes 786436
  368.7 6.0 %copy-start.59 = (bf16[256,2048]{1,0:T(8,128)(2,1)S(1)}, bf16[256,2048]{1,0:T(8,128)(2,1)}, u32[]{:S(2)}) copy-start(bf16[256,2048]{1,0:T(8,128)(2,1)} %get-tuple-element.114) | copy-start | bytes 3145732
  368.7 6.0 %copy-start.64 = (bf16[256,512]{1,0:T(8,128)(2,1)S(1)}, bf16[256,512]{1,0:T(8,128)(2,1)}, u32[]{:S(2)}) copy-start(bf16[256,512]{1,0:T(8,128)(2,1)} %get-tuple-element.113) | copy-start | bytes 786436
  377.5 3.0 copy-start.20
  377.5 3.0 copy-start.34
  377.5 6.5 %copy-start.27 = (bf16[256,2048]{1,0:T(8,128)(2,1)S(1)}, bf16[256,2048]{1,0:T(8,128)(2,1)}, u32[]{:S(2)}) copy-start(bf16[256,2048]{1,0:T(8,128)(2,1)} %copy-done.26) | copy-start | bytes 3145732
  377.5 6.5 %copy-start.44 = (bf16[256,512]{1,0:T(8,128)(2,1)S(1)}, bf16[256,512]{1,0:T(8,128)(2,1)}, u32[]{:S(2)}) copy-start(bf16[256,512]{1,0:T(8,128)(2,1)} %get-tuple-element.189) | copy-start | bytes 786436
  377.5 6.6 %copy-start.58 = (bf16[256,2048]{1,0:T(8,128)(2,1)S(1)}, bf16[256,2048]{1,0:T(8,128)(2,1)}, u32[]{:S(2)}) copy-start(bf16[256,2048]{1,0:T(8,128)(2,1)} %get-tuple-element.112) | copy-start | bytes 3145732
  377.6 6.6 %copy-start.63 = (bf16[256,512]{1,0:T(8,128)(2,1)S(1)}, bf16[256,512]{1,0:T(8,128)(2,1)}, u32[]{:S(2)}) copy-start(bf16[256,512]{1,0:T(8,128)(2,1)} %get-tuple-element.110) | copy-start | bytes 786436
  380.6 6.2 %copy-start.39 = (bf16[256,2048]{1,0:T(8,128)(2,1)S(1)}, bf16[256,2048]{1,0:T(8,128)(2,1)}, u32[]{:S(2)}) copy-start(bf16[256,2048]{1,0:T(8,128)(2,1)} %copy-done.38) | copy-start | bytes 3145732
  380.6 6.2 %copy-start.57 = (bf16[256,2048]{1,0:T(8,128)(2,1)S(1)}, bf16[256,2048]{1,0:T(8,128)(2,1)}, u32[]{:S(2)}) copy-start(bf16[256,2048]{1,0:T(8,128)(2,1)} %get-tuple-element.111) | copy-start | bytes 3145732
  382.3 16.6 %collective-permute-start.1 = (f32[3,1792]{1,0:T(4,128)S(1)}, f32[3,1792]{1,0:T(4,128)S(1)}, u32[]{:S(2)}, u32[]{:S(2)}) collective-permute-start(f32[3,1792]{1,0:T(4,128)S(1)} %pad_add_fusion.1), channel_id=1, source_target_pairs={{4,0},{8,4},{12,8},{16,12},{20,16},{24,20},{28,24},{5,1},{9,5},{13... | collective-permute-start | bytes 64520 | tf_op jit(solution)/shard_map/ppermute | solution.py:28
  393.9 3.2 copy-start.35
  393.9 3.2 copy-start.56
  393.9 3.2 copy-start.62
  398.9 3.0 copy-start.31
  398.9 3.0 copy-start.68
  400.7 5.6 copy-start.32
  414.2 4.3 copy-start.33
  414.2 4.3 copy-start.60
  414.3 4.3 copy-start.61
  552.9 16.6 %copy-start.42 = (f32[32,1024]{1,0:T(8,128)S(1)}, f32[32,1024]{1,0:T(8,128)}, u32[]{:S(2)}) copy-start(f32[32,1024]{1,0:T(8,128)} %get-tuple-element.123) | copy-start | bytes 393220
  552.9 16.6 %copy-start.47 = (f32[32,1024]{1,0:T(8,128)S(1)}, f32[32,1024]{1,0:T(8,128)}, u32[]{:S(2)}) copy-start(f32[32,1024]{1,0:T(8,128)} %get-tuple-element.124) | copy-start | bytes 393220
  571.6 5.7 copy-start.1
  (11 other events, 16.8 us)

commit v4 on v3

--- a/solution.py
+++ b/solution.py
@@ -44,20 +44,6 @@
         out.append(flat[start : start + a.size].reshape(a.shape))
         start += a.size
     return out
-
-
-def own_order(width, fast):
-    blocks = 32
-    per = width // blocks
-    row = lax.broadcasted_iota(jnp.int32, (width, width), 0)
-    col = lax.broadcasted_iota(jnp.int32, (width, width), 1)
-    if not fast:
-        return (row == col).astype(jnp.bfloat16)
-    me = lax.axis_index("seq") * 4 + lax.axis_index("batch")
-    j = col // per
-    flipped = (j & 1) * 16 + (j & 2) * 4 + (j & 4) + (j & 8) // 4 + (j & 16) // 16
-    source = (flipped ^ me) * per + col % per
-    return (row == source).astype(jnp.bfloat16)
 
 
 def rms_scale(value_rows):
@@ -193,6 +179,14 @@
     return (rows <= at) & (rows >= seg_start(at, info))
 
 
+def attend_start(q, heads, acc, top, total):
+    for i in range(PAIRS):
+        heads[2 * i], heads[2 * i + 1] = halves_of(q[:, i * TILE : (i + 1) * TILE])
+    acc[...] = jnp.zeros_like(acc)
+    total[...] = jnp.zeros_like(total)
+    top[...] = jnp.full(top.shape, NEGATIVE_FILL, jnp.float32)
+
+
 def attend_block(info, block, keys, values_t, heads, acc, top, total):
     allowed = attn_mask(info, block)
     for h in range(QUERY_HEADS):
@@ -220,11 +214,7 @@
 
 
 def attn_forward_kernel(info, q, kv, out, out_t, lse, heads, acc, top, total):
-    for i in range(PAIRS):
-        heads[2 * i], heads[2 * i + 1] = halves_of(q[:, i * TILE : (i + 1) * TILE])
-    acc[...] = jnp.zeros_like(acc)
-    total[...] = jnp.zeros_like(total)
-    top[...] = jnp.full(top.shape, NEGATIVE_FILL, jnp.float32)
+    attend_start(q, heads, acc, top, total)
     low, count = block_range(info)
 
     def step(j, carry):
@@ -380,9 +370,9 @@
     return seg_start(at, info) - info[0]
 
 
-def ssm_forward_kernel(info, x, bc, step_in, head_params, y, state, dt_out, cum_out, dt_t, cum_t):
+def ssm_states(info, x, bc, step_in, head_params, state, dt_out, cum_out, dt_t, cum_t):
     rows = x.shape[0]
-    bias, rate, skip = head_params[0:1], head_params[1:2], head_params[2:3]
+    bias, rate = head_params[0:1], head_params[1:2]
     raw = step_in[...] + bias
     dt = jnp.maximum(raw, 0.0) + jnp.log1p(jnp.exp(-jnp.abs(raw)))
     dt = jnp.where(head_lanes(rows), dt, 0.0)
@@ -394,29 +384,35 @@
     cum_out[...] = cum
     dt_t[...] = dt.T
     cum_t[...] = cum.T
-    starts = chunk_places(info, rows)
     last_start = seg_start(info[0] + rows - 1, info) - info[0]
     place = lax.broadcasted_iota(jnp.int32, (rows, 1), 0)
     end = cum[rows - 1 : rows]
     leave = jnp.where(place >= last_start, jnp.exp(jnp.minimum(end - cum, 0.0)) * dt, 0.0)
-    narrow_b, narrow_c = bc[:, :NS], bc[:, NS:]
-    b_t = narrow_b.astype(jnp.float32).T.astype(jnp.bfloat16)
-    products = dot_nt(narrow_c, narrow_b)
+    b_t = bc[:, :NS].astype(jnp.float32).T.astype(jnp.bfloat16)
     through = jnp.where(last_start < 0, jnp.exp(end), 0.0)
     high = through.astype(jnp.bfloat16).astype(jnp.float32)
     line = lax.broadcasted_iota(jnp.int32, (16, TILE), 0)
     both = jnp.where(line == 0, high, jnp.where(line == 1, through - high, 0.0))
     spread = spread_heads(x.shape[1])
     state[NS:] = dot(both.astype(jnp.bfloat16), spread).astype(jnp.bfloat16)
-    skips = jnp.broadcast_to(skip, (8, TILE))
-    skip_row = two_part(skips, spread)[:1]
+    for i in range(MH // 2):
+        cols = slice(i * TILE, (i + 1) * TILE)
+        weighed = x[:, cols].astype(jnp.float32) * lane_pick(leave, 2 * i)
+        state[:NS, cols] = dot(b_t, weighed.astype(jnp.bfloat16)).astype(jnp.bfloat16)
+
+
+def ssm_local(info, x, bc, head_params, y, cum, dt_t, cum_t):
+    rows = x.shape[0]
+    row = lax.broadcasted_iota(jnp.int32, (rows, rows), 0)
+    col = lax.broadcasted_iota(jnp.int32, (rows, rows), 1)
+    starts = chunk_places(info, rows)
+    products = dot_nt(bc[:, NS:], bc[:, :NS])
+    skips = jnp.broadcast_to(head_params[2:3], (8, TILE))
+    skip_row = two_part(skips, spread_heads(x.shape[1]))[:1]
     lane = lax.broadcasted_iota(jnp.int32, (SPAN, TILE), 1)
     for i in range(MH // 2):
         cols = slice(i * TILE, (i + 1) * TILE)
         tile = x[:, cols]
-        state[:NS, cols] = dot(
-            b_t, (tile.astype(jnp.float32) * lane_pick(leave, 2 * i)).astype(jnp.bfloat16)
-        ).astype(jnp.bfloat16)
         for part in range(rows // SPAN):
             here = slice(part * SPAN, (part + 1) * SPAN)
             upto = (part + 1) * SPAN
@@ -429,6 +425,11 @@
                 sides.append(dot(mixing.astype(jnp.bfloat16), tile[:upto]))
             own = skip_row[:, cols] * tile[here].astype(jnp.float32)
             y[here, cols] = jnp.where(lane < MP, sides[0], sides[1]) + own
+
+
+def ssm_forward_kernel(info, x, bc, step_in, head_params, y, state, dt_out, cum_out, dt_t, cum_t):
+    ssm_states(info, x, bc, step_in, head_params, state, dt_out, cum_out, dt_t, cum_t)
+    ssm_local(info, x, bc, head_params, y, cum_out, dt_t, cum_t)
 
 
 def ssm_forward(info, x, bc, step_in, head_params):
@@ -804,17 +805,14 @@
 
 def column_chunks(widths):
     pairs = []
-    for k in range(0, len(widths), 2):
-        pieces = max(1, max(widths[k], widths[k + 1]) // 1024)
-        halves = []
-        for p in (k, k + 1):
-            tiles, first, cuts = widths[p] // TILE, 0, []
-            for i in range(pieces):
-                cols = (tiles // pieces + (1 if i < tiles % pieces else 0)) * TILE
-                cuts.append((p, first, cols))
-                first += cols
-            halves.append(cuts)
-        pairs += list(zip(*halves))
+    for p, width in enumerate(widths):
+        tiles, first, cuts = width // TILE, 0, []
+        pieces = 2 * max(1, width // 2048)
+        for i in range(pieces):
+            cols = (tiles // pieces + (1 if i < tiles % pieces else 0)) * TILE
+            cuts.append((p, first, cols))
+            first += cols
+        pairs += [tuple(cuts[i : i + 2]) for i in range(0, pieces, 2)]
     return pairs
 
 
@@ -825,68 +823,6 @@
     else:
         plan += [("y", [(0, 4, 8)]), ("x", [(0, 4, 4), (8, 4, 12)])]
     return plan + [("core", [(0, 16, 16)])]
-
-
-def weight_gather_kernel(count, pairs, *refs):
-    ins, outs = refs[:count], refs[count : 2 * count]
-    send, recv, local = refs[2 * count :]
-    others = partners()
-    greet(list(others.values()))
-    block = ins[0].shape[0]
-    own = []
-    for p in range(count):
-        copy = pltpu.make_async_copy(ins[p], outs[p].at[pl.ds(0, block)], local.at[p])
-        copy.start()
-        own.append(copy)
-    for copy in own:
-        copy.wait()
-    plans = [gather_plan(True), gather_plan(False)]
-    started = {}
-    for wave in range(len(pairs) + 5):
-        for n in reversed(range(len(pairs))):
-            stage = wave - n
-            if stage < 0 or stage > 5:
-                continue
-            for side in range(2):
-                p, column, cols = pairs[n][side]
-                if stage > 0:
-                    for copy in started[n, side, stage - 1]:
-                        copy.wait_recv()
-                if stage == 5:
-                    continue
-                name, moves = plans[side][stage]
-                copies = []
-                for k, (first, rows, there) in enumerate(moves):
-                    copy = remote(
-                        outs[p].at[pl.ds(first * block, rows * block), pl.ds(column, cols)],
-                        outs[p].at[pl.ds(there * block, rows * block), pl.ds(column, cols)],
-                        send.at[2 * n + side, stage, k],
-                        recv.at[2 * n + side, stage, k],
-                        others[name],
-                    )
-                    copy.start()
-                    copies.append(copy)
-                started[n, side, stage] = copies
-    for copies in started.values():
-        for copy in copies:
-            copy.wait_send()
-
-
-def weight_gather(parts):
-    count = len(parts)
-    outs = [shape_of((32 * p.shape[0], p.shape[1]), p.dtype) for p in parts]
-    pairs = column_chunks([p.shape[1] for p in parts])
-    dma = pltpu.SemaphoreType.DMA
-    return comm_call(
-        lambda *refs: weight_gather_kernel(count, pairs, *refs),
-        outs,
-        [ANY] * count,
-        parts,
-        [ANY] * count,
-        [dma((2 * len(pairs), 5, 2)), dma((2 * len(pairs), 5, 2)), dma((count,))],
-        0,
-        64 * sum(p.size for p in parts),
-    )
 
 
 def bit_apart(r):
@@ -986,35 +922,198 @@
     ]
 
 
-def mixer_forward_kernel(
-    info, q, pairs, state_own, out, out_t, lse, kv, state_in, heads, acc, top, total,
-    arrived, sent, before, scan_send, scan_recv, send, recv,
-):
+RIM = 8
+COLS = 384
+
+
+def own_order_into(target):
+    width = target.shape[0]
+    per = width // 32
+    me = lax.axis_index("seq") * 4 + lax.axis_index("batch")
+    step = 128
+
+    def fill(i, carry):
+        first = pl.multiple_of(i * step, step)
+        row = lax.broadcasted_iota(jnp.int32, (step, width), 0) + first
+        col = lax.broadcasted_iota(jnp.int32, (step, width), 1)
+        j = col // per
+        flipped = (j & 1) * 16 + (j & 2) * 4 + (j & 4) + (j & 8) // 4 + (j & 16) // 16
+        source = (flipped ^ me) * per + col % per
+        target[pl.ds(first, step)] = jnp.where(row == source, 1.0, 0.0).astype(target.dtype)
+        return carry
+
+    lax.fori_loop(0, width // step, fill, 0)
+
+
+def three_part(left, right):
+    high = left.astype(jnp.bfloat16)
+    rest = left - high.astype(jnp.float32)
+    mid = rest.astype(jnp.bfloat16)
+    low = (rest - mid.astype(jnp.float32)).astype(jnp.bfloat16)
+    return dot(high, right) + dot(mid, right) + dot(low, right)
+
+
+class Gather:
+    def __init__(self, ins, outs, pairs, send, recv, local, others):
+        self.ins, self.outs, self.pairs = ins, outs, pairs
+        self.send, self.recv, self.local, self.others = send, recv, local, others
+        self.plans = [gather_plan(True), gather_plan(False)]
+        self.started = {}
+        self.block = ins[0].shape[0]
+
+    def own(self):
+        copies = []
+        for p in range(len(self.ins)):
+            copy = pltpu.make_async_copy(
+                self.ins[p], self.outs[p].at[pl.ds(0, self.block)], self.local.at[p]
+            )
+            copy.start()
+            copies.append(copy)
+        for copy in copies:
+            copy.wait()
+
+    def step(self, n, stage):
+        for side in range(2):
+            p, column, cols = self.pairs[n][side]
+            if stage > 0:
+                for copy in self.started[n, side, stage - 1]:
+                    copy.wait_recv()
+            if stage == 5:
+                continue
+            name, moves = self.plans[side][stage]
+            copies = []
+            for k, (first, rows, there) in enumerate(moves):
+                block = self.block
+                copy = remote(
+                    self.outs[p].at[pl.ds(first * block, rows * block), pl.ds(column, cols)],
+                    self.outs[p].at[pl.ds(there * block, rows * block), pl.ds(column, cols)],
+                    self.send.at[2 * n + side, stage, k],
+                    self.recv.at[2 * n + side, stage, k],
+                    self.others[name],
+                )
+                copy.start()
+                copies.append(copy)
+            self.started[n, side, stage] = copies
+
+    def finish(self):
+        for copies in self.started.values():
+            for copy in copies:
+                copy.wait_send()
+
+
+def around():
+    seq, batch = lax.axis_index("seq"), lax.axis_index("batch")
+    return ((seq + 7) % 8, batch), ((seq + 1) % 8, batch)
+
+
+def conv_masks(info, rows):
+    at = lax.broadcasted_iota(jnp.int32, (rows, 1), 0) + info[0]
+    start = seg_start(at, info)
+    return [jnp.where(at - (CONV - 1) + i >= start, 1.0, 0.0) for i in range(CONV)]
+
+
+def conv_forward(info, raw, conv_w, conv_b, pre, x, bc):
+    rows = x.shape[0]
+    masks = conv_masks(info, rows)
+    tiles = pre.shape[1] // TILE
+    split = x.shape[1] // TILE
+    for i in range(tiles):
+        cols = slice(i * TILE, (i + 1) * TILE)
+        total = jnp.broadcast_to(conv_b[:, cols], (rows, TILE))
+        for k in range(CONV):
+            first = RIM - (CONV - 1) + k
+            shifted_rows = jnp.where(masks[k] > 0.0, raw[first : first + rows, cols], 0.0)
+            total = total + conv_w[k : k + 1, cols] * shifted_rows
+        pre[:, cols] = total
+        out = (total * jax.nn.sigmoid(total)).astype(jnp.bfloat16)
+        if i < split:
+            x[:, cols] = out
+        else:
+            bc[:, (i - split) * TILE : (i - split + 1) * TILE] = out
+
+
+def front_kernel(count, pairs, info, layer_x, layer_g, gains, cosine, sine, head_params, conv_w, conv_b, *refs):
+    ins, refs = refs[:count], refs[count:]
+    fulls, refs = refs[:count], refs[count:]
+    (
+        x_own, g_own, gains_own, normed, q, kv, gate_z, raw, pre, x, bc, y, state, dt, cum,
+        out, out_t, lse, state_in, order,
+    ) = refs[:20]
+    (
+        attn_proj, dt_t, cum_t, heads, acc, top, total, arrived, sent, before,
+        scan_send, scan_recv, send, recv, w_send, w_recv, w_local, rim_send, rim_recv,
+    ) = refs[20:]
     others = partners()
-    greet([others["far"], others["near"], others["x"]])
+    previous, following = around()
+    greet(list(others.values()) + [previous, following])
     me = lax.axis_index("seq")
-    rows = pairs.shape[0]
+    rows, width = layer_x.shape
+    gather = Gather(ins, fulls, pairs, w_send, w_recv, w_local, others)
+    gather.own()
+
+    def pump(*steps):
+        for n, stage in steps:
+            gather.step(n, stage)
+
+    pump((0, 0), (1, 0))
+    own_order_into(order)
+    pump((0, 1), (1, 1))
+    x_own[...] = dot(layer_x[...], order[...]).astype(jnp.bfloat16)
+    pump((0, 2), (2, 0))
+    gains_own[...] = three_part(gains[...], order[...])
+    wide = x_own[...].astype(jnp.float32)
+    scale = lax.rsqrt(jnp.mean(wide * wide, axis=-1, keepdims=True) + NORM_EPS)
+    normed[...] = (wide * scale * gains_own[0:1]).astype(jnp.bfloat16)
+    pump((1, 2), (0, 3), (2, 1), (3, 0))
+    g_own[...] = dot(layer_g[...], order[...]).astype(jnp.bfloat16)
+    pump((0, 4), (1, 3), (3, 1), (4, 0))
+    pump((0, 5))
+
+    full_conv, full_mix = fulls[0], fulls[1]
+    xbc = pre.shape[1]
+    conv_cols = full_conv.shape[1] // COLS
+    attn_cols = attn_proj.shape[1] // COLS
+    gate_cols = gate_z.shape[1] // COLS
+
+    def project(weights, first, target, row, count_cols):
+        def one(j, carry):
+            cols = pl.ds(pl.multiple_of(j * COLS, TILE), COLS)
+            there = pl.ds(pl.multiple_of(first + j * COLS, TILE), COLS)
+            target[row : row + rows, cols] = dot(normed[...], weights[:, there])
+            return carry
+
+        lax.fori_loop(0, count_cols, one, 0)
 
     def at(r):
         return kv.at[pl.ds(r * rows, rows)]
 
-    scan = StateScan(True, state_own, state_in, arrived, sent, before, scan_send, scan_recv, others)
-    kv[:rows] = pairs[...]
     routes = {4: ("far", 0), 2: ("near", 0), 6: ("near", 4)}
     routes.update({r: ("x", r - 1) for r in (1, 3, 5, 7)})
     copies = {
         r: remote(at(src), at(r), send.at[r], recv.at[r], others[name])
         for r, (name, src) in routes.items()
     }
+    project(full_conv, 0, raw, RIM, conv_cols)
+    rim = remote(
+        raw.at[pl.ds(rows, RIM)], raw.at[pl.ds(0, RIM)], rim_send.at[0], rim_recv.at[0], following
+    )
+    rim.start()
+    pump((1, 4), (2, 2), (4, 1), (5, 0))
+    rim.wait_recv()
+    conv_forward(info, raw, conv_w, conv_b, pre, x, bc)
+    step_in = raw.at[pl.ds(RIM, rows), pl.ds(xbc, TILE)]
+    ssm_states(info, x, bc, step_in, head_params, state, dt, cum, dt_t, cum_t)
+    scan = StateScan(True, state, state_in, arrived, sent, before, scan_send, scan_recv, others)
+    scan.step(0)
+    pump((1, 5))
+    project(full_mix, 0, attn_proj, 0, attn_cols)
+    rope_kernel(attn_proj, cosine, sine, q, kv.at[pl.ds(0, rows)])
     copies[4].start()
     copies[2].start()
     copies[1].start()
-    scan.step(0)
-    for i in range(PAIRS):
-        heads[2 * i], heads[2 * i + 1] = halves_of(q[:, i * TILE : (i + 1) * TILE])
-    acc[...] = jnp.zeros_like(acc)
-    total[...] = jnp.zeros_like(total)
-    top[...] = jnp.full(top.shape, NEGATIVE_FILL, jnp.float32)
+    pump((5, 1), (2, 3), (3, 2))
+    project(full_mix, attn_proj.shape[1], gate_z, 0, gate_cols)
+    attend_start(q, heads, acc, top, total)
 
     def attend(r):
         block = bit_apart(r)
@@ -1026,89 +1125,294 @@
             values_t = kv[place, TILE:].astype(jnp.float32).T.astype(jnp.bfloat16)
             attend_block(info, block, keys, values_t, heads, acc, top, total)
 
-    attend(0)
+    def several(first, gap, count_blocks):
+        def body(j, carry):
+            attend(first + j * gap)
+            return carry
+
+        lax.fori_loop(0, count_blocks, body, 0)
+
     scan.step(1)
     copies[4].wait_recv()
     copies[6].start()
     copies[5].start()
-    attend(4)
     copies[2].wait_recv()
     copies[3].start()
     copies[6].wait_recv()
     copies[7].start()
+    several(0, 4, 2)
+    pump((3, 3), (4, 2), (2, 4))
+    ssm_local(info, x, bc, head_params, y, cum, dt_t, cum_t)
     scan.step(2)
-
-    def several(first, gap, count):
-        def body(j, carry):
-            attend(first + j * gap)
-            return carry
-
-        lax.fori_loop(0, count, body, 0)
-
     several(2, 4, 2)
+    pump((4, 3), (5, 2), (3, 4))
     for r in (1, 3, 5, 7):
         copies[r].wait_recv()
     several(1, 2, 4)
     lse[...] = top[...] + jnp.log(total[...])
     attend_write(acc, total, out, out_t)
     scan.step(3)
+    pump((5, 3), (4, 4), (2, 5))
+    pump((5, 4), (3, 5), (4, 5), (5, 5))
+    gather.finish()
     scan.finish()
+    rim.wait_send()
     for copy in copies.values():
         copy.wait_send()
 
 
-def mixer_forward(info, q, pairs, state_own):
-    rows = q.shape[0]
-    f32 = jnp.float32
+def front(info, layer_x, layer_g, gains, cosine, sine, head_params, conv_w, conv_b, shards):
+    count = len(shards)
+    rows, width = layer_x.shape
+    f32, narrow = jnp.float32, jnp.bfloat16
+    pairs = column_chunks([p.shape[1] for p in shards])
+    query_width = QUERY_HEADS * HEAD_SIZE
+    pair_width = 2 * KEY_VALUE_HEADS * HEAD_SIZE
+    ssm_width = MH * MP
+    xbc = conv_w.shape[1]
+    fulls = [shape_of((32 * p.shape[0], p.shape[1]), p.dtype) for p in shards]
+    outs = fulls + [
+        shape_of((rows, width), narrow),
+        shape_of((rows, width), narrow),
+        shape_of(gains.shape, f32),
+        shape_of((rows, width), narrow),
+        shape_of((rows, query_width), narrow),
+        shape_of((8 * rows, pair_width), narrow),
+        shape_of((rows, ssm_width), f32),
+        shape_of((rows + RIM, shards[0].shape[1]), f32),
+        shape_of((rows, xbc), f32),
+        shape_of((rows, ssm_width), narrow),
+        shape_of((rows, 2 * NS), narrow),
+        shape_of((rows, ssm_width), f32),
+        shape_of((STATE_ROWS, ssm_width), narrow),
+        shape_of((rows, TILE), f32),
+        shape_of((rows, TILE), f32),
+        shape_of((rows, query_width), narrow),
+        shape_of((query_width, rows), f32),
+        shape_of((QUERY_HEADS, rows), f32),
+        shape_of((NS, ssm_width), narrow),
+        shape_of((width, width), narrow),
+    ]
     dma = pltpu.SemaphoreType.DMA
-    width = state_own.shape[1]
-    outs = (
-        shape_of(q.shape, jnp.bfloat16),
-        shape_of(q.shape[::-1], f32),
-        shape_of((QUERY_HEADS, rows), f32),
-        shape_of((8 * rows, pairs.shape[1]), jnp.bfloat16),
-        shape_of((NS, width), jnp.bfloat16),
-    )
-    return comm_call(
-        mixer_forward_kernel,
+    scratch = [
+        pltpu.VMEM((rows, query_width + pair_width), f32),
+        pltpu.VMEM((TILE, rows), f32),
+        pltpu.VMEM((TILE, rows), f32),
+        pltpu.VMEM((QUERY_HEADS, rows, TILE), narrow),
+        pltpu.VMEM((QUERY_HEADS, HEAD_SIZE, rows), f32),
+        pltpu.VMEM((QUERY_HEADS, rows), f32),
+        pltpu.VMEM((QUERY_HEADS, rows), f32),
+        *scan_scratch(ssm_width),
+        dma((8,)),
+        dma((8,)),
+        dma((2 * len(pairs), 5, 2)),
+        dma((2 * len(pairs), 5, 2)),
+        dma((count,)),
+        dma((1,)),
+        dma((1,)),
+    ]
+    result = comm_call(
+        lambda *refs: front_kernel(count, pairs, *refs),
         outs,
-        [INTO_VMEM] * 5,
-        (info, q, pairs, state_own),
-        [pl.BlockSpec(memory_space=pltpu.SMEM)] + [INTO_VMEM] * 3,
-        [
-            pltpu.VMEM((QUERY_HEADS, rows, TILE), jnp.bfloat16),
-            pltpu.VMEM((QUERY_HEADS, HEAD_SIZE, rows), f32),
-            pltpu.VMEM((QUERY_HEADS, rows), f32),
-            pltpu.VMEM((QUERY_HEADS, rows), f32),
-            *scan_scratch(width),
-            dma((8,)),
-            dma((8,)),
-        ],
-        1,
-        100_000_000,
-    )
-
-
-def mixer_backward_kernel(swaps, info, q, kv, grad, out_t, lse, pull, *refs):
-    give, refs = refs[:swaps], refs[swaps:]
-    dq, d_own, d_state, refs = refs[0], refs[1], refs[2], refs[3:]
-    take, refs = refs[:swaps], refs[swaps:]
+        [INTO_VMEM] * 2 + [ANY] * (count - 2) + [INTO_VMEM] * 20,
+        (info, layer_x, layer_g, gains, cosine, sine, head_params, conv_w, conv_b, *shards),
+        [pl.BlockSpec(memory_space=pltpu.SMEM)] + [INTO_VMEM] * 8 + [ANY] * count,
+        scratch,
+        0,
+        200_000_000,
+    )
+    return result[:count], result[count:]
+
+
+def turn_over(value):
+    return value.astype(jnp.float32).T.astype(jnp.bfloat16)
+
+
+class Scatter:
+    def __init__(self, ins, outs, arrived, pairs, send, recv, others):
+        self.ins, self.outs, self.arrived, self.pairs = ins, outs, arrived, pairs
+        self.send, self.recv, self.others = send, recv, others
+        self.routes = (("y", "x", "near", "far"), ("x", "y", "near", "far"))
+        self.size = ins[0].shape[0]
+        self.started = {}
+
+    def source(self, p, stage):
+        return self.ins[p] if stage == 0 else self.arrived[4 * p + stage - 1]
+
+    def pieces(self, side, stage):
+        rows = self.size >> stage
+        if side == 1 and stage == 0:
+            quarter = rows // 4
+            return [quarter, 3 * quarter], [0, 2 * quarter], quarter
+        return [rows // 2], [0], rows // 2
+
+    def step(self, n, stage):
+        for side in range(2):
+            if stage > 0:
+                self.take(n, side, stage - 1)
+            if stage < 4:
+                self.begin(n, side, stage)
+
+    def begin(self, n, side, stage):
+        p, column, width = self.pairs[n][side]
+        cols = pl.ds(column, width)
+        sent, unused_kept, rows = self.pieces(side, stage)
+        copies = []
+        for k, first in enumerate(sent):
+            copy = remote(
+                self.source(p, stage).at[pl.ds(first, rows), cols],
+                self.arrived[4 * p + stage].at[pl.ds(k * rows, rows), cols],
+                self.send.at[2 * n + side, stage, k],
+                self.recv.at[2 * n + side, stage, k],
+                self.others[self.routes[side][stage]],
+            )
+            copy.start()
+            copies.append(copy)
+        self.started[n, side, stage] = copies
+
+    def take(self, n, side, stage):
+        p, column, width = self.pairs[n][side]
+        cols = slice(column, column + width)
+        source, got = self.source(p, stage), self.arrived[4 * p + stage]
+        target = self.outs[p] if stage == 3 else got
+        unused_sent, kept, rows = self.pieces(side, stage)
+        for k, first in enumerate(kept):
+            self.started[n, side, stage][k].wait_recv()
+
+            def add(i, carry):
+                at = pl.multiple_of(i * 32, 32)
+                there = pl.ds(k * rows + at, 32)
+                total = source[pl.ds(first + at, 32), cols].astype(jnp.float32) + got[
+                    there, cols
+                ].astype(jnp.float32)
+                target[there, cols] = total.astype(target.dtype)
+                return carry
+
+            lax.fori_loop(0, rows // 32, add, 0)
+
+    def finish(self):
+        for copies in self.started.values():
+            for copy in copies:
+                copy.wait_send()
+
+
+def scatter_scratch(widths, size):
+    scratch = []
+    for width in widths:
+        scratch += [pltpu.VMEM((size >> (s + 1), width), jnp.bfloat16) for s in range(4)]
+    return scratch
+
+
+def weight_products(left_t, right, theirs, target):
+    rows = right.shape[0]
+    step = 256 if right.shape[1] % 256 == 0 else TILE
+
+    def one(j, carry):
+        cols = pl.ds(pl.multiple_of(j * step, step), step)
+        product = dot(left_t[:, :rows], right[:, cols]) + dot(left_t[:, rows:], theirs[:, cols])
+        target[:, cols] = product.astype(target.dtype)
+        return carry
+
+    lax.fori_loop(0, right.shape[1] // step, one, 0)
+
+
+def conv_back_start(info, dx, d_bc, pre, raw, d_pre, g_conv):
+    rows, split = dx.shape[0], dx.shape[1] // TILE
+    masks = conv_masks(info, rows)
+    g_conv[...] = jnp.zeros_like(g_conv)
+    for i in range(pre.shape[1] // TILE):
+        cols = slice(i * TILE, (i + 1) * TILE)
+        if i < split:
+            grad = dx[:, cols]
+        else:
+            grad = d_bc[:, (i - split) * TILE : (i - split + 1) * TILE]
+        value = pre[:, cols]
+        sig = jax.nn.sigmoid(value)
+        grad = grad * (sig * (1.0 + value * (1.0 - sig)))
+        d_pre[:rows, cols] = grad
+        for k in range(CONV):
+            first = RIM - (CONV - 1) + k
+            term = jnp.where(masks[k] > 0.0, raw[first : first + rows, cols], 0.0)
+            g_conv[k : k + 1, cols] = jnp.sum(grad * term, axis=0, keepdims=True)
+        g_conv[CONV : CONV + 1, cols] = jnp.sum(grad, axis=0, keepdims=True)
+
+
+def conv_back_end(info, d_pre, conv_w, d_raw):
+    rows = d_raw.shape[0]
+    at = lax.broadcasted_iota(jnp.int32, (rows, 1), 0) + info[0]
+    masks = [
+        jnp.where(seg_start(at + (CONV - 1) - k, info) <= at, 1.0, 0.0) for k in range(CONV)
+    ]
+    for i in range(d_pre.shape[1] // TILE):
+        cols = slice(i * TILE, (i + 1) * TILE)
+        total = jnp.zeros((rows, TILE), jnp.float32)
+        for k in range(CONV):
+            first = CONV - 1 - k
+            part = jnp.where(masks[k] > 0.0, d_pre[first : first + rows, cols], 0.0)
+            total = total + conv_w[k : k + 1, cols] * part
+        d_raw[:, cols] = total.astype(jnp.bfloat16)
+
+
+def back_kernel(pairs, *refs):
     (
-        heads, grads, delta, acc, dkv, from_x, from_far, from_near,
+        info, head_params, conv_w, cosine, sine, q, kv, grad, out_t, lse, pull, x, bc, dt, cum,
+        d_ssm, raw, state_in, pre, normed, normed_two, d_mixer, grad_rows, hidden, joined, d_gu,
+        d_z,
+    ) = refs[:27]
+    (
+        d_conv, d_attn, g_conv, head_sums, g_skip, their_normed, out_down, out_gu, out_out, out_z,
+    ) = refs[27:37]
+    refs = refs[37:]
+    partials, refs = refs[:4], refs[4:]
+    arrived_w, refs = refs[:16], refs[16:]
+    (
+        half_grad, half_two, half_mixer, their_hidden, their_joined, their_gu, their_z, left_t,
+        heads, grads, delta, acc, dkv, from_x, from_far, from_near, dq, d_pair, d_state,
+        dx, d_bc, d_cum, d_dt, cols_t, d_rows, d_pre,
         arrived, sent, before, scan_send, scan_recv, send, recv, swap_send, swap_recv,
+        w_send, w_recv, rim_send, rim_recv,
     ) = refs
     others = partners()
-    greet([others["far"], others["near"], others["x"], others["core"]])
+    previous, following = around()
+    greet(list(others.values()) + [previous, following])
     me = lax.axis_index("seq")
     rows = q.shape[0]
+    half = normed.shape[1] // 2
+    xbc = pre.shape[1]
     scan = StateScan(False, pull, d_state, arrived, sent, before, scan_send, scan_recv, others)
     scan.step(0)
-    swapped = [
-        remote(give[k], take[k], swap_send.at[k], swap_recv.at[k], others["core"])
-        for k in range(swaps)
+    behind = pl.ds(half, half)
+    given = [
+        (grad_rows.at[:, behind], half_grad),
+        (hidden, their_hidden),
+        (normed_two.at[:, behind], half_two),
+        (d_gu, their_gu),
+        (d_mixer.at[:, behind], half_mixer),
+        (joined, their_joined),
+        (normed.at[:, behind], their_normed),
+        (d_z, their_z),
     ]
-    for copy in swapped:
+    swaps = [
+        remote(give, take, swap_send.at[k], swap_recv.at[k], others["core"])
+        for k, (give, take) in enumerate(given)
+    ]
+    for copy in swaps:
         copy.start()
+    scatter = Scatter(
+        partials, (out_down, out_gu, out_out, out_z), arrived_w, pairs, w_send, w_recv, others
+    )
+
+    def weights(k, left, left_half, right, theirs):
+        swaps[2 * k].wait_recv()
+        swaps[2 * k + 1].wait_recv()
+        left_t[:, :rows] = turn_over(left[:, :half])
+        left_t[:, rows:] = turn_over(left_half[...])
+        weight_products(left_t, right, theirs, partials[k])
+
+    def pump(*steps):
+        for n, stage in steps:
+            scatter.step(n, stage)
+
     attend_back_start(q, grad, out_t, heads, grads, delta, acc)
 
     def block_back(r):
@@ -1132,6 +1436,11 @@
             return carry
 
         lax.fori_loop(0, count, body, 0)
+
+    def add(target, source):
+        target[...] = (target[...].astype(jnp.float32) + source[...].astype(jnp.float32)).astype(
+            jnp.bfloat16
+        )
 
     several(1, 2, 4)
     over_x = [
@@ -1141,13 +1450,9 @@
     for copy in over_x:
         copy.start()
     scan.step(1)
+    weights(0, grad_rows, half_grad, hidden, their_hidden)
+    pump((0, 0))
     several(4, 2, 2)
-
-    def add(target, source):
-        target[...] = (target[...].astype(jnp.float32) + source[...].astype(jnp.float32)).astype(
-            jnp.bfloat16
-        )
-
     over_far = [
         remote(dkv.at[4 + 2 * k], from_far.at[k], send.at[4 + k], recv.at[4 + k], others["far"])
         for k in range(2)
@@ -1157,6 +1462,8 @@
         add(dkv.at[4 + 2 * k], from_x.at[2 + k])
         over_far[k].start()
     scan.step(2)
+    weights(1, normed_two, half_two, d_gu, their_gu)
+    pump((1, 0), (0, 1))
     several(0, 2, 2)
     for k in range(2):
         over_x[k].wait_recv()
@@ -1165,218 +1472,271 @@
     add(dkv.at[2], from_far.at[1])
     over_near = remote(dkv.at[2], from_near, send.at[6], recv.at[6], others["near"])
     over_near.start()
+    pump((2, 0), (1, 1), (0, 2))
+    ssm_back_kernel(
+        info, x, bc, dt, cum, d_ssm, head_params, dx, d_bc, d_cum, d_dt, g_skip, cols_t, d_rows
+    )
+    scan.step(3)
+    weights(2, d_mixer, half_mixer, joined, their_joined)
+    pump((3, 0), (2, 1), (1, 2), (0, 3))
+    d_step = d_conv.at[:, pl.ds(xbc, TILE)]
+    step_in = raw.at[pl.ds(RIM, rows), pl.ds(xbc, TILE)]
+    state_back_kernel(
+        info, x, bc, dt, cum, d_ssm, head_params, step_in, state_in, d_state, dx, d_bc, d_cum,
+        d_dt, dx, d_bc, d_step, head_sums,
+    )
+    conv_back_start(info, dx, d_bc, pre, raw, d_pre, g_conv)
+    rim = remote(
+        d_pre.at[pl.ds(0, RIM)], d_pre.at[pl.ds(rows, RIM)], rim_send.at[0], rim_recv.at[0],
+        previous,
+    )
+    rim.start()
+    weights(3, normed, their_normed, d_z, their_z)
+    pump((4, 0), (3, 1), (2, 2), (1, 3), (0, 4))
     over_far[0].wait_recv()
+    over_near.wait_recv()
     attend_back_write(acc, dq)
-    scan.step(3)
-    over_near.wait_recv()
-    d_own[...] = (
+    d_pair[...] = (
         dkv[0].astype(jnp.float32)
         + from_far[0].astype(jnp.float32)
         + from_near[...].astype(jnp.float32)
     )
+    rope_back_kernel(dq, d_pair, cosine, sine, d_attn)
+    rim.wait_recv()
+    conv_back_end(info, d_pre, conv_w, d_conv.at[:, pl.ds(0, xbc)])
+    pump((4, 1), (3, 2), (2, 3), (1, 4))
+    pump((4, 2), (3, 3), (2, 4))
+    pump((4, 3), (3, 4))
+    pump((4, 4))
+    scatter.finish()
     scan.finish()
-    for copy in over_x + over_far + [over_near]:
+    rim.wait_send()
+    for copy in over_x + over_far + [over_near] + swaps:
         copy.wait_send()
-    for copy in swapped:
-        copy.wait()
-
-
-def mixer_backward(info, q, kv, grad, out_t, lse, pull, give):
-    rows = q.shape[0]
-    f32 = jnp.float32
+
+
+def back(info, *args):
+    (
+        head_params, conv_w, cosine, sine, q, kv, grad, out_t, lse, pull, x, bc, dt, cum,
+        d_ssm, raw, state_in, pre, normed, normed_two, d_mixer, grad_rows, hidden, joined, d_gu,
+        d_z,
+    ) = args
+    rows, query_width = q.shape
+    width = normed.shape[1]
+    half = width // 2
+    pair = kv.shape[1]
+    ssm_width, xbc = x.shape[1], pre.shape[1]
+    f32, narrow = jnp.float32, jnp.bfloat16
     dma = pltpu.SemaphoreType.DMA
-    width = pull.shape[1]
-    pair = kv.shape[1]
-    swaps = len(give)
-    narrow = jnp.bfloat16
+    widths = [hidden.shape[1], d_gu.shape[1], joined.shape[1], d_z.shape[1]]
+    pairs = column_chunks(widths)
+    own = half // 16
     outs = [
-        shape_of(q.shape, f32),
-        shape_of((rows, pair), f32),
-        shape_of((NS, width), narrow),
-    ] + [shape_of(a.shape, a.dtype) for a in give]
-    result = comm_call(
-        lambda *refs: mixer_backward_kernel(swaps, *refs),
+        shape_of((rows, xbc + TILE), narrow),
+        shape_of((rows, query_width + pair), narrow),
+        shape_of((8, xbc), f32),
+        shape_of((8, TILE), f32),
+        shape_of((8, TILE), f32),
+        shape_of((rows, half), narrow),
+    ] + [shape_of((own, w), f32) for w in widths]
+    scratch = [pltpu.VMEM((half, w), narrow) for w in widths]
+    scratch += scatter_scratch(widths, half)
+    scratch += [pltpu.VMEM((rows, half), narrow)] * 3
+    scratch += [pltpu.VMEM(a.shape, narrow) for a in (hidden, joined, d_gu, d_z)]
+    scratch += [
+        pltpu.VMEM((half, 2 * rows), narrow),
+        pltpu.VMEM((QUERY_HEADS, rows, TILE), narrow),
+        pltpu.VMEM((QUERY_HEADS, rows, TILE), narrow),
+        pltpu.VMEM((QUERY_HEADS, rows), f32),
+        pltpu.VMEM((QUERY_HEADS, HEAD_SIZE, rows), f32),
+        pltpu.VMEM((8, rows, pair), narrow),
+        pltpu.VMEM((4, rows, pair), narrow),
+        pltpu.VMEM((2, rows, pair), narrow),
+        pltpu.VMEM((rows, pair), narrow),
+        pltpu.VMEM((rows, query_width), f32),
+        pltpu.VMEM((rows, pair), f32),
+        pltpu.VMEM((NS, ssm_width), narrow),
+        pltpu.VMEM((rows, ssm_width), f32),
+        pltpu.VMEM((rows, 2 * NS), f32),
+        pltpu.VMEM((rows, TILE), f32),
+        pltpu.VMEM((rows, TILE), f32),
+        pltpu.VMEM((TILE, rows), f32),
+        pltpu.VMEM((TILE, rows), f32),
+        pltpu.VMEM((rows + RIM, xbc), f32),
+        *scan_scratch(ssm_width),
+        dma((7,)),
+        dma((7,)),
+        dma((8,)),
+        dma((8,)),
+        dma((2 * len(pairs), 4, 2)),
+        dma((2 * len(pairs), 4, 2)),
+        dma((1,)),
+        dma((1,)),
+    ]
+    return comm_call(
+        lambda *refs: back_kernel(pairs, *refs),
         outs,
-        [INTO_VMEM] * 3 + [ANY] * swaps,
-        (info, q, kv, grad, out_t, lse, pull, *give),
-        [pl.BlockSpec(memory_space=pltpu.SMEM)] + [INTO_VMEM] * 6 + [ANY] * swaps,
-        [
-            pltpu.VMEM((QUERY_HEADS, rows, TILE), narrow),
-            pltpu.VMEM((QUERY_HEADS, rows, TILE), narrow),
-            pltpu.VMEM((QUERY_HEADS, rows), f32),
-            pltpu.VMEM((QUERY_HEADS, HEAD_SIZE, rows), f32),
-            pltpu.VMEM((8, rows, pair), narrow),
-            pltpu.VMEM((4, rows, pair), narrow),
-            pltpu.VMEM((2, rows, pair), narrow),
-            pltpu.VMEM((rows, pair), narrow),
-            *scan_scratch(width),
-            dma((7,)),
-            dma((7,)),
-            dma((swaps,)),
-            dma((swaps,)),
-        ],
+        [INTO_VMEM] * len(outs),
+        (info, *args),
+        [pl.BlockSpec(memory_space=pltpu.SMEM)] + [INTO_VMEM] * len(args),
+        scratch,
         2,
-        100_000_000,
-    )
-    return result[0], result[1], result[2], result[3:]
-
-
-def core_swap_kernel(count, *refs):
-    give, take = refs[:count], refs[count : 2 * count]
-    send, recv = refs[2 * count :]
-    other = partners()["core"]
-    greet([other])
-    copies = [remote(give[k], take[k], send.at[k], recv.at[k], other) for k in range(count)]
-    for copy in copies:
-        copy.start()
-    for copy in copies:
-        copy.wait()
-
-
-def core_swap(give):
-    count = len(give)
-    dma = pltpu.SemaphoreType.DMA
-    return comm_call(
-        lambda *refs: core_swap_kernel(count, *refs),
-        [shape_of(a.shape, a.dtype) for a in give],
-        [ANY] * count,
-        give,
-        [ANY] * count,
-        [dma((count,)), dma((count,))],
-        3,
-        2 * sum(a.size for a in give),
-    )
-
-
-def weight_scatter_kernel(count, pairs, *refs):
-    ins, small, refs = refs[:count], refs[count], refs[count + 1 :]
-    outs, small_out, refs = refs[:count], refs[count], refs[count + 1 :]
-    arrived, kept, refs = refs[: 4 * count], refs[4 * count : 7 * count], refs[7 * count :]
-    small_in, small_mid, send, recv, small_send, small_recv = refs
+        200_000_000,
+        limit=62,
+    )
+
+
+def dot_nt_two(left, right):
+    high = left.astype(jnp.bfloat16)
+    low = (left - high.astype(jnp.float32)).astype(jnp.bfloat16)
+    return dot_nt(high, right) + dot_nt(low, right)
+
+
+def last_kernel(pairs, *refs):
+    (
+        d_conv, d_attn, d_z, full_conv, full_mix, normed, their_normed, x_own, d_middle, gains,
+        order, g_mlp, small,
+    ) = refs[:13]
+    input_grad, out_conv, out_attn, small_out = refs[13:17]
+    refs = refs[17:]
+    partials, arrived_w = refs[:2], refs[2:10]
+    (
+        their_conv, their_attn, left_t, d_normed, small_own, small_in, small_mid, swap_send,
+        swap_recv, w_send, w_recv, small_send, small_recv,
+    ) = refs[10:]
     others = partners()
     greet(list(others.values()))
-    size = ins[0].shape[0]
-    routes = (("y", "x", "near", "far"), ("x", "y", "near", "far"))
-
-    def pieces(side, stage):
-        rows = size >> stage
-        half = rows // 2
-        if side == 1 and stage == 0:
-            quarter = rows // 4
-            return [(quarter, quarter), (3 * quarter, quarter)], [(0, quarter), (2 * quarter, quarter)]
-        return [(half, half)], [(0, half)]
-
-    started = {}
-
-    def begin(n, side, stage):
-        p, column, width = pairs[n][side]
-        cols = pl.ds(column, width)
-        source = ins[p] if stage == 0 else kept[3 * p + stage - 1]
-        target = arrived[4 * p + stage]
-        copies, row = [], 0
-        for k, (first, rows) in enumerate(pieces(side, stage)[0]):
+    rows, width = normed.shape
+    half = width // 2
+    swaps = [
+        remote(give, take, swap_send.at[k], swap_recv.at[k], others["core"])
+        for k, (give, take) in enumerate(((d_conv, their_conv), (d_attn, their_attn)))
+    ]
+    for copy in swaps:
+        copy.start()
+    scatter = Scatter(partials, (out_conv, out_attn), arrived_w, pairs, w_send, w_recv, others)
+    left_t[:, :rows] = turn_over(normed[:, :half])
+    left_t[:, rows:] = turn_over(their_normed[...])
+    swaps[0].wait_recv()
+    weight_products(left_t, d_conv, their_conv, partials[0])
+    scatter.step(0, 0)
+    swaps[1].wait_recv()
+    weight_products(left_t, d_attn, their_attn, partials[1])
+    scatter.step(1, 0)
+    step = 256
+    attn = d_attn.shape[1]
+
+    def back_out(j, carry):
+        here = pl.ds(pl.multiple_of(j * step, step), step)
+        d_normed[:, here] = (
+            dot_nt(d_conv[...], full_conv[here])
+            + dot_nt(d_attn[...], full_mix[here, :attn])
+            + dot_nt(d_z[...], full_mix[here, attn:])
+        )
+        return carry
+
+    lax.fori_loop(0, width // step, back_out, 0)
+    scatter.step(0, 1)
+    wide = x_own[...].astype(jnp.float32)
+    r = lax.rsqrt(jnp.mean(wide * wide, axis=-1, keepdims=True) + NORM_EPS)
+    grads = d_normed[...]
+    g_norm = jnp.sum(grads * wide * r, axis=0, keepdims=True)
+    line = lax.broadcasted_iota(jnp.int32, (8, width), 0)
+    both = jnp.where(line == 0, g_norm, jnp.where(line == 1, g_mlp[...], 0.0))
+    both = dot_nt_two(both, order[...])
+    small_own[16:] = small[...]
+    for k in range(width // TILE):
+        for which in range(2):
+            small_own[8 * which + k : 8 * which + k + 1] = both[
+                which : which + 1, k * TILE : (k + 1) * TILE
+            ]
+    names = ("core", "y", "x", "near", "far")
+    small_copies = []
+
+    def small_step(k):
+        if k > 0:
+            small_copies[k - 1].wait_recv()
+            was = small_own if k == 1 else small_mid.at[k - 2]
+            now = small_out if k == 5 else small_mid.at[k - 1]
+            now[...] = was[...] + small_in[k - 1]
+        if k < 5:
+            source = small_own if k == 0 else small_mid.at[k - 1]
             copy = remote(
-                source.at[pl.ds(first, rows), cols],
-                target.at[pl.ds(row, rows), cols],
-                send.at[2 * n + side, stage, k],
-                recv.at[2 * n + side, stage, k],
-                others[routes[side][stage]],
+                source, small_in.at[k], small_send.at[k], small_recv.at[k], others[names[k]]
             )
             copy.start()
-            copies.append(copy)
-            row += rows
-        started[n, side, stage] = copies
-
-    def take(n, side, stage):
-        p, column, width = pairs[n][side]
-        cols = slice(column, column + width)
-        source = ins[p] if stage == 0 else kept[3 * p + stage - 1]
-        target = outs[p] if stage == 3 else kept[3 * p + stage]
-        got = arrived[4 * p + stage]
-        row = 0
-        for k, (first, rows) in enumerate(pieces(side, stage)[1]):
-            started[n, side, stage][k].wait_recv()
-
-            def add(i, carry):
-                at = pl.multiple_of(i * 32, 32)
-                here = pl.ds(first + at, 32)
-                there = pl.ds(row + at, 32)
-                total = source[here, cols].astype(jnp.float32) + got[there, cols].astype(
-                    jnp.float32
-                )
-                target[there, cols] = total.astype(target.dtype)
-                return carry
-
-            lax.fori_loop(0, rows // 32, add, 0)
-            row += rows
-
-    names = ("core", "y", "x", "near", "far")
-    small_copies = []
-    for wave in range(max(len(pairs) + 5, 6)):
-        if wave <= 5:
-            if wave > 0:
-                small_copies[wave - 1].wait_recv()
-                was = small if wave == 1 else small_mid.at[wave - 2]
-                now = small_out if wave == 5 else small_mid.at[wave - 1]
-                now[...] = was[...] + small_in[wave - 1]
-            if wave < 5:
-                source = small if wave == 0 else small_mid.at[wave - 1]
-                copy = remote(
-                    source,
-                    small_in.at[wave],
-                    small_send.at[wave],
-                    small_recv.at[wave],
-                    others[names[wave]],
-                )
-                copy.start()
-                small_copies.append(copy)
-        for n in range(len(pairs)):
-            stage = wave - n
-            if stage < 0 or stage > 4:
-                continue
-            for side in range(2):
-                if stage > 0:
-                    take(n, side, stage - 1)
-                if stage < 4:
-                    begin(n, side, stage)
-    for copies in list(started.values()) + [small_copies]:
-        for copy in copies:
-            copy.wait_send()
-
-
-def weight_scatter(parts, small):
-    count = len(parts)
-    size = parts[0].shape[0]
+            small_copies.append(copy)
+
+    small_step(0)
+    scatter.step(1, 1)
+    inner = grads * gains[0:1]
+    coeff = jnp.mean(inner * wide, axis=-1, keepdims=True)
+    d_normed[...] = d_middle[...] + r * (inner - wide * (r * r * coeff))
+    small_step(1)
+    scatter.step(0, 2)
+
+    def plain(j, carry):
+        here = pl.ds(pl.multiple_of(j * step, step), step)
+        input_grad[:, here] = dot_nt_two(d_normed[...], order[here])
+        return carry
+
+    lax.fori_loop(0, width // step, plain, 0)
+    small_step(2)
+    scatter.step(1, 2)
+    scatter.step(0, 3)
+    small_step(3)
+    scatter.step(1, 3)
+    scatter.step(0, 4)
+    small_step(4)
+    scatter.step(1, 4)
+    small_step(5)
+    scatter.finish()
+    for copy in swaps + small_copies:
+        copy.wait_send()
+
+
+def last(d_conv, d_attn, d_z, full_conv, full_mix, normed, their_normed, x_own, d_middle, gains, order, g_mlp, small):
+    args = (
+        d_conv, d_attn, d_z, full_conv, full_mix, normed, their_normed, x_own, d_middle, gains,
+        order, g_mlp, small,
+    )
+    rows, width = normed.shape
+    half = width // 2
     f32, narrow = jnp.float32, jnp.bfloat16
     dma = pltpu.SemaphoreType.DMA
-    pairs = column_chunks([p.shape[1] for p in parts])
-    outs = [shape_of((size // 16, p.shape[1]), f32) for p in parts]
-    outs.append(shape_of(small.shape, f32))
-    scratch = []
-    for p in parts:
-        scratch += [pltpu.VMEM((size >> (s + 1), p.shape[1]), narrow) for s in range(4)]
-    for p in parts:
-        scratch += [pltpu.VMEM((size >> (s + 1), p.shape[1]), narrow) for s in range(3)]
+    widths = [d_conv.shape[1], d_attn.shape[1]]
+    pairs = column_chunks(widths)
+    total = (small.shape[0] + 16, TILE)
+    outs = [shape_of((rows, width), f32)]
+    outs += [shape_of((half // 16, w), f32) for w in widths]
+    outs.append(shape_of(total, f32))
+    scratch = [pltpu.VMEM((half, w), narrow) for w in widths]
+    scratch += scatter_scratch(widths, half)
     scratch += [
-        pltpu.VMEM((5, *small.shape), f32),
-        pltpu.VMEM((4, *small.shape), f32),
+        pltpu.VMEM(d_conv.shape, narrow),
+        pltpu.VMEM(d_attn.shape, narrow),
+        pltpu.VMEM((half, 2 * rows), narrow),
+        pltpu.VMEM((rows, width), f32),
+        pltpu.VMEM(total, f32),
+        pltpu.VMEM((5, *total), f32),
+        pltpu.VMEM((4, *total), f32),
+        dma((2,)),
+        dma((2,)),
         dma((2 * len(pairs), 4, 2)),
         dma((2 * len(pairs), 4, 2)),
         dma((5,)),
         dma((5,)),
     ]
-    result = comm_call(
-        lambda *refs: weight_scatter_kernel(count, pairs, *refs),
+    return comm_call(
+        lambda *refs: last_kernel(pairs, *refs),
         outs,
-        [INTO_VMEM] * (count + 1),
-        (*parts, small),
-        [INTO_VMEM] * (count + 1),
+        [INTO_VMEM] * len(outs),
+        args,
+        [INTO_VMEM] * len(args),
         scratch,
         4,
-        8 * sum(p.size for p in parts),
-        limit=60,
-    )
-    return result[:count], result[count]
+        100_000_000,
+    )
 
 
 def pair_heads(value, back=False):
@@ -1425,135 +1785,114 @@
     freqs = ROPE_BASE ** (-jnp.arange(half, dtype=jnp.float32) / half)
     angles = device_places.astype(jnp.float32)[:, None] * jnp.tile(freqs, TILE // half)[None, :]
     cosine, sine = jnp.cos(angles), jnp.sin(angles)
-    order = own_order(width, fast)
-    wide_order = order.astype(jnp.float32)
-
-    def to_own(value):
-        if not fast:
-            return value
-        return jnp.dot(value, order, preferred_element_type=jnp.float32).astype(value.dtype)
+    head_params = jnp.pad(
+        jnp.stack([dt_bias, jnp.exp(a_log), d_skip]), ((0, 5), (0, TILE - MH))
+    )
+    step_pad = jnp.pad(w_dt, ((0, 0), (0, TILE - MH)))
+    shards = (
+        jnp.concatenate([w_ssm_in[:, ssm_width:], step_pad], axis=1),
+        jnp.concatenate([pair_heads(w_attn), w_ssm_in[:, :ssm_width]], axis=1),
+        pair_heads(w_out.T),
+        w_gate_up,
+        w_down.T,
+    )
+    gains = jnp.pad(jnp.stack([norm_gain, mlp_gain]), ((0, 6), (0, 0)))
+    if fast:
+        full, made = front(
+            info,
+            layer_input[0],
+            out_grad[0],
+            gains,
+            cosine,
+            sine,
+            head_params,
+            jnp.pad(conv_w, ((0, 4), (0, 0))),
+            conv_b[None],
+            shards,
+        )
+        (
+            x_narrow, grad_rows, gains, normed, queries, all_pairs, gate_z, raw_rows, pre_conv,
+            inputs_x, inputs_bc, ssm_own, state_own, steps_dt, running_decay,
+            attended, attended_t, log_total, state_in, order,
+        ) = made
+        full_conv, full_mix, full_out, full_gu, full_down = full
+        norm_gain, mlp_gain = gains[0], gains[1]
+        x_rows = x_narrow.astype(jnp.float32)
+        scale_one = rms_scale(x_rows)
+    else:
+        order = None
+        ext_pos = first_pos - (CONV - 1) + jnp.arange(token_rows + CONV - 1, dtype=jnp.int32)
+        ext_segment = segments(seq_lens, ext_pos)[0]
+
+        def conv_local(ext_rows, conv_weight, conv_bias):
+            return conv_mix(ext_rows, ext_segment, conv_weight, conv_bias)
+
+        full = [lax.all_gather(p, ("seq", "batch"), axis=0, tiled=True) for p in shards]
+        full_conv, full_mix, full_out, full_gu, full_down = full
+        x_rows = layer_input[0].astype(jnp.float32)
+        grad_rows = out_grad[0]
+        scale_one = rms_scale(x_rows)
+        normed = (x_rows * scale_one * norm_gain).astype(jnp.bfloat16)
+        conv_proj = jnp.dot(normed, full_conv, preferred_element_type=jnp.float32)
+        mix_proj = jnp.dot(normed, full_mix, preferred_element_type=jnp.float32)
+        queries, own_pairs = big_call(
+            rope_kernel,
+            (
+                shape_of((token_rows, query_width), jnp.bfloat16),
+                shape_of((token_rows, 2 * key_value_width), jnp.bfloat16),
+            ),
+            mix_proj[:, :attn_width],
+            cosine,
+            sine,
+        )
+        gate_z = mix_proj[:, attn_width:]
+        raw_xbc = conv_proj[:, :xbc_width]
+        step_proj = conv_proj[:, xbc_width:]
+        rim_rows = shifted(raw_xbc[token_rows - (CONV - 1) :], "seq", 1)
+        extended = jnp.concatenate([rim_rows, raw_xbc], axis=0)
+        conv_out, conv_pullback = jax.vjp(conv_local, extended, conv_w, conv_b)
+        conv_narrow = conv_out.astype(jnp.bfloat16)
+        inputs_x, inputs_bc = conv_narrow[:, :ssm_width], conv_narrow[:, ssm_width:]
+        ssm_own, state_own, steps_dt, running_decay = ssm_forward(
+            info, inputs_x, inputs_bc, step_proj, head_params
+        )
+        all_pairs = lax.all_gather(own_pairs, "seq", axis=0, tiled=True)
+        state_in = scan_states(state_own, True)
+        attended, attended_t, log_total = attn_forward(info, queries, all_pairs)
 
     def to_plain(value):
         if not fast:
             return value
         return jnp.einsum("tc,dc->td", value, order, preferred_element_type=jnp.float32)
 
-    def to_plain_wide(value):
-        if not fast:
-            return value
-        return jnp.einsum("tc,dc->td", value, wide_order, precision=HIGHEST)
-
-    def gain_own(value):
-        if not fast:
-            return value
-        return jnp.dot(value, wide_order, precision=HIGHEST)
-
-    gains = gain_own(jnp.stack([norm_gain, mlp_gain]))
-    norm_gain, mlp_gain = gains[0], gains[1]
-    x_rows = to_own(layer_input[0]).astype(jnp.float32)
-    grad_rows = to_own(out_grad[0])
-    head_params = jnp.pad(
-        jnp.stack([dt_bias, jnp.exp(a_log), d_skip]), ((0, 5), (0, TILE - MH))
-    )
-    step_pad = jnp.pad(w_dt, ((0, 0), (0, TILE - MH)))
-    out_shard = pair_heads(w_out.T)
-    down_shard = w_down.T
-    shards = (
-        jnp.concatenate([w_ssm_in[:, ssm_width:], step_pad], axis=1),
-        jnp.concatenate([pair_heads(w_attn), w_ssm_in[:, :ssm_width]], axis=1),
-        out_shard[:, : w_out.shape[0] // 2],
-        out_shard[:, w_out.shape[0] // 2 :],
-        w_gate_up[:, :FF],
-        w_gate_up[:, FF:],
-        down_shard[:, : FF // 2],
-        down_shard[:, FF // 2 :],
-    )
-    if fast:
-        full = weight_gather(shards)
-    else:
-        full = [lax.all_gather(p, ("seq", "batch"), axis=0, tiled=True) for p in shards]
-    full_conv, full_mix, out_a, out_b, full_gate, full_up, down_a, down_b = full
-    scale_one = rms_scale(x_rows)
-    normed = (x_rows * scale_one * norm_gain).astype(jnp.bfloat16)
-    conv_proj = jnp.dot(normed, full_conv, preferred_element_type=jnp.float32)
-    mix_proj = jnp.dot(normed, full_mix, preferred_element_type=jnp.float32)
-    queries, own_pairs = big_call(
-        rope_kernel,
-        (
-            shape_of((token_rows, query_width), jnp.bfloat16),
-            shape_of((token_rows, 2 * key_value_width), jnp.bfloat16),
-        ),
-        mix_proj[:, :attn_width],
-        cosine,
-        sine,
-    )
-    gate_z = mix_proj[:, attn_width:]
-    raw_xbc = conv_proj[:, :xbc_width]
-    step_proj = conv_proj[:, xbc_width:]
-    rim_rows = shifted(raw_xbc[token_rows - (CONV - 1) :], "seq", 1)
-    extended = jnp.concatenate([rim_rows, raw_xbc], axis=0)
-    ext_pos = first_pos - (CONV - 1) + jnp.arange(token_rows + CONV - 1, dtype=jnp.int32)
-    ext_segment = segments(seq_lens, ext_pos)[0]
-
-    def conv_local(ext_rows, conv_weight, conv_bias):
-        return conv_mix(ext_rows, ext_segment, conv_weight, conv_bias)
-
-    conv_out, conv_pullback = jax.vjp(conv_local, extended, conv_w, conv_b)
-    conv_narrow = conv_out.astype(jnp.bfloat16)
-    inputs_x, inputs_bc = conv_narrow[:, :ssm_width], conv_narrow[:, ssm_width:]
-    ssm_local, state_own, steps_dt, running_decay = ssm_forward(
-        info, inputs_x, inputs_bc, step_proj, head_params
-    )
-    if fast:
-        attended, attended_t, log_total, all_pairs, state_in = mixer_forward(
-            info, queries, own_pairs, state_own
-        )
-    else:
-        all_pairs = lax.all_gather(own_pairs, "seq", axis=0, tiled=True)
-        state_in = scan_states(state_own, True)
-        attended, attended_t, log_total = attn_forward(info, queries, all_pairs)
     ssm_flat, ssm_normed, scale_gated = ssm_finish(
-        info, ssm_local, inputs_bc, running_decay, state_in, gate_z, ssm_gain[None]
+        info, ssm_own, inputs_bc, running_decay, state_in, gate_z, ssm_gain[None]
     )
     joined = jnp.concatenate([attended, ssm_normed], axis=1)
-    half_in = joined.shape[1] // 2
-
-    def narrow_out(left, parts):
-        cut = left.shape[1] // 2
-        return jnp.einsum(
-            "tc,dc->td", left[:, :cut], parts[0], preferred_element_type=jnp.float32
-        ) + jnp.einsum("tc,dc->td", left[:, cut:], parts[1], preferred_element_type=jnp.float32)
-
-    middle = x_rows + narrow_out(joined, (out_a, out_b))
+
+    def into_width(left, weight):
+        return jnp.einsum("tc,dc->td", left, weight, preferred_element_type=jnp.float32)
+
+    def out_of_width(left, weight):
+        return jnp.dot(left, weight, preferred_element_type=jnp.float32)
+
+    middle = x_rows + into_width(joined, full_out)
     scale_two = rms_scale(middle)
     normed_two = (middle * scale_two * mlp_gain).astype(jnp.bfloat16)
-    gate_part = jnp.dot(normed_two, full_gate, preferred_element_type=jnp.float32)
-    up_part = jnp.dot(normed_two, full_up, preferred_element_type=jnp.float32)
-    hidden = (jax.nn.silu(gate_part) * up_part).astype(jnp.bfloat16)
-    layer_out = middle + narrow_out(hidden, (down_a, down_b))
-    d_hidden = jnp.concatenate(
-        [
-            jnp.dot(grad_rows, down_a, preferred_element_type=jnp.float32),
-            jnp.dot(grad_rows, down_b, preferred_element_type=jnp.float32),
-        ],
-        axis=1,
-    )
+    gate_up = out_of_width(normed_two, full_gu)
+    gate_part, up_part = gate_up[:, :FF], gate_up[:, FF:]
     sig_gate = jax.nn.sigmoid(gate_part)
-    d_gate = (d_hidden * up_part * (sig_gate * (1.0 + gate_part * (1.0 - sig_gate)))).astype(
-        jnp.bfloat16
-    )
-    d_up = (d_hidden * gate_part * sig_gate).astype(jnp.bfloat16)
-    d_normed_two = narrow_out(jnp.concatenate([d_gate, d_up], axis=1), (full_gate, full_up))
+    hidden = (gate_part * sig_gate * up_part).astype(jnp.bfloat16)
+    layer_out = middle + into_width(hidden, full_down)
+    d_hidden = out_of_width(grad_rows, full_down)
+    d_gate = d_hidden * up_part * (sig_gate * (1.0 + gate_part * (1.0 - sig_gate)))
+    d_up = d_hidden * gate_part * sig_gate
+    d_gate_up = jnp.concatenate([d_gate, d_up], axis=1).astype(jnp.bfloat16)
+    d_normed_two = into_width(d_gate_up, full_gu)
     d_middle_norm, g_mlp_gain = norm_back(middle, scale_two, mlp_gain, d_normed_two)
     d_middle = grad_rows.astype(jnp.float32) + d_middle_norm
     d_mixer = d_middle.astype(jnp.bfloat16)
-    d_joined = jnp.concatenate(
-        [
-            jnp.dot(d_mixer, out_a, preferred_element_type=jnp.float32),
-            jnp.dot(d_mixer, out_b, preferred_element_type=jnp.float32),
-        ],
-        axis=1,
-    )
+    d_joined = out_of_width(d_mixer, full_out)
     attended_gradient = d_joined[:, :query_width].astype(jnp.bfloat16)
     d_ssm_out, d_gate_z, pull, g_ssm_gain = gate_back(
         info,
@@ -1566,22 +1905,64 @@
         inputs_bc,
     )
     pull = jnp.concatenate([pull, state_own[NS:]], axis=0)
-    lefts = [normed, normed_two, d_mixer, grad_rows]
-    rights = [hidden, joined, d_gate, d_up]
     if fast:
-        cut = width // 2
-        d_queries, own_d_pairs, d_state, theirs = mixer_backward(
+        (
+            d_conv_proj, d_attn_proj, g_conv, head_sums, g_skip_rows, their_normed,
+            sum_down, sum_gu, sum_out, sum_z,
+        ) = back(
             info,
+            head_params,
+            jnp.pad(conv_w, ((0, 4), (0, 0))),
+            cosine,
+            sine,
             queries,
             all_pairs,
             attended_gradient,
             attended_t,
             log_total,
             pull,
-            [a[:, cut:] for a in lefts] + rights,
-        )
-        lefts = [jnp.concatenate([a[:, :cut], b], axis=0) for a, b in zip(lefts, theirs)]
-        rights = [jnp.concatenate([a, b], axis=0) for a, b in zip(rights, theirs[4:])]
+            inputs_x,
+            inputs_bc,
+            steps_dt,
+            running_decay,
+            d_ssm_out,
+            raw_rows,
+            state_in,
+            pre_conv,
+            normed,
+            normed_two,
+            d_mixer,
+            grad_rows,
+            hidden,
+            joined,
+            d_gate_up,
+            d_gate_z,
+        )
+        small = (
+            g_ssm_gain[0],
+            g_conv[:CONV],
+            g_conv[CONV],
+            head_sums[0, :MH],
+            head_sums[1, :MH],
+            g_skip_rows[0, :MH],
+        )
+        input_grad, sum_conv, sum_attn, totals = last(
+            d_conv_proj,
+            d_attn_proj,
+            d_gate_z,
+            full_conv,
+            full_mix,
+            normed,
+            their_normed,
+            x_narrow,
+            d_middle,
+            gains,
+            order,
+            g_mlp_gain[None],
+            pack_small(small),
+        )
+        small_sums = [totals[:8].reshape(-1), totals[8:16].reshape(-1)]
+        small_sums += unpack_small(totals[16:], small)
     else:
         d_state = scan_states(pull, False)
         d_queries, d_pairs = attn_backward(
@@ -1590,96 +1971,75 @@
         own_d_pairs = lax.psum_scatter(
             d_pairs.astype(jnp.float32), "seq", scatter_dimension=0, tiled=True
         )
-    dx_part, d_bc_part, d_cum_part, d_dt_part, g_skip_rows = ssm_back(
-        info, inputs_x, inputs_bc, steps_dt, running_decay, d_ssm_out, head_params
-    )
-    g_inputs_x, g_inputs_bc, d_step_pad, head_sums = state_back(
-        info,
-        inputs_x,
-        inputs_bc,
-        steps_dt,
-        running_decay,
-        d_ssm_out,
-        head_params,
-        step_proj,
-        state_in,
-        d_state,
-        dx_part,
-        d_bc_part,
-        d_cum_part,
-        d_dt_part,
-    )
-    g_a_log, g_dt_bias, g_d_skip = head_sums[0, :MH], head_sums[1, :MH], g_skip_rows[0, :MH]
-    d_conv_out = jnp.concatenate([g_inputs_x, g_inputs_bc], axis=1)
-    g_extended, g_conv_w, g_conv_b = conv_pullback(d_conv_out)
-    back_rim = shifted(g_extended[: CONV - 1], "seq", -1)
-    d_raw = g_extended[CONV - 1 :] + jnp.concatenate(
-        [jnp.zeros((token_rows - (CONV - 1), xbc_width), jnp.float32), back_rim], axis=0
-    )
-    d_conv_proj = jnp.concatenate([d_raw.astype(jnp.bfloat16), d_step_pad], axis=1)
-    (d_attn_proj,) = big_call(
-        rope_back_kernel,
-        (shape_of((token_rows, attn_width), jnp.bfloat16),),
-        d_queries,
-        own_d_pairs,
-        cosine,
-        sine,
-    )
-    d_mix_proj = jnp.concatenate([d_attn_proj, d_gate_z], axis=1)
-    d_normed = jnp.einsum(
-        "tc,dc->td", d_conv_proj, full_conv, preferred_element_type=jnp.float32
-    ) + jnp.einsum("tc,dc->td", d_mix_proj, full_mix, preferred_element_type=jnp.float32)
-    d_input_norm, g_norm_gain = norm_back(x_rows, scale_one, norm_gain, d_normed)
-    input_grad = d_middle + d_input_norm
-    last = [d_conv_proj, d_mix_proj]
-    if fast:
-        last = [jnp.concatenate([a, b], axis=0) for a, b in zip(last, core_swap(last))]
-
-    def partial(left, right):
-        grad = jnp.einsum("td,tc->dc", left, right, preferred_element_type=jnp.float32)
-        return grad.astype(jnp.bfloat16) if fast else grad
-
-    all_normed, all_normed_two, all_d_mixer, all_grad = lefts
-    all_hidden, all_joined, all_d_gate, all_d_up = rights
-    half_ff = FF // 2
-    partials = [
-        partial(all_grad, all_hidden[:, :half_ff]),
-        partial(all_grad, all_hidden[:, half_ff:]),
-        partial(all_normed_two, all_d_gate),
-        partial(all_normed_two, all_d_up),
-        partial(all_d_mixer, all_joined[:, :half_in]),
-        partial(all_d_mixer, all_joined[:, half_in:]),
-        partial(all_normed, last[0]),
-        partial(all_normed, last[1]),
-    ]
-    gain_grads = to_plain_wide(jnp.stack([g_norm_gain, g_mlp_gain]))
-    small = (
-        gain_grads[0],
-        gain_grads[1],
-        g_ssm_gain[0],
-        g_conv_w,
-        g_conv_b,
-        g_a_log,
-        g_dt_bias,
-        g_d_skip,
-    )
-    if fast:
-        sums, small_total = weight_scatter(partials, pack_small(small))
-    else:
+        dx_part, d_bc_part, d_cum_part, d_dt_part, g_skip_rows = ssm_back(
+            info, inputs_x, inputs_bc, steps_dt, running_decay, d_ssm_out, head_params
+        )
+        g_inputs_x, g_inputs_bc, d_step_pad, head_sums = state_back(
+            info,
+            inputs_x,
+            inputs_bc,
+            steps_dt,
+            running_decay,
+            d_ssm_out,
+            head_params,
+            step_proj,
+            state_in,
+            d_state,
+            dx_part,
+            d_bc_part,
+            d_cum_part,
+            d_dt_part,
+        )
+        g_extended, g_conv_w, g_conv_b = conv_pullback(
+            jnp.concatenate([g_inputs_x, g_inputs_bc], axis=1)
+        )
+        back_rim = shifted(g_extended[: CONV - 1], "seq", -1)
+        d_raw = g_extended[CONV - 1 :] + jnp.concatenate(
+            [jnp.zeros((token_rows - (CONV - 1), xbc_width), jnp.float32), back_rim], axis=0
+        )
+        d_conv_proj = jnp.concatenate([d_raw.astype(jnp.bfloat16), d_step_pad], axis=1)
+        (d_attn_proj,) = big_call(
+            rope_back_kernel,
+            (shape_of((token_rows, attn_width), jnp.bfloat16),),
+            d_queries,
+            own_d_pairs,
+            cosine,
+            sine,
+        )
+        d_mix_proj = jnp.concatenate([d_attn_proj, d_gate_z], axis=1)
+        d_normed = into_width(d_conv_proj, full_conv) + into_width(d_mix_proj, full_mix)
+        d_input_norm, g_norm_gain = norm_back(x_rows, scale_one, norm_gain, d_normed)
+        input_grad = d_middle + d_input_norm
         axes = ("seq", "batch")
-        sums = [lax.psum_scatter(g, axes, scatter_dimension=0, tiled=True) for g in partials]
-        small_total = lax.psum(pack_small(small), axes)
-    small_sums = unpack_small(small_total, small)
-    g_conv_in, g_mix_in = sums[6], sums[7]
-    grad_attn = pair_heads(g_mix_in[:, :attn_width], True)
-    grad_ssm_in = jnp.concatenate([g_mix_in[:, attn_width:], g_conv_in[:, :xbc_width]], axis=1)
-    grad_dt = g_conv_in[:, xbc_width : xbc_width + MH]
-    grad_out = pair_heads(jnp.concatenate(sums[4:6], axis=1), True).T
-    grad_gate_up = jnp.concatenate(sums[2:4], axis=1)
-    grad_down = jnp.concatenate(sums[:2], axis=1).T
+
+        def summed(left, right):
+            grad = jnp.einsum("td,tc->dc", left, right, preferred_element_type=jnp.float32)
+            return lax.psum_scatter(grad, axes, scatter_dimension=0, tiled=True)
+
+        sum_down, sum_gu = summed(grad_rows, hidden), summed(normed_two, d_gate_up)
+        sum_out, sum_conv = summed(d_mixer, joined), summed(normed, d_conv_proj)
+        sum_mix = summed(normed, d_mix_proj)
+        sum_attn, sum_z = sum_mix[:, :attn_width], sum_mix[:, attn_width:]
+        small = (
+            g_norm_gain,
+            g_mlp_gain,
+            g_ssm_gain[0],
+            g_conv_w,
+            g_conv_b,
+            head_sums[0, :MH],
+            head_sums[1, :MH],
+            g_skip_rows[0, :MH],
+        )
+        small_sums = unpack_small(lax.psum(pack_small(small), axes), small)
+    grad_attn = pair_heads(sum_attn, True)
+    grad_ssm_in = jnp.concatenate([sum_z, sum_conv[:, :xbc_width]], axis=1)
+    grad_dt = sum_conv[:, xbc_width : xbc_width + MH]
+    grad_out = pair_heads(sum_out, True).T
+    grad_gate_up = sum_gu
+    grad_down = sum_down.T
     return (
         to_plain(layer_out.astype(jnp.bfloat16)).astype(jnp.bfloat16)[None],
-        to_plain_wide(input_grad)[None],
+        input_grad[None],
         grad_attn,
         grad_ssm_in,
         grad_dt,

time: 588 us -> 464 us (0.79)
  Pallas kernels: 434 us -> 375 us
  matrix products: 77.7 us -> 24.9 us
  other arithmetic: 24.9 us -> 16 us
    dot_general x28 -> x5, matrix products: 73.1 us -> 19 us  [the longest x2 11.8 us: into_width(): jnp.einsum('tc,dc->td', left, weight, preferred_element_type=jnp.float32)]
    pallas_call x5 -> x3, Pallas kernels: 406 us -> 368 us  [comm_call(): pl.pallas_call(kernel, out_shape=list(outs), in_specs=in_specs, out_specs...]
    pallas_call x7 -> x2, Pallas kernels: 28 us -> 6.64 us  [big_call(): pl.pallas_call(kernel, out_shape=list(outs), in_specs=specs, out_specs=[p...]
    slice x18 -> x5, local copies, waits for them, and re-layouts: 9.9 us -> 3.56 us  [the longest x1 1.04 us: on_device(): grad_ssm_in = jnp.concatenate([sum_z, sum_conv[:, :xbc_width]], axis=1)]
    unnamed x142 -> x58, local copies, waits for them, and re-layouts: 9.33 us -> 13.8 us
  transfers between devices with their start and end apart: 2 -> 0, of which waited for: 0 -> 0; matrix products, arithmetic and copies ran while one was open for 6% -> 0% of each run, Pallas kernels for 0% -> 0%
where the time goes in v4:
time: 464 us; the launch traced here: 457 us
  Pallas kernels  375 us (81%)
  local copies, waits for them, and re-layouts  39.4 us (8%)
  matrix products  24.9 us (5%)
  other arithmetic  16 us (3%)
    pallas_call x3, Pallas kernels, comm_call(): pl.pallas_call(kernel, out_shape=list(outs), in_specs=in_specs, out_specs...  368 us
    unnamed x58, local copies, waits for them, and re-layouts  13.8 us
    dot_general x2, matrix products, into_width(): jnp.einsum('tc,dc->td', left, weight, preferred_element_type=jnp.float32)  11.8 us

profile of v4, /device:TPU:0, one launch (start us, length us, event | category | flops | bytes accessed | tf_op | source)
XLA Modules:
  0.0 456.7 jit_solution(6387365305050129076)
XLA Ops:
  0.7 0.9 reduce-window.4
  1.5 0.7 exponential_bitcast_fusion
  2.2 0.7 select_reduce_fusion
  3.6 2.5 pad_add_fusion.refs_0_.info
  6.2 1.3 select_maximum_fusion.1.refs_6_.refs_1_
  7.4 0.7 broadcast_in_dim.39.gain
  8.1 1.3 broadcast_in_dim.38.refs_8_
  9.4 0.8 copy.39
  10.2 0.7 slice.133
  10.9 0.8 slice.165
  12.0 1.3 select_maximum_fusion.refs_3_
  13.3 0.8 slice.132
  14.3 1.4 pad.23.refs_7_.refs_2_
  15.7 0.9 slice.166
  16.6 0.7 pad_maximum_fusion.4.refs_11_
  17.3 0.9 slice.134
  18.2 0.7 pad_maximum_fusion.3.refs_10_
  18.9 0.7 fusion.3.refs_9_
  19.5 1.2 multiply_sine_fusion
  20.8 180.0 %shard_map.288 = (bf16[1024,1920]{1,0:T(8,128)(2,1)}, bf16[1024,2304]{1,0:T(8,128)(2,1)}, bf16[1024,2048]{1,0:T(8,128)(2,1)}, bf16[1024,4096]{1,0:T(8,128)(2,1)}...) custom-call(s32[4]{0:T(128)} %pad_add_fusion.refs_0_.info, ...), custom_call_target="tpu_custom_call" | custom-call | bytes 200000000 | tf_op jit(solution)/shard_map/pallas_call | solution.py:793
  200.8 0.8 slice.137
  201.5 0.8 slice.142
  202.3 1.0 constant_dynamic-update-slice_fusion.1
  203.3 1.4 copy-done.2
  204.7 1.0 copy-done.4
  205.7 0.9 copy-done.5
  206.6 0.9 copy-done.7
  207.5 2.7 shard_map.289
  210.4 4.4 multiply_reduce_fusion.2
  215.1 0.8 copy-done.23
  215.9 2.3 fusion.8
  218.4 3.4 multiply_convert_fusion.1
  221.9 5.9 %fusion.1 = bf16[1,256,1024]{2,1,0:T(8,128)(2,1)} fusion(bf16[1024,1024]{1,0:T(8,128)(2,1)} %get-tuple-element.74.refs_10_, f32[256,1024]{1,0:T(8,128)S(1)} %get-tuple-element.160, bf16[256,2048]{1,0:T(8,128)(2,1)S(1)} %get-tuple-element.146.refs_23_, bf16[1024,2048]{1,0:T(8,128)(2,1)} %get-tuple-element.73), kind=kOutput, calls=%fused_computation.9 | convolution fusion | flops 1611399168 | bytes 8912896 | tf_op jit(solution)/shard_map/tc,dc->td/dot_general | solution.py:1866
  227.7 7.3 %multiply_reduce_fusion = (f32[1024]{0:T(1024)}, f32[256]{0:T(256)S(1)}, f32[256,1024]{1,0:T(8,128)S(1)}) fusion(f32[256,1024]{1,0:T(8,128)S(1)} %get-tuple-element.160, f32[256]{0:T(256)S(1)} %add_rsqrt_fusion, f32[1024]{0:T(1024)S(1)} %bitcast.75, bf16[1024,4096]{1,0:T(8,128)(2,1)} %get-tuple-element.72, bf16[256,2048]{1,0:T(8,128)(2,1)} %get-tuple-element.145, ...), kind=kOutput, calls=%fused_computation.10 | convolution fusion | flops 2153249536 | bytes 12593152 | tf_op jit(solution)/shard_map/tc,dc->td/dot_general | solution.py:1874
  235.1 1.5 pad_maximum_fusion.refs_25_
  236.6 1.3 fusion.5
  238.0 1.4 copy-done.24
  239.4 1.5 fusion.9
  240.9 0.7 slice.189.refs_7_
  241.9 3.9 shard_map.290
  245.8 0.9 copy-done
  246.7 1.1 copy-done.1
  247.9 0.8 pad_maximum_fusion.1.refs_10_
  248.7 131.4 %shard_map.291 = (bf16[256,1920]{1,0:T(8,128)(2,1)}, bf16[256,768]{1,0:T(8,128)(2,1)}, f32[8,1792]{1,0:T(8,128)}, f32[8,128]{1,0:T(8,128)}, f32[8,128]{1,0:T(8,1...) custom-call(s32[4]{0:T(128)} %pad_add_fusion.refs_0_.info, ...), custom_call_target="tpu_custom_call" | custom-call | bytes 200000000 | tf_op jit(solution)/shard_map/pallas_call | solution.py:793
  380.1 0.8 slice_bitcast_fusion.6
  380.9 0.8 slice_reduce_fusion
  381.7 0.8 slice.143
  383.3 56.9 %shard_map.292 = (f32[256,1024]{1,0:T(8,128)}, f32[32,1920]{1,0:T(8,128)}, f32[32,768]{1,0:T(8,128)}, f32[104,128]{1,0:T(8,128)}) custom-call(bf16[256,1920]{1,0:T(8,128)(2,1)} %get-tuple-element.91.refs_0_, bf16[256,768]{1,0:T(8,128)(2,1)} %get-tuple-element.92.refs_1_, bf16[256,1536]{1,0:T(8,128)(2,1)} %copy-done, ...), custom_call_target="tpu_custom_call" | custom-call | bytes 100000000 | tf_op jit(solution)/shard_map/pallas_call | solution.py:793
  440.2 1.4 slice_bitcast_fusion.1
  441.6 1.3 slice_bitcast_fusion.2
  442.9 1.3 slice_bitcast_fusion.3
  444.2 0.7 slice.151
  444.9 1.0 slice.150
  445.9 0.7 copy.44
  446.6 0.8 pad_maximum_fusion.2
  447.4 0.8 slice.158
  448.2 0.8 slice_bitcast_fusion
  450.2 0.8 slice.149
  450.9 0.8 slice.148
  452.1 0.6 pad_maximum_fusion.5
  453.1 0.7 maximum_bitcast_fusion
  453.8 1.0 copy.53
  454.8 0.8 copy.54
  455.6 0.7 copy.55
  (77 shorter events, 4.6 us)
Async XLA Ops:
  0.6 18.2 %slice-start = ((bf16[32,3328]{1,0:T(8,128)(2,1)}), bf16[32,1792]{1,0:T(8,128)(2,1)S(1)}, s32[]{:S(2)}) async-start(bf16[32,3328]{1,0:T(8,128)(2,1)} %param.20), calls=%async_computation | async-start | bytes 229376 | tf_op jit(solution)/shard_map/slice | solution.py:1793
  17.3 186.0 %copy-start.9 = (s32[4]{0:T(128)S(1)}, s32[4]{0:T(128)}, u32[]{:S(2)}) copy-start(s32[4]{0:T(128)} %pad_add_fusion.refs_0_.info) | copy-start | bytes 52
  203.3 1.4 copy-start.2
  204.7 1.0 copy-start.4
  205.7 0.9 copy-start.5
  206.6 0.9 copy-start.7
  207.5 2.9 copy-start.18
  210.3 4.6 %copy-start.3 = (f32[256,1536]{1,0:T(8,128)}, f32[256,1536]{1,0:T(8,128)S(1)}, u32[]{:S(2)}) copy-start(f32[256,1536]{1,0:T(8,128)S(1)} %get-tuple-element.80.ssm_out) | copy-start | bytes 4718596
  210.4 4.5 copy-start.13
  210.4 5.5 %copy-start.23 = (bf16[1024,4096]{1,0:T(8,128)(2,1)S(1)}, bf16[1024,4096]{1,0:T(8,128)(2,1)}, u32[]{:S(2)}) copy-start(bf16[1024,4096]{1,0:T(8,128)(2,1)} %get-tuple-element.72) | copy-start | bytes 25165828
  215.9 2.4 copy-start.12
  215.9 2.4 copy-start.10
  215.9 2.5 copy-start.25
  221.9 5.9 %copy-start.14 = (bf16[256,2048]{1,0:T(8,128)(2,1)}, bf16[256,2048]{1,0:T(8,128)(2,1)S(1)}, u32[]{:S(2)}) copy-start(bf16[256,2048]{1,0:T(8,128)(2,1)S(1)} %get-tuple-element.146.refs_23_) | copy-start | bytes 3145732
  227.7 7.3 %copy-start.16 = (bf16[256,2048]{1,0:T(8,128)(2,1)S(1)}, bf16[256,2048]{1,0:T(8,128)(2,1)}, u32[]{:S(2)}) copy-start(bf16[256,2048]{1,0:T(8,128)(2,1)} %get-tuple-element.144) | copy-start | bytes 3145732
  227.7 7.3 %copy-start.17 = (bf16[256,2048]{1,0:T(8,128)(2,1)S(1)}, bf16[256,2048]{1,0:T(8,128)(2,1)}, u32[]{:S(2)}) copy-start(bf16[256,2048]{1,0:T(8,128)(2,1)} %get-tuple-element.145) | copy-start | bytes 3145732
  236.6 2.8 copy-start.24
  238.0 2.9 copy-start.11
  240.9 0.9 copy-start.6
  240.9 1.1 copy-start.8
  245.8 0.9 copy-start
  246.7 1.1 copy-start.1
  383.3 63.3 %copy-start.22 = (f32[32,1536]{1,0:T(8,128)S(1)}, f32[32,1536]{1,0:T(8,128)}, u32[]{:S(2)}) copy-start(f32[32,1536]{1,0:T(8,128)} %get-tuple-element.102) | copy-start | bytes 589828
  440.2 12.5 %copy-start.20 = (f32[32,2048]{1,0:T(8,128)S(1)}, f32[32,2048]{1,0:T(8,128)}, u32[]{:S(2)}) copy-start(f32[32,2048]{1,0:T(8,128)} %get-tuple-element.104) | copy-start | bytes 786436
  444.9 8.9 %copy-start.15 = (f32[256,1024]{1,0:T(8,128)S(1)}, f32[256,1024]{1,0:T(8,128)}, u32[]{:S(2)}) copy-start(f32[256,1024]{1,0:T(8,128)} %get-tuple-element.100) | copy-start | bytes 3145732
  451.9 2.8 copy-start.19
  452.9 2.7 copy-start.21

commit v5 on v4

--- a/solution.py
+++ b/solution.py
@@ -1,5 +1,6 @@
 import jax
 import jax.numpy as jnp
+import numpy as np
 from jax import lax
 from jax.experimental import pallas as pl
 from jax.experimental.pallas import tpu as pltpu
@@ -479,7 +480,7 @@
         cols = slice(i * TILE, (i + 1) * TILE)
         gate = z[:, cols]
         gated = ssm_out[:, cols] * (gate * jax.nn.sigmoid(gate))
-        normed[:, cols] = (gated * r * gain[:, cols]).astype(jnp.bfloat16)
+        normed[:, cols] = (gated * r * gain[i : i + 1]).astype(jnp.bfloat16)
 
 
 def ssm_finish(info, y, bc, cum, state_in, z, gain):
@@ -515,8 +516,8 @@
         gate = z[:, cols]
         gated = ssm_out[:, cols] * (gate * jax.nn.sigmoid(gate))
         product = dy[:, cols] * gated
-        g_gain[:, cols] = jnp.sum(product * r, axis=0, keepdims=True)
-        inner = inner + product * gain[:, cols]
+        g_gain[i : i + 1] = jnp.sum(product * r, axis=0, keepdims=True)
+        inner = inner + product * gain[i : i + 1]
     coeff = jnp.sum(inner, axis=1, keepdims=True) * (1.0 / (tiles * TILE))
     for i in range(tiles):
         cols = slice(i * TILE, (i + 1) * TILE)
@@ -524,7 +525,7 @@
         sig = jax.nn.sigmoid(gate)
         silu = gate * sig
         out = ssm_out[:, cols]
-        d_gated = r * (dy[:, cols] * gain[:, cols] - out * silu * (r * r * coeff))
+        d_gated = r * (dy[:, cols] * gain[i : i + 1] - out * silu * (r * r * coeff))
         d_ssm = d_gated * silu
         d_out[:, cols] = d_ssm
         d_z[:, cols] = (d_gated * out * (sig * (1.0 + gate * (1.0 - sig)))).astype(jnp.bfloat16)
@@ -541,7 +542,7 @@
             shape_of((rows, width), jnp.float32),
             shape_of((rows, width), jnp.bfloat16),
             shape_of((NS, width), jnp.bfloat16),
-            shape_of((1, width), jnp.float32),
+            shape_of(gain.shape, jnp.float32),
         ),
         info,
         dy,
@@ -556,7 +557,7 @@
     )
 
 
-def ssm_back_kernel(info, x, bc, dt, cum, grad, head_params, dx, d_bc, d_cum, d_dt, g_skip, cols_t, d_rows):
+def ssm_back_kernel(info, x, bc, dt, cum, grad, head_params, dx, d_bc, d_cum, d_dt, g_skip, cols_t, d_rows, between=None):
     rows, width = x.shape
     skip = head_params[2:3]
     cols_t[...] = cum[...].T
@@ -605,6 +606,8 @@
             dx[here, cols] = (
                 jnp.where(lane < MP, sides[0], sides[1]) + skip_row[:, cols] * wide[here]
             )
+        if between is not None:
+            between(i)
     all_steps = jnp.concatenate(step_sums, axis=0)
     d_dt[...] = all_steps
     d_cum[...] = d_rows[...].T - all_steps * dt[...]
@@ -803,26 +806,57 @@
     )(*args)
 
 
-def column_chunks(widths):
+def column_chunks(widths, aim=512):
     pairs = []
     for p, width in enumerate(widths):
         tiles, first, cuts = width // TILE, 0, []
-        pieces = 2 * max(1, width // 2048)
+        pieces = 2 * max(1, (width + aim // 2) // (2 * aim))
         for i in range(pieces):
             cols = (tiles // pieces + (1 if i < tiles % pieces else 0)) * TILE
-            cuts.append((p, first, cols))
+            cuts.append((p, first, cols, ("xy", "yx")[i % 2]))
             first += cols
         pairs += [tuple(cuts[i : i + 2]) for i in range(0, pieces, 2)]
     return pairs
 
 
-def gather_plan(x_first):
-    plan = [("far", [(0, 1, 1)]), ("near", [(0, 2, 2)])]
-    if x_first:
-        plan += [("x", [(0, 4, 4)]), ("y", [(0, 8, 8)])]
-    else:
-        plan += [("y", [(0, 4, 8)]), ("x", [(0, 4, 4), (8, 4, 12)])]
-    return plan + [("core", [(0, 16, 16)])]
+def pairs_of(pairs, array):
+    return [n for n, (one, other) in enumerate(pairs) if one[0] == array]
+
+
+BITS = {"far": 1, "near": 2, "x": 4, "y": 8, "core": 16}
+ORDERS = {
+    "xy": ("far", "near", "x", "y"),
+    "yx": ("far", "near", "y", "x"),
+}
+
+
+def runs(places):
+    out = []
+    for place in places:
+        if out and out[-1][0] + out[-1][1] == place:
+            out[-1] = (out[-1][0], out[-1][1] + 1)
+        else:
+            out.append((place, 1))
+    return out
+
+
+def gather_plan(order):
+    held, plan = [0], []
+    for name in ORDERS[order] + ("core",):
+        plan.append((name, [(f, k, f + BITS[name]) for f, k in runs(held)]))
+        held = sorted(held + [block + BITS[name] for block in held])
+    return plan
+
+
+def scatter_plan(order):
+    held, plan = list(range(16)), []
+    for name in reversed(ORDERS[order]):
+        bit = BITS[name]
+        sent = [i for i, block in enumerate(held) if block & bit]
+        kept = [i for i, block in enumerate(held) if not block & bit]
+        plan.append((name, runs(sent), runs(kept)))
+        held = [held[i] for i in kept]
+    return plan
 
 
 def bit_apart(r):
@@ -848,65 +882,78 @@
     target[NS:] = tail.astype(jnp.bfloat16)
 
 
+SCAN_PARTS = 2
+
+
 class StateScan:
     def __init__(self, forward, own, result, arrived, sent, before, send, recv, others):
         me = lax.axis_index("seq")
         self.seconds = []
         for bit in (me % 2, me // 2 % 2, me // 4):
             self.seconds.append(bit == 1 if forward else bit == 0)
-        self.own, self.result, self.arrived, self.sent, self.before = (
-            own, result, arrived, sent, before,
-        )
         route = (others["x"], others["near"], others["far"])
-        sources = (own, sent.at[0], sent.at[1])
-        self.copies = [
-            remote(sources[k], arrived.at[k], send.at[k], recv.at[k], route[k]) for k in range(3)
-        ]
+        width = own.shape[1] // SCAN_PARTS
+        self.parts = []
+        for part in range(SCAN_PARTS):
+            cols = pl.ds(part * width, width)
+            here = (slice(None), cols)
+            sources = (own.at[here], sent.at[0].at[here], sent.at[1].at[here])
+            targets = [arrived.at[k].at[here] for k in range(3)]
+            copies = [
+                remote(sources[k], targets[k], send.at[k, part], recv.at[k, part], route[k])
+                for k in range(3)
+            ]
+            befores = [before.at[k].at[here] for k in range(2)]
+            self.parts.append((sources, targets, copies, befores, result.at[here]))
 
     def step(self, k):
+        for part in self.parts:
+            self.part_step(k, *part)
+
+    def part_step(self, k, sources, targets, copies, before, result):
         if k == 0:
-            self.copies[0].start()
+            copies[0].start()
             return
-        self.copies[k - 1].wait_recv()
-        other = self.arrived.at[k - 1]
-        mine = self.own if k == 1 else self.sent.at[k - 2]
+        copies[k - 1].wait_recv()
+        other, mine = targets[k - 1], sources[k - 1]
         second = self.seconds[k - 1]
-        before, result = self.before, self.result
 
         @pl.when(second)
         def _():
             if k < 3:
-                join_into(self.sent.at[k - 1], other, mine)
+                join_into(sources[k], other, mine)
             if k == 1:
-                before[0] = other[...]
+                before[0][...] = other[...]
             elif k == 2:
-                join_into(before.at[1], other, before.at[0])
+                join_into(before[1], other, before[0])
             else:
-                decay = before[1, NS : NS + 1].astype(jnp.float32) + before[
-                    1, NS + 1 : NS + 2
-                ].astype(jnp.float32)
+                last = before[1]
+                decay = last[NS : NS + 1].astype(jnp.float32) + last[NS + 1 : NS + 2].astype(
+                    jnp.float32
+                )
                 result[...] = (
-                    decay * other[:NS].astype(jnp.float32) + before[1, :NS].astype(jnp.float32)
+                    decay * other[:NS].astype(jnp.float32) + last[:NS].astype(jnp.float32)
                 ).astype(jnp.bfloat16)
 
         @pl.when(jnp.logical_not(second))
         def _():
             if k < 3:
-                join_into(self.sent.at[k - 1], mine, other)
+                join_into(sources[k], mine, other)
             if k == 1:
-                line = lax.broadcasted_iota(jnp.int32, before.shape[1:], 0)
-                before[0] = jnp.where(line == NS, 1.0, 0.0).astype(jnp.bfloat16)
+                line = lax.broadcasted_iota(jnp.int32, before[0].shape, 0)
+                before[0][...] = jnp.where(line == NS, 1.0, 0.0).astype(jnp.bfloat16)
             elif k == 2:
-                before[1] = before[0]
+                before[1][...] = before[0][...]
             else:
-                result[...] = before[1, :NS]
+                result[...] = before[1][:NS]
 
         if k < 3:
-            self.copies[k].start()
+            copies[k].start()
 
     def finish(self):
-        for copy in self.copies:
-            copy.wait_send()
+        for part in self.parts:
+            for copy in part[2]:
+                copy.wait_send()
 
 
 def scan_scratch(width):
@@ -917,8 +964,8 @@
         pltpu.VMEM((3, rows, width), narrow),
         pltpu.VMEM((2, rows, width), narrow),
         pltpu.VMEM((2, rows, width), narrow),
-        dma((3,)),
-        dma((3,)),
+        dma((3, SCAN_PARTS)),
+        dma((3, SCAN_PARTS)),
     ]
 
 
@@ -953,11 +1000,70 @@
     return dot(high, right) + dot(mid, right) + dot(low, right)
 
 
+def places_of(lens, rows):
+    one, two, three = lens[0, 0], lens[0, 1], lens[0, 2]
+    return [lax.axis_index("seq") * rows, one, one + two, one + two + three]
+
+
+def head_rows(bias, rate_log, skip, target):
+    lane = lax.broadcasted_iota(jnp.int32, (1, TILE), 1)
+    for k, source in enumerate((bias, rate_log, skip)):
+        row = jnp.zeros((1, TILE), jnp.float32)
+        for h in range(MH):
+            row = jnp.where(lane == h, source[h], row)
+        if k == 1:
+            row = jnp.where(lane < MH, jnp.exp(row), 0.0)
+        target[k : k + 1] = row
+
+
+def pair_columns(value, back):
+    tiles = [value[:, i * TILE : (i + 1) * TILE] for i in range(PAIRS)]
+    turned = [pltpu.roll(tile, HEAD_SIZE, 1) for tile in tiles]
+    lane = lax.broadcasted_iota(jnp.int32, tiles[0].shape, 1)
+
+    def head(i, side):
+        return tiles[i // 2] if i % 2 == side else turned[i // 2]
+
+    out = []
+    for i in range(PAIRS):
+        if back:
+            first, second = 2 * i, 2 * i + 1
+            group = QUERY_HEADS // KEY_VALUE_HEADS
+            first, second = [2 * (h % group) + h // group for h in (first, second)]
+        else:
+            first, second = i, i + PAIRS
+        out.append(jnp.where(lane < HEAD_SIZE, head(first, 0), head(second, 1)))
+    return jnp.concatenate(out, axis=1)
+
+
+def shards_into(w_attn, w_ssm_in, w_dt, w_out, w_down, conv, mix, out, down):
+    f32, narrow = jnp.float32, jnp.bfloat16
+    ssm_width = MH * MP
+    xbc = w_ssm_in.shape[1] - ssm_width
+    query = QUERY_HEADS * HEAD_SIZE
+    attn = w_attn.shape[1]
+    conv[:, :xbc] = w_ssm_in[:, ssm_width:]
+    conv[:, xbc:] = jnp.zeros((conv.shape[0], TILE), narrow)
+    conv[:, xbc : xbc + MH] = w_dt[...]
+    mix[:, :query] = pair_columns(w_attn[:, :query].astype(f32), False).astype(narrow)
+    mix[:, query:attn] = w_attn[:, query:]
+    mix[:, attn:] = w_ssm_in[:, :ssm_width]
+    turned = []
+    for i in range(w_out.shape[0] // TILE):
+        here = slice(i * TILE, (i + 1) * TILE)
+        tile = w_out[here].astype(f32).T
+        if i < PAIRS:
+            turned.append(tile)
+        else:
+            out[:, here] = tile.astype(narrow)
+        down[:, here] = w_down[here].astype(f32).T.astype(narrow)
+    out[:, :query] = pair_columns(jnp.concatenate(turned, axis=1), False).astype(narrow)
+
+
 class Gather:
     def __init__(self, ins, outs, pairs, send, recv, local, others):
         self.ins, self.outs, self.pairs = ins, outs, pairs
         self.send, self.recv, self.local, self.others = send, recv, local, others
-        self.plans = [gather_plan(True), gather_plan(False)]
         self.started = {}
         self.block = ins[0].shape[0]
 
@@ -974,13 +1080,13 @@
 
     def step(self, n, stage):
         for side in range(2):
-            p, column, cols = self.pairs[n][side]
+            p, column, cols, order = self.pairs[n][side]
             if stage > 0:
                 for copy in self.started[n, side, stage - 1]:
                     copy.wait_recv()
             if stage == 5:
                 continue
-            name, moves = self.plans[side][stage]
+            name, moves = gather_plan(order)[stage]
             copies = []
             for k, (first, rows, there) in enumerate(moves):
                 block = self.block
@@ -1019,7 +1125,7 @@
     split = x.shape[1] // TILE
     for i in range(tiles):
         cols = slice(i * TILE, (i + 1) * TILE)
-        total = jnp.broadcast_to(conv_b[:, cols], (rows, TILE))
+        total = jnp.broadcast_to(conv_b[i : i + 1], (rows, TILE))
         for k in range(CONV):
             first = RIM - (CONV - 1) + k
             shifted_rows = jnp.where(masks[k] > 0.0, raw[first : first + rows, cols], 0.0)
@@ -1032,42 +1138,66 @@
             bc[:, (i - split) * TILE : (i - split + 1) * TILE] = out
 
 
-def front_kernel(count, pairs, info, layer_x, layer_g, gains, cosine, sine, head_params, conv_w, conv_b, *refs):
-    ins, refs = refs[:count], refs[count:]
+def front_kernel(
+    count, pairs, lens, bias, rate_log, skip, layer_x, layer_g, norm_gain, mlp_gain, freqs, conv_w,
+    conv_b, w_attn, w_ssm_in, w_dt, w_out, w_gate_up, w_down, *refs
+):
     fulls, refs = refs[:count], refs[count:]
     (
         x_own, g_own, gains_own, normed, q, kv, gate_z, raw, pre, x, bc, y, state, dt, cum,
-        out, out_t, lse, state_in, order,
-    ) = refs[:20]
+        out, out_t, lse, state_in, order, cosine, sine, head_params,
+    ) = refs[:23]
     (
+        s_conv, s_mix, s_out, s_down, gains,
         attn_proj, dt_t, cum_t, heads, acc, top, total, arrived, sent, before,
         scan_send, scan_recv, send, recv, w_send, w_recv, w_local, rim_send, rim_recv,
-    ) = refs[20:]
+    ) = refs[23:]
+    ins = (s_conv, s_mix, s_out, w_gate_up, s_down)
     others = partners()
     previous, following = around()
     greet(list(others.values()) + [previous, following])
     me = lax.axis_index("seq")
     rows, width = layer_x.shape
+    info = places_of(lens, rows)
+    shards_into(w_attn, w_ssm_in, w_dt, w_out, w_down, s_conv, s_mix, s_out, s_down)
     gather = Gather(ins, fulls, pairs, w_send, w_recv, w_local, others)
     gather.own()
 
-    def pump(*steps):
-        for n, stage in steps:
-            gather.step(n, stage)
-
-    pump((0, 0), (1, 0))
+    first = len(pairs_of(pairs, 0)) + len(pairs_of(pairs, 1))
+    waves = {}
+    for n in reversed(range(len(pairs))):
+        for stage in range(6):
+            late = 1 if n >= first and stage >= 2 else 0
+            waves.setdefault(n + stage + late, []).append((n, stage))
+
+    def pump(*which):
+        for wave in which:
+            for n, stage in waves.pop(wave, []):
+                gather.step(n, stage)
+
+    conv_wave = pairs_of(pairs, 0)[-1] + 5
+    mix_wave = pairs_of(pairs, 1)[-1] + 5
+    pump(0)
     own_order_into(order)
-    pump((0, 1), (1, 1))
+    head_rows(bias, rate_log, skip, head_params)
+    gains[...] = jnp.zeros_like(gains)
+    for k, source in enumerate((norm_gain, mlp_gain)):
+        for i in range(width // TILE):
+            gains[k : k + 1, i * TILE : (i + 1) * TILE] = source[i : i + 1]
+    pump(1)
+    at = lax.broadcasted_iota(jnp.int32, (rows, 1), 0) + info[0]
+    angles = (at - seg_start(at, info)).astype(jnp.float32) * freqs[...]
+    cosine[...] = jnp.cos(angles)
+    sine[...] = jnp.sin(angles)
     x_own[...] = dot(layer_x[...], order[...]).astype(jnp.bfloat16)
-    pump((0, 2), (2, 0))
+    pump(2)
     gains_own[...] = three_part(gains[...], order[...])
     wide = x_own[...].astype(jnp.float32)
     scale = lax.rsqrt(jnp.mean(wide * wide, axis=-1, keepdims=True) + NORM_EPS)
     normed[...] = (wide * scale * gains_own[0:1]).astype(jnp.bfloat16)
-    pump((1, 2), (0, 3), (2, 1), (3, 0))
+    pump(3)
     g_own[...] = dot(layer_g[...], order[...]).astype(jnp.bfloat16)
-    pump((0, 4), (1, 3), (3, 1), (4, 0))
-    pump((0, 5))
+    pump(*range(4, conv_wave + 1))
 
     full_conv, full_mix = fulls[0], fulls[1]
     xbc = pre.shape[1]
@@ -1098,20 +1228,20 @@
         raw.at[pl.ds(rows, RIM)], raw.at[pl.ds(0, RIM)], rim_send.at[0], rim_recv.at[0], following
     )
     rim.start()
-    pump((1, 4), (2, 2), (4, 1), (5, 0))
+    pump(*range(conv_wave + 1, mix_wave))
     rim.wait_recv()
     conv_forward(info, raw, conv_w, conv_b, pre, x, bc)
     step_in = raw.at[pl.ds(RIM, rows), pl.ds(xbc, TILE)]
     ssm_states(info, x, bc, step_in, head_params, state, dt, cum, dt_t, cum_t)
     scan = StateScan(True, state, state_in, arrived, sent, before, scan_send, scan_recv, others)
     scan.step(0)
-    pump((1, 5))
+    pump(mix_wave)
     project(full_mix, 0, attn_proj, 0, attn_cols)
     rope_kernel(attn_proj, cosine, sine, q, kv.at[pl.ds(0, rows)])
     copies[4].start()
     copies[2].start()
     copies[1].start()
-    pump((5, 1), (2, 3), (3, 2))
+    pump(mix_wave + 1)
     project(full_mix, attn_proj.shape[1], gate_z, 0, gate_cols)
     attend_start(q, heads, acc, top, total)
 
@@ -1140,20 +1270,24 @@
     copies[3].start()
     copies[6].wait_recv()
     copies[7].start()
+    pump(mix_wave + 2)
     several(0, 4, 2)
-    pump((3, 3), (4, 2), (2, 4))
+    pump(mix_wave + 3)
     ssm_local(info, x, bc, head_params, y, cum, dt_t, cum_t)
     scan.step(2)
+    pump(mix_wave + 4)
     several(2, 4, 2)
-    pump((4, 3), (5, 2), (3, 4))
+    pump(mix_wave + 5)
     for r in (1, 3, 5, 7):
         copies[r].wait_recv()
-    several(1, 2, 4)
+    several(1, 2, 2)
+    pump(mix_wave + 6)
+    several(5, 2, 2)
+    pump(mix_wave + 7)
     lse[...] = top[...] + jnp.log(total[...])
     attend_write(acc, total, out, out_t)
     scan.step(3)
-    pump((5, 3), (4, 4), (2, 5))
-    pump((5, 4), (3, 5), (4, 5), (5, 5))
+    pump(*sorted(waves))
     gather.finish()
     scan.finish()
     rim.wait_send()
@@ -1161,25 +1295,31 @@
         copy.wait_send()
 
 
-def front(info, layer_x, layer_g, gains, cosine, sine, head_params, conv_w, conv_b, shards):
-    count = len(shards)
+def front(lens, bias, rate_log, skip, layer_x, layer_g, norm_gain, mlp_gain, freqs, conv_w, conv_b, weights):
+    w_attn, w_ssm_in, w_dt, w_out, w_gate_up, w_down = weights
     rows, width = layer_x.shape
     f32, narrow = jnp.float32, jnp.bfloat16
-    pairs = column_chunks([p.shape[1] for p in shards])
+    block = w_attn.shape[0]
     query_width = QUERY_HEADS * HEAD_SIZE
     pair_width = 2 * KEY_VALUE_HEADS * HEAD_SIZE
     ssm_width = MH * MP
     xbc = conv_w.shape[1]
-    fulls = [shape_of((32 * p.shape[0], p.shape[1]), p.dtype) for p in shards]
+    widths = [
+        xbc + TILE, w_attn.shape[1] + ssm_width, w_out.shape[0], w_gate_up.shape[1],
+        w_down.shape[0],
+    ]
+    count = len(widths)
+    pairs = column_chunks(widths)
+    fulls = [shape_of((width, w), narrow) for w in widths]
     outs = fulls + [
         shape_of((rows, width), narrow),
         shape_of((rows, width), narrow),
-        shape_of(gains.shape, f32),
+        shape_of((8, width), f32),
         shape_of((rows, width), narrow),
         shape_of((rows, query_width), narrow),
         shape_of((8 * rows, pair_width), narrow),
         shape_of((rows, ssm_width), f32),
-        shape_of((rows + RIM, shards[0].shape[1]), f32),
+        shape_of((rows + RIM, widths[0]), f32),
         shape_of((rows, xbc), f32),
         shape_of((rows, ssm_width), narrow),
         shape_of((rows, 2 * NS), narrow),
@@ -1192,9 +1332,14 @@
         shape_of((QUERY_HEADS, rows), f32),
         shape_of((NS, ssm_width), narrow),
         shape_of((width, width), narrow),
+        shape_of((rows, TILE), f32),
+        shape_of((rows, TILE), f32),
+        shape_of((8, TILE), f32),
     ]
     dma = pltpu.SemaphoreType.DMA
     scratch = [
+        *(pltpu.VMEM((block, widths[k]), narrow) for k in (0, 1, 2, 4)),
+        pltpu.VMEM((8, width), f32),
         pltpu.VMEM((rows, query_width + pair_width), f32),
         pltpu.VMEM((TILE, rows), f32),
         pltpu.VMEM((TILE, rows), f32),
@@ -1205,8 +1350,8 @@
         *scan_scratch(ssm_width),
         dma((8,)),
         dma((8,)),
-        dma((2 * len(pairs), 5, 2)),
-        dma((2 * len(pairs), 5, 2)),
+        dma((2 * len(pairs), 5, 4)),
+        dma((2 * len(pairs), 5, 4)),
         dma((count,)),
         dma((1,)),
         dma((1,)),
@@ -1214,14 +1359,166 @@
     result = comm_call(
         lambda *refs: front_kernel(count, pairs, *refs),
         outs,
-        [INTO_VMEM] * 2 + [ANY] * (count - 2) + [INTO_VMEM] * 20,
-        (info, layer_x, layer_g, gains, cosine, sine, head_params, conv_w, conv_b, *shards),
-        [pl.BlockSpec(memory_space=pltpu.SMEM)] + [INTO_VMEM] * 8 + [ANY] * count,
+        [INTO_VMEM] * 2 + [ANY] * (count - 2) + [INTO_VMEM] * 23,
+        (
+            lens, bias, rate_log, skip, layer_x, layer_g, norm_gain, mlp_gain, freqs, conv_w,
+            conv_b, *weights,
+        ),
+        [pl.BlockSpec(memory_space=pltpu.SMEM)] * 4 + [INTO_VMEM] * 13,
         scratch,
         0,
         200_000_000,
     )
     return result[:count], result[count:]
+
+
+def middle_kernel(
+    lens, y, bc, cum, state_in, state_own, z, ssm_gain, attended, x_own, g_own, gains, order,
+    hbm_out, hbm_gu, hbm_down,
+    layer_out, joined, hidden, d_gu, normed_two, d_mixer, d_middle, d_ssm, d_z, pull, att_grad,
+    g_ssm, g_mlp,
+    w_out, w_gu, w_down, ssm_out, scale, middle, gate_up, d_normed, dy, narrow, sems,
+):
+    rows, width = x_own.shape
+    info = places_of(lens, rows)
+    copies = [
+        pltpu.make_async_copy(src, dst, sems.at[k])
+        for k, (src, dst) in enumerate(((hbm_out, w_out), (hbm_gu, w_gu), (hbm_down, w_down)))
+    ]
+    for copy in copies:
+        copy.start()
+    attn = attended.shape[1]
+    ff = hidden.shape[1]
+    step = 256
+
+    def tiles(count, body):
+        def one(j, carry):
+            body(pl.ds(pl.multiple_of(j * step, step), step), j * step)
+            return carry
+
+        lax.fori_loop(0, count // step, one, 0)
+
+    joined[:, :attn] = attended[...]
+    ssm_finish_kernel(
+        info, y, bc, cum, state_in, z, ssm_gain, ssm_out,
+        joined.at[:, pl.ds(attn, joined.shape[1] - attn)], scale,
+    )
+    copies[0].wait()
+
+    def add_mixers(here, first):
+        middle[:, here] = x_own[:, here].astype(jnp.float32) + dot_nt(joined[...], w_out[here])
+
+    tiles(width, add_mixers)
+    wide = middle[...]
+    r = lax.rsqrt(jnp.mean(wide * wide, axis=-1, keepdims=True) + NORM_EPS)
+    normed_two[...] = (wide * r * gains[1:2]).astype(jnp.bfloat16)
+    copies[1].wait()
+
+    def up_project(here, first):
+        there = pl.ds(pl.multiple_of(ff + first, step), step)
+        gate = dot(normed_two[...], w_gu[:, here])
+        up = dot(normed_two[...], w_gu[:, there])
+        gate_up[:, here] = gate
+        gate_up[:, there] = up
+        hidden[:, here] = (gate * jax.nn.sigmoid(gate) * up).astype(jnp.bfloat16)
+
+    tiles(ff, up_project)
+    copies[2].wait()
+
+    def down_project(here, first):
+        narrow[:, here] = (middle[:, here] + dot_nt(hidden[...], w_down[here])).astype(jnp.bfloat16)
+
+    tiles(width, down_project)
+
+    def plain(here, first):
+        layer_out[:, here] = dot_nt(narrow[...], order[here]).astype(jnp.bfloat16)
+
+    tiles(width, plain)
+
+    def down_back(here, first):
+        there = pl.ds(pl.multiple_of(ff + first, step), step)
+        d_hidden = dot(g_own[...], w_down[:, here])
+        gate, up = gate_up[:, here], gate_up[:, there]
+        sig = jax.nn.sigmoid(gate)
+        d_gate = d_hidden * up * (sig * (1.0 + gate * (1.0 - sig)))
+        d_gu[:, here] = d_gate.astype(jnp.bfloat16)
+        d_gu[:, there] = (d_hidden * gate * sig).astype(jnp.bfloat16)
+
+    tiles(ff, down_back)
+
+    def up_back(here, first):
+        d_normed[:, here] = dot_nt(d_gu[...], w_gu[here])
+
+    tiles(width, up_back)
+    grads = d_normed[...]
+    wide = middle[...]
+    g_mlp[...] = jnp.sum(grads * wide * r, axis=0, keepdims=True)
+    inner = grads * gains[1:2]
+    coeff = jnp.mean(inner * wide, axis=-1, keepdims=True)
+    total = g_own[...].astype(jnp.float32) + r * (inner - wide * (r * r * coeff))
+    d_middle[...] = total
+    d_mixer[...] = total.astype(jnp.bfloat16)
+
+    def att_back(here, first):
+        att_grad[:, here] = dot(d_mixer[...], w_out[:, here]).astype(jnp.bfloat16)
+
+    tiles(attn, att_back)
+
+    def ssm_part(here, first):
+        there = pl.ds(pl.multiple_of(attn + first, step), step)
+        dy[:, here] = dot(d_mixer[...], w_out[:, there])
+
+    tiles(dy.shape[1], ssm_part)
+    gate_back_kernel(
+        info, dy, ssm_out, z, scale, ssm_gain, cum, bc, d_ssm, d_z, pull.at[pl.ds(0, NS)], g_ssm
+    )
+    pull[NS:] = state_own[NS:]
+
+
+def middle_part(lens, y, bc, cum, state_in, state_own, z, ssm_gain, attended, x_own, g_own, gains, order, w_out, w_gu, w_down):
+    rows, width = x_own.shape
+    ssm_width, attn = y.shape[1], attended.shape[1]
+    ff = w_down.shape[1]
+    f32, narrow = jnp.float32, jnp.bfloat16
+    outs = [
+        shape_of((rows, width), narrow),
+        shape_of((rows, attn + ssm_width), narrow),
+        shape_of((rows, ff), narrow),
+        shape_of((rows, 2 * ff), narrow),
+        shape_of((rows, width), narrow),
+        shape_of((rows, width), narrow),
+        shape_of((rows, width), f32),
+        shape_of((rows, ssm_width), f32),
+        shape_of((rows, ssm_width), narrow),
+        shape_of((STATE_ROWS, ssm_width), narrow),
+        shape_of((rows, attn), narrow),
+        shape_of(ssm_gain.shape, f32),
+        shape_of((1, width), f32),
+    ]
+    args = (
+        lens, y, bc, cum, state_in, state_own, z, ssm_gain, attended, x_own, g_own, gains, order,
+        w_out, w_gu, w_down,
+    )
+    return pl.pallas_call(
+        middle_kernel,
+        out_shape=outs,
+        in_specs=[pl.BlockSpec(memory_space=pltpu.SMEM)] + [INTO_VMEM] * 12 + [ANY] * 3,
+        out_specs=[INTO_VMEM] * len(outs),
+        scratch_shapes=[
+            pltpu.VMEM(w_out.shape, narrow),
+            pltpu.VMEM(w_gu.shape, narrow),
+            pltpu.VMEM(w_down.shape, narrow),
+            pltpu.VMEM((rows, ssm_width), f32),
+            pltpu.VMEM((rows, TILE), f32),
+            pltpu.VMEM((rows, width), f32),
+            pltpu.VMEM((rows, 2 * ff), f32),
+            pltpu.VMEM((rows, width), f32),
+            pltpu.VMEM((rows, ssm_width), f32),
+            pltpu.VMEM((rows, width), narrow),
+            pltpu.SemaphoreType.DMA((3,)),
+        ],
+        compiler_params=pltpu.CompilerParams(vmem_limit_bytes=60 * 1024 * 1024),
+    )(*args)
 
 
 def turn_over(value):
@@ -1232,19 +1529,11 @@
     def __init__(self, ins, outs, arrived, pairs, send, recv, others):
         self.ins, self.outs, self.arrived, self.pairs = ins, outs, arrived, pairs
         self.send, self.recv, self.others = send, recv, others
-        self.routes = (("y", "x", "near", "far"), ("x", "y", "near", "far"))
-        self.size = ins[0].shape[0]
+        self.block = ins[0].shape[0] // 16
         self.started = {}
 
     def source(self, p, stage):
         return self.ins[p] if stage == 0 else self.arrived[4 * p + stage - 1]
-
-    def pieces(self, side, stage):
-        rows = self.size >> stage
-        if side == 1 and stage == 0:
-            quarter = rows // 4
-            return [quarter, 3 * quarter], [0, 2 * quarter], quarter
-        return [rows // 2], [0], rows // 2
 
     def step(self, n, stage):
         for side in range(2):
@@ -1254,41 +1543,44 @@
                 self.begin(n, side, stage)
 
     def begin(self, n, side, stage):
-        p, column, width = self.pairs[n][side]
+        p, column, width, order = self.pairs[n][side]
         cols = pl.ds(column, width)
-        sent, unused_kept, rows = self.pieces(side, stage)
-        copies = []
-        for k, first in enumerate(sent):
+        name, sent, unused_kept = scatter_plan(order)[stage]
+        copies, row, block = [], 0, self.block
+        for k, (first, count) in enumerate(sent):
             copy = remote(
-                self.source(p, stage).at[pl.ds(first, rows), cols],
-                self.arrived[4 * p + stage].at[pl.ds(k * rows, rows), cols],
+                self.source(p, stage).at[pl.ds(first * block, count * block), cols],
+                self.arrived[4 * p + stage].at[pl.ds(row * block, count * block), cols],
                 self.send.at[2 * n + side, stage, k],
                 self.recv.at[2 * n + side, stage, k],
-                self.others[self.routes[side][stage]],
+                self.others[name],
             )
             copy.start()
             copies.append(copy)
+            row += count
         self.started[n, side, stage] = copies
 
     def take(self, n, side, stage):
-        p, column, width = self.pairs[n][side]
+        p, column, width, order = self.pairs[n][side]
         cols = slice(column, column + width)
         source, got = self.source(p, stage), self.arrived[4 * p + stage]
         target = self.outs[p] if stage == 3 else got
-        unused_sent, kept, rows = self.pieces(side, stage)
-        for k, first in enumerate(kept):
+        unused_name, unused_sent, kept = scatter_plan(order)[stage]
+        row, block = 0, self.block
+        for k, (first, count) in enumerate(kept):
             self.started[n, side, stage][k].wait_recv()
 
             def add(i, carry):
-                at = pl.multiple_of(i * 32, 32)
-                there = pl.ds(k * rows + at, 32)
-                total = source[pl.ds(first + at, 32), cols].astype(jnp.float32) + got[
+                at = pl.multiple_of(i * block, block)
+                there = pl.ds(row * block + at, block)
+                total = source[pl.ds(first * block + at, block), cols].astype(jnp.float32) + got[
                     there, cols
                 ].astype(jnp.float32)
                 target[there, cols] = total.astype(target.dtype)
                 return carry
 
-            lax.fori_loop(0, rows // 32, add, 0)
+            lax.fori_loop(0, count, add, 0)
+            row += count
 
     def finish(self):
         for copies in self.started.values():
@@ -1355,7 +1647,7 @@
 
 def back_kernel(pairs, *refs):
     (
-        info, head_params, conv_w, cosine, sine, q, kv, grad, out_t, lse, pull, x, bc, dt, cum,
+        lens, head_params, conv_w, cosine, sine, q, kv, grad, out_t, lse, pull, x, bc, dt, cum,
         d_ssm, raw, state_in, pre, normed, normed_two, d_mixer, grad_rows, hidden, joined, d_gu,
         d_z,
     ) = refs[:27]
@@ -1377,6 +1669,7 @@
     greet(list(others.values()) + [previous, following])
     me = lax.axis_index("seq")
     rows = q.shape[0]
+    info = places_of(lens, rows)
     half = normed.shape[1] // 2
     xbc = pre.shape[1]
     scan = StateScan(False, pull, d_state, arrived, sent, before, scan_send, scan_recv, others)
@@ -1442,6 +1735,8 @@
             jnp.bfloat16
         )
 
+    weights(0, grad_rows, half_grad, hidden, their_hidden)
+    pump((0, 0))
     several(1, 2, 4)
     over_x = [
         remote(dkv.at[2 * k + 1], from_x.at[k], send.at[k], recv.at[k], others["x"])
@@ -1450,8 +1745,8 @@
     for copy in over_x:
         copy.start()
     scan.step(1)
-    weights(0, grad_rows, half_grad, hidden, their_hidden)
-    pump((0, 0))
+    weights(1, normed_two, half_two, d_gu, their_gu)
+    pump((1, 0), (0, 1))
     several(4, 2, 2)
     over_far = [
         remote(dkv.at[4 + 2 * k], from_far.at[k], send.at[4 + k], recv.at[4 + k], others["far"])
@@ -1462,8 +1757,7 @@
         add(dkv.at[4 + 2 * k], from_x.at[2 + k])
         over_far[k].start()
     scan.step(2)
-    weights(1, normed_two, half_two, d_gu, their_gu)
-    pump((1, 0), (0, 1))
+    pump((2, 0), (1, 1), (0, 2))
     several(0, 2, 2)
     for k in range(2):
         over_x[k].wait_recv()
@@ -1472,13 +1766,14 @@
     add(dkv.at[2], from_far.at[1])
     over_near = remote(dkv.at[2], from_near, send.at[6], recv.at[6], others["near"])
     over_near.start()
-    pump((2, 0), (1, 1), (0, 2))
+    weights(2, d_mixer, half_mixer, joined, their_joined)
+    weights(3, normed, their_normed, d_z, their_z)
+    pump((3, 0), (2, 1), (1, 2), (0, 3))
     ssm_back_kernel(
         info, x, bc, dt, cum, d_ssm, head_params, dx, d_bc, d_cum, d_dt, g_skip, cols_t, d_rows
     )
+    pump((4, 0), (3, 1), (2, 2), (1, 3), (0, 4))
     scan.step(3)
-    weights(2, d_mixer, half_mixer, joined, their_joined)
-    pump((3, 0), (2, 1), (1, 2), (0, 3))
     d_step = d_conv.at[:, pl.ds(xbc, TILE)]
     step_in = raw.at[pl.ds(RIM, rows), pl.ds(xbc, TILE)]
     state_back_kernel(
@@ -1491,8 +1786,7 @@
         previous,
     )
     rim.start()
-    weights(3, normed, their_normed, d_z, their_z)
-    pump((4, 0), (3, 1), (2, 2), (1, 3), (0, 4))
+    pump((4, 1), (3, 2), (2, 3), (1, 4))
     over_far[0].wait_recv()
     over_near.wait_recv()
     attend_back_write(acc, dq)
@@ -1504,7 +1798,6 @@
     rope_back_kernel(dq, d_pair, cosine, sine, d_attn)
     rim.wait_recv()
     conv_back_end(info, d_pre, conv_w, d_conv.at[:, pl.ds(0, xbc)])
-    pump((4, 1), (3, 2), (2, 3), (1, 4))
     pump((4, 2), (3, 3), (2, 4))
     pump((4, 3), (3, 4))
     pump((4, 4))
@@ -1515,7 +1808,7 @@
         copy.wait_send()
 
 
-def back(info, *args):
+def back(lens, *args):
     (
         head_params, conv_w, cosine, sine, q, kv, grad, out_t, lse, pull, x, bc, dt, cum,
         d_ssm, raw, state_in, pre, normed, normed_two, d_mixer, grad_rows, hidden, joined, d_gu,
@@ -1529,7 +1822,7 @@
     f32, narrow = jnp.float32, jnp.bfloat16
     dma = pltpu.SemaphoreType.DMA
     widths = [hidden.shape[1], d_gu.shape[1], joined.shape[1], d_z.shape[1]]
-    pairs = column_chunks(widths)
+    pairs = column_chunks(widths, 1024)
     own = half // 16
     outs = [
         shape_of((rows, xbc + TILE), narrow),
@@ -1568,8 +1861,8 @@
         dma((7,)),
         dma((8,)),
         dma((8,)),
-        dma((2 * len(pairs), 4, 2)),
-        dma((2 * len(pairs), 4, 2)),
+        dma((2 * len(pairs), 4, 4)),
+        dma((2 * len(pairs), 4, 4)),
         dma((1,)),
         dma((1,)),
     ]
@@ -1577,7 +1870,7 @@
         lambda *refs: back_kernel(pairs, *refs),
         outs,
         [INTO_VMEM] * len(outs),
-        (info, *args),
+        (lens, *args),
         [pl.BlockSpec(memory_space=pltpu.SMEM)] + [INTO_VMEM] * len(args),
         scratch,
         2,
@@ -1595,14 +1888,17 @@
 def last_kernel(pairs, *refs):
     (
         d_conv, d_attn, d_z, full_conv, full_mix, normed, their_normed, x_own, d_middle, gains,
-        order, g_mlp, small,
-    ) = refs[:13]
-    input_grad, out_conv, out_attn, small_out = refs[13:17]
-    refs = refs[17:]
+        order, g_mlp, g_ssm, g_conv, head_sums, g_skip, sum_down, sum_out, sum_z,
+    ) = refs[:19]
+    (
+        input_grad, g_attn_out, g_in_out, g_dt_out, g_out_out, g_down_out,
+        norm_total, mlp_total, ssm_total, conv_total, conv_b_total, head_total,
+    ) = refs[19:31]
+    refs = refs[31:]
     partials, arrived_w = refs[:2], refs[2:10]
     (
-        their_conv, their_attn, left_t, d_normed, small_own, small_in, small_mid, swap_send,
-        swap_recv, w_send, w_recv, small_send, small_recv,
+        out_conv, out_attn, their_conv, their_attn, left_t, d_normed, small_own, small_in, small_mid,
+        small_out, swap_send, swap_recv, w_send, w_recv, small_send, small_recv,
     ) = refs[10:]
     others = partners()
     greet(list(others.values()))
@@ -1620,9 +1916,10 @@
     swaps[0].wait_recv()
     weight_products(left_t, d_conv, their_conv, partials[0])
     scatter.step(0, 0)
+    scatter.step(1, 0)
     swaps[1].wait_recv()
     weight_products(left_t, d_attn, their_attn, partials[1])
-    scatter.step(1, 0)
+    scatter.step(2, 0)
     step = 256
     attn = d_attn.shape[1]
 
@@ -1637,6 +1934,7 @@
 
     lax.fori_loop(0, width // step, back_out, 0)
     scatter.step(0, 1)
+    scatter.step(1, 1)
     wide = x_own[...].astype(jnp.float32)
     r = lax.rsqrt(jnp.mean(wide * wide, axis=-1, keepdims=True) + NORM_EPS)
     grads = d_normed[...]
@@ -1644,7 +1942,15 @@
     line = lax.broadcasted_iota(jnp.int32, (8, width), 0)
     both = jnp.where(line == 0, g_norm, jnp.where(line == 1, g_mlp[...], 0.0))
     both = dot_nt_two(both, order[...])
-    small_own[16:] = small[...]
+    small_own[16:] = jnp.zeros((small_own.shape[0] - 16, TILE), jnp.float32)
+    small_own[16:28] = g_ssm[...]
+    small_own[28:30] = head_sums[0:2]
+    small_own[30:31] = g_skip[0:1]
+    conv_tiles = g_conv.shape[1] // TILE
+    for k in range(CONV + 1):
+        for i in range(conv_tiles):
+            place = 32 + 16 * k + i
+            small_own[place : place + 1] = g_conv[k : k + 1, i * TILE : (i + 1) * TILE]
     for k in range(width // TILE):
         for which in range(2):
             small_own[8 * which + k : 8 * which + k + 1] = both[
@@ -1667,13 +1973,16 @@
             copy.start()
             small_copies.append(copy)
 
+    scatter.step(2, 1)
+    scatter.step(0, 2)
     small_step(0)
-    scatter.step(1, 1)
     inner = grads * gains[0:1]
     coeff = jnp.mean(inner * wide, axis=-1, keepdims=True)
     d_normed[...] = d_middle[...] + r * (inner - wide * (r * r * coeff))
+    scatter.step(1, 2)
     small_step(1)
-    scatter.step(0, 2)
+    scatter.step(0, 3)
+    scatter.step(2, 2)
 
     def plain(j, carry):
         here = pl.ds(pl.multiple_of(j * step, step), step)
@@ -1682,36 +1991,71 @@
 
     lax.fori_loop(0, width // step, plain, 0)
     small_step(2)
-    scatter.step(1, 2)
-    scatter.step(0, 3)
+    query = QUERY_HEADS * HEAD_SIZE
+    g_in_out[:, : sum_z.shape[1]] = sum_z[...]
+    moved = pair_columns(sum_out[:, :query], True)
+    for i in range(sum_out.shape[1] // TILE):
+        here = slice(i * TILE, (i + 1) * TILE)
+        tile = moved[:, here] if i < PAIRS else sum_out[:, here]
+        g_out_out[here] = tile.T
+        g_down_out[here] = sum_down[:, here].T
+    scatter.step(1, 3)
+    scatter.step(2, 3)
     small_step(3)
-    scatter.step(1, 3)
     scatter.step(0, 4)
     small_step(4)
     scatter.step(1, 4)
+    scatter.step(2, 4)
     small_step(5)
+    norm_total[...] = small_out[:8]
+    mlp_total[...] = small_out[8:16]
+    ssm_total[...] = small_out[16:28]
+    head_total[...] = small_out[24:32]
+    for k in range(CONV):
+        for i in range(conv_tiles):
+            place = 32 + 16 * k + i
+            conv_total[k : k + 1, i * TILE : (i + 1) * TILE] = small_out[place : place + 1]
+    conv_b_total[...] = small_out[32 + 16 * CONV : 32 + 16 * CONV + conv_tiles]
+    g_in_out[:, g_in_out.shape[1] - g_conv.shape[1] :] = out_conv[:, : g_conv.shape[1]]
+    g_dt_out[...] = out_conv[:, g_conv.shape[1] : g_conv.shape[1] + MH]
+    query = QUERY_HEADS * HEAD_SIZE
+    g_attn_out[:, :query] = pair_columns(out_attn[:, :query], True)
+    g_attn_out[:, query:] = out_attn[:, query:]
     scatter.finish()
     for copy in swaps + small_copies:
         copy.wait_send()
 
 
-def last(d_conv, d_attn, d_z, full_conv, full_mix, normed, their_normed, x_own, d_middle, gains, order, g_mlp, small):
-    args = (
-        d_conv, d_attn, d_z, full_conv, full_mix, normed, their_normed, x_own, d_middle, gains,
-        order, g_mlp, small,
-    )
+def last(*args):
+    d_conv, d_attn, d_z, normed = args[0], args[1], args[2], args[5]
+    g_conv = args[13]
     rows, width = normed.shape
     half = width // 2
     f32, narrow = jnp.float32, jnp.bfloat16
     dma = pltpu.SemaphoreType.DMA
     widths = [d_conv.shape[1], d_attn.shape[1]]
     pairs = column_chunks(widths)
-    total = (small.shape[0] + 16, TILE)
-    outs = [shape_of((rows, width), f32)]
-    outs += [shape_of((half // 16, w), f32) for w in widths]
-    outs.append(shape_of(total, f32))
+    total = (32 + 16 * (CONV + 1), TILE)
+    block = half // 16
+    xbc = g_conv.shape[1]
+    joined, ff = args[17].shape[1], args[16].shape[1]
+    outs = [
+        shape_of((rows, width), f32),
+        shape_of((block, widths[1]), f32),
+        shape_of((block, d_z.shape[1] + xbc), f32),
+        shape_of((block, MH), f32),
+        shape_of((joined, block), f32),
+        shape_of((ff, block), f32),
+        shape_of((8, TILE), f32),
+        shape_of((8, TILE), f32),
+        shape_of((12, TILE), f32),
+        shape_of((CONV, xbc), f32),
+        shape_of((xbc // TILE, TILE), f32),
+        shape_of((8, TILE), f32),
+    ]
     scratch = [pltpu.VMEM((half, w), narrow) for w in widths]
     scratch += scatter_scratch(widths, half)
+    scratch += [pltpu.VMEM((block, w), f32) for w in widths]
     scratch += [
         pltpu.VMEM(d_conv.shape, narrow),
         pltpu.VMEM(d_attn.shape, narrow),
@@ -1720,10 +2064,11 @@
         pltpu.VMEM(total, f32),
         pltpu.VMEM((5, *total), f32),
         pltpu.VMEM((4, *total), f32),
+        pltpu.VMEM(total, f32),
         dma((2,)),
         dma((2,)),
-        dma((2 * len(pairs), 4, 2)),
-        dma((2 * len(pairs), 4, 2)),
+        dma((2 * len(pairs), 4, 4)),
+        dma((2 * len(pairs), 4, 4)),
         dma((5,)),
         dma((5,)),
     ]
@@ -1748,7 +2093,7 @@
     return jnp.concatenate([moved.reshape(rows, width), value[:, width:]], axis=1)
 
 
-def on_device(
+def plain_layer(
     layer_input,
     seq_lengths,
     w_attn,
@@ -1773,8 +2118,6 @@
     attn_width = query_width + 2 * key_value_width
     ssm_width = MH * MP
     xbc_width = ssm_width + 2 * NS
-    width = layer_input.shape[2]
-    fast = is_fast(width)
     seq_lens = seq_lengths[0]
     first_pos = lax.axis_index("seq") * token_rows
     positions = first_pos + jnp.arange(token_rows, dtype=jnp.int32)
@@ -1796,77 +2139,47 @@
         w_gate_up,
         w_down.T,
     )
-    gains = jnp.pad(jnp.stack([norm_gain, mlp_gain]), ((0, 6), (0, 0)))
-    if fast:
-        full, made = front(
-            info,
-            layer_input[0],
-            out_grad[0],
-            gains,
-            cosine,
-            sine,
-            head_params,
-            jnp.pad(conv_w, ((0, 4), (0, 0))),
-            conv_b[None],
-            shards,
-        )
+    ext_pos = first_pos - (CONV - 1) + jnp.arange(token_rows + CONV - 1, dtype=jnp.int32)
+    ext_segment = segments(seq_lens, ext_pos)[0]
+
+    def conv_local(ext_rows, conv_weight, conv_bias):
+        return conv_mix(ext_rows, ext_segment, conv_weight, conv_bias)
+
+    full = [lax.all_gather(p, ("seq", "batch"), axis=0, tiled=True) for p in shards]
+    full_conv, full_mix, full_out, full_gu, full_down = full
+    x_rows = layer_input[0].astype(jnp.float32)
+    grad_rows = out_grad[0]
+    scale_one = rms_scale(x_rows)
+    normed = (x_rows * scale_one * norm_gain).astype(jnp.bfloat16)
+    conv_proj = jnp.dot(normed, full_conv, preferred_element_type=jnp.float32)
+    mix_proj = jnp.dot(normed, full_mix, preferred_element_type=jnp.float32)
+    queries, own_pairs = big_call(
+        rope_kernel,
         (
-            x_narrow, grad_rows, gains, normed, queries, all_pairs, gate_z, raw_rows, pre_conv,
-            inputs_x, inputs_bc, ssm_own, state_own, steps_dt, running_decay,
-            attended, attended_t, log_total, state_in, order,
-        ) = made
-        full_conv, full_mix, full_out, full_gu, full_down = full
-        norm_gain, mlp_gain = gains[0], gains[1]
-        x_rows = x_narrow.astype(jnp.float32)
-        scale_one = rms_scale(x_rows)
-    else:
-        order = None
-        ext_pos = first_pos - (CONV - 1) + jnp.arange(token_rows + CONV - 1, dtype=jnp.int32)
-        ext_segment = segments(seq_lens, ext_pos)[0]
-
-        def conv_local(ext_rows, conv_weight, conv_bias):
-            return conv_mix(ext_rows, ext_segment, conv_weight, conv_bias)
-
-        full = [lax.all_gather(p, ("seq", "batch"), axis=0, tiled=True) for p in shards]
-        full_conv, full_mix, full_out, full_gu, full_down = full
-        x_rows = layer_input[0].astype(jnp.float32)
-        grad_rows = out_grad[0]
-        scale_one = rms_scale(x_rows)
-        normed = (x_rows * scale_one * norm_gain).astype(jnp.bfloat16)
-        conv_proj = jnp.dot(normed, full_conv, preferred_element_type=jnp.float32)
-        mix_proj = jnp.dot(normed, full_mix, preferred_element_type=jnp.float32)
-        queries, own_pairs = big_call(
-            rope_kernel,
-            (
-                shape_of((token_rows, query_width), jnp.bfloat16),
-                shape_of((token_rows, 2 * key_value_width), jnp.bfloat16),
-            ),
-            mix_proj[:, :attn_width],
-            cosine,
-            sine,
-        )
-        gate_z = mix_proj[:, attn_width:]
-        raw_xbc = conv_proj[:, :xbc_width]
-        step_proj = conv_proj[:, xbc_width:]
-        rim_rows = shifted(raw_xbc[token_rows - (CONV - 1) :], "seq", 1)
-        extended = jnp.concatenate([rim_rows, raw_xbc], axis=0)
-        conv_out, conv_pullback = jax.vjp(conv_local, extended, conv_w, conv_b)
-        conv_narrow = conv_out.astype(jnp.bfloat16)
-        inputs_x, inputs_bc = conv_narrow[:, :ssm_width], conv_narrow[:, ssm_width:]
-        ssm_own, state_own, steps_dt, running_decay = ssm_forward(
-            info, inputs_x, inputs_bc, step_proj, head_params
-        )
-        all_pairs = lax.all_gather(own_pairs, "seq", axis=0, tiled=True)
-        state_in = scan_states(state_own, True)
-        attended, attended_t, log_total = attn_forward(info, queries, all_pairs)
-
-    def to_plain(value):
-        if not fast:
-            return value
-        return jnp.einsum("tc,dc->td", value, order, preferred_element_type=jnp.float32)
+            shape_of((token_rows, query_width), jnp.bfloat16),
+            shape_of((token_rows, 2 * key_value_width), jnp.bfloat16),
+        ),
+        mix_proj[:, :attn_width],
+        cosine,
+        sine,
+    )
+    gate_z = mix_proj[:, attn_width:]
+    raw_xbc = conv_proj[:, :xbc_width]
+    step_proj = conv_proj[:, xbc_width:]
+    rim_rows = shifted(raw_xbc[token_rows - (CONV - 1) :], "seq", 1)
+    extended = jnp.concatenate([rim_rows, raw_xbc], axis=0)
+    conv_out, conv_pullback = jax.vjp(conv_local, extended, conv_w, conv_b)
+    conv_narrow = conv_out.astype(jnp.bfloat16)
+    inputs_x, inputs_bc = conv_narrow[:, :ssm_width], conv_narrow[:, ssm_width:]
+    ssm_own, state_own, steps_dt, running_decay = ssm_forward(
+        info, inputs_x, inputs_bc, step_proj, head_params
+    )
+    all_pairs = lax.all_gather(own_pairs, "seq", axis=0, tiled=True)
+    state_in = scan_states(state_own, True)
+    attended, attended_t, log_total = attn_forward(info, queries, all_pairs)
 
     ssm_flat, ssm_normed, scale_gated = ssm_finish(
-        info, ssm_own, inputs_bc, running_decay, state_in, gate_z, ssm_gain[None]
+        info, ssm_own, inputs_bc, running_decay, state_in, gate_z, ssm_gain.reshape(-1, TILE)
     )
     joined = jnp.concatenate([attended, ssm_normed], axis=1)
 
@@ -1900,137 +2213,78 @@
         ssm_flat,
         gate_z,
         scale_gated,
-        ssm_gain[None],
+        ssm_gain.reshape(-1, TILE),
         running_decay,
         inputs_bc,
     )
     pull = jnp.concatenate([pull, state_own[NS:]], axis=0)
-    if fast:
-        (
-            d_conv_proj, d_attn_proj, g_conv, head_sums, g_skip_rows, their_normed,
-            sum_down, sum_gu, sum_out, sum_z,
-        ) = back(
-            info,
-            head_params,
-            jnp.pad(conv_w, ((0, 4), (0, 0))),
-            cosine,
-            sine,
-            queries,
-            all_pairs,
-            attended_gradient,
-            attended_t,
-            log_total,
-            pull,
-            inputs_x,
-            inputs_bc,
-            steps_dt,
-            running_decay,
-            d_ssm_out,
-            raw_rows,
-            state_in,
-            pre_conv,
-            normed,
-            normed_two,
-            d_mixer,
-            grad_rows,
-            hidden,
-            joined,
-            d_gate_up,
-            d_gate_z,
-        )
-        small = (
-            g_ssm_gain[0],
-            g_conv[:CONV],
-            g_conv[CONV],
-            head_sums[0, :MH],
-            head_sums[1, :MH],
-            g_skip_rows[0, :MH],
-        )
-        input_grad, sum_conv, sum_attn, totals = last(
-            d_conv_proj,
-            d_attn_proj,
-            d_gate_z,
-            full_conv,
-            full_mix,
-            normed,
-            their_normed,
-            x_narrow,
-            d_middle,
-            gains,
-            order,
-            g_mlp_gain[None],
-            pack_small(small),
-        )
-        small_sums = [totals[:8].reshape(-1), totals[8:16].reshape(-1)]
-        small_sums += unpack_small(totals[16:], small)
-    else:
-        d_state = scan_states(pull, False)
-        d_queries, d_pairs = attn_backward(
-            info, queries, all_pairs, attended_gradient, attended_t, log_total
-        )
-        own_d_pairs = lax.psum_scatter(
-            d_pairs.astype(jnp.float32), "seq", scatter_dimension=0, tiled=True
-        )
-        dx_part, d_bc_part, d_cum_part, d_dt_part, g_skip_rows = ssm_back(
-            info, inputs_x, inputs_bc, steps_dt, running_decay, d_ssm_out, head_params
-        )
-        g_inputs_x, g_inputs_bc, d_step_pad, head_sums = state_back(
-            info,
-            inputs_x,
-            inputs_bc,
-            steps_dt,
-            running_decay,
-            d_ssm_out,
-            head_params,
-            step_proj,
-            state_in,
-            d_state,
-            dx_part,
-            d_bc_part,
-            d_cum_part,
-            d_dt_part,
-        )
-        g_extended, g_conv_w, g_conv_b = conv_pullback(
-            jnp.concatenate([g_inputs_x, g_inputs_bc], axis=1)
-        )
-        back_rim = shifted(g_extended[: CONV - 1], "seq", -1)
-        d_raw = g_extended[CONV - 1 :] + jnp.concatenate(
-            [jnp.zeros((token_rows - (CONV - 1), xbc_width), jnp.float32), back_rim], axis=0
-        )
-        d_conv_proj = jnp.concatenate([d_raw.astype(jnp.bfloat16), d_step_pad], axis=1)
-        (d_attn_proj,) = big_call(
-            rope_back_kernel,
-            (shape_of((token_rows, attn_width), jnp.bfloat16),),
-            d_queries,
-            own_d_pairs,
-            cosine,
-            sine,
-        )
-        d_mix_proj = jnp.concatenate([d_attn_proj, d_gate_z], axis=1)
-        d_normed = into_width(d_conv_proj, full_conv) + into_width(d_mix_proj, full_mix)
-        d_input_norm, g_norm_gain = norm_back(x_rows, scale_one, norm_gain, d_normed)
-        input_grad = d_middle + d_input_norm
-        axes = ("seq", "batch")
-
-        def summed(left, right):
-            grad = jnp.einsum("td,tc->dc", left, right, preferred_element_type=jnp.float32)
-            return lax.psum_scatter(grad, axes, scatter_dimension=0, tiled=True)
-
-        sum_down, sum_gu = summed(grad_rows, hidden), summed(normed_two, d_gate_up)
-        sum_out, sum_conv = summed(d_mixer, joined), summed(normed, d_conv_proj)
-        sum_mix = summed(normed, d_mix_proj)
-        sum_attn, sum_z = sum_mix[:, :attn_width], sum_mix[:, attn_width:]
-        small = (
-            g_norm_gain,
-            g_mlp_gain,
-            g_ssm_gain[0],
-            g_conv_w,
-            g_conv_b,
-            head_sums[0, :MH],
-            head_sums[1, :MH],
-            g_skip_rows[0, :MH],
-        )
-        small_sums = unpack_small(lax.psum(pack_small(small), axes), small)
+    d_state = scan_states(pull, False)
+    d_queries, d_pairs = attn_backward(
+        info, queries, all_pairs, attended_gradient, attended_t, log_total
+    )
+    own_d_pairs = lax.psum_scatter(
+        d_pairs.astype(jnp.float32), "seq", scatter_dimension=0, tiled=True
+    )
+    dx_part, d_bc_part, d_cum_part, d_dt_part, g_skip_rows = ssm_back(
+        info, inputs_x, inputs_bc, steps_dt, running_decay, d_ssm_out, head_params
+    )
+    g_inputs_x, g_inputs_bc, d_step_pad, head_sums = state_back(
+        info,
+        inputs_x,
+        inputs_bc,
+        steps_dt,
+        running_decay,
+        d_ssm_out,
+        head_params,
+        step_proj,
+        state_in,
+        d_state,
+        dx_part,
+        d_bc_part,
+        d_cum_part,
+        d_dt_part,
+    )
+    g_extended, g_conv_w, g_conv_b = conv_pullback(
+        jnp.concatenate([g_inputs_x, g_inputs_bc], axis=1)
+    )
+    back_rim = shifted(g_extended[: CONV - 1], "seq", -1)
+    d_raw = g_extended[CONV - 1 :] + jnp.concatenate(
+        [jnp.zeros((token_rows - (CONV - 1), xbc_width), jnp.float32), back_rim], axis=0
+    )
+    d_conv_proj = jnp.concatenate([d_raw.astype(jnp.bfloat16), d_step_pad], axis=1)
+    (d_attn_proj,) = big_call(
+        rope_back_kernel,
+        (shape_of((token_rows, attn_width), jnp.bfloat16),),
+        d_queries,
+        own_d_pairs,
+        cosine,
+        sine,
+    )
+    d_mix_proj = jnp.concatenate([d_attn_proj, d_gate_z], axis=1)
+    d_normed = into_width(d_conv_proj, full_conv) + into_width(d_mix_proj, full_mix)
+    d_input_norm, g_norm_gain = norm_back(x_rows, scale_one, norm_gain, d_normed)
+    input_grad = d_middle + d_input_norm
+    axes = ("seq", "batch")
+
+    def summed(left, right):
+        grad = jnp.einsum("td,tc->dc", left, right, preferred_element_type=jnp.float32)
+        return lax.psum_scatter(grad, axes, scatter_dimension=0, tiled=True)
+
+    sum_down, sum_gu = summed(grad_rows, hidden), summed(normed_two, d_gate_up)
+    sum_out, sum_conv = summed(d_mixer, joined), summed(normed, d_conv_proj)
+    sum_mix = summed(normed, d_mix_proj)
+    sum_attn, sum_z = sum_mix[:, :attn_width], sum_mix[:, attn_width:]
+    small = (
+        g_norm_gain,
+        g_mlp_gain,
+        g_ssm_gain.reshape(-1),
+        g_conv_w,
+        g_conv_b,
+        head_sums[0, :MH],
+        head_sums[1, :MH],
+        g_skip_rows[0, :MH],
+    )
+    small_sums = unpack_small(lax.psum(pack_small(small), axes), small)
     grad_attn = pair_heads(sum_attn, True)
     grad_ssm_in = jnp.concatenate([sum_z, sum_conv[:, :xbc_width]], axis=1)
     grad_dt = sum_conv[:, xbc_width : xbc_width + MH]
@@ -2038,7 +2292,7 @@
     grad_gate_up = sum_gu
     grad_down = sum_down.T
     return (
-        to_plain(layer_out.astype(jnp.bfloat16)).astype(jnp.bfloat16)[None],
+        layer_out.astype(jnp.bfloat16)[None],
         input_grad[None],
         grad_attn,
         grad_ssm_in,
@@ -2047,6 +2301,98 @@
         grad_gate_up,
         grad_down,
         *small_sums,
+    )
+
+
+def on_device(
+    layer_input,
+    seq_lengths,
+    w_attn,
+    w_ssm_in,
+    w_dt,
+    w_out,
+    w_gate_up,
+    w_down,
+    norm_gain,
+    mlp_gain,
+    ssm_gain,
+    conv_w,
+    conv_b,
+    a_log,
+    dt_bias,
+    d_skip,
+    out_grad,
+):
+    if not is_fast(layer_input.shape[2]):
+        return plain_layer(
+            layer_input, seq_lengths, w_attn, w_ssm_in, w_dt, w_out, w_gate_up, w_down, norm_gain,
+            mlp_gain, ssm_gain, conv_w, conv_b, a_log, dt_bias, d_skip, out_grad,
+        )
+    half = HEAD_SIZE // 2
+    freqs = np.float32(ROPE_BASE) ** (-np.arange(half, dtype=np.float32) / np.float32(half))
+    freqs = jnp.asarray(np.tile(freqs.astype(np.float32), TILE // half)[None])
+    full, made = front(
+        seq_lengths,
+        dt_bias,
+        a_log,
+        d_skip,
+        layer_input[0],
+        out_grad[0],
+        norm_gain.reshape(-1, TILE),
+        mlp_gain.reshape(-1, TILE),
+        freqs,
+        conv_w,
+        conv_b.reshape(-1, TILE),
+        (w_attn, w_ssm_in, w_dt, w_out, w_gate_up, w_down),
+    )
+    full_conv, full_mix, full_out, full_gu, full_down = full
+    (
+        x_own, g_own, gains, normed, queries, all_pairs, gate_z, raw_rows, pre_conv, inputs_x,
+        inputs_bc, ssm_own, state_own, steps_dt, running_decay, attended, attended_t, log_total,
+        state_in, order, cosine, sine, head_params,
+    ) = made
+    (
+        layer_out, joined, hidden, d_gate_up, normed_two, d_mixer, d_middle, d_ssm_out, d_gate_z,
+        pull, attended_gradient, g_ssm_gain, g_mlp_gain,
+    ) = middle_part(
+        seq_lengths, ssm_own, inputs_bc, running_decay, state_in, state_own, gate_z,
+        ssm_gain.reshape(-1, TILE), attended, x_own, g_own, gains, order, full_out, full_gu,
+        full_down,
+    )
+    (
+        d_conv_proj, d_attn_proj, g_conv, head_sums, g_skip_rows, their_normed, sum_down, sum_gu,
+        sum_out, sum_z,
+    ) = back(
+        seq_lengths, head_params, conv_w, cosine, sine, queries, all_pairs, attended_gradient,
+        attended_t, log_total, pull, inputs_x, inputs_bc, steps_dt, running_decay, d_ssm_out,
+        raw_rows, state_in, pre_conv, normed, normed_two, d_mixer, g_own, hidden, joined,
+        d_gate_up, d_gate_z,
+    )
+    (
+        input_grad, grad_attn, grad_ssm_in, grad_dt, grad_out, grad_down, g_norm, g_mlp, g_ssm,
+        g_conv_w, g_conv_b, heads,
+    ) = last(
+        d_conv_proj, d_attn_proj, d_gate_z, full_conv, full_mix, normed, their_normed, x_own,
+        d_middle, gains, order, g_mlp_gain, g_ssm_gain, g_conv, head_sums, g_skip_rows, sum_down,
+        sum_out, sum_z,
+    )
+    return (
+        layer_out[None],
+        input_grad[None],
+        grad_attn,
+        grad_ssm_in,
+        grad_dt,
+        grad_out,
+        sum_gu,
+        grad_down,
+        g_norm.reshape(-1),
+        g_mlp.reshape(-1),
+        g_ssm.reshape(-1),
+        g_conv_w,
+        g_conv_b.reshape(-1),
+        heads[4, :MH],
+        heads[5, :MH],
+        heads[6, :MH],
     )
 
 

time: 464 us -> 409 us (0.88)
  matrix products: 24.9 us -> 0 us
  local copies, waits for them, and re-layouts: 39.4 us -> 17.4 us
  other arithmetic: 16 us -> 0 us
  Pallas kernels: 375 us -> 384 us
    dot_general x6 -> x0, matrix products: 24.9 us -> none  [the longest x2 11.8 us: into_width(): jnp.einsum('tc,dc->td', left, weight, preferred_element_type=jnp.float32)]
    pallas_call x2 -> x1, Pallas kernels: 6.64 us -> 27.5 us  [middle_part(): pl.pallas_call(middle_kernel, out_shape=outs, in_specs=[pl.BlockSpec(memo...]
    slice x24 -> x0, local copies, waits for them, and re-layouts: 16.1 us -> none  [the longest x4 4 us: unpack_small(): out.append(flat[start:start + a.size].reshape(a.shape))]
    pallas_call x3, Pallas kernels: 368 us -> 357 us  [comm_call(): pl.pallas_call(kernel, out_shape=list(outs), in_specs=in_specs, out_specs...]
    another operation x4 -> x0, other arithmetic: 5.99 us -> none  [the longest x1 2.53 us: on_device(): info = jnp.stack([first_pos, ends[0], ends[1], ends[2]]).astype(jnp.int32)]
    concatenate x7 -> x0, other arithmetic: 5.76 us -> none  [the longest x1 1.55 us: on_device(): d_gate_up = jnp.concatenate([d_gate, d_up], axis=1).astype(jnp.bfloat16)]
    unnamed x58 -> x35, local copies, waits for them, and re-layouts: 13.8 us -> 16 us
where the time goes in v5:
time: 409 us; the launch traced here: 403 us
  Pallas kernels  384 us (94%)
  local copies, waits for them, and re-layouts  17.4 us (4%)
    pallas_call x3, Pallas kernels, comm_call(): pl.pallas_call(kernel, out_shape=list(outs), in_specs=in_specs, out_specs...  357 us
    pallas_call x1, Pallas kernels, middle_part(): pl.pallas_call(middle_kernel, out_shape=outs, in_specs=[pl.BlockSpec(memo...  27.5 us
    unnamed x35, local copies, waits for them, and re-layouts  16 us

profile of v5, /device:TPU:0, one launch (start us, length us, event | category | flops | bytes accessed | tf_op | source)
XLA Modules:
  0.0 402.6 jit_solution(13763874157949123176)
XLA Ops:
  0.6 1.4 copy.34.refs_13_
  2.0 1.9 copy.35.refs_14_
  3.9 1.9 copy.36.refs_16_
  5.8 164.9 %shard_map.297 = (bf16[1024,1920]{1,0:T(8,128)(2,1)}, bf16[1024,2304]{1,0:T(8,128)(2,1)}, bf16[1024,2048]{1,0:T(8,128)(2,1)}, bf16[1024,4096]{1,0:T(8,128)(2,1)}...) custom-call(s32[1,3]{1,0:T(1,128)} %refs_0_.3, ...), custom_call_target="tpu_custom_call" | custom-call | bytes 200000000 | tf_op jit(solution)/shard_map/pallas_call | solution.py:796
  170.7 27.5 %shard_map.298 = (bf16[256,1024]{1,0:T(8,128)(2,1)}, bf16[256,2048]{1,0:T(8,128)(2,1)}, bf16[256,2048]{1,0:T(8,128)(2,1)}, bf16[256,4096]{1,0:T(8,128)(2,1)}, bf...) custom-call(s32[1,3]{1,0:T(1,128)} %refs_0_.3, ...), custom_call_target="tpu_custom_call" | custom-call | tf_op jit(solution)/shard_map/pallas_call | solution.py:1502
  198.3 133.2 %shard_map.299 = (bf16[256,1920]{1,0:T(8,128)(2,1)}, bf16[256,768]{1,0:T(8,128)(2,1)}, f32[8,1792]{1,0:T(8,128)}, f32[8,128]{1,0:T(8,128)}, f32[8,128]{1,0:T(8,1...) custom-call(s32[1,3]{1,0:T(1,128)} %refs_0_.3, ...), custom_call_target="tpu_custom_call" | custom-call | bytes 200000000 | tf_op jit(solution)/shard_map/pallas_call | solution.py:796
  331.5 58.6 %shard_map.300 = (f32[256,1024]{1,0:T(8,128)}, f32[32,768]{1,0:T(8,128)}, f32[32,3328]{1,0:T(8,128)}, f32[32,24]{1,0:T(8,128)}, f32[2048,32]{1,0:T(8,128)}, /*in...) custom-call(bf16[256,1920]{1,0:T(8,128)(2,1)} %get-tuple-element.115, ...), custom_call_target="tpu_custom_call" | custom-call | bytes 100000000 | tf_op jit(solution)/shard_map/pallas_call | solution.py:796
  390.1 0.0 copy-start
  390.1 0.0 copy-start.1
  390.1 1.3 slice_bitcast_fusion
  391.5 1.4 copy.37
  392.9 0.0 copy-start.4
  392.9 2.3 copy.38
  395.1 0.0 copy-done
  395.1 0.0 copy-start.3
  395.1 0.0 copy-start.2
  395.1 1.0 copy.39
  396.2 0.0 copy-done.1
  396.2 0.0 copy-start.9
  396.2 0.0 copy-start.8
  396.2 0.0 copy-start.7
  396.2 0.0 copy-start.5
  396.2 0.0 copy-start.6
  396.2 1.0 copy.49
  397.2 0.0 copy-done.4
  397.2 0.6 copy.50
  397.8 0.0 copy-done.3
  397.8 0.8 copy.51
  398.6 0.0 copy-done.2
  398.6 0.8 copy.52
  399.4 0.0 copy-done.9
  399.4 0.6 copy.53
  400.0 0.0 copy-done.8
  400.0 0.6 copy.54
  400.6 0.0 copy-done.7
  400.6 0.6 copy.55
  401.2 0.0 copy-done.5
  401.2 0.6 copy.56
  401.8 0.0 copy-done.6
  401.8 0.6 copy.57
Async XLA Ops:
  390.1 5.0 %copy-start = (f32[2048,32]{1,0:T(8,128)S(1)}, f32[2048,32]{1,0:T(8,128)}, u32[]{:S(2)}) copy-start(f32[2048,32]{1,0:T(8,128)} %get-tuple-element.149) | copy-start | bytes 786436
  390.1 6.0 %copy-start.1 = (f32[256,1024]{1,0:T(8,128)S(1)}, f32[256,1024]{1,0:T(8,128)}, u32[]{:S(2)}) copy-start(f32[256,1024]{1,0:T(8,128)} %get-tuple-element.129) | copy-start | bytes 3145732
  392.9 4.3 %copy-start.4 = (f32[32,768]{1,0:T(8,128)S(1)}, f32[32,768]{1,0:T(8,128)}, u32[]{:S(2)}) copy-start(f32[32,768]{1,0:T(8,128)} %get-tuple-element.179) | copy-start | bytes 294916
  395.1 2.7 copy-start.3
  395.1 3.4 copy-start.2
  396.2 3.2 copy-start.9
  396.2 3.8 copy-start.8
  396.2 4.4 %copy-start.7 = (f32[12,128]{1,0:T(8,128)S(1)}, f32[12,128]{1,0:T(8,128)}, u32[]{:S(2)}) copy-start(f32[12,128]{1,0:T(8,128)} %get-tuple-element.138) | copy-start | bytes 18436
  396.2 5.0 %copy-start.5 = (f32[4,1792]{1,0:T(4,128)S(1)}, f32[4,1792]{1,0:T(4,128)}, u32[]{:S(2)}) copy-start(f32[4,1792]{1,0:T(4,128)} %get-tuple-element.188) | copy-start | bytes 86020
  396.2 5.6 %copy-start.6 = (f32[14,128]{1,0:T(8,128)S(1)}, f32[14,128]{1,0:T(8,128)}, u32[]{:S(2)}) copy-start(f32[14,128]{1,0:T(8,128)} %get-tuple-element.140) | copy-start | bytes 21508

commit v6 on v5

--- a/solution.py
+++ b/solution.py
@@ -806,17 +806,21 @@
     )(*args)
 
 
-def column_chunks(widths, aim=512):
-    pairs = []
+def column_chunks(widths, aim=512, lean=0, z_last=None):
+    pairs, late = [], []
     for p, width in enumerate(widths):
-        tiles, first, cuts = width // TILE, 0, []
-        pieces = 2 * max(1, (width + aim // 2) // (2 * aim))
-        for i in range(pieces):
-            cols = (tiles // pieces + (1 if i < tiles % pieces else 0)) * TILE
-            cuts.append((p, first, cols, ("xy", "yx")[i % 2]))
-            first += cols
-        pairs += [tuple(cuts[i : i + 2]) for i in range(0, pieces, 2)]
-    return pairs
+        tiles, first = width // TILE, 0
+        orders, to = (("xyz", "yxz"), late) if p == z_last else (("xy", "yx"), pairs)
+        count = max(1, (width + aim // 2) // (2 * aim)) if p != z_last else max(1, width // 512)
+        for i in range(count):
+            both = tiles // count + (1 if i < tiles % count else 0)
+            one = (both + (0 if p == z_last else lean) + 1) // 2
+            pair = []
+            for cols, order in ((one * TILE, orders[0]), ((both - one) * TILE, orders[1])):
+                pair.append((p, first, cols, order))
+                first += cols
+            to.append(tuple(pair))
+    return pairs + late
 
 
 def pairs_of(pairs, array):
@@ -827,6 +831,8 @@
 ORDERS = {
     "xy": ("far", "near", "x", "y"),
     "yx": ("far", "near", "y", "x"),
+    "xyz": ("x", "y", "far", "near"),
+    "yxz": ("y", "x", "far", "near"),
 }
 
 
@@ -1036,7 +1042,7 @@
     return jnp.concatenate(out, axis=1)
 
 
-def shards_into(w_attn, w_ssm_in, w_dt, w_out, w_down, conv, mix, out, down):
+def shards_into(w_attn, w_ssm_in, w_dt, w_out, conv, mix, out):
     f32, narrow = jnp.float32, jnp.bfloat16
     ssm_width = MH * MP
     xbc = w_ssm_in.shape[1] - ssm_width
@@ -1044,20 +1050,17 @@
     attn = w_attn.shape[1]
     conv[:, :xbc] = w_ssm_in[:, ssm_width:]
     conv[:, xbc:] = jnp.zeros((conv.shape[0], TILE), narrow)
-    conv[:, xbc : xbc + MH] = w_dt[...]
+    block = conv.shape[0]
+    row = lax.broadcasted_iota(jnp.int32, (block, block), 0)
+    same = row == lax.broadcasted_iota(jnp.int32, (block, block), 1)
+    conv[:, xbc : xbc + MH] = dot_nt(jnp.where(same, 1.0, 0.0).astype(narrow), w_dt[...]).astype(
+        narrow
+    )
     mix[:, :query] = pair_columns(w_attn[:, :query].astype(f32), False).astype(narrow)
     mix[:, query:attn] = w_attn[:, query:]
     mix[:, attn:] = w_ssm_in[:, :ssm_width]
-    turned = []
-    for i in range(w_out.shape[0] // TILE):
-        here = slice(i * TILE, (i + 1) * TILE)
-        tile = w_out[here].astype(f32).T
-        if i < PAIRS:
-            turned.append(tile)
-        else:
-            out[:, here] = tile.astype(narrow)
-        down[:, here] = w_down[here].astype(f32).T.astype(narrow)
-    out[:, :query] = pair_columns(jnp.concatenate(turned, axis=1), False).astype(narrow)
+    out[:, :query] = pair_columns(w_out[:, :query].astype(f32), False).astype(narrow)
+    out[:, query:] = w_out[:, query:]
 
 
 class Gather:
@@ -1148,27 +1151,29 @@
         out, out_t, lse, state_in, order, cosine, sine, head_params,
     ) = refs[:23]
     (
-        s_conv, s_mix, s_out, s_down, gains,
+        s_conv, s_mix, s_out, gains,
         attn_proj, dt_t, cum_t, heads, acc, top, total, arrived, sent, before,
         scan_send, scan_recv, send, recv, w_send, w_recv, w_local, rim_send, rim_recv,
     ) = refs[23:]
-    ins = (s_conv, s_mix, s_out, w_gate_up, s_down)
+    ins = (s_conv, s_mix, s_out, w_gate_up, w_down)
     others = partners()
     previous, following = around()
     greet(list(others.values()) + [previous, following])
     me = lax.axis_index("seq")
     rows, width = layer_x.shape
     info = places_of(lens, rows)
-    shards_into(w_attn, w_ssm_in, w_dt, w_out, w_down, s_conv, s_mix, s_out, s_down)
+    shards_into(w_attn, w_ssm_in, w_dt, w_out, s_conv, s_mix, s_out)
     gather = Gather(ins, fulls, pairs, w_send, w_recv, w_local, others)
     gather.own()
 
     first = len(pairs_of(pairs, 0)) + len(pairs_of(pairs, 1))
+    small = pairs_of(pairs, 2)
     waves = {}
     for n in reversed(range(len(pairs))):
         for stage in range(6):
             late = 1 if n >= first and stage >= 2 else 0
-            waves.setdefault(n + stage + late, []).append((n, stage))
+            wave = n - small[0] + 2 * stage if n in small else n + stage + late
+            waves.setdefault(wave, []).append((n, stage))
 
     def pump(*which):
         for wave in which:
@@ -1305,11 +1310,11 @@
     ssm_width = MH * MP
     xbc = conv_w.shape[1]
     widths = [
-        xbc + TILE, w_attn.shape[1] + ssm_width, w_out.shape[0], w_gate_up.shape[1],
-        w_down.shape[0],
+        xbc + TILE, w_attn.shape[1] + ssm_width, w_out.shape[1], w_gate_up.shape[1],
+        w_down.shape[1],
     ]
     count = len(widths)
-    pairs = column_chunks(widths)
+    pairs = column_chunks(widths, z_last=2)
     fulls = [shape_of((width, w), narrow) for w in widths]
     outs = fulls + [
         shape_of((rows, width), narrow),
@@ -1338,7 +1343,7 @@
     ]
     dma = pltpu.SemaphoreType.DMA
     scratch = [
-        *(pltpu.VMEM((block, widths[k]), narrow) for k in (0, 1, 2, 4)),
+        *(pltpu.VMEM((block, widths[k]), narrow) for k in (0, 1, 2)),
         pltpu.VMEM((8, width), f32),
         pltpu.VMEM((rows, query_width + pair_width), f32),
         pltpu.VMEM((TILE, rows), f32),
@@ -1389,7 +1394,7 @@
         copy.start()
     attn = attended.shape[1]
     ff = hidden.shape[1]
-    step = 256
+    step = 512
 
     def tiles(count, body):
         def one(j, carry):
@@ -1678,10 +1683,10 @@
     given = [
         (grad_rows.at[:, behind], half_grad),
         (hidden, their_hidden),
+        (d_mixer.at[:, behind], half_mixer),
+        (joined, their_joined),
         (normed_two.at[:, behind], half_two),
         (d_gu, their_gu),
-        (d_mixer.at[:, behind], half_mixer),
-        (joined, their_joined),
         (normed.at[:, behind], their_normed),
         (d_z, their_z),
     ]
@@ -1696,14 +1701,22 @@
     )
 
     def weights(k, left, left_half, right, theirs):
-        swaps[2 * k].wait_recv()
-        swaps[2 * k + 1].wait_recv()
+        first = 2 * (0, 2, 1, 3)[k]
+        swaps[first].wait_recv()
+        swaps[first + 1].wait_recv()
         left_t[:, :rows] = turn_over(left[:, :half])
         left_t[:, rows:] = turn_over(left_half[...])
         weight_products(left_t, right, theirs, partials[k])
 
-    def pump(*steps):
-        for n, stage in steps:
+    small = pairs_of(pairs, 2)
+    waves = {}
+    for n in range(len(pairs)):
+        for stage in range(5):
+            begin = n - small[0] if n in small else n
+            waves.setdefault(begin + stage, []).append((n, stage))
+
+    def pump(wave):
+        for n, stage in waves.pop(wave):
             scatter.step(n, stage)
 
     attend_back_start(q, grad, out_t, heads, grads, delta, acc)
@@ -1736,7 +1749,8 @@
         )
 
     weights(0, grad_rows, half_grad, hidden, their_hidden)
-    pump((0, 0))
+    weights(2, d_mixer, half_mixer, joined, their_joined)
+    pump(0)
     several(1, 2, 4)
     over_x = [
         remote(dkv.at[2 * k + 1], from_x.at[k], send.at[k], recv.at[k], others["x"])
@@ -1746,7 +1760,7 @@
         copy.start()
     scan.step(1)
     weights(1, normed_two, half_two, d_gu, their_gu)
-    pump((1, 0), (0, 1))
+    pump(1)
     several(4, 2, 2)
     over_far = [
         remote(dkv.at[4 + 2 * k], from_far.at[k], send.at[4 + k], recv.at[4 + k], others["far"])
@@ -1757,7 +1771,7 @@
         add(dkv.at[4 + 2 * k], from_x.at[2 + k])
         over_far[k].start()
     scan.step(2)
-    pump((2, 0), (1, 1), (0, 2))
+    pump(2)
     several(0, 2, 2)
     for k in range(2):
         over_x[k].wait_recv()
@@ -1766,13 +1780,12 @@
     add(dkv.at[2], from_far.at[1])
     over_near = remote(dkv.at[2], from_near, send.at[6], recv.at[6], others["near"])
     over_near.start()
-    weights(2, d_mixer, half_mixer, joined, their_joined)
     weights(3, normed, their_normed, d_z, their_z)
-    pump((3, 0), (2, 1), (1, 2), (0, 3))
+    pump(3)
     ssm_back_kernel(
         info, x, bc, dt, cum, d_ssm, head_params, dx, d_bc, d_cum, d_dt, g_skip, cols_t, d_rows
     )
-    pump((4, 0), (3, 1), (2, 2), (1, 3), (0, 4))
+    pump(4)
     scan.step(3)
     d_step = d_conv.at[:, pl.ds(xbc, TILE)]
     step_in = raw.at[pl.ds(RIM, rows), pl.ds(xbc, TILE)]
@@ -1786,7 +1799,7 @@
         previous,
     )
     rim.start()
-    pump((4, 1), (3, 2), (2, 3), (1, 4))
+    pump(5)
     over_far[0].wait_recv()
     over_near.wait_recv()
     attend_back_write(acc, dq)
@@ -1798,9 +1811,8 @@
     rope_back_kernel(dq, d_pair, cosine, sine, d_attn)
     rim.wait_recv()
     conv_back_end(info, d_pre, conv_w, d_conv.at[:, pl.ds(0, xbc)])
-    pump((4, 2), (3, 3), (2, 4))
-    pump((4, 3), (3, 4))
-    pump((4, 4))
+    for wave in sorted(waves):
+        pump(wave)
     scatter.finish()
     scan.finish()
     rim.wait_send()
@@ -1822,7 +1834,7 @@
     f32, narrow = jnp.float32, jnp.bfloat16
     dma = pltpu.SemaphoreType.DMA
     widths = [hidden.shape[1], d_gu.shape[1], joined.shape[1], d_z.shape[1]]
-    pairs = column_chunks(widths, 1024)
+    pairs = column_chunks(widths, 1024, 4, 2)
     own = half // 16
     outs = [
         shape_of((rows, xbc + TILE), narrow),
@@ -1888,13 +1900,13 @@
 def last_kernel(pairs, *refs):
     (
         d_conv, d_attn, d_z, full_conv, full_mix, normed, their_normed, x_own, d_middle, gains,
-        order, g_mlp, g_ssm, g_conv, head_sums, g_skip, sum_down, sum_out, sum_z,
-    ) = refs[:19]
+        order, g_mlp, g_ssm, g_conv, head_sums, g_skip, sum_out, sum_z,
+    ) = refs[:18]
     (
-        input_grad, g_attn_out, g_in_out, g_dt_out, g_out_out, g_down_out,
+        input_grad, g_attn_out, g_in_out, g_dt_out, g_out_out,
         norm_total, mlp_total, ssm_total, conv_total, conv_b_total, head_total,
-    ) = refs[19:31]
-    refs = refs[31:]
+    ) = refs[18:29]
+    refs = refs[29:]
     partials, arrived_w = refs[:2], refs[2:10]
     (
         out_conv, out_attn, their_conv, their_attn, left_t, d_normed, small_own, small_in, small_mid,
@@ -1993,12 +2005,8 @@
     small_step(2)
     query = QUERY_HEADS * HEAD_SIZE
     g_in_out[:, : sum_z.shape[1]] = sum_z[...]
-    moved = pair_columns(sum_out[:, :query], True)
-    for i in range(sum_out.shape[1] // TILE):
-        here = slice(i * TILE, (i + 1) * TILE)
-        tile = moved[:, here] if i < PAIRS else sum_out[:, here]
-        g_out_out[here] = tile.T
-        g_down_out[here] = sum_down[:, here].T
+    g_out_out[:, :query] = pair_columns(sum_out[:, :query], True)
+    g_out_out[:, query:] = sum_out[:, query:]
     scatter.step(1, 3)
     scatter.step(2, 3)
     small_step(3)
@@ -2038,14 +2046,13 @@
     total = (32 + 16 * (CONV + 1), TILE)
     block = half // 16
     xbc = g_conv.shape[1]
-    joined, ff = args[17].shape[1], args[16].shape[1]
+    joined = args[16].shape[1]
     outs = [
         shape_of((rows, width), f32),
         shape_of((block, widths[1]), f32),
         shape_of((block, d_z.shape[1] + xbc), f32),
         shape_of((block, MH), f32),
-        shape_of((joined, block), f32),
-        shape_of((ff, block), f32),
+        shape_of((block, joined), f32),
         shape_of((8, TILE), f32),
         shape_of((8, TILE), f32),
         shape_of((12, TILE), f32),
@@ -2082,6 +2089,30 @@
         4,
         100_000_000,
     )
+
+
+def settle_kernel(*refs):
+    count = len(refs) // 2
+    sems = refs[2 * count]
+    copies = [
+        pltpu.make_async_copy(refs[k], refs[count + k], sems.at[k]) for k in range(count)
+    ]
+    for copy in copies:
+        copy.start()
+    for copy in copies:
+        copy.wait()
+
+
+def settle(*arrays):
+    count = len(arrays)
+    return pl.pallas_call(
+        settle_kernel,
+        out_shape=[shape_of(a.shape, a.dtype) for a in arrays],
+        in_specs=[ANY] * count,
+        out_specs=[INTO_VMEM] * count,
+        scratch_shapes=[pltpu.SemaphoreType.DMA((count,))],
+        compiler_params=pltpu.CompilerParams(vmem_limit_bytes=60 * 1024 * 1024),
+    )(*arrays)
 
 
 def pair_heads(value, back=False):
@@ -2343,7 +2374,7 @@
         freqs,
         conv_w,
         conv_b.reshape(-1, TILE),
-        (w_attn, w_ssm_in, w_dt, w_out, w_gate_up, w_down),
+        (w_attn, w_ssm_in, w_dt.T, w_out.T, w_gate_up, w_down.T),
     )
     full_conv, full_mix, full_out, full_gu, full_down = full
     (
@@ -2369,12 +2400,19 @@
         d_gate_up, d_gate_z,
     )
     (
-        input_grad, grad_attn, grad_ssm_in, grad_dt, grad_out, grad_down, g_norm, g_mlp, g_ssm,
-        g_conv_w, g_conv_b, heads,
+        input_grad, grad_attn, grad_ssm_in, grad_dt, grad_out, g_norm, g_mlp, g_ssm, g_conv_w,
+        g_conv_b, heads,
     ) = last(
         d_conv_proj, d_attn_proj, d_gate_z, full_conv, full_mix, normed, their_normed, x_own,
-        d_middle, gains, order, g_mlp_gain, g_ssm_gain, g_conv, head_sums, g_skip_rows, sum_down,
-        sum_out, sum_z,
+        d_middle, gains, order, g_mlp_gain, g_ssm_gain, g_conv, head_sums, g_skip_rows, sum_out,
+        sum_z,
+    )
+    (
+        input_grad, grad_attn, grad_ssm_in, grad_dt, grad_out, sum_gu, sum_down, g_norm, g_mlp,
+        g_ssm, g_conv_w, g_conv_b, heads,
+    ) = settle(
+        input_grad, grad_attn, grad_ssm_in, grad_dt, grad_out, sum_gu, sum_down, g_norm, g_mlp,
+        g_ssm, g_conv_w, g_conv_b, heads,
     )
     return (
         layer_out[None],
@@ -2382,9 +2420,9 @@
         grad_attn,
         grad_ssm_in,
         grad_dt,
-        grad_out,
+        grad_out.T,
         sum_gu,
-        grad_down,
+        sum_down.T,
         g_norm.reshape(-1),
         g_mlp.reshape(-1),
         g_ssm.reshape(-1),

time: 409 us -> 382 us (0.934)
  local copies, waits for them, and re-layouts: 17.4 us -> 2.71 us
  Pallas kernels: 384 us -> 371 us
    unnamed x35 -> x1, local copies, waits for them, and re-layouts: 16 us -> 1.39 us
    pallas_call x3, Pallas kernels: 357 us -> 344 us  [comm_call(): pl.pallas_call(kernel, out_shape=list(outs), in_specs=in_specs, out_specs...]
where the time goes in v6:
time: 382 us; the launch traced here: 375 us
  Pallas kernels  371 us (97%)
    pallas_call x3, Pallas kernels, comm_call(): pl.pallas_call(kernel, out_shape=list(outs), in_specs=in_specs, out_specs...  344 us
    pallas_call x1, Pallas kernels, middle_part(): pl.pallas_call(middle_kernel, out_shape=outs, in_specs=[pl.BlockSpec(memo...  23.6 us

profile of v6, /device:TPU:0, one launch (start us, length us, event | category | flops | bytes accessed | tf_op | source)
XLA Modules:
  0.0 375.0 jit_solution(13791611088546414488)
XLA Ops:
  0.7 160.9 %shard_map.297 = (bf16[1024,1920]{1,0:T(8,128)(2,1)}, bf16[1024,2304]{1,0:T(8,128)(2,1)}, bf16[1024,2048]{1,0:T(8,128)(2,1)}, bf16[1024,4096]{1,0:T(8,128)(2,1)}...) custom-call(s32[1,3]{1,0:T(1,128)} %refs_0_.3, ...), custom_call_target="tpu_custom_call" | custom-call | bytes 200000000 | tf_op jit(solution)/shard_map/pallas_call | solution.py:796
  161.5 23.6 %shard_map.298 = (bf16[256,1024]{1,0:T(8,128)(2,1)}, bf16[256,2048]{1,0:T(8,128)(2,1)}, bf16[256,2048]{1,0:T(8,128)(2,1)}, bf16[256,4096]{1,0:T(8,128)(2,1)}, bf...) custom-call(s32[1,3]{1,0:T(1,128)} %refs_0_.3, ...), custom_call_target="tpu_custom_call" | custom-call | tf_op jit(solution)/shard_map/pallas_call | solution.py:1507
  185.2 126.4 %shard_map.299 = (bf16[256,1920]{1,0:T(8,128)(2,1)}, bf16[256,768]{1,0:T(8,128)(2,1)}, f32[8,1792]{1,0:T(8,128)}, f32[8,128]{1,0:T(8,128)}, f32[8,128]{1,0:T(8,1...) custom-call(s32[1,3]{1,0:T(1,128)} %refs_0_.3, ...), custom_call_target="tpu_custom_call" | custom-call | bytes 200000000 | tf_op jit(solution)/shard_map/pallas_call | solution.py:796
  311.6 57.1 %shard_map.300 = (f32[256,1024]{1,0:T(8,128)}, f32[32,768]{1,0:T(8,128)}, f32[32,3328]{1,0:T(8,128)}, f32[32,24]{1,0:T(8,128)}, f32[32,2048]{1,0:T(8,128)}, /*in...) custom-call(bf16[256,1920]{1,0:T(8,128)(2,1)} %get-tuple-element.127, ...), custom_call_target="tpu_custom_call" | custom-call | bytes 100000000 | tf_op jit(solution)/shard_map/pallas_call | solution.py:796
  368.7 3.3 shard_map.301
  372.0 1.3 slice_bitcast_fusion
  373.4 1.4 copy.34

commit v7 on v6

--- a/solution.py
+++ b/solution.py
@@ -1063,6 +1063,28 @@
     out[:, query:] = w_out[:, query:]
 
 
+class Stage:
+    def __init__(self, sources, targets, sems):
+        self.copies = [
+            pltpu.make_async_copy(source, target, sems.at[k])
+            for k, (source, target) in enumerate(zip(sources, targets))
+        ]
+        self.open = {}
+
+    def start(self, *which):
+        for k in which:
+            self.copies[k].start()
+            self.open[k] = True
+
+    def need(self, *which):
+        for k in which:
+            if self.open.pop(k, False):
+                self.copies[k].wait()
+
+    def finish(self):
+        self.need(*list(self.open))
+
+
 class Gather:
     def __init__(self, ins, outs, pairs, send, recv, local, others):
         self.ins, self.outs, self.pairs = ins, outs, pairs
@@ -1145,16 +1167,19 @@
     count, pairs, lens, bias, rate_log, skip, layer_x, layer_g, norm_gain, mlp_gain, freqs, conv_w,
     conv_b, w_attn, w_ssm_in, w_dt, w_out, w_gate_up, w_down, *refs
 ):
-    fulls, refs = refs[:count], refs[count:]
+    fulls, made, refs = refs[:count], refs[count : count + 23], refs[count + 23 :]
+    near, refs = refs[:25], refs[25:]
+    writes = Stage((*near,), (*fulls[:2], *made), refs[-1])
+    fulls = (*near[:2], *fulls[2:])
     (
         x_own, g_own, gains_own, normed, q, kv, gate_z, raw, pre, x, bc, y, state, dt, cum,
         out, out_t, lse, state_in, order, cosine, sine, head_params,
-    ) = refs[:23]
+    ) = near[2:]
     (
         s_conv, s_mix, s_out, gains,
         attn_proj, dt_t, cum_t, heads, acc, top, total, arrived, sent, before,
         scan_send, scan_recv, send, recv, w_send, w_recv, w_local, rim_send, rim_recv,
-    ) = refs[23:]
+    ) = refs[:-1]
     ins = (s_conv, s_mix, s_out, w_gate_up, w_down)
     others = partners()
     previous, following = around()
@@ -1240,6 +1265,7 @@
     ssm_states(info, x, bc, step_in, head_params, state, dt, cum, dt_t, cum_t)
     scan = StateScan(True, state, state_in, arrived, sent, before, scan_send, scan_recv, others)
     scan.step(0)
+    writes.start(0, 9, 10, 11, 12, 14, 15, 16)
     pump(mix_wave)
     project(full_mix, 0, attn_proj, 0, attn_cols)
     rope_kernel(attn_proj, cosine, sine, q, kv.at[pl.ds(0, rows)])
@@ -1248,6 +1274,7 @@
     copies[1].start()
     pump(mix_wave + 1)
     project(full_mix, attn_proj.shape[1], gate_z, 0, gate_cols)
+    writes.start(1, 8, 6, 2, 3, 4, 5, 21, 22, 23, 24)
     attend_start(q, heads, acc, top, total)
 
     def attend(r):
@@ -1279,12 +1306,14 @@
     several(0, 4, 2)
     pump(mix_wave + 3)
     ssm_local(info, x, bc, head_params, y, cum, dt_t, cum_t)
+    writes.start(13)
     scan.step(2)
     pump(mix_wave + 4)
     several(2, 4, 2)
     pump(mix_wave + 5)
     for r in (1, 3, 5, 7):
         copies[r].wait_recv()
+    writes.start(7)
     several(1, 2, 2)
     pump(mix_wave + 6)
     several(5, 2, 2)
@@ -1292,8 +1321,10 @@
     lse[...] = top[...] + jnp.log(total[...])
     attend_write(acc, total, out, out_t)
     scan.step(3)
+    writes.start(17, 18, 19, 20)
     pump(*sorted(waves))
     gather.finish()
+    writes.finish()
     scan.finish()
     rim.wait_send()
     for copy in copies.values():
@@ -1342,7 +1373,8 @@
         shape_of((8, TILE), f32),
     ]
     dma = pltpu.SemaphoreType.DMA
-    scratch = [
+    scratch = [pltpu.VMEM(o.shape, o.dtype) for o in (*outs[:2], *outs[count:])]
+    scratch += [
         *(pltpu.VMEM((block, widths[k]), narrow) for k in (0, 1, 2)),
         pltpu.VMEM((8, width), f32),
         pltpu.VMEM((rows, query_width + pair_width), f32),
@@ -1360,11 +1392,12 @@
         dma((count,)),
         dma((1,)),
         dma((1,)),
+        dma((25,)),
     ]
     result = comm_call(
         lambda *refs: front_kernel(count, pairs, *refs),
         outs,
-        [INTO_VMEM] * 2 + [ANY] * (count - 2) + [INTO_VMEM] * 23,
+        [ANY] * len(outs),
         (
             lens, bias, rate_log, skip, layer_x, layer_g, norm_gain, mlp_gain, freqs, conv_w,
             conv_b, *weights,
@@ -1657,15 +1690,15 @@
         d_z,
     ) = refs[:27]
     (
-        d_conv, d_attn, g_conv, head_sums, g_skip, their_normed, out_down, out_gu, out_out, out_z,
-    ) = refs[27:37]
-    refs = refs[37:]
+        d_conv, d_attn, g_conv, head_sums, g_skip, p_conv, p_attn, out_down, out_gu, out_out, out_z,
+    ) = refs[27:38]
+    refs = refs[38:]
     partials, refs = refs[:4], refs[4:]
     arrived_w, refs = refs[:16], refs[16:]
     (
-        half_grad, half_two, half_mixer, their_hidden, their_joined, their_gu, their_z, left_t,
-        heads, grads, delta, acc, dkv, from_x, from_far, from_near, dq, d_pair, d_state,
-        dx, d_bc, d_cum, d_dt, cols_t, d_rows, d_pre,
+        half_grad, half_two, half_mixer, their_hidden, their_joined, their_gu, their_z, their_normed,
+        their_conv, their_attn, left_t, heads, grads, delta, acc, dkv, from_x, from_far, from_near, dq, d_pair,
+        d_cum, d_dt, cols_t, d_rows, d_pre,
         arrived, sent, before, scan_send, scan_recv, send, recv, swap_send, swap_recv,
         w_send, w_recv, rim_send, rim_recv,
     ) = refs
@@ -1677,6 +1710,9 @@
     info = places_of(lens, rows)
     half = normed.shape[1] // 2
     xbc = pre.shape[1]
+    dx = d_pre.at[pl.ds(0, rows), pl.ds(0, x.shape[1])]
+    d_bc = d_pre.at[pl.ds(0, rows), pl.ds(x.shape[1], 2 * NS)]
+    d_state = arrived.at[0, pl.ds(0, NS)]
     scan = StateScan(False, pull, d_state, arrived, sent, before, scan_send, scan_recv, others)
     scan.step(0)
     behind = pl.ds(half, half)
@@ -1712,7 +1748,7 @@
     waves = {}
     for n in range(len(pairs)):
         for stage in range(5):
-            begin = n - small[0] if n in small else n
+            begin = 1 + (n - small[0]) // 2 if n in small else n
             waves.setdefault(begin + stage, []).append((n, stage))
 
     def pump(wave):
@@ -1749,8 +1785,8 @@
         )
 
     weights(0, grad_rows, half_grad, hidden, their_hidden)
+    pump(0)
     weights(2, d_mixer, half_mixer, joined, their_joined)
-    pump(0)
     several(1, 2, 4)
     over_x = [
         remote(dkv.at[2 * k + 1], from_x.at[k], send.at[k], recv.at[k], others["x"])
@@ -1809,10 +1845,22 @@
         + from_near[...].astype(jnp.float32)
     )
     rope_back_kernel(dq, d_pair, cosine, sine, d_attn)
+    last_swaps = [
+        remote(give, take, swap_send.at[8 + k], swap_recv.at[8 + k], others["core"])
+        for k, (give, take) in enumerate(((d_attn, their_attn), (d_conv, their_conv)))
+    ]
+    last_swaps[0].start()
     rim.wait_recv()
     conv_back_end(info, d_pre, conv_w, d_conv.at[:, pl.ds(0, xbc)])
+    last_swaps[1].start()
+    pump(6)
+    last_swaps[0].wait_recv()
+    weight_products(left_t, d_attn, their_attn, p_attn)
+    last_swaps[1].wait_recv()
+    weight_products(left_t, d_conv, their_conv, p_conv)
     for wave in sorted(waves):
         pump(wave)
+    swaps += last_swaps
     scatter.finish()
     scan.finish()
     rim.wait_send()
@@ -1842,13 +1890,17 @@
         shape_of((8, xbc), f32),
         shape_of((8, TILE), f32),
         shape_of((8, TILE), f32),
-        shape_of((rows, half), narrow),
+        shape_of((half, xbc + TILE), narrow),
+        shape_of((half, query_width + pair), narrow),
     ] + [shape_of((own, w), f32) for w in widths]
     scratch = [pltpu.VMEM((half, w), narrow) for w in widths]
     scratch += scatter_scratch(widths, half)
     scratch += [pltpu.VMEM((rows, half), narrow)] * 3
     scratch += [pltpu.VMEM(a.shape, narrow) for a in (hidden, joined, d_gu, d_z)]
     scratch += [
+        pltpu.VMEM((rows, half), narrow),
+        pltpu.VMEM((rows, xbc + TILE), narrow),
+        pltpu.VMEM((rows, query_width + pair), narrow),
         pltpu.VMEM((half, 2 * rows), narrow),
         pltpu.VMEM((QUERY_HEADS, rows, TILE), narrow),
         pltpu.VMEM((QUERY_HEADS, rows, TILE), narrow),
@@ -1860,9 +1912,6 @@
         pltpu.VMEM((rows, pair), narrow),
         pltpu.VMEM((rows, query_width), f32),
         pltpu.VMEM((rows, pair), f32),
-        pltpu.VMEM((NS, ssm_width), narrow),
-        pltpu.VMEM((rows, ssm_width), f32),
-        pltpu.VMEM((rows, 2 * NS), f32),
         pltpu.VMEM((rows, TILE), f32),
         pltpu.VMEM((rows, TILE), f32),
         pltpu.VMEM((TILE, rows), f32),
@@ -1871,8 +1920,8 @@
         *scan_scratch(ssm_width),
         dma((7,)),
         dma((7,)),
-        dma((8,)),
-        dma((8,)),
+        dma((10,)),
+        dma((10,)),
         dma((2 * len(pairs), 4, 4)),
         dma((2 * len(pairs), 4, 4)),
         dma((1,)),
@@ -1899,39 +1948,30 @@
 
 def last_kernel(pairs, *refs):
     (
-        d_conv, d_attn, d_z, full_conv, full_mix, normed, their_normed, x_own, d_middle, gains,
-        order, g_mlp, g_ssm, g_conv, head_sums, g_skip, sum_out, sum_z,
+        p_conv, p_attn, d_conv, d_attn, d_z, gains, g_mlp, g_ssm, g_conv, head_sums, g_skip,
+        sum_out, sum_z, *far_in,
     ) = refs[:18]
     (
         input_grad, g_attn_out, g_in_out, g_dt_out, g_out_out,
         norm_total, mlp_total, ssm_total, conv_total, conv_b_total, head_total,
     ) = refs[18:29]
     refs = refs[29:]
-    partials, arrived_w = refs[:2], refs[2:10]
+    arrived_w, near_in, refs = refs[:8], refs[8:13], refs[13:]
+    full_conv, full_mix, x_own, order, d_middle = near_in
     (
-        out_conv, out_attn, their_conv, their_attn, left_t, d_normed, small_own, small_in, small_mid,
-        small_out, swap_send, swap_recv, w_send, w_recv, small_send, small_recv,
-    ) = refs[10:]
+        out_conv, out_attn, d_normed, small_own, small_in, small_mid, small_out, in_sems,
+        w_send, w_recv, small_send, small_recv,
+    ) = refs
+    stage = Stage(far_in, near_in, in_sems)
+    stage.start(*range(5))
     others = partners()
     greet(list(others.values()))
-    rows, width = normed.shape
-    half = width // 2
-    swaps = [
-        remote(give, take, swap_send.at[k], swap_recv.at[k], others["core"])
-        for k, (give, take) in enumerate(((d_conv, their_conv), (d_attn, their_attn)))
-    ]
-    for copy in swaps:
-        copy.start()
-    scatter = Scatter(partials, (out_conv, out_attn), arrived_w, pairs, w_send, w_recv, others)
-    left_t[:, :rows] = turn_over(normed[:, :half])
-    left_t[:, rows:] = turn_over(their_normed[...])
-    swaps[0].wait_recv()
-    weight_products(left_t, d_conv, their_conv, partials[0])
+    rows, width = d_normed.shape
+    scatter = Scatter((p_conv, p_attn), (out_conv, out_attn), arrived_w, pairs, w_send, w_recv, others)
     scatter.step(0, 0)
     scatter.step(1, 0)
-    swaps[1].wait_recv()
-    weight_products(left_t, d_attn, their_attn, partials[1])
     scatter.step(2, 0)
+    stage.need(0, 1)
     step = 256
     attn = d_attn.shape[1]
 
@@ -1945,6 +1985,7 @@
         return carry
 
     lax.fori_loop(0, width // step, back_out, 0)
+    stage.need(2, 3, 4)
     scatter.step(0, 1)
     scatter.step(1, 1)
     wide = x_own[...].astype(jnp.float32)
@@ -2030,23 +2071,22 @@
     g_attn_out[:, :query] = pair_columns(out_attn[:, :query], True)
     g_attn_out[:, query:] = out_attn[:, query:]
     scatter.finish()
-    for copy in swaps + small_copies:
+    for copy in small_copies:
         copy.wait_send()
 
 
-def last(*args):
-    d_conv, d_attn, d_z, normed = args[0], args[1], args[2], args[5]
-    g_conv = args[13]
-    rows, width = normed.shape
-    half = width // 2
+def last(near, far):
+    p_conv, p_attn, d_z, g_conv, sum_out = near[0], near[1], near[4], near[8], near[11]
+    rows, width = far[2].shape
+    half = p_conv.shape[0]
     f32, narrow = jnp.float32, jnp.bfloat16
     dma = pltpu.SemaphoreType.DMA
-    widths = [d_conv.shape[1], d_attn.shape[1]]
+    widths = [p_conv.shape[1], p_attn.shape[1]]
     pairs = column_chunks(widths)
     total = (32 + 16 * (CONV + 1), TILE)
     block = half // 16
     xbc = g_conv.shape[1]
-    joined = args[16].shape[1]
+    joined = sum_out.shape[1]
     outs = [
         shape_of((rows, width), f32),
         shape_of((block, widths[1]), f32),
@@ -2060,20 +2100,16 @@
         shape_of((xbc // TILE, TILE), f32),
         shape_of((8, TILE), f32),
     ]
-    scratch = [pltpu.VMEM((half, w), narrow) for w in widths]
-    scratch += scatter_scratch(widths, half)
+    scratch = scatter_scratch(widths, half)
+    scratch += [pltpu.VMEM(a.shape, a.dtype) for a in far]
     scratch += [pltpu.VMEM((block, w), f32) for w in widths]
     scratch += [
-        pltpu.VMEM(d_conv.shape, narrow),
-        pltpu.VMEM(d_attn.shape, narrow),
-        pltpu.VMEM((half, 2 * rows), narrow),
         pltpu.VMEM((rows, width), f32),
         pltpu.VMEM(total, f32),
         pltpu.VMEM((5, *total), f32),
         pltpu.VMEM((4, *total), f32),
         pltpu.VMEM(total, f32),
-        dma((2,)),
-        dma((2,)),
+        dma((5,)),
         dma((2 * len(pairs), 4, 4)),
         dma((2 * len(pairs), 4, 4)),
         dma((5,)),
@@ -2083,8 +2119,8 @@
         lambda *refs: last_kernel(pairs, *refs),
         outs,
         [INTO_VMEM] * len(outs),
-        args,
-        [INTO_VMEM] * len(args),
+        (*near, *far),
+        [INTO_VMEM] * len(near) + [ANY] * len(far),
         scratch,
         4,
         100_000_000,
@@ -2391,8 +2427,8 @@
         full_down,
     )
     (
-        d_conv_proj, d_attn_proj, g_conv, head_sums, g_skip_rows, their_normed, sum_down, sum_gu,
-        sum_out, sum_z,
+        d_conv_proj, d_attn_proj, g_conv, head_sums, g_skip_rows, part_conv, part_attn, sum_down,
+        sum_gu, sum_out, sum_z,
     ) = back(
         seq_lengths, head_params, conv_w, cosine, sine, queries, all_pairs, attended_gradient,
         attended_t, log_total, pull, inputs_x, inputs_bc, steps_dt, running_decay, d_ssm_out,
@@ -2403,9 +2439,11 @@
         input_grad, grad_attn, grad_ssm_in, grad_dt, grad_out, g_norm, g_mlp, g_ssm, g_conv_w,
         g_conv_b, heads,
     ) = last(
-        d_conv_proj, d_attn_proj, d_gate_z, full_conv, full_mix, normed, their_normed, x_own,
-        d_middle, gains, order, g_mlp_gain, g_ssm_gain, g_conv, head_sums, g_skip_rows, sum_out,
-        sum_z,
+        (
+            part_conv, part_attn, d_conv_proj, d_attn_proj, d_gate_z, gains, g_mlp_gain,
+            g_ssm_gain, g_conv, head_sums, g_skip_rows, sum_out, sum_z,
+        ),
+        (full_conv, full_mix, x_own, order, d_middle),
     )
     (
         input_grad, grad_attn, grad_ssm_in, grad_dt, grad_out, sum_gu, sum_down, g_norm, g_mlp,

time: 382 us -> 371 us (0.971)
  Pallas kernels: 371 us -> 361 us
    pallas_call x3, Pallas kernels: 344 us -> 334 us  [comm_call(): pl.pallas_call(kernel, out_shape=list(outs), in_specs=in_specs, out_specs...]
where the time goes in v7:
time: 371 us; the launch traced here: 364 us
  Pallas kernels  361 us (97%)
    pallas_call x3, Pallas kernels, comm_call(): pl.pallas_call(kernel, out_shape=list(outs), in_specs=in_specs, out_specs...  334 us
    pallas_call x1, Pallas kernels, middle_part(): pl.pallas_call(middle_kernel, out_shape=outs, in_specs=[pl.BlockSpec(memo...  23.6 us

profile of v7, /device:TPU:0, one launch (start us, length us, event | category | flops | bytes accessed | tf_op | source)
XLA Modules:
  0.0 364.3 jit_solution(2168889482359336831)
XLA Ops:
  0.7 153.1 %shard_map.297 = (bf16[1024,1920]{1,0:T(8,128)(2,1)}, bf16[1024,2304]{1,0:T(8,128)(2,1)}, bf16[1024,2048]{1,0:T(8,128)(2,1)}, bf16[1024,4096]{1,0:T(8,128)(2,1)}...) custom-call(s32[1,3]{1,0:T(1,128)} %refs_0_.3, ...), custom_call_target="tpu_custom_call" | custom-call | bytes 200000000 | tf_op jit(solution)/shard_map/pallas_call | solution.py:796
  153.7 23.6 %shard_map.298 = (bf16[256,1024]{1,0:T(8,128)(2,1)}, bf16[256,2048]{1,0:T(8,128)(2,1)}, bf16[256,2048]{1,0:T(8,128)(2,1)}, bf16[256,4096]{1,0:T(8,128)(2,1)}, bf...) custom-call(s32[1,3]{1,0:T(1,128)} %refs_0_.3, ...), custom_call_target="tpu_custom_call" | custom-call | tf_op jit(solution)/shard_map/pallas_call | solution.py:1540
  177.4 134.6 %shard_map.299 = (bf16[256,1920]{1,0:T(8,128)(2,1)}, bf16[256,768]{1,0:T(8,128)(2,1)}, f32[8,1792]{1,0:T(8,128)}, f32[8,128]{1,0:T(8,128)}, f32[8,128]{1,0:T(8,1...) custom-call(s32[1,3]{1,0:T(1,128)} %refs_0_.3, ...), custom_call_target="tpu_custom_call" | custom-call | bytes 200000000 | tf_op jit(solution)/shard_map/pallas_call | solution.py:796
  311.9 46.1 %shard_map.300 = (f32[256,1024]{1,0:T(8,128)}, f32[32,768]{1,0:T(8,128)}, f32[32,3328]{1,0:T(8,128)}, f32[32,24]{1,0:T(8,128)}, f32[32,2048]{1,0:T(8,128)}, /*in...) custom-call(bf16[512,1920]{1,0:T(8,128)(2,1)} %get-tuple-element.128, ...), custom_call_target="tpu_custom_call" | custom-call | bytes 100000000 | tf_op jit(solution)/shard_map/pallas_call | solution.py:796
  358.0 3.3 shard_map.301
  361.3 1.3 slice_bitcast_fusion
  362.6 1.4 copy.34

commit v8 on v7

--- a/solution.py
+++ b/solution.py
@@ -1413,10 +1413,16 @@
 def middle_kernel(
     lens, y, bc, cum, state_in, state_own, z, ssm_gain, attended, x_own, g_own, gains, order,
     hbm_out, hbm_gu, hbm_down,
-    layer_out, joined, hidden, d_gu, normed_two, d_mixer, d_middle, d_ssm, d_z, pull, att_grad,
+    far_layer, far_joined, far_hidden, far_gu, far_two, far_mixer, far_middle, d_ssm, d_z, pull, att_grad,
     g_ssm, g_mlp,
-    w_out, w_gu, w_down, ssm_out, scale, middle, gate_up, d_normed, dy, narrow, sems,
+    w_out, w_gu, w_down, ssm_out, scale, middle, gate_up, d_normed, dy, narrow, layer_out,
+    joined, hidden, d_gu, normed_two, d_mixer, d_middle, sems, out_sems,
 ):
+    writes = Stage(
+        (layer_out, joined, hidden, d_gu, normed_two, d_mixer, d_middle),
+        (far_layer, far_joined, far_hidden, far_gu, far_two, far_mixer, far_middle),
+        out_sems,
+    )
     rows, width = x_own.shape
     info = places_of(lens, rows)
     copies = [
@@ -1441,6 +1447,7 @@
         info, y, bc, cum, state_in, z, ssm_gain, ssm_out,
         joined.at[:, pl.ds(attn, joined.shape[1] - attn)], scale,
     )
+    writes.start(1)
     copies[0].wait()
 
     def add_mixers(here, first):
@@ -1450,6 +1457,7 @@
     wide = middle[...]
     r = lax.rsqrt(jnp.mean(wide * wide, axis=-1, keepdims=True) + NORM_EPS)
     normed_two[...] = (wide * r * gains[1:2]).astype(jnp.bfloat16)
+    writes.start(4)
     copies[1].wait()
 
     def up_project(here, first):
@@ -1461,6 +1469,7 @@
         hidden[:, here] = (gate * jax.nn.sigmoid(gate) * up).astype(jnp.bfloat16)
 
     tiles(ff, up_project)
+    writes.start(2)
     copies[2].wait()
 
     def down_project(here, first):
@@ -1472,6 +1481,7 @@
         layer_out[:, here] = dot_nt(narrow[...], order[here]).astype(jnp.bfloat16)
 
     tiles(width, plain)
+    writes.start(0)
 
     def down_back(here, first):
         there = pl.ds(pl.multiple_of(ff + first, step), step)
@@ -1483,6 +1493,7 @@
         d_gu[:, there] = (d_hidden * gate * sig).astype(jnp.bfloat16)
 
     tiles(ff, down_back)
+    writes.start(3)
 
     def up_back(here, first):
         d_normed[:, here] = dot_nt(d_gu[...], w_gu[here])
@@ -1496,6 +1507,7 @@
     total = g_own[...].astype(jnp.float32) + r * (inner - wide * (r * r * coeff))
     d_middle[...] = total
     d_mixer[...] = total.astype(jnp.bfloat16)
+    writes.start(5, 6)
 
     def att_back(here, first):
         att_grad[:, here] = dot(d_mixer[...], w_out[:, here]).astype(jnp.bfloat16)
@@ -1511,6 +1523,7 @@
         info, dy, ssm_out, z, scale, ssm_gain, cum, bc, d_ssm, d_z, pull.at[pl.ds(0, NS)], g_ssm
     )
     pull[NS:] = state_own[NS:]
+    writes.finish()
 
 
 def middle_part(lens, y, bc, cum, state_in, state_own, z, ssm_gain, attended, x_own, g_own, gains, order, w_out, w_gu, w_down):
@@ -1541,7 +1554,7 @@
         middle_kernel,
         out_shape=outs,
         in_specs=[pl.BlockSpec(memory_space=pltpu.SMEM)] + [INTO_VMEM] * 12 + [ANY] * 3,
-        out_specs=[INTO_VMEM] * len(outs),
+        out_specs=[ANY] * 7 + [INTO_VMEM] * (len(outs) - 7),
         scratch_shapes=[
             pltpu.VMEM(w_out.shape, narrow),
             pltpu.VMEM(w_gu.shape, narrow),
@@ -1553,7 +1566,9 @@
             pltpu.VMEM((rows, width), f32),
             pltpu.VMEM((rows, ssm_width), f32),
             pltpu.VMEM((rows, width), narrow),
+            *(pltpu.VMEM(o.shape, o.dtype) for o in outs[:7]),
             pltpu.SemaphoreType.DMA((3,)),
+            pltpu.SemaphoreType.DMA((7,)),
         ],
         compiler_params=pltpu.CompilerParams(vmem_limit_bytes=60 * 1024 * 1024),
     )(*args)
@@ -1684,15 +1699,19 @@
 
 
 def back_kernel(pairs, *refs):
+    lens, far, refs = refs[0], refs[1:27], refs[27:]
+    outs, near, refs = refs[:11], refs[11:37], refs[37:]
+    loads = Stage(far, near, refs[-1])
+    loads.start(21, 22, 9, 20, 23, 4, 5, 6, 7, 8, 19, 24, 18, 25, *range(10, 18), *range(4))
     (
-        lens, head_params, conv_w, cosine, sine, q, kv, grad, out_t, lse, pull, x, bc, dt, cum,
+        head_params, conv_w, cosine, sine, q, kv, grad, out_t, lse, pull, x, bc, dt, cum,
         d_ssm, raw, state_in, pre, normed, normed_two, d_mixer, grad_rows, hidden, joined, d_gu,
         d_z,
-    ) = refs[:27]
+    ) = near
     (
         d_conv, d_attn, g_conv, head_sums, g_skip, p_conv, p_attn, out_down, out_gu, out_out, out_z,
-    ) = refs[27:38]
-    refs = refs[38:]
+    ) = outs
+    refs = refs[:-1]
     partials, refs = refs[:4], refs[4:]
     arrived_w, refs = refs[:16], refs[16:]
     (
@@ -1714,17 +1733,18 @@
     d_bc = d_pre.at[pl.ds(0, rows), pl.ds(x.shape[1], 2 * NS)]
     d_state = arrived.at[0, pl.ds(0, NS)]
     scan = StateScan(False, pull, d_state, arrived, sent, before, scan_send, scan_recv, others)
+    loads.need(9)
     scan.step(0)
     behind = pl.ds(half, half)
     given = [
-        (grad_rows.at[:, behind], half_grad),
-        (hidden, their_hidden),
-        (d_mixer.at[:, behind], half_mixer),
-        (joined, their_joined),
-        (normed_two.at[:, behind], half_two),
-        (d_gu, their_gu),
-        (normed.at[:, behind], their_normed),
-        (d_z, their_z),
+        (far[21].at[:, behind], half_grad),
+        (far[22], their_hidden),
+        (far[20].at[:, behind], half_mixer),
+        (far[23], their_joined),
+        (far[19].at[:, behind], half_two),
+        (far[24], their_gu),
+        (far[18].at[:, behind], their_normed),
+        (far[25], their_z),
     ]
     swaps = [
         remote(give, take, swap_send.at[k], swap_recv.at[k], others["core"])
@@ -1738,6 +1758,7 @@
 
     def weights(k, left, left_half, right, theirs):
         first = 2 * (0, 2, 1, 3)[k]
+        loads.need(*((21, 22), (19, 24), (20, 23), (18, 25))[k])
         swaps[first].wait_recv()
         swaps[first + 1].wait_recv()
         left_t[:, :rows] = turn_over(left[:, :half])
@@ -1755,6 +1776,7 @@
         for n, stage in waves.pop(wave):
             scatter.step(n, stage)
 
+    loads.need(4, 5, 6, 7, 8)
     attend_back_start(q, grad, out_t, heads, grads, delta, acc)
 
     def block_back(r):
@@ -1818,6 +1840,7 @@
     over_near.start()
     weights(3, normed, their_normed, d_z, their_z)
     pump(3)
+    loads.need(*range(10, 18), *range(4))
     ssm_back_kernel(
         info, x, bc, dt, cum, d_ssm, head_params, dx, d_bc, d_cum, d_dt, g_skip, cols_t, d_rows
     )
@@ -1861,6 +1884,7 @@
     for wave in sorted(waves):
         pump(wave)
     swaps += last_swaps
+    loads.finish()
     scatter.finish()
     scan.finish()
     rim.wait_send()
@@ -1893,7 +1917,8 @@
         shape_of((half, xbc + TILE), narrow),
         shape_of((half, query_width + pair), narrow),
     ] + [shape_of((own, w), f32) for w in widths]
-    scratch = [pltpu.VMEM((half, w), narrow) for w in widths]
+    scratch = [pltpu.VMEM(a.shape, a.dtype) for a in args]
+    scratch += [pltpu.VMEM((half, w), narrow) for w in widths]
     scratch += scatter_scratch(widths, half)
     scratch += [pltpu.VMEM((rows, half), narrow)] * 3
     scratch += [pltpu.VMEM(a.shape, narrow) for a in (hidden, joined, d_gu, d_z)]
@@ -1926,13 +1951,14 @@
         dma((2 * len(pairs), 4, 4)),
         dma((1,)),
         dma((1,)),
+        dma((len(args),)),
     ]
     return comm_call(
         lambda *refs: back_kernel(pairs, *refs),
         outs,
         [INTO_VMEM] * len(outs),
         (lens, *args),
-        [pl.BlockSpec(memory_space=pltpu.SMEM)] + [INTO_VMEM] * len(args),
+        [pl.BlockSpec(memory_space=pltpu.SMEM)] + [ANY] * len(args),
         scratch,
         2,
         200_000_000,

time: 371 us -> 366 us (0.987)
  Pallas kernels: 361 us -> 356 us
    pallas_call x3, Pallas kernels: 334 us -> 328 us  [comm_call(): pl.pallas_call(kernel, out_shape=list(outs), in_specs=in_specs, out_specs...]
where the time goes in v8:
time: 366 us; the launch traced here: 360 us
  Pallas kernels  356 us (97%)
    pallas_call x3, Pallas kernels, comm_call(): pl.pallas_call(kernel, out_shape=list(outs), in_specs=in_specs, out_specs...  328 us
    pallas_call x1, Pallas kernels, middle_part(): pl.pallas_call(middle_kernel, out_shape=outs, in_specs=[pl.BlockSpec(memo...  24.2 us

profile of v8, /device:TPU:0, one launch (start us, length us, event | category | flops | bytes accessed | tf_op | source)
XLA Modules:
  0.0 359.6 jit_solution(11309940173630637533)
XLA Ops:
  0.7 153.1 %shard_map.297 = (bf16[1024,1920]{1,0:T(8,128)(2,1)}, bf16[1024,2304]{1,0:T(8,128)(2,1)}, bf16[1024,2048]{1,0:T(8,128)(2,1)}, bf16[1024,4096]{1,0:T(8,128)(2,1)}...) custom-call(s32[1,3]{1,0:T(1,128)} %refs_0_.3, ...), custom_call_target="tpu_custom_call" | custom-call | bytes 200000000 | tf_op jit(solution)/shard_map/pallas_call | solution.py:796
  153.7 24.2 %shard_map.298 = (bf16[256,1024]{1,0:T(8,128)(2,1)}, bf16[256,2048]{1,0:T(8,128)(2,1)}, bf16[256,2048]{1,0:T(8,128)(2,1)}, bf16[256,4096]{1,0:T(8,128)(2,1)}, bf...) custom-call(s32[1,3]{1,0:T(1,128)} %refs_0_.3, ...), custom_call_target="tpu_custom_call" | custom-call | tf_op jit(solution)/shard_map/pallas_call | solution.py:1553
  178.0 129.3 %shard_map.299 = (bf16[256,1920]{1,0:T(8,128)(2,1)}, bf16[256,768]{1,0:T(8,128)(2,1)}, f32[8,1792]{1,0:T(8,128)}, f32[8,128]{1,0:T(8,128)}, f32[8,128]{1,0:T(8,1...) custom-call(s32[1,3]{1,0:T(1,128)} %refs_0_.3, ...), custom_call_target="tpu_custom_call" | custom-call | bytes 200000000 | tf_op jit(solution)/shard_map/pallas_call | solution.py:796
  307.3 46.0 %shard_map.300 = (f32[256,1024]{1,0:T(8,128)}, f32[32,768]{1,0:T(8,128)}, f32[32,3328]{1,0:T(8,128)}, f32[32,24]{1,0:T(8,128)}, f32[32,2048]{1,0:T(8,128)}, /*in...) custom-call(bf16[512,1920]{1,0:T(8,128)(2,1)} %get-tuple-element.128, ...), custom_call_target="tpu_custom_call" | custom-call | bytes 100000000 | tf_op jit(solution)/shard_map/pallas_call | solution.py:796
  353.3 3.3 shard_map.301
  356.6 1.3 slice_bitcast_fusion
  358.0 1.4 copy.34

commit v9 on v8

--- a/solution.py
+++ b/solution.py
@@ -1413,16 +1413,10 @@
 def middle_kernel(
     lens, y, bc, cum, state_in, state_own, z, ssm_gain, attended, x_own, g_own, gains, order,
     hbm_out, hbm_gu, hbm_down,
-    far_layer, far_joined, far_hidden, far_gu, far_two, far_mixer, far_middle, d_ssm, d_z, pull, att_grad,
+    layer_out, joined, hidden, d_gu, normed_two, d_mixer, d_middle, d_ssm, d_z, pull, att_grad,
     g_ssm, g_mlp,
-    w_out, w_gu, w_down, ssm_out, scale, middle, gate_up, d_normed, dy, narrow, layer_out,
-    joined, hidden, d_gu, normed_two, d_mixer, d_middle, sems, out_sems,
+    w_out, w_gu, w_down, ssm_out, scale, middle, gate_up, d_normed, dy, narrow, sems,
 ):
-    writes = Stage(
-        (layer_out, joined, hidden, d_gu, normed_two, d_mixer, d_middle),
-        (far_layer, far_joined, far_hidden, far_gu, far_two, far_mixer, far_middle),
-        out_sems,
-    )
     rows, width = x_own.shape
     info = places_of(lens, rows)
     copies = [
@@ -1447,7 +1441,6 @@
         info, y, bc, cum, state_in, z, ssm_gain, ssm_out,
         joined.at[:, pl.ds(attn, joined.shape[1] - attn)], scale,
     )
-    writes.start(1)
     copies[0].wait()
 
     def add_mixers(here, first):
@@ -1457,7 +1450,6 @@
     wide = middle[...]
     r = lax.rsqrt(jnp.mean(wide * wide, axis=-1, keepdims=True) + NORM_EPS)
     normed_two[...] = (wide * r * gains[1:2]).astype(jnp.bfloat16)
-    writes.start(4)
     copies[1].wait()
 
     def up_project(here, first):
@@ -1469,7 +1461,6 @@
         hidden[:, here] = (gate * jax.nn.sigmoid(gate) * up).astype(jnp.bfloat16)
 
     tiles(ff, up_project)
-    writes.start(2)
     copies[2].wait()
 
     def down_project(here, first):
@@ -1481,7 +1472,6 @@
         layer_out[:, here] = dot_nt(narrow[...], order[here]).astype(jnp.bfloat16)
 
     tiles(width, plain)
-    writes.start(0)
 
     def down_back(here, first):
         there = pl.ds(pl.multiple_of(ff + first, step), step)
@@ -1493,7 +1483,6 @@
         d_gu[:, there] = (d_hidden * gate * sig).astype(jnp.bfloat16)
 
     tiles(ff, down_back)
-    writes.start(3)
 
     def up_back(here, first):
         d_normed[:, here] = dot_nt(d_gu[...], w_gu[here])
@@ -1507,7 +1496,6 @@
     total = g_own[...].astype(jnp.float32) + r * (inner - wide * (r * r * coeff))
     d_middle[...] = total
     d_mixer[...] = total.astype(jnp.bfloat16)
-    writes.start(5, 6)
 
     def att_back(here, first):
         att_grad[:, here] = dot(d_mixer[...], w_out[:, here]).astype(jnp.bfloat16)
@@ -1523,7 +1511,6 @@
         info, dy, ssm_out, z, scale, ssm_gain, cum, bc, d_ssm, d_z, pull.at[pl.ds(0, NS)], g_ssm
     )
     pull[NS:] = state_own[NS:]
-    writes.finish()
 
 
 def middle_part(lens, y, bc, cum, state_in, state_own, z, ssm_gain, attended, x_own, g_own, gains, order, w_out, w_gu, w_down):
@@ -1554,7 +1541,7 @@
         middle_kernel,
         out_shape=outs,
         in_specs=[pl.BlockSpec(memory_space=pltpu.SMEM)] + [INTO_VMEM] * 12 + [ANY] * 3,
-        out_specs=[ANY] * 7 + [INTO_VMEM] * (len(outs) - 7),
+        out_specs=[INTO_VMEM] * len(outs),
         scratch_shapes=[
             pltpu.VMEM(w_out.shape, narrow),
             pltpu.VMEM(w_gu.shape, narrow),
@@ -1566,9 +1553,7 @@
             pltpu.VMEM((rows, width), f32),
             pltpu.VMEM((rows, ssm_width), f32),
             pltpu.VMEM((rows, width), narrow),
-            *(pltpu.VMEM(o.shape, o.dtype) for o in outs[:7]),
             pltpu.SemaphoreType.DMA((3,)),
-            pltpu.SemaphoreType.DMA((7,)),
         ],
         compiler_params=pltpu.CompilerParams(vmem_limit_bytes=60 * 1024 * 1024),
     )(*args)
@@ -2092,7 +2077,7 @@
             conv_total[k : k + 1, i * TILE : (i + 1) * TILE] = small_out[place : place + 1]
     conv_b_total[...] = small_out[32 + 16 * CONV : 32 + 16 * CONV + conv_tiles]
     g_in_out[:, g_in_out.shape[1] - g_conv.shape[1] :] = out_conv[:, : g_conv.shape[1]]
-    g_dt_out[...] = out_conv[:, g_conv.shape[1] : g_conv.shape[1] + MH]
+    g_dt_out[...] = out_conv[:, g_conv.shape[1] :].T[:MH]
     query = QUERY_HEADS * HEAD_SIZE
     g_attn_out[:, :query] = pair_columns(out_attn[:, :query], True)
     g_attn_out[:, query:] = out_attn[:, query:]
@@ -2117,7 +2102,7 @@
         shape_of((rows, width), f32),
         shape_of((block, widths[1]), f32),
         shape_of((block, d_z.shape[1] + xbc), f32),
-        shape_of((block, MH), f32),
+        shape_of((MH, block), f32),
         shape_of((block, joined), f32),
         shape_of((8, TILE), f32),
         shape_of((8, TILE), f32),
@@ -2483,7 +2468,7 @@
         input_grad[None],
         grad_attn,
         grad_ssm_in,
-        grad_dt,
+        grad_dt.T,
         grad_out.T,
         sum_gu,
         sum_down.T,

time: 366 us -> 364 us (level)
  no operation moved by 1% of the time
where the time goes in v9:
time: 364 us; the launch traced here: 358 us
  Pallas kernels  355 us (98%)
    pallas_call x3, Pallas kernels, comm_call(): pl.pallas_call(kernel, out_shape=list(outs), in_specs=in_specs, out_specs...  328 us
    pallas_call x1, Pallas kernels, middle_part(): pl.pallas_call(middle_kernel, out_shape=outs, in_specs=[pl.BlockSpec(memo...  23.6 us

profile of v9, /device:TPU:0, one launch (start us, length us, event | category | flops | bytes accessed | tf_op | source)
XLA Modules:
  0.0 357.6 jit_solution(16157952252038926777)
XLA Ops:
  0.7 153.1 %shard_map.297 = (bf16[1024,1920]{1,0:T(8,128)(2,1)}, bf16[1024,2304]{1,0:T(8,128)(2,1)}, bf16[1024,2048]{1,0:T(8,128)(2,1)}, bf16[1024,4096]{1,0:T(8,128)(2,1)}...) custom-call(s32[1,3]{1,0:T(1,128)} %refs_0_.3, ...), custom_call_target="tpu_custom_call" | custom-call | bytes 200000000 | tf_op jit(solution)/shard_map/pallas_call | solution.py:796
  153.7 23.6 %shard_map.298 = (bf16[256,1024]{1,0:T(8,128)(2,1)}, bf16[256,2048]{1,0:T(8,128)(2,1)}, bf16[256,2048]{1,0:T(8,128)(2,1)}, bf16[256,4096]{1,0:T(8,128)(2,1)}, bf...) custom-call(s32[1,3]{1,0:T(1,128)} %refs_0_.3, ...), custom_call_target="tpu_custom_call" | custom-call | tf_op jit(solution)/shard_map/pallas_call | solution.py:1540
  177.4 129.4 %shard_map.299 = (bf16[256,1920]{1,0:T(8,128)(2,1)}, bf16[256,768]{1,0:T(8,128)(2,1)}, f32[8,1792]{1,0:T(8,128)}, f32[8,128]{1,0:T(8,128)}, f32[8,128]{1,0:T(8,1...) custom-call(s32[1,3]{1,0:T(1,128)} %refs_0_.3, ...), custom_call_target="tpu_custom_call" | custom-call | bytes 200000000 | tf_op jit(solution)/shard_map/pallas_call | solution.py:796
  306.7 46.0 %shard_map.300 = (f32[256,1024]{1,0:T(8,128)}, f32[32,768]{1,0:T(8,128)}, f32[32,3328]{1,0:T(8,128)}, f32[24,32]{1,0:T(8,128)}, f32[32,2048]{1,0:T(8,128)}, /*in...) custom-call(bf16[512,1920]{1,0:T(8,128)(2,1)} %get-tuple-element.128, ...), custom_call_target="tpu_custom_call" | custom-call | bytes 100000000 | tf_op jit(solution)/shard_map/pallas_call | solution.py:796
  352.7 3.3 shard_map.301
  356.1 1.3 slice_bitcast_fusion
